TPU v7x, 32 devices: a whole 2x2x4 slice. The times are simulated.
32 devices in a mesh: gx: 4 (over y, x), gy: 8 (over z, core).
Axes of the slice: x: 2, y: 2, z: 4, core: 2. Of those that a mesh axis runs over, the one named last changes fastest.
Arguments:
- xi_coarse: float32 [512, 1024], P('gx', 'gy'), may hold values from -6 to 6
- xi_middle: float32 [1024, 2048], P('gx', 'gy'), may hold values from -6 to 6
- xi_fine: float32 [2048, 4096], P('gx', 'gy'), may hold values from -6 to 6
- coef_middle: bfloat16 [4, 9, 512, 1024], P(None, None, 'gx', 'gy'), may hold values from -1.1953125 to 1.1953125
- coef_fine: bfloat16 [4, 9, 1024, 2048], P(None, None, 'gx', 'gy'), may hold values from -1.1953125 to 1.1953125
- kern_u: bfloat16 [4, 16, 1024, 512], P('gx', 'gy'), may hold values from -0.25 to 0.25
- kern_v: bfloat16 [4, 16, 1024, 512], P('gx', 'gy'), may hold values from -0.25 to 0.25
- vis_data: bfloat16 [4, 16, 1024, 1024], P('gx', 'gy'), may hold values from -6 to 6
- facet_tiles: int32 [4, 16, 2], P('gx', 'gy'), may hold values from 0 to 7, as said below
- facet_weight: float32 [4, 16, 2], P('gx', 'gy'), may hold values from 0.5 to 1.5
- facet_count: int32 [4, 16], P('gx', 'gy'), may hold values from 256 to 1024, as said below
Outputs:
- grad_coarse: float32 [512, 1024], P('gx', 'gy')
- grad_middle: float32 [1024, 2048], P('gx', 'gy')
- grad_fine: float32 [2048, 4096], P('gx', 'gy')
- potential: float32 [], replicated
Inputs may be any that keep to these rules, and one draw needn't show every extreme that they name: `facet_tiles`: every tile column of a row is named by some facet of that row. `facet_count`: bins 0 to the count minus one of a facet are used.
All inputs are finite; a program needn't handle non-finite values.
Results may differ from a plain program's by a relative error of at most 0.0085.
Values may be sent and summed in bfloat16 or wider, within the bound.
No kernel may reach another device: no remote copies, remote signals or barrier semaphores. Data moves between devices by JAX's collectives and lax.ppermute only.
A program may use at most 320 MiB of HBM per device.

v0:
```python
import jax
import jax.numpy as jnp
from jax import lax
from jax.sharding import PartitionSpec as P

inv_noise = 0.125


def extended(x, sides, width):
    for axis, dim in sides:
        size, length = (lax.axis_size(axis), x.shape[dim])
        up = [(i, (i + 1) % size) for i in range(size - 1)]
        down = [(j, i) for i, j in up]
        last = lax.slice_in_dim(x, length - width, length, axis=dim)
        leading = lax.slice_in_dim(x, 0, width, axis=dim)
        before = lax.ppermute(last, axis, up)
        after = lax.ppermute(leading, axis, down)
        x = jnp.concatenate([before, x, after], axis=dim)
    return x


def as_sent(x):

    def short(part):
        return part.astype(jnp.bfloat16) if part.dtype == jnp.float32 else part

    return jax.tree.map(short, x)


def alternate(quads, rows, cols):
    return quads.reshape(2, 2, rows, cols).transpose(2, 0, 3, 1).reshape(2 * rows, 2 * cols)


def widen(field):
    return extended(field, (("gx", 0), ("gy", 1)), 1)


def refine(field, weights):
    rows, cols = (weights.shape[2], weights.shape[3])
    padded = widen(field)
    quads = []
    for child in range(4):
        total = jnp.zeros((rows, cols), jnp.float32)
        for near in range(9):
            shift_r, shift_c = (near // 3 - 1, near % 3 - 1)
            window = padded[1 + shift_r : 1 + shift_r + rows, 1 + shift_c : 1 + shift_c + cols]
            total = total + weights[child, near].astype(jnp.float32) * window
        quads.append(total)
    return alternate(jnp.stack(quads), rows, cols)


def back(grad, weights):
    rows, cols = (weights.shape[2], weights.shape[3])
    quads = grad.reshape(rows, 2, cols, 2).transpose(1, 3, 0, 2).reshape(4, rows, cols)
    parts = []
    for near in range(9):
        total = jnp.zeros((rows, cols), jnp.float32)
        for child in range(4):
            total = total + weights[child, near].astype(jnp.float32) * quads[child]
        parts.append(total)
    padded = extended(as_sent(jnp.stack(parts)), (("gx", 1), ("gy", 2)), 1)
    result = jnp.zeros((rows, cols), jnp.float32)
    for near in range(9):
        shift_r, shift_c = (near // 3 - 1, near % 3 - 1)
        result = (
            result
            + padded[near, 1 - shift_r : 1 - shift_r + rows, 1 - shift_c : 1 - shift_c + cols]
        )
    return result


def body(
    xi_coarse,
    xi_middle,
    xi_fine,
    coef_middle,
    coef_fine,
    kern_u,
    kern_v,
    vis_data,
    facet_tiles,
    facet_weight,
    facet_count,
):
    level_middle = refine(xi_coarse, coef_middle) + xi_middle
    level_fine = refine(level_middle, coef_fine) + xi_fine
    sky_tile = level_fine.astype(jnp.bfloat16)
    side = sky_tile.shape[0]
    bins = vis_data.shape[2]
    lists = facet_tiles[0]
    weights = facet_weight[0]
    piece = lax.all_gather(sky_tile, "gy", axis=1, tiled=True)
    count = piece.shape[1] // side
    tile_ids = jnp.arange(count, dtype=jnp.int32)
    mixing = jnp.sum(
        weights[:, :, None] * (lists[:, :, None] == tile_ids[None, None, :]).astype(jnp.float32),
        axis=1,
    )
    blocks = piece.reshape(side, count, side).astype(jnp.float32)
    sums = jnp.sum(mixing[:, None, :, None] * blocks[None], axis=2)
    amp = jnp.einsum(
        "fbx,fxy->fby", kern_u[0], sums.astype(jnp.bfloat16), preferred_element_type=jnp.float32
    ).astype(jnp.bfloat16)
    vis = jnp.einsum("fby,fcy->fbc", amp, kern_v[0], preferred_element_type=jnp.float32)
    live = (jnp.arange(bins, dtype=jnp.int32)[None, :] < facet_count[0][:, None]).astype(
        jnp.float32
    )
    resid = live[:, :, None] * (vis - vis_data[0].astype(jnp.float32))
    likelihood = 0.5 * inv_noise * jnp.sum(resid * resid)
    dvis = (inv_noise * resid).astype(jnp.bfloat16)
    damp = jnp.einsum("fbc,fcy->fby", dvis, kern_v[0], preferred_element_type=jnp.float32).astype(
        jnp.bfloat16
    )
    dsum = jnp.einsum("fbx,fby->fxy", kern_u[0], damp, preferred_element_type=jnp.float32)
    number = lax.axis_size("gy") * side // side
    tile_ids = jnp.arange(number, dtype=jnp.int32)
    mixing = jnp.sum(
        weights[:, :, None] * (lists[:, :, None] == tile_ids[None, None, :]).astype(jnp.float32),
        axis=1,
    )
    dsky = lax.psum_scatter(
        jnp.sum(mixing[:, :, None, None] * dsum[:, None], axis=0)
        .reshape(lax.axis_size("gy") * side, side)
        .astype(jnp.bfloat16),
        "gy",
        scatter_dimension=0,
        tiled=True,
    ).astype(jnp.float32)
    grad_fine = dsky + xi_fine
    dmiddle = back(dsky, coef_fine)
    grad_middle = dmiddle + xi_middle
    grad_coarse = back(dmiddle, coef_middle) + xi_coarse
    prior = 0.5 * (
        jnp.sum(xi_coarse * xi_coarse) + jnp.sum(xi_middle * xi_middle) + jnp.sum(xi_fine * xi_fine)
    )
    total = lax.psum(prior + likelihood, ("gx", "gy"))
    cells = lax.axis_size("gx") * lax.axis_size("gy") * side * side
    return (grad_coarse, grad_middle, grad_fine, total / cells)


def solution(mesh):
    placed = (
        P("gx", "gy"),
        P("gx", "gy"),
        P("gx", "gy"),
        P(None, None, "gx", "gy"),
        P(None, None, "gx", "gy"),
        P("gx", "gy", None, None),
        P("gx", "gy", None, None),
        P("gx", "gy", None, None),
        P("gx", "gy", None),
        P("gx", "gy", None),
        P("gx", "gy"),
    )
    return jax.shard_map(
        body,
        mesh=mesh,
        in_specs=placed,
        out_specs=(P("gx", "gy"), P("gx", "gy"), P("gx", "gy"), P()),
        check_vma=False,
    )
```

profile of v0, /device:TPU:10, one launch (start us, length us, event | category | flops | bytes accessed | tf_op | source)
XLA Modules:
  0.0 534.0 jit_solution(5848307226257766120)
XLA Ops:
  8.1 3.5 collective-permute-start
  14.1 3.9 collective-permute-done.1
  20.8 3.6 collective-permute-start.3
  30.0 8.6 %copy.42 = f32[2,2,128,128]{1,3,0,2:T(8,128)} copy(f32[2,2,128,128]{3,2,1,0:T(8,128)S(1)} %bitcast.1337) | data formatting | bytes 524288 | tf_op jit(solution)/shard_map/reshape | solution.py:31
  38.7 12.7 %reshape.1141 = f32[256,256]{1,0:T(8,128)S(1)} reshape(f32[128,2,128,2]{3,2,1,0:T(8,128)} %bitcast.1322) | data formatting | bytes 524288 | tf_op jit(solution)/shard_map/reshape | solution.py:31
  52.1 2.5 collective-permute-start.4
  54.6 3.3 collective-permute-start.5
  58.0 3.0 collective-permute-done.5
  63.3 3.3 collective-permute-start.7
  76.4 31.9 %copy.43 = f32[2,2,256,256]{1,3,0,2:T(8,128)} copy(f32[2,2,256,256]{3,2,1,0:T(8,128)S(1)} %bitcast.1335) | data formatting | bytes 2097152 | tf_op jit(solution)/shard_map/reshape | solution.py:31
  108.3 47.0 %reshape.1143 = f32[512,512]{1,0:T(8,128)S(1)} reshape(f32[256,2,256,2]{3,2,1,0:T(8,128)} %bitcast.88) | data formatting | bytes 2097152 | tf_op jit(solution)/shard_map/reshape | solution.py:31
  155.4 2.8 multiply_reduce_fusion.3
  158.7 46.0 %all-gather.2.cloned.1.call-done = bf16[512,4096]{1,0:T(8,128)(2,1)} async-done(((bf16[512,512]{1,0:T(8,128)(2,1)}), bf16[512,4096]{1,0:T(8,128)(2,1)}) %all-gather.2.cloned.1.call-update) | async-done | bytes 4194320 | tf_op jit(solution)/shard_map/all_gather | solution.py:92
  204.7 9.6 %copy.57 = f32[64,8,8,512]{3,2,1,0:T(8,128)} copy(bf16[64,8,8,512]{3,1,2,0:T(8,128)(2,1)} %bitcast.1336) | data formatting | bytes 12582912
  214.2 9.0 %multiply_reduce_fusion.1 = bf16[2,512,512]{2,1,0:T(8,128)(2,1)S(1)} fusion(f32[512,8,512]{2,1,0:T(8,128)} %bitcast.1324, f32[2,8]{1,0:T(2,128)S(1)} %fusion.325), kind=kLoop, calls=%fused_computation.1 | loop fusion | flops 7864320 | bytes 9437248 | tf_op jit(solution)/shard_map/reduce_sum | solution.py:100
  223.3 9.7 %multiply_reduce_fusion.2 = (f32[]{:T(128)}, f32[2,1024,1024]{2,1,0:T(8,128)}) fusion(bf16[1,2,1024,1024]{3,2,1,0:T(8,128)(2,1)} %param.18, f32[2,1024]{1,0:T(2,128)S(1)} %compare_convert_fusion, bf16[1,2,1024,512]{3,2,1,0:T(8,128)(2,1)} %param.17, bf16[1,2,1024,512]{3,2,1,0:T(8,128)(2,1)S(1)} %copy-done, bf16[2,512,512]{2,1,0:T(8,128)(2,1)S(1)} %multiply_reduce_fusion.1), kind=kOutput, calls=%fused_computation.4 | convolution fusion | flops 3232759808 | bytes 17833988 | tf_op jit(solution)/shard_map/fby,fcy->fbc/dot_general | solution.py:104
  233.0 10.2 %fusion.14 = f32[2,512,512]{1,2,0:T(8,128)} fusion(bf16[1,2,1024,512]{3,2,1,0:T(8,128)(2,1)S(1)} %copy-done, f32[2,1024,1024]{2,1,0:T(8,128)} %get-tuple-element.35, bf16[1,2,1024,1024]{3,2,1,0:T(8,128)(2,1)} %param.18, f32[2,1024]{1,0:T(2,128)S(1)} %compare_convert_fusion, bf16[1,2,1024,512]{3,2,1,0:T(8,128)(2,1)} %param.17), kind=kOutput, calls=%fused_computation.19 | convolution fusion | flops 3232759808 | bytes 18882560 | tf_op jit(solution)/shard_map/fbx,fby->fxy/dot_general | solution.py:114
  245.1 4.0 multiply_reduce_fusion
  249.2 47.0 %reduce-scatter.2.cloned.1.call-done = bf16[512,512]{1,0:T(8,128)(2,1)} async-done(((bf16[4096,512]{1,0:T(8,128)(2,1)}), bf16[512,512]{1,0:T(8,128)(2,1)}) %reduce-scatter.2.cloned.1.call-update) | async-done | bytes 524304 | tf_op jit(solution)/shard_map/reduce_scatter | solution.py:121
  296.2 68.5 %reshape.1144 = f32[256,2,256,2]{3,2,1,0:T(8,128)} reshape(bf16[512,512]{1,0:T(8,128)(2,1)} %reduce-scatter.2.cloned.1.call-done) | data formatting | bytes 1572864 | tf_op jit(solution)/shard_map/reshape | solution.py:54
  364.7 36.8 %copy.48 = f32[2,2,256,256]{3,2,1,0:T(8,128)S(1)} copy(f32[2,2,256,256]{1,3,0,2:T(8,128)} %bitcast.94) | data formatting | bytes 2097152 | tf_op jit(solution)/shard_map/transpose | solution.py:54
  412.4 3.4 collective-permute-start.8
  415.8 2.7 collective-permute-start.9
  418.5 3.8 collective-permute-done.9
  430.6 4.5 collective-permute-done.11
  436.8 18.1 %reshape.1320 = f32[128,2,128,2]{3,2,1,0:T(8,128)} reshape(f32[1,256,256]{2,1,0:T(8,128)S(1)} %get-tuple-element.5) | data formatting | bytes 524288 | tf_op jit(solution)/shard_map/add | solution.py:66
  454.9 10.1 %copy.53 = f32[2,2,128,128]{3,2,1,0:T(8,128)S(1)} copy(f32[2,2,128,128]{1,3,0,2:T(8,128)} %bitcast.1323) | data formatting | bytes 524288 | tf_op jit(solution)/shard_map/transpose | solution.py:54
  465.4 2.6 collective-permute-start.12
  468.0 3.4 collective-permute-start.13
  474.6 38.0 %psum.7 = f32[]{:T(128)} all-reduce(f32[]{:T(128)S(6)} %add.666), channel_id=1, replica_groups=mesh['gx'=4,'gy'=8] {'gx','gy'}, use_global_device_ids=true, to_apply=%region_8.0 | all-reduce | flops 1 | bytes 8 | tf_op jit(solution)/shard_map/psum | solution.py:136
  513.5 3.5 collective-permute-start.14
  521.4 3.8 collective-permute-done.15
  (101 shorter events, 54.2 us)
Async XLA Ops:
  7.2 216.1 %copy-start = (bf16[1,2,1024,512]{3,2,1,0:T(8,128)(2,1)S(1)}, bf16[1,2,1024,512]{3,2,1,0:T(8,128)(2,1)}, u32[]{:S(2)}) copy-start(bf16[1,2,1024,512]{3,2,1,0:T(8,128)(2,1)} %param.16) | copy-start | bytes 6291460
  7.2 22.5 %copy-start.4 = (f32[128,128]{1,0:T(8,128)S(1)}, f32[128,128]{1,0:T(8,128)}, u32[]{:S(2)}) copy-start(f32[128,128]{1,0:T(8,128)} %param.11) | copy-start | bytes 196612
  7.2 22.5 %copy-start.2 = (bf16[4,9,128,128]{3,2,1,0:T(8,128)(2,1)S(1)}, bf16[4,9,128,128]{3,2,1,0:T(8,128)(2,1)}, u32[]{:S(2)}) copy-start(bf16[4,9,128,128]{3,2,1,0:T(8,128)(2,1)} %param.14) | copy-start | bytes 3538948
  7.2 197.5 %all-gather.2.cloned.1.call-start = ((), (), s32[]{:S(2)}) async-start(), calls=%async_computation.1 | async-start | bytes 4718592 | tf_op jit(solution)/shard_map/all_gather | solution.py:92
  8.1 6.0 %collective-permute-start = (f32[1,128]{1,0:T(1,128)S(1)}, f32[1,128]{1,0:T(1,128)S(1)}, u32[]{:S(2)}, u32[]{:S(2)}) collective-permute-start(f32[1,128]{1,0:T(1,128)S(1)} %get-tuple-element.32), channel_id=1, source_target_pairs={{0,8},{8,16},{16,24},{1,9},{9,17},{17,25},{2,10},{10,18},{18,26},{... | collective-permute-start | bytes 1544 | tf_op jit(solution)/shard_map/ppermute | solution.py:16
  11.6 6.3 %collective-permute-start.1 = (f32[1,128]{1,0:T(1,128)S(1)}, f32[1,128]{1,0:T(1,128)S(1)}, u32[]{:S(2)}, u32[]{:S(2)}) collective-permute-start(f32[1,128]{1,0:T(1,128)S(1)} %get-tuple-element.33), channel_id=1, source_target_pairs={{8,0},{16,8},{24,16},{9,1},{17,9},{25,17},{10,2},{18,10},{26,18},{... | collective-permute-start | bytes 1544 | tf_op jit(solution)/shard_map/ppermute | solution.py:17
  18.9 5.6 %collective-permute-start.2 = (f32[130,1]{1,0:T(8,128)S(1)}, f32[130,1]{1,0:T(8,128)S(1)}, u32[]{:S(2)}, u32[]{:S(2)}) collective-permute-start(f32[130,1]{1,0:T(8,128)S(1)} %get-tuple-element.28), channel_id=1, source_target_pairs={{0,1},{1,2},{2,3},{3,4},{4,5},{5,6},{6,7},{8,9},{9,10},{10,11},{11... | collective-permute-start | bytes 1568 | tf_op jit(solution)/shard_map/ppermute | solution.py:16
  20.8 5.6 %collective-permute-start.3 = (f32[130,1]{1,0:T(8,128)S(1)}, f32[130,1]{1,0:T(8,128)S(1)}, u32[]{:S(2)}, u32[]{:S(2)}) collective-permute-start(f32[130,1]{1,0:T(8,128)S(1)} %get-tuple-element.29), channel_id=1, source_target_pairs={{1,0},{2,1},{3,2},{4,3},{5,4},{6,5},{7,6},{9,8},{10,9},{11,10},{12... | collective-permute-start | bytes 1568 | tf_op jit(solution)/shard_map/ppermute | solution.py:17
  38.7 12.7 %copy-start.8 = (f32[256,256]{1,0:T(8,128)S(1)}, f32[256,256]{1,0:T(8,128)}, u32[]{:S(2)}) copy-start(f32[256,256]{1,0:T(8,128)} %param.12) | copy-start | bytes 786436
  52.1 5.8 %collective-permute-start.4 = (f32[1,256]{1,0:T(1,128)S(1)}, f32[1,256]{1,0:T(1,128)S(1)}, u32[]{:S(2)}, u32[]{:S(2)}) collective-permute-start(f32[1,256]{1,0:T(1,128)S(1)} %get-tuple-element.26), channel_id=1, source_target_pairs={{0,8},{8,16},{16,24},{1,9},{9,17},{17,25},{2,10},{10,18},{18,26},{... | collective-permute-start | bytes 3080 | tf_op jit(solution)/shard_map/ppermute | solution.py:16
  54.6 6.4 %collective-permute-start.5 = (f32[1,256]{1,0:T(1,128)S(1)}, f32[1,256]{1,0:T(1,128)S(1)}, u32[]{:S(2)}, u32[]{:S(2)}) collective-permute-start(f32[1,256]{1,0:T(1,128)S(1)} %get-tuple-element.27), channel_id=1, source_target_pairs={{8,0},{16,8},{24,16},{9,1},{17,9},{25,17},{10,2},{18,10},{26,18},{... | collective-permute-start | bytes 3080 | tf_op jit(solution)/shard_map/ppermute | solution.py:17
  61.1 6.3 %collective-permute-start.6 = (f32[258,1]{1,0:T(8,128)S(1)}, f32[258,1]{1,0:T(8,128)S(1)}, u32[]{:S(2)}, u32[]{:S(2)}) collective-permute-start(f32[258,1]{1,0:T(8,128)S(1)} %get-tuple-element.20), channel_id=1, source_target_pairs={{0,1},{1,2},{2,3},{3,4},{4,5},{5,6},{6,7},{8,9},{9,10},{10,11},{11... | collective-permute-start | bytes 3104 | tf_op jit(solution)/shard_map/ppermute | solution.py:16
  63.3 5.9 %collective-permute-start.7 = (f32[258,1]{1,0:T(8,128)S(1)}, f32[258,1]{1,0:T(8,128)S(1)}, u32[]{:S(2)}, u32[]{:S(2)}) collective-permute-start(f32[258,1]{1,0:T(8,128)S(1)} %get-tuple-element.21), channel_id=1, source_target_pairs={{1,0},{2,1},{3,2},{4,3},{5,4},{6,5},{7,6},{9,8},{10,9},{11,10},{12... | collective-permute-start | bytes 3104 | tf_op jit(solution)/shard_map/ppermute | solution.py:17
  155.4 3.1 copy-start.10
  155.4 3.1 copy-start.11
  155.4 3.2 copy-start.12
  158.3 137.9 %reduce-scatter.2.cloned.1.call-start = ((), (), s32[]{:S(2)}) async-start(), calls=%async_computation.2 | async-start | bytes 4718592 | tf_op jit(solution)/shard_map/reduce_scatter | solution.py:121
  412.4 6.1 %collective-permute-start.8 = (bf16[9,1,256]{2,1,0:T(2,128)(2,1)S(1)}, bf16[9,1,256]{2,1,0:T(2,128)(2,1)S(1)}, u32[]{:S(2)}, u32[]{:S(2)}) collective-permute-start(bf16[9,1,256]{2,1,0:T(2,128)(2,1)S(1)} %get-tuple-element.12), channel_id=1, source_target_pairs={{0,8},{8,16},{16,24},{1,9},{9,17},{17,25},{2,10},{10,18},{18,26},{... | collective-permute-start | bytes 13832 | tf_op jit(solution)/shard_map/ppermute | solution.py:16
  415.8 6.5 %collective-permute-start.9 = (bf16[9,1,256]{2,1,0:T(2,128)(2,1)S(1)}, bf16[9,1,256]{2,1,0:T(2,128)(2,1)S(1)}, u32[]{:S(2)}, u32[]{:S(2)}) collective-permute-start(bf16[9,1,256]{2,1,0:T(2,128)(2,1)S(1)} %get-tuple-element.13), channel_id=1, source_target_pairs={{8,0},{16,8},{24,16},{9,1},{17,9},{25,17},{10,2},{18,10},{26,18},{... | collective-permute-start | bytes 13832 | tf_op jit(solution)/shard_map/ppermute | solution.py:17
  422.6 12.8 %copy-start.9 = (f32[256,256]{1,0:T(8,128)S(1)}, f32[256,256]{1,0:T(8,128)}, u32[]{:S(2)}) copy-start(f32[256,256]{1,0:T(8,128)} %param.12) | copy-start | bytes 786436
  425.3 4.9 collective-permute-start.10
  427.7 7.3 %collective-permute-start.11 = (bf16[9,258,1]{1,0,2:T(8,128)(2,1)S(1)}, bf16[9,258,1]{1,0,2:T(8,128)(2,1)S(1)}, u32[]{:S(2)}, u32[]{:S(2)}) collective-permute-start(bf16[9,258,1]{1,0,2:T(8,128)(2,1)S(1)} %copy.51), channel_id=1, source_target_pairs={{0,1},{1,2},{2,3},{3,4},{4,5},{5,6},{6,7},{8,9},{9,10},{10,11},{11... | collective-permute-start | bytes 13940 | tf_op jit(solution)/shard_map/ppermute | solution.py:16
  454.9 10.1 %copy-start.3 = (bf16[4,9,128,128]{3,2,1,0:T(8,128)(2,1)S(1)}, bf16[4,9,128,128]{3,2,1,0:T(8,128)(2,1)}, u32[]{:S(2)}) copy-start(bf16[4,9,128,128]{3,2,1,0:T(8,128)(2,1)} %param.14) | copy-start | bytes 3538948
  465.1 53.8 %copy-start.5 = (f32[512,512]{1,0:T(8,128)S(1)}, f32[512,512]{1,0:T(8,128)}, u32[]{:S(2)}) copy-start(f32[512,512]{1,0:T(8,128)} %param.13) | copy-start | bytes 3145732
  465.3 47.9 %copy-start.6 = (bf16[9,128,128]{2,1,0:T(8,128)(2,1)}, bf16[9,128,128]{2,1,0:T(8,128)(2,1)S(1)}, u32[]{:S(2)}) copy-start(bf16[9,128,128]{2,1,0:T(8,128)(2,1)S(1)} %constant_dynamic-update-slice_fusion.1) | copy-start | bytes 884740
  465.4 47.9 %collective-permute-start.12 = (bf16[9,1,128]{2,1,0:T(2,128)(2,1)S(1)}, bf16[9,1,128]{2,1,0:T(2,128)(2,1)S(1)}, u32[]{:S(2)}, u32[]{:S(2)}) collective-permute-start(bf16[9,1,128]{2,1,0:T(2,128)(2,1)S(1)} %get-tuple-element.18), channel_id=1, source_target_pairs={{0,8},{8,16},{16,24},{1,9},{9,17},{17,25},{2,10},{10,18},{18,26},{... | collective-permute-start | bytes 6920 | tf_op jit(solution)/shard_map/ppermute | solution.py:16
  468.0 45.3 %collective-permute-start.13 = (bf16[9,1,128]{2,1,0:T(2,128)(2,1)S(1)}, bf16[9,1,128]{2,1,0:T(2,128)(2,1)S(1)}, u32[]{:S(2)}, u32[]{:S(2)}) collective-permute-start(bf16[9,1,128]{2,1,0:T(2,128)(2,1)S(1)} %get-tuple-element.19), channel_id=1, source_target_pairs={{8,0},{16,8},{24,16},{9,1},{17,9},{25,17},{10,2},{18,10},{26,18},{... | collective-permute-start | bytes 6920 | tf_op jit(solution)/shard_map/ppermute | solution.py:17
  513.4 11.9 %copy-start.7 = (bf16[9,128,128]{2,1,0:T(8,128)(2,1)S(1)}, bf16[9,128,128]{2,1,0:T(8,128)(2,1)}, u32[]{:S(2)}) copy-start(bf16[9,128,128]{2,1,0:T(8,128)(2,1)} %copy-done.6) | copy-start | bytes 884740
  513.4 12.7 %copy-start.1 = (bf16[1,2,1024,512]{3,2,1,0:T(8,128)(2,1)S(1)}, bf16[1,2,1024,512]{3,2,1,0:T(8,128)(2,1)}, u32[]{:S(2)}) copy-start(bf16[1,2,1024,512]{3,2,1,0:T(8,128)(2,1)} %param.16) | copy-start | bytes 6291460
  513.5 7.9 %collective-permute-start.14 = (bf16[9,130,1]{2,1,0:T(8,128)(2,1)S(1)}, bf16[9,130,1]{2,1,0:T(8,128)(2,1)S(1)}, u32[]{:S(2)}, u32[]{:S(2)}) collective-permute-start(bf16[9,130,1]{2,1,0:T(8,128)(2,1)S(1)} %get-tuple-element.16), channel_id=1, source_target_pairs={{1,0},{2,1},{3,2},{4,3},{5,4},{6,5},{7,6},{9,8},{10,9},{11,10},{12... | collective-permute-start | bytes 7028 | tf_op jit(solution)/shard_map/ppermute | solution.py:17
  517.0 8.2 %collective-permute-start.15 = (bf16[9,130,1]{2,1,0:T(8,128)(2,1)S(1)}, bf16[9,130,1]{2,1,0:T(8,128)(2,1)S(1)}, u32[]{:S(2)}, u32[]{:S(2)}) collective-permute-start(bf16[9,130,1]{2,1,0:T(8,128)(2,1)S(1)} %get-tuple-element.17), channel_id=1, source_target_pairs={{0,1},{1,2},{2,3},{3,4},{4,5},{5,6},{6,7},{8,9},{9,10},{10,11},{11... | collective-permute-start | bytes 7028 | tf_op jit(solution)/shard_map/ppermute | solution.py:16
Sparse Core Ops, SparseCore 0:
  158.4 46.2 all-gather.1
  249.3 46.8 reduce-scatter.1
where the time goes:
time: 537 us; the launch traced here: 534 us
  local copies, waits for them, and re-layouts  251 us (47%)
  waiting for transfers between devices  117 us (22%)
  starting transfers between devices  44.9 us (8%)
  other arithmetic  44.9 us (8%)
  blocking collectives  38 us (7%)
  matrix products  19.9 us (4%)
  between operations  19 us (4%)
    reshape x4, local copies, waits for them, and re-layouts, alternate(): quads.reshape(2, 2, rows, cols).transpose(2, 0, 3, 1)  100 us
    reshape x1, local copies, waits for them, and re-layouts, back(): grad.reshape(rows, 2, cols, 2).transpose(1, 3, 0, 2).reshape(4, rows, cols)  68.5 us
    reduce_scatter x1, waiting for transfers between devices, body(): lax.psum_scatter(jnp.sum(mixing[:, :, None, None] * dsum[:, None], axis=0...  47 us
    transpose x2, local copies, waits for them, and re-layouts, back(): grad.reshape(rows, 2, cols, 2).transpose(1, 3, 0, 2).reshape(4, rows, cols)  46.8 us
    all_gather x1, waiting for transfers between devices, body(): piece = lax.all_gather(sky_tile, 'gy', axis=1, tiled=True)  46 us
    psum x1, blocking collectives, body(): total = lax.psum(prior + likelihood, ('gx', 'gy'))  38 us
    ppermute x8, starting transfers between devices, extended(): after = lax.ppermute(leading, axis, down)  24.2 us
    ppermute x8, starting transfers between devices, extended(): before = lax.ppermute(last, axis, up)  20.5 us
  transfers between devices with their start and end apart: 18, of which 11 were waited for; matrix products, arithmetic and copies ran while one was open for 1% of the time, Pallas kernels for 0%

commit v1 on v0

v1 whole, which is shorter than its diff:
```python
import functools

import jax
import jax.numpy as jnp
from jax import lax
from jax.experimental import pallas as pl
from jax.experimental.pallas import tpu as pltpu
from jax.sharding import PartitionSpec as P

inv_noise = 0.125
vmem = 56 * 1024 * 1024
f32 = jnp.float32
bf16 = jnp.bfloat16


def extended(x, sides, width):
    for axis, dim in sides:
        size, length = (lax.axis_size(axis), x.shape[dim])
        up = [(i, (i + 1) % size) for i in range(size - 1)]
        down = [(j, i) for i, j in up]
        last = lax.slice_in_dim(x, length - width, length, axis=dim)
        leading = lax.slice_in_dim(x, 0, width, axis=dim)
        before = lax.ppermute(last, axis, up)
        after = lax.ppermute(leading, axis, down)
        x = jnp.concatenate([before, x, after], axis=dim)
    return x


def widen(field):
    return extended(field, (("gx", 0), ("gy", 1)), 1)


def halves(x):
    high = x.astype(bf16)
    return high, (x - high.astype(f32)).astype(bf16)


def interleaver(cols, transposed):
    shape = (2 * cols, 2 * cols)
    split = lax.broadcasted_iota(jnp.int32, shape, 1 if transposed else 0)
    whole = lax.broadcasted_iota(jnp.int32, shape, 0 if transposed else 1)
    place = jnp.where(split >= cols, 2 * (split - cols) + 1, 2 * split)
    return (place == whole).astype(f32).astype(bf16)


def refine_kernel(blk, pad_ref, coef_ref, xi_ref, out_ref, sq_ref, win, perm, lhs, mix):
    rows, cols = win.shape[1:]
    step = pl.program_id(0)

    @pl.when(step == 0)
    def _():
        for near in range(9):
            r, c = near // 3, near % 3
            win[near] = pad_ref[r : r + rows, c : c + cols]
        perm[...] = interleaver(cols, False)
        sq_ref[...] = jnp.zeros_like(sq_ref)

    base = step * blk

    def part(i, carry):
        r0 = pl.multiple_of(i * 16, 16)
        total = [jnp.zeros((16, cols), f32) for _ in range(4)]
        for near in range(9):
            w = win[near, pl.ds(pl.multiple_of(base + r0, 16), 16), :]
            for child in range(4):
                total[child] += coef_ref[child, near, pl.ds(r0, 16), :].astype(f32) * w
        for child in range(4):
            a, b = child // 2, child % 2
            high, low = halves(total[child])
            lhs[pl.ds(2 * a * blk + r0, 16), b * cols : (b + 1) * cols] = high
            lhs[pl.ds((2 * a + 1) * blk + r0, 16), b * cols : (b + 1) * cols] = low
        return carry

    lax.fori_loop(0, blk // 16, part, 0)
    field = jnp.dot(lhs[...], perm[...], preferred_element_type=f32)
    xi = xi_ref[...]
    for tile in range(2 * cols // 128):
        lanes = slice(tile * 128, (tile + 1) * 128)
        for a in range(2):
            mix[tile, pl.ds(a, blk, stride=2), :] = (
                field[2 * a * blk : (2 * a + 1) * blk, lanes]
                + field[(2 * a + 1) * blk : (2 * a + 2) * blk, lanes]
            )
        out_ref[:, lanes] = (mix[tile] + xi[:, lanes]).astype(out_ref.dtype)
    sq_ref[...] += jnp.sum((xi * xi).reshape(2 * blk // 8, 8, 2 * cols), axis=0)


def refine(padded, coef, xi, dtype):
    rows, cols = coef.shape[2:]
    blk = 64
    return pl.pallas_call(
        functools.partial(refine_kernel, blk),
        grid=(rows // blk,),
        in_specs=[
            pl.BlockSpec((rows + 2, cols + 2), lambda i: (0, 0)),
            pl.BlockSpec((4, 9, blk, cols), lambda i: (0, 0, i, 0)),
            pl.BlockSpec((2 * blk, 2 * cols), lambda i: (i, 0)),
        ],
        out_specs=[
            pl.BlockSpec((2 * blk, 2 * cols), lambda i: (i, 0)),
            pl.BlockSpec((8, 2 * cols), lambda i: (0, 0)),
        ],
        out_shape=[
            jax.ShapeDtypeStruct((2 * rows, 2 * cols), dtype),
            jax.ShapeDtypeStruct((8, 2 * cols), f32),
        ],
        scratch_shapes=[
            pltpu.VMEM((9, rows, cols), f32),
            pltpu.VMEM((2 * cols, 2 * cols), bf16),
            pltpu.VMEM((4 * blk, 2 * cols), bf16),
            pltpu.VMEM((2 * cols // 128, 2 * blk, 128), f32),
        ],
        compiler_params=pltpu.CompilerParams(vmem_limit_bytes=vmem),
        name="refine",
    )(padded, coef, xi)


def back_kernel(blk, g_ref, coef_ref, xi_ref, grad_ref, main_ref, cols_ref, terms, perm, mix, rowed):
    rows, cols = terms.shape[1:]
    step = pl.program_id(0)

    @pl.when(step == 0)
    def _():
        perm[...] = interleaver(cols, True)

    base = step * blk
    g = g_ref[...]
    grad_ref[...] = g.astype(f32) + xi_ref[...]
    if g.dtype == bf16:
        split = jnp.dot(g, perm[...], preferred_element_type=f32)
    else:
        high, low = halves(g)
        both = jnp.dot(jnp.concatenate([high, low]), perm[...], preferred_element_type=f32)
        split = both[: 2 * blk] + both[2 * blk :]
    for tile in range(2 * cols // 128):
        mix[tile] = split[:, tile * 128 : (tile + 1) * 128]

    def part(i, carry):
        r0 = pl.multiple_of(i * 16, 16)
        quads = []
        for a in range(2):
            for b in range(2):
                tiles = range(b * cols // 128, (b + 1) * cols // 128)
                lines = [mix[t, pl.ds(2 * r0 + a, 16, stride=2), :] for t in tiles]
                quads.append(jnp.concatenate(lines, axis=1))
        for near in range(9):
            total = jnp.zeros((16, cols), f32)
            for child in range(4):
                total += coef_ref[child, near, pl.ds(r0, 16), :].astype(f32) * quads[child]
            terms[near, pl.ds(pl.multiple_of(base + r0, 16), 16), :] = total
        return carry

    lax.fori_loop(0, blk // 16, part, 0)

    @pl.when(step == pl.num_programs(0) - 1)
    def _():
        rowed[...] = jnp.zeros_like(rowed)
        for near in range(9):
            r, c = near // 3, near % 3
            rowed[c, 7 + r : 7 + r + rows, :] += terms[near]
        lane = lax.broadcasted_iota(jnp.int32, (rows + 16, cols), 1)
        from_left = pltpu.roll(rowed[2], 1, 1)
        from_right = pltpu.roll(rowed[0], cols - 1, 1)
        main_ref[...] = (
            rowed[1]
            + jnp.where(lane == 0, 0.0, from_left)
            + jnp.where(lane == cols - 1, 0.0, from_right)
        )
        cols_ref[0] = rowed[0, :, :128]
        cols_ref[1] = rowed[2, :, cols - 128 :]


def back(g, coef, xi):
    rows, cols = coef.shape[2:]
    blk = 64
    grad, main, side = pl.pallas_call(
        functools.partial(back_kernel, blk),
        grid=(rows // blk,),
        in_specs=[
            pl.BlockSpec((2 * blk, 2 * cols), lambda i: (i, 0)),
            pl.BlockSpec((4, 9, blk, cols), lambda i: (0, 0, i, 0)),
            pl.BlockSpec((2 * blk, 2 * cols), lambda i: (i, 0)),
        ],
        out_specs=[
            pl.BlockSpec((2 * blk, 2 * cols), lambda i: (i, 0)),
            pl.BlockSpec((rows + 16, cols), lambda i: (0, 0)),
            pl.BlockSpec((2, rows + 16, 128), lambda i: (0, 0, 0)),
        ],
        out_shape=[
            jax.ShapeDtypeStruct((2 * rows, 2 * cols), f32),
            jax.ShapeDtypeStruct((rows + 16, cols), f32),
            jax.ShapeDtypeStruct((2, rows + 16, 128), f32),
        ],
        scratch_shapes=[
            pltpu.VMEM((9, rows, cols), f32),
            pltpu.VMEM((2 * cols, 2 * cols), bf16),
            pltpu.VMEM((2 * cols // 128, 2 * blk, 128), f32),
            pltpu.VMEM((3, rows + 16, cols), f32),
        ],
        compiler_params=pltpu.CompilerParams(vmem_limit_bytes=vmem),
        name="back",
    )(g, coef, xi)
    size = lax.axis_size("gy")
    right = [(i, i + 1) for i in range(size - 1)]
    left = [(j, i) for i, j in right]
    from_left = lax.ppermute(side[1, 7 : 9 + rows, 127], "gy", right)
    from_right = lax.ppermute(side[0, 7 : 9 + rows, 0], "gy", left)
    main = main[7 : 9 + rows]
    ends = jnp.pad(from_left[:, None], ((0, 0), (0, cols - 1))) + jnp.pad(
        from_right[:, None], ((0, 0), (cols - 1, 0))
    )
    size = lax.axis_size("gx")
    down = [(i, i + 1) for i in range(size - 1)]
    up = [(j, i) for i, j in down]
    from_above = lax.ppermute(main[-1:] + ends[-1:], "gx", down)
    from_below = lax.ppermute(main[:1] + ends[:1], "gx", up)
    result = (
        main[1:-1]
        + ends[1:-1]
        + jnp.pad(from_above, ((0, rows - 1), (0, 0)))
        + jnp.pad(from_below, ((rows - 1, 0), (0, 0)))
    )
    return grad, result


def facet_kernel(
    blk, lists, weights, counts, one_ref, two_ref, ku_ref, kv_ref, data_ref, out_ref, lik_ref, sums, dsum
):
    facet, step = pl.program_id(0), pl.program_id(1)
    facets, steps = pl.num_programs(0), pl.num_programs(1)

    @pl.when((facet == 0) & (step == 0))
    def _():
        lik_ref[...] = jnp.zeros_like(lik_ref)

    @pl.when(step == 0)
    def _():
        sums[...] = (
            weights[facet, 0] * one_ref[0].astype(f32) + weights[facet, 1] * two_ref[0].astype(f32)
        ).astype(bf16)
        dsum[facet] = jnp.zeros(dsum.shape[1:], f32)

    count = counts[facet] - step * blk

    @pl.when(count > 0)
    def _():
        ku, kv = ku_ref[0, 0], kv_ref[0, 0]
        amp = jnp.dot(ku, sums[...], preferred_element_type=f32).astype(bf16)
        vis = lax.dot_general(amp, kv, (((1,), (1,)), ((), ())), preferred_element_type=f32)
        live = lax.broadcasted_iota(jnp.int32, vis.shape, 0) < count
        resid = jnp.where(live, vis - data_ref[0, 0].astype(f32), 0.0)
        lik_ref[...] += jnp.sum((resid * resid).reshape(blk // 8, 8, vis.shape[1]), axis=0)
        dvis = (inv_noise * resid).astype(bf16)
        damp = jnp.dot(dvis, kv, preferred_element_type=f32).astype(bf16)
        dsum[facet] += lax.dot_general(
            ku, damp, (((0,), (0,)), ((), ())), preferred_element_type=f32
        )

    @pl.when((facet == facets - 1) & (step == steps - 1))
    def _():
        for t in range(out_ref.shape[0]):
            total = None
            for f in range(dsum.shape[0]):
                scale = jnp.float32(0.0)
                for s in range(lists.shape[1]):
                    scale += jnp.where(lists[f, s] == t, weights[f, s], 0.0)
                term = scale * dsum[f]
                total = term if total is None else total + term
            out_ref[t] = total.astype(bf16)


def facets(tiles, ku, kv, data, lists, weights, counts):
    number, bins, side = ku.shape[1:]
    blk = 256
    return pl.pallas_call(
        functools.partial(facet_kernel, blk),
        grid_spec=pltpu.PrefetchScalarGridSpec(
            num_scalar_prefetch=3,
            grid=(number, bins // blk),
            in_specs=[
                pl.BlockSpec((1, side, side), lambda f, i, ls, ws, cs: (ls[f, 0], 0, 0)),
                pl.BlockSpec((1, side, side), lambda f, i, ls, ws, cs: (ls[f, 1], 0, 0)),
                pl.BlockSpec((1, 1, blk, side), lambda f, i, ls, ws, cs: (0, f, i, 0)),
                pl.BlockSpec((1, 1, bins, side), lambda f, i, ls, ws, cs: (0, f, 0, 0)),
                pl.BlockSpec((1, 1, blk, bins), lambda f, i, ls, ws, cs: (0, f, i, 0)),
            ],
            out_specs=[
                pl.BlockSpec(tiles.shape, lambda f, i, ls, ws, cs: (0, 0, 0)),
                pl.BlockSpec((8, bins), lambda f, i, ls, ws, cs: (0, 0)),
            ],
            scratch_shapes=[
                pltpu.VMEM((side, side), bf16),
                pltpu.VMEM((number, side, side), f32),
            ],
        ),
        out_shape=[
            jax.ShapeDtypeStruct(tiles.shape, bf16),
            jax.ShapeDtypeStruct((8, bins), f32),
        ],
        compiler_params=pltpu.CompilerParams(vmem_limit_bytes=vmem),
        name="facets",
    )(lists, weights, counts, tiles, tiles, ku, kv, data)


def body(
    xi_coarse,
    xi_middle,
    xi_fine,
    coef_middle,
    coef_fine,
    kern_u,
    kern_v,
    vis_data,
    facet_tiles,
    facet_weight,
    facet_count,
):
    side = xi_fine.shape[0]
    level_middle, sq_middle = refine(widen(xi_coarse), coef_middle, xi_middle, f32)
    sky, sq_fine = refine(widen(level_middle), coef_fine, xi_fine, bf16)
    tiles = lax.all_gather(sky, "gy", axis=0)
    dtiles, lik = facets(
        tiles, kern_u, kern_v, vis_data, facet_tiles[0], facet_weight[0], facet_count[0]
    )
    potential = 0.5 * (jnp.sum(xi_coarse * xi_coarse) + jnp.sum(sq_middle) + jnp.sum(sq_fine))
    potential = (potential + 0.5 * inv_noise * jnp.sum(lik))[None]
    for axis in ("gy", "gx"):
        size = lax.axis_size(axis)
        hop = 1
        while hop < size:
            potential += lax.ppermute(potential, axis, [(i, i ^ hop) for i in range(size)])
            hop *= 2
    dsky = lax.psum_scatter(dtiles, "gy", scatter_dimension=0, tiled=False)
    grad_fine, dmiddle = back(dsky, coef_fine, xi_fine)
    grad_middle, dcoarse = back(dmiddle, coef_middle, xi_middle)
    grad_coarse = dcoarse + xi_coarse
    cells = lax.axis_size("gx") * lax.axis_size("gy") * side * side
    return (grad_coarse, grad_middle, grad_fine, potential[0] / cells)


def solution(mesh):
    placed = (
        P("gx", "gy"),
        P("gx", "gy"),
        P("gx", "gy"),
        P(None, None, "gx", "gy"),
        P(None, None, "gx", "gy"),
        P("gx", "gy", None, None),
        P("gx", "gy", None, None),
        P("gx", "gy", None, None),
        P("gx", "gy", None),
        P("gx", "gy", None),
        P("gx", "gy"),
    )
    return jax.shard_map(
        body,
        mesh=mesh,
        in_specs=placed,
        out_specs=(P("gx", "gy"), P("gx", "gy"), P("gx", "gy"), P()),
        check_vma=False,
    )
```

time: 537 us -> 249 us (0.46)
  local copies, waits for them, and re-layouts: 251 us -> 4.34 us
  blocking collectives: 38 us -> 0 us
  Pallas kernels: 0 us -> 33.5 us
  other arithmetic: 44.9 us -> 12.8 us
  matrix products: 19.9 us -> 0 us
  starting transfers between devices: 44.9 us -> 53.8 us
    reshape x5 -> x0, local copies, waits for them, and re-layouts: 169 us -> none  [the longest x4 100 us: alternate(): quads.reshape(2, 2, rows, cols).transpose(2, 0, 3, 1)]
    transpose x2 -> x0, local copies, waits for them, and re-layouts: 46.8 us -> none  [back(): grad.reshape(rows, 2, cols, 2).transpose(1, 3, 0, 2).reshape(4, rows, cols)]
    psum x1 -> x0, blocking collectives: 38 us -> none  [body(): total = lax.psum(prior + likelihood, ('gx', 'gy'))]
    pallas_call x0 -> x5, Pallas kernels: none -> 33.5 us  [the longest x1 15.7 us: facets(): pl.pallas_call(functools.partial(facet_kernel, blk), grid_spec=pltpu.Pref...]
    ppermute x0 -> x13, starting transfers between devices: none -> 30.9 us  [the longest x5 9.37 us: body(): lax.ppermute(potential, axis, [(i, i ^ hop) for i in range(size)])]
    dot_general x2 -> x0, matrix products: 19.9 us -> none  [the longest x1 10.2 us: body(): jnp.einsum('fbx,fby->fxy', kern_u[0], damp, preferred_element_type=jnp.fl...]
    add x1 -> x0, local copies, waits for them, and re-layouts: 18.1 us -> none  [back(): result + padded[near, 1 - shift_r:1 - shift_r + rows, 1 - shift_c:1 - shi...]
    ppermute x0 -> x13, waiting for transfers between devices: none -> 15 us  [the longest x5 6.92 us: body(): lax.ppermute(potential, axis, [(i, i ^ hop) for i in range(size)])]
  transfers between devices with their start and end apart: 18 -> 23, of which waited for: 11 -> 16; matrix products, arithmetic and copies ran while one was open for 1% -> 1% of each run, Pallas kernels for 0% -> 0%
where the time goes in v1:
time: 249 us; the launch traced here: 246 us
  waiting for transfers between devices  120 us (48%)
  starting transfers between devices  53.8 us (22%)
  Pallas kernels  33.5 us (13%)
  between operations  21.6 us (9%)
  other arithmetic  12.8 us (5%)
  local copies, waits for them, and re-layouts  4.34 us (2%)
    reduce_scatter x1, waiting for transfers between devices, body(): dsky = lax.psum_scatter(dtiles, 'gy', scatter_dimension=0, tiled=False)  47.4 us
    all_gather x1, waiting for transfers between devices, body(): tiles = lax.all_gather(sky, 'gy', axis=0)  46.4 us
    pallas_call x1, Pallas kernels, facets(): pl.pallas_call(functools.partial(facet_kernel, blk), grid_spec=pltpu.Pref...  15.7 us
    ppermute x4, starting transfers between devices, extended(): after = lax.ppermute(leading, axis, down)  12.8 us
    ppermute x4, waiting for transfers between devices, extended(): after = lax.ppermute(leading, axis, down)  10.5 us
    ppermute x4, starting transfers between devices, extended(): before = lax.ppermute(last, axis, up)  10 us
    ppermute x5, starting transfers between devices, body(): lax.ppermute(potential, axis, [(i, i ^ hop) for i in range(size)])  9.37 us
    pallas_call x2, Pallas kernels, refine(): pl.pallas_call(functools.partial(refine_kernel, blk), grid=(rows // blk,)...  9.19 us
  transfers between devices with their start and end apart: 23, of which 16 were waited for; matrix products, arithmetic and copies ran while one was open for 1% of the time, Pallas kernels for 0%

profile of v1, /device:TPU:10, one launch (start us, length us, event | category | flops | bytes accessed | tf_op | source)
XLA Modules:
  0.0 246.1 jit_solution(11637110511537335277)
XLA Ops:
  7.9 3.4 %collective-permute-start = (f32[1,128]{1,0:T(1,128)S(1)}, f32[1,128]{1,0:T(1,128)S(1)}, u32[]{:S(2)}, u32[]{:S(2)}) collective-permute-start(f32[1,128]{1,0:T(1,128)S(1)} %get-tuple-element.44), channel_id=1, source_target_pairs={{0,8},{8,16},{16,24},{1,9},{9,17},{17,25},{2,10},{10,18},{18,26},{... | collective-permute-start | bytes 1544 | tf_op jit(solution)/shard_map/ppermute | solution.py:23
  11.3 2.4 collective-permute-start.1
  13.8 3.9 %collective-permute-done.1 = f32[1,128]{1,0:T(1,128)S(1)} collective-permute-done((f32[1,128]{1,0:T(1,128)S(1)}, f32[1,128]{1,0:T(1,128)S(1)}, u32[]{:S(2)}, u32[]{:S(2)}) %collective-permute-start.1) | collective-permute-done | bytes 544 | tf_op jit(solution)/shard_map/ppermute | solution.py:24
  18.6 1.9 collective-permute-start.2
  20.5 3.6 %collective-permute-start.3 = (f32[130,1]{1,0:T(8,128)S(1)}, f32[130,1]{1,0:T(8,128)S(1)}, u32[]{:S(2)}, u32[]{:S(2)}) collective-permute-start(f32[130,1]{1,0:T(8,128)S(1)} %get-tuple-element.41), channel_id=1, source_target_pairs={{1,0},{2,1},{3,2},{4,3},{5,4},{6,5},{7,6},{9,8},{10,9},{11,10},{12... | collective-permute-start | bytes 1568 | tf_op jit(solution)/shard_map/ppermute | solution.py:24
  27.7 2.9 %refine.2 = (f32[256,256]{1,0:T(8,128)}, f32[8,256]{1,0:T(8,128)}) custom-call(f32[130,130]{1,0:T(8,128)} %pad_maximum_fusion.2.pad_ref, bf16[4,9,128,128]{3,2,1,0:T(8,128)(2,1)} %coef_ref.7, f32[256,256]{1,0:T(8,128)} %xi_ref.7), custom_call_target="tpu_custom_call" | custom-call | tf_op jit(solution)/shard_map/refine/pallas_call | solution.py:91
  31.3 2.5 %collective-permute-start.4 = (f32[1,256]{1,0:T(1,128)S(1)}, f32[1,256]{1,0:T(1,128)S(1)}, u32[]{:S(2)}, u32[]{:S(2)}) collective-permute-start(f32[1,256]{1,0:T(1,128)S(1)} %get-tuple-element.36), channel_id=1, source_target_pairs={{0,8},{8,16},{16,24},{1,9},{9,17},{17,25},{2,10},{10,18},{18,26},{... | collective-permute-start | bytes 3080 | tf_op jit(solution)/shard_map/ppermute | solution.py:23
  33.8 3.3 %collective-permute-start.5 = (f32[1,256]{1,0:T(1,128)S(1)}, f32[1,256]{1,0:T(1,128)S(1)}, u32[]{:S(2)}, u32[]{:S(2)}) collective-permute-start(f32[1,256]{1,0:T(1,128)S(1)} %get-tuple-element.37), channel_id=1, source_target_pairs={{8,0},{16,8},{24,16},{9,1},{17,9},{25,17},{10,2},{18,10},{26,18},{... | collective-permute-start | bytes 3080 | tf_op jit(solution)/shard_map/ppermute | solution.py:24
  37.1 3.0 %collective-permute-done.5 = f32[1,256]{1,0:T(1,128)S(1)} collective-permute-done((f32[1,256]{1,0:T(1,128)S(1)}, f32[1,256]{1,0:T(1,128)S(1)}, u32[]{:S(2)}, u32[]{:S(2)}) %collective-permute-start.5) | collective-permute-done | bytes 1056 | tf_op jit(solution)/shard_map/ppermute | solution.py:24
  41.2 2.2 collective-permute-start.6
  43.4 3.3 %collective-permute-start.7 = (f32[258,1]{1,0:T(8,128)S(1)}, f32[258,1]{1,0:T(8,128)S(1)}, u32[]{:S(2)}, u32[]{:S(2)}) collective-permute-start(f32[258,1]{1,0:T(8,128)S(1)} %get-tuple-element.35), channel_id=1, source_target_pairs={{1,0},{2,1},{3,2},{4,3},{5,4},{6,5},{7,6},{9,8},{10,9},{11,10},{12... | collective-permute-start | bytes 3104 | tf_op jit(solution)/shard_map/ppermute | solution.py:24
  49.3 1.9 pad_maximum_fusion.pad_ref
  51.2 6.3 %refine.3 = (bf16[512,512]{1,0:T(8,128)(2,1)}, f32[8,512]{1,0:T(8,128)}) custom-call(f32[258,258]{1,0:T(8,128)} %pad_maximum_fusion.pad_ref, bf16[4,9,256,256]{3,2,1,0:T(8,128)(2,1)} %coef_ref.6, f32[512,512]{1,0:T(8,128)} %xi_ref.6), custom_call_target="tpu_custom_call" | custom-call | tf_op jit(solution)/shard_map/refine/pallas_call | solution.py:91
  57.7 46.4 %all-gather.3.cloned.1.call-done = bf16[4096,512]{1,0:T(8,128)(2,1)} async-done(((bf16[512,512]{1,0:T(8,128)(2,1)}), bf16[4096,512]{1,0:T(8,128)(2,1)}) %all-gather.3.cloned.1.call-update) | async-done | bytes 4194320 | tf_op jit(solution)/shard_map/all_gather | solution.py:321
  104.0 15.7 %facets.1 = (bf16[8,512,512]{2,1,0:T(8,128)(2,1)}, f32[8,1024]{1,0:T(8,128)}) custom-call(s32[2,2]{1,0:T(2,128)} %bitcast.14, f32[2,2]{1,0:T(2,128)} %bitcast.15, s32[2]{0:T(128)} %bitcast.16, bf16[8,512,512]{2,1,0:T(8,128)(2,1)} %bitcast.9, bf16[8,512,512]{2,1,0:T(8,128)(2,1)} %bitcast.10, bf16[1,2,1024,512]{3,2,1,0:T(8,128)(2,1)} %ku_ref.1, ...), custom_call_target="tpu_custom_call" | custom-call | tf_op jit(solution)/shard_map/facets/pallas_call | solution.py:275
  119.8 47.4 %reduce-scatter.2.cloned.1.call-done = bf16[1,512,512]{2,1,0:T(8,128)(2,1)} async-done(((bf16[8,512,512]{2,1,0:T(8,128)(2,1)}), bf16[1,512,512]{2,1,0:T(8,128)(2,1)}) %reduce-scatter.2.cloned.1.call-update) | async-done | bytes 524304 | tf_op jit(solution)/shard_map/reduce_scatter | solution.py:333
  167.2 5.8 %back.2 = (f32[512,512]{1,0:T(8,128)}, f32[272,256]{1,0:T(8,128)}, f32[2,272,128]{2,1,0:T(8,128)}) custom-call(bf16[512,512]{1,0:T(8,128)(2,1)} %bitcast.11, bf16[4,9,256,256]{3,2,1,0:T(8,128)(2,1)} %coef_ref.6, f32[512,512]{1,0:T(8,128)} %xi_ref.6), custom_call_target="tpu_custom_call" | custom-call | tf_op jit(solution)/shard_map/back/pallas_call | solution.py:176
  174.2 3.7 %collective-permute-start.8 = (f32[258]{0:T(512)S(1)}, f32[258]{0:T(512)S(1)}, u32[]{:S(2)}, u32[]{:S(2)}) collective-permute-start(f32[258]{0:T(512)S(1)} %get-tuple-element.29), channel_id=1, source_target_pairs={{0,1},{1,2},{2,3},{3,4},{4,5},{5,6},{6,7},{8,9},{9,10},{10,11},{11... | collective-permute-start | bytes 3104 | tf_op jit(solution)/shard_map/ppermute | solution.py:206
  177.9 1.9 collective-permute-start.9
  182.0 3.4 %collective-permute-start.10 = (f32[1,256]{1,0:T(1,128)S(1)}, f32[1,256]{1,0:T(1,128)S(1)}, u32[]{:S(2)}, u32[]{:S(2)}) collective-permute-start(f32[1,256]{1,0:T(1,128)S(1)} %get-tuple-element.32), channel_id=1, source_target_pairs={{0,8},{8,16},{16,24},{1,9},{9,17},{17,25},{2,10},{10,18},{18,26},{... | collective-permute-start | bytes 3080 | tf_op jit(solution)/shard_map/ppermute | solution.py:215
  185.4 2.4 collective-permute-start.11
  187.8 4.0 %collective-permute-done.11 = f32[1,256]{1,0:T(1,128)S(1)} collective-permute-done((f32[1,256]{1,0:T(1,128)S(1)}, f32[1,256]{1,0:T(1,128)S(1)}, u32[]{:S(2)}, u32[]{:S(2)}) %collective-permute-start.11) | collective-permute-done | bytes 1056 | tf_op jit(solution)/shard_map/ppermute | solution.py:216
  193.6 2.8 %back.3 = (f32[256,256]{1,0:T(8,128)}, f32[144,128]{1,0:T(8,128)}, f32[2,144,128]{2,1,0:T(8,128)}) custom-call(f32[256,256]{1,0:T(8,128)} %fusion.3.g_ref, bf16[4,9,128,128]{3,2,1,0:T(8,128)(2,1)} %coef_ref.7, f32[256,256]{1,0:T(8,128)} %xi_ref.7), custom_call_target="tpu_custom_call" | custom-call | tf_op jit(solution)/shard_map/back/pallas_call | solution.py:176
  197.5 2.2 collective-permute-start.13
  199.6 2.1 collective-permute-start.12
  201.9 2.6 %collective-permute-done.12 = f32[130]{0:T(256)S(1)} collective-permute-done((f32[130]{0:T(256)S(1)}, f32[130]{0:T(256)S(1)}, u32[]{:S(2)}, u32[]{:S(2)}) %collective-permute-start.12) | collective-permute-done | bytes 552 | tf_op jit(solution)/shard_map/ppermute | solution.py:206
  205.4 2.5 %collective-permute-start.14 = (f32[1,128]{1,0:T(1,128)S(1)}, f32[1,128]{1,0:T(1,128)S(1)}, u32[]{:S(2)}, u32[]{:S(2)}) collective-permute-start(f32[1,128]{1,0:T(1,128)S(1)} %get-tuple-element.38), channel_id=1, source_target_pairs={{0,8},{8,16},{16,24},{1,9},{9,17},{17,25},{2,10},{10,18},{18,26},{... | collective-permute-start | bytes 1544 | tf_op jit(solution)/shard_map/ppermute | solution.py:215
  207.9 3.4 %collective-permute-start.15 = (f32[1,128]{1,0:T(1,128)S(1)}, f32[1,128]{1,0:T(1,128)S(1)}, u32[]{:S(2)}, u32[]{:S(2)}) collective-permute-start(f32[1,128]{1,0:T(1,128)S(1)} %get-tuple-element.39), channel_id=1, source_target_pairs={{8,0},{16,8},{24,16},{9,1},{17,9},{25,17},{10,2},{18,10},{26,18},{... | collective-permute-start | bytes 1544 | tf_op jit(solution)/shard_map/ppermute | solution.py:216
  214.2 2.2 multiply_reduce_fusion
  221.6 2.2 collective-permute-done.17
  224.5 3.8 %collective-permute-start.18 = (f32[1]{0:T(128)}, f32[1]{0:T(128)}, u32[]{:S(2)}, u32[]{:S(2)}) collective-permute-start(f32[1]{0:T(128)} %add.98), channel_id=1, source_target_pairs={{0,4},{1,5},{2,6},{3,7},{4,0},{5,1},{6,2},{7,3},{8,12},{9,13},{10,... | collective-permute-start | bytes 20 | tf_op jit(solution)/shard_map/ppermute | solution.py:331
  235.3 2.2 collective-permute-done.20
  (50 shorter events, 27.2 us)
Async XLA Ops:
  7.2 96.9 %all-gather.3.cloned.1.call-start = ((), (), s32[]{:S(2)}) async-start(), calls=%async_computation.2 | async-start | bytes 4718592 | tf_op jit(solution)/shard_map/all_gather | solution.py:321
  7.9 5.8 %collective-permute-start = (f32[1,128]{1,0:T(1,128)S(1)}, f32[1,128]{1,0:T(1,128)S(1)}, u32[]{:S(2)}, u32[]{:S(2)}) collective-permute-start(f32[1,128]{1,0:T(1,128)S(1)} %get-tuple-element.44), channel_id=1, source_target_pairs={{0,8},{8,16},{16,24},{1,9},{9,17},{17,25},{2,10},{10,18},{18,26},{... | collective-permute-start | bytes 1544 | tf_op jit(solution)/shard_map/ppermute | solution.py:23
  11.3 6.3 %collective-permute-start.1 = (f32[1,128]{1,0:T(1,128)S(1)}, f32[1,128]{1,0:T(1,128)S(1)}, u32[]{:S(2)}, u32[]{:S(2)}) collective-permute-start(f32[1,128]{1,0:T(1,128)S(1)} %get-tuple-element.45), channel_id=1, source_target_pairs={{8,0},{16,8},{24,16},{9,1},{17,9},{25,17},{10,2},{18,10},{26,18},{... | collective-permute-start | bytes 1544 | tf_op jit(solution)/shard_map/ppermute | solution.py:24
  18.6 5.6 %collective-permute-start.2 = (f32[130,1]{1,0:T(8,128)S(1)}, f32[130,1]{1,0:T(8,128)S(1)}, u32[]{:S(2)}, u32[]{:S(2)}) collective-permute-start(f32[130,1]{1,0:T(8,128)S(1)} %get-tuple-element.40), channel_id=1, source_target_pairs={{0,1},{1,2},{2,3},{3,4},{4,5},{5,6},{6,7},{8,9},{9,10},{10,11},{11... | collective-permute-start | bytes 1568 | tf_op jit(solution)/shard_map/ppermute | solution.py:23
  20.5 5.6 %collective-permute-start.3 = (f32[130,1]{1,0:T(8,128)S(1)}, f32[130,1]{1,0:T(8,128)S(1)}, u32[]{:S(2)}, u32[]{:S(2)}) collective-permute-start(f32[130,1]{1,0:T(8,128)S(1)} %get-tuple-element.41), channel_id=1, source_target_pairs={{1,0},{2,1},{3,2},{4,3},{5,4},{6,5},{7,6},{9,8},{10,9},{11,10},{12... | collective-permute-start | bytes 1568 | tf_op jit(solution)/shard_map/ppermute | solution.py:24
  31.3 5.8 %collective-permute-start.4 = (f32[1,256]{1,0:T(1,128)S(1)}, f32[1,256]{1,0:T(1,128)S(1)}, u32[]{:S(2)}, u32[]{:S(2)}) collective-permute-start(f32[1,256]{1,0:T(1,128)S(1)} %get-tuple-element.36), channel_id=1, source_target_pairs={{0,8},{8,16},{16,24},{1,9},{9,17},{17,25},{2,10},{10,18},{18,26},{... | collective-permute-start | bytes 3080 | tf_op jit(solution)/shard_map/ppermute | solution.py:23
  33.8 6.4 %collective-permute-start.5 = (f32[1,256]{1,0:T(1,128)S(1)}, f32[1,256]{1,0:T(1,128)S(1)}, u32[]{:S(2)}, u32[]{:S(2)}) collective-permute-start(f32[1,256]{1,0:T(1,128)S(1)} %get-tuple-element.37), channel_id=1, source_target_pairs={{8,0},{16,8},{24,16},{9,1},{17,9},{25,17},{10,2},{18,10},{26,18},{... | collective-permute-start | bytes 3080 | tf_op jit(solution)/shard_map/ppermute | solution.py:24
  41.2 6.3 %collective-permute-start.6 = (f32[258,1]{1,0:T(8,128)S(1)}, f32[258,1]{1,0:T(8,128)S(1)}, u32[]{:S(2)}, u32[]{:S(2)}) collective-permute-start(f32[258,1]{1,0:T(8,128)S(1)} %get-tuple-element.34), channel_id=1, source_target_pairs={{0,1},{1,2},{2,3},{3,4},{4,5},{5,6},{6,7},{8,9},{9,10},{10,11},{11... | collective-permute-start | bytes 3104 | tf_op jit(solution)/shard_map/ppermute | solution.py:23
  43.4 5.9 %collective-permute-start.7 = (f32[258,1]{1,0:T(8,128)S(1)}, f32[258,1]{1,0:T(8,128)S(1)}, u32[]{:S(2)}, u32[]{:S(2)}) collective-permute-start(f32[258,1]{1,0:T(8,128)S(1)} %get-tuple-element.35), channel_id=1, source_target_pairs={{1,0},{2,1},{3,2},{4,3},{5,4},{6,5},{7,6},{9,8},{10,9},{11,10},{12... | collective-permute-start | bytes 3104 | tf_op jit(solution)/shard_map/ppermute | solution.py:24
  57.6 109.5 %reduce-scatter.2.cloned.1.call-start = ((), (), s32[]{:S(2)}) async-start(), calls=%async_computation.1 | async-start | bytes 4718592 | tf_op jit(solution)/shard_map/reduce_scatter | solution.py:333
  167.2 44.1 %copy-start.3 = (f32[8,256]{1,0:T(8,128)S(1)}, f32[8,256]{1,0:T(8,128)}, u32[]{:S(2)}) copy-start(f32[8,256]{1,0:T(8,128)} %get-tuple-element.25) | copy-start | bytes 24580
  167.2 44.8 %copy-start.2 = (f32[8,512]{1,0:T(8,128)S(1)}, f32[8,512]{1,0:T(8,128)}, u32[]{:S(2)}) copy-start(f32[8,512]{1,0:T(8,128)} %get-tuple-element.26) | copy-start | bytes 49156
  167.2 45.5 %copy-start.1 = (f32[8,1024]{1,0:T(8,128)S(1)}, f32[8,1024]{1,0:T(8,128)}, u32[]{:S(2)}) copy-start(f32[8,1024]{1,0:T(8,128)} %get-tuple-element.27) | copy-start | bytes 98308
  167.2 47.0 %copy-start = (f32[128,128]{1,0:T(8,128)S(1)}, f32[128,128]{1,0:T(8,128)}, u32[]{:S(2)}) copy-start(f32[128,128]{1,0:T(8,128)} %param.11) | copy-start | bytes 196612
  174.2 5.6 %collective-permute-start.8 = (f32[258]{0:T(512)S(1)}, f32[258]{0:T(512)S(1)}, u32[]{:S(2)}, u32[]{:S(2)}) collective-permute-start(f32[258]{0:T(512)S(1)} %get-tuple-element.29), channel_id=1, source_target_pairs={{0,1},{1,2},{2,3},{3,4},{4,5},{5,6},{6,7},{8,9},{9,10},{10,11},{11... | collective-permute-start | bytes 3104 | tf_op jit(solution)/shard_map/ppermute | solution.py:206
  177.9 3.2 %collective-permute-start.9 = (f32[258]{0:T(512)S(1)}, f32[258]{0:T(512)S(1)}, u32[]{:S(2)}, u32[]{:S(2)}) collective-permute-start(f32[258]{0:T(512)S(1)} %get-tuple-element.28), channel_id=1, source_target_pairs={{1,0},{2,1},{3,2},{4,3},{5,4},{6,5},{7,6},{9,8},{10,9},{11,10},{12... | collective-permute-start | bytes 3104 | tf_op jit(solution)/shard_map/ppermute | solution.py:207
  182.0 5.8 %collective-permute-start.10 = (f32[1,256]{1,0:T(1,128)S(1)}, f32[1,256]{1,0:T(1,128)S(1)}, u32[]{:S(2)}, u32[]{:S(2)}) collective-permute-start(f32[1,256]{1,0:T(1,128)S(1)} %get-tuple-element.32), channel_id=1, source_target_pairs={{0,8},{8,16},{16,24},{1,9},{9,17},{17,25},{2,10},{10,18},{18,26},{... | collective-permute-start | bytes 3080 | tf_op jit(solution)/shard_map/ppermute | solution.py:215
  185.4 6.4 %collective-permute-start.11 = (f32[1,256]{1,0:T(1,128)S(1)}, f32[1,256]{1,0:T(1,128)S(1)}, u32[]{:S(2)}, u32[]{:S(2)}) collective-permute-start(f32[1,256]{1,0:T(1,128)S(1)} %get-tuple-element.33), channel_id=1, source_target_pairs={{8,0},{16,8},{24,16},{9,1},{17,9},{25,17},{10,2},{18,10},{26,18},{... | collective-permute-start | bytes 3080 | tf_op jit(solution)/shard_map/ppermute | solution.py:216
  197.5 4.3 %collective-permute-start.13 = (f32[130]{0:T(256)S(1)}, f32[130]{0:T(256)S(1)}, u32[]{:S(2)}, u32[]{:S(2)}) collective-permute-start(f32[130]{0:T(256)S(1)} %get-tuple-element.31), channel_id=1, source_target_pairs={{1,0},{2,1},{3,2},{4,3},{5,4},{6,5},{7,6},{9,8},{10,9},{11,10},{12... | collective-permute-start | bytes 1568 | tf_op jit(solution)/shard_map/ppermute | solution.py:207
  199.6 4.9 %collective-permute-start.12 = (f32[130]{0:T(256)S(1)}, f32[130]{0:T(256)S(1)}, u32[]{:S(2)}, u32[]{:S(2)}) collective-permute-start(f32[130]{0:T(256)S(1)} %get-tuple-element.30), channel_id=1, source_target_pairs={{0,1},{1,2},{2,3},{3,4},{4,5},{5,6},{6,7},{8,9},{9,10},{10,11},{11... | collective-permute-start | bytes 1568 | tf_op jit(solution)/shard_map/ppermute | solution.py:206
  205.4 8.5 %collective-permute-start.14 = (f32[1,128]{1,0:T(1,128)S(1)}, f32[1,128]{1,0:T(1,128)S(1)}, u32[]{:S(2)}, u32[]{:S(2)}) collective-permute-start(f32[1,128]{1,0:T(1,128)S(1)} %get-tuple-element.38), channel_id=1, source_target_pairs={{0,8},{8,16},{16,24},{1,9},{9,17},{17,25},{2,10},{10,18},{18,26},{... | collective-permute-start | bytes 1544 | tf_op jit(solution)/shard_map/ppermute | solution.py:215
  207.9 6.3 %collective-permute-start.15 = (f32[1,128]{1,0:T(1,128)S(1)}, f32[1,128]{1,0:T(1,128)S(1)}, u32[]{:S(2)}, u32[]{:S(2)}) collective-permute-start(f32[1,128]{1,0:T(1,128)S(1)} %get-tuple-element.39), channel_id=1, source_target_pairs={{8,0},{16,8},{24,16},{9,1},{17,9},{25,17},{10,2},{18,10},{26,18},{... | collective-permute-start | bytes 1544 | tf_op jit(solution)/shard_map/ppermute | solution.py:216
  218.4 1.2 collective-permute-start.16
  220.3 3.6 %collective-permute-start.17 = (f32[1]{0:T(128)}, f32[1]{0:T(128)}, u32[]{:S(2)}, u32[]{:S(2)}) collective-permute-start(f32[1]{0:T(128)} %add.97), channel_id=1, source_target_pairs={{0,2},{1,3},{2,0},{3,1},{4,6},{5,7},{6,4},{7,5},{8,10},{9,11},{10,... | collective-permute-start | bytes 20 | tf_op jit(solution)/shard_map/ppermute | solution.py:331
  224.5 4.5 %collective-permute-start.18 = (f32[1]{0:T(128)}, f32[1]{0:T(128)}, u32[]{:S(2)}, u32[]{:S(2)}) collective-permute-start(f32[1]{0:T(128)} %add.98), channel_id=1, source_target_pairs={{0,4},{1,5},{2,6},{3,7},{4,0},{5,1},{6,2},{7,3},{8,12},{9,13},{10,... | collective-permute-start | bytes 20 | tf_op jit(solution)/shard_map/ppermute | solution.py:331
  229.7 3.6 %collective-permute-start.19 = (f32[1]{0:T(128)}, f32[1]{0:T(128)}, u32[]{:S(2)}, u32[]{:S(2)}) collective-permute-start(f32[1]{0:T(128)} %add.99), channel_id=1, source_target_pairs={{0,8},{8,0},{16,24},{24,16},{1,9},{9,1},{17,25},{25,17},{2,10},{10... | collective-permute-start | bytes 20 | tf_op jit(solution)/shard_map/ppermute | solution.py:331
  233.9 3.6 %collective-permute-start.20 = (f32[1]{0:T(128)}, f32[1]{0:T(128)}, u32[]{:S(2)}, u32[]{:S(2)}) collective-permute-start(f32[1]{0:T(128)} %add.100), channel_id=1, source_target_pairs={{0,16},{8,24},{16,0},{24,8},{1,17},{9,25},{17,1},{25,9},{2,18},{10... | collective-permute-start | bytes 20 | tf_op jit(solution)/shard_map/ppermute | solution.py:331
Sparse Core Ops, SparseCore 0:
  57.7 46.2 all-gather.2
  119.9 47.2 reduce-scatter.1

commit v2 on v1

--- a/solution.py
+++ b/solution.py
@@ -115,7 +115,9 @@
     )(padded, coef, xi)
 
 
-def back_kernel(blk, g_ref, coef_ref, xi_ref, grad_ref, main_ref, cols_ref, terms, perm, mix, rowed):
+def back_kernel(blk, number, *refs):
+    parts = refs[:number]
+    coef_ref, xi_ref, grad_ref, main_ref, cols_ref, terms, perm, mix, rowed = refs[number:]
     rows, cols = terms.shape[1:]
     step = pl.program_id(0)
 
@@ -124,14 +126,13 @@
         perm[...] = interleaver(cols, True)
 
     base = step * blk
-    g = g_ref[...]
-    grad_ref[...] = g.astype(f32) + xi_ref[...]
-    if g.dtype == bf16:
-        split = jnp.dot(g, perm[...], preferred_element_type=f32)
-    else:
-        high, low = halves(g)
-        both = jnp.dot(jnp.concatenate([high, low]), perm[...], preferred_element_type=f32)
-        split = both[: 2 * blk] + both[2 * blk :]
+    g = parts[0][...].astype(f32)
+    for part in parts[1:]:
+        g += part[...].astype(f32)
+    grad_ref[...] = g + xi_ref[...]
+    high, low = halves(g)
+    both = jnp.dot(jnp.concatenate([high, low]), perm[...], preferred_element_type=f32)
+    split = both[: 2 * blk] + both[2 * blk :]
     for tile in range(2 * cols // 128):
         mix[tile] = split[:, tile * 128 : (tile + 1) * 128]
 
@@ -170,14 +171,14 @@
         cols_ref[1] = rowed[2, :, cols - 128 :]
 
 
-def back(g, coef, xi):
+def back(parts, coef, xi):
     rows, cols = coef.shape[2:]
     blk = 64
     grad, main, side = pl.pallas_call(
-        functools.partial(back_kernel, blk),
+        functools.partial(back_kernel, blk, len(parts)),
         grid=(rows // blk,),
-        in_specs=[
-            pl.BlockSpec((2 * blk, 2 * cols), lambda i: (i, 0)),
+        in_specs=[pl.BlockSpec((2 * blk, 2 * cols), lambda i: (i, 0))] * len(parts)
+        + [
             pl.BlockSpec((4, 9, blk, cols), lambda i: (0, 0, i, 0)),
             pl.BlockSpec((2 * blk, 2 * cols), lambda i: (i, 0)),
         ],
@@ -199,7 +200,7 @@
         ],
         compiler_params=pltpu.CompilerParams(vmem_limit_bytes=vmem),
         name="back",
-    )(g, coef, xi)
+    )(*parts, coef, xi)
     size = lax.axis_size("gy")
     right = [(i, i + 1) for i in range(size - 1)]
     left = [(j, i) for i, j in right]
@@ -224,23 +225,30 @@
 
 
 def facet_kernel(
-    blk, lists, weights, counts, one_ref, two_ref, ku_ref, kv_ref, data_ref, out_ref, lik_ref, sums, dsum
+    blk, number, sel, weights, counts, *refs
 ):
-    facet, step = pl.program_id(0), pl.program_id(1)
-    facets, steps = pl.num_programs(0), pl.num_programs(1)
-
-    @pl.when((facet == 0) & (step == 0))
-    def _():
+    tiles = refs[:number]
+    ku_ref, kv_ref, data_ref, out_ref, lik_ref, sums, dsum, held, sems = refs[number:]
+    step = pl.program_id(0)
+
+    @pl.when(step == 0)
+    def _():
+        for s in range(held.shape[0]):
+            for i in range(number):
+
+                @pl.when(sel[s] == i)
+                def _():
+                    pltpu.make_async_copy(tiles[i], held.at[s], sems.at[s]).start()
+
         lik_ref[...] = jnp.zeros_like(lik_ref)
-
-    @pl.when(step == 0)
-    def _():
-        sums[...] = (
-            weights[facet, 0] * one_ref[0].astype(f32) + weights[facet, 1] * two_ref[0].astype(f32)
-        ).astype(bf16)
-        dsum[facet] = jnp.zeros(dsum.shape[1:], f32)
-
-    count = counts[facet] - step * blk
+        dsum[...] = jnp.zeros_like(dsum)
+        total = jnp.zeros(dsum.shape, f32)
+        for s in range(held.shape[0]):
+            pltpu.make_async_copy(tiles[0], held.at[s], sems.at[s]).wait()
+            total += weights[s] * held[s].astype(f32)
+        sums[...] = total.astype(bf16)
+
+    count = counts[0] - step * blk
 
     @pl.when(count > 0)
     def _():
@@ -252,54 +260,92 @@
         lik_ref[...] += jnp.sum((resid * resid).reshape(blk // 8, 8, vis.shape[1]), axis=0)
         dvis = (inv_noise * resid).astype(bf16)
         damp = jnp.dot(dvis, kv, preferred_element_type=f32).astype(bf16)
-        dsum[facet] += lax.dot_general(
-            ku, damp, (((0,), (0,)), ((), ())), preferred_element_type=f32
-        )
-
-    @pl.when((facet == facets - 1) & (step == steps - 1))
-    def _():
-        for t in range(out_ref.shape[0]):
-            total = None
-            for f in range(dsum.shape[0]):
-                scale = jnp.float32(0.0)
-                for s in range(lists.shape[1]):
-                    scale += jnp.where(lists[f, s] == t, weights[f, s], 0.0)
-                term = scale * dsum[f]
-                total = term if total is None else total + term
-            out_ref[t] = total.astype(bf16)
-
-
-def facets(tiles, ku, kv, data, lists, weights, counts):
-    number, bins, side = ku.shape[1:]
+        dsum[...] += lax.dot_general(ku, damp, (((0,), (0,)), ((), ())), preferred_element_type=f32)
+
+    @pl.when(step == pl.num_programs(0) - 1)
+    def _():
+        out_ref[...] = dsum[...].astype(bf16)
+
+
+def facet(f, tiles, ku, kv, data, sel, weights, count):
+    bins, side = ku.shape[2:]
     blk = 256
+    slots = sel.shape[0]
     return pl.pallas_call(
-        functools.partial(facet_kernel, blk),
+        functools.partial(facet_kernel, blk, len(tiles)),
         grid_spec=pltpu.PrefetchScalarGridSpec(
             num_scalar_prefetch=3,
-            grid=(number, bins // blk),
-            in_specs=[
-                pl.BlockSpec((1, side, side), lambda f, i, ls, ws, cs: (ls[f, 0], 0, 0)),
-                pl.BlockSpec((1, side, side), lambda f, i, ls, ws, cs: (ls[f, 1], 0, 0)),
-                pl.BlockSpec((1, 1, blk, side), lambda f, i, ls, ws, cs: (0, f, i, 0)),
-                pl.BlockSpec((1, 1, bins, side), lambda f, i, ls, ws, cs: (0, f, 0, 0)),
-                pl.BlockSpec((1, 1, blk, bins), lambda f, i, ls, ws, cs: (0, f, i, 0)),
+            grid=(bins // blk,),
+            in_specs=[pl.BlockSpec(memory_space=pl.ANY)] * len(tiles)
+            + [
+                pl.BlockSpec((1, 1, blk, side), lambda i, *_: (0, f, i, 0)),
+                pl.BlockSpec((1, 1, bins, side), lambda i, *_: (0, f, 0, 0)),
+                pl.BlockSpec((1, 1, blk, bins), lambda i, *_: (0, f, i, 0)),
             ],
             out_specs=[
-                pl.BlockSpec(tiles.shape, lambda f, i, ls, ws, cs: (0, 0, 0)),
-                pl.BlockSpec((8, bins), lambda f, i, ls, ws, cs: (0, 0)),
+                pl.BlockSpec((side, side), lambda i, *_: (0, 0)),
+                pl.BlockSpec((8, bins), lambda i, *_: (0, 0)),
             ],
             scratch_shapes=[
                 pltpu.VMEM((side, side), bf16),
-                pltpu.VMEM((number, side, side), f32),
+                pltpu.VMEM((side, side), f32),
+                pltpu.VMEM((slots, side, side), bf16),
+                pltpu.SemaphoreType.DMA((slots,)),
             ],
         ),
         out_shape=[
-            jax.ShapeDtypeStruct(tiles.shape, bf16),
+            jax.ShapeDtypeStruct((side, side), bf16),
             jax.ShapeDtypeStruct((8, bins), f32),
         ],
         compiler_params=pltpu.CompilerParams(vmem_limit_bytes=vmem),
-        name="facets",
-    )(lists, weights, counts, tiles, tiles, ku, kv, data)
+        name="facet",
+    )(sel, weights, count, *tiles, ku, kv, data)
+
+
+def mix_kernel(number, scale, *refs):
+    dsums, outs = refs[:number], refs[number:]
+    for d, out in enumerate(outs):
+        total = None
+        for f, dsum in enumerate(dsums):
+            term = scale[d, f] * dsum[...].astype(f32)
+            total = term if total is None else total + term
+        out[...] = total.astype(bf16)
+
+
+def mixed(dsums, scale):
+    rows, cols = dsums[0].shape
+    blk = 128
+    return pl.pallas_call(
+        functools.partial(mix_kernel, len(dsums)),
+        grid_spec=pltpu.PrefetchScalarGridSpec(
+            num_scalar_prefetch=1,
+            grid=(rows // blk,),
+            in_specs=[pl.BlockSpec((blk, cols), lambda i, _: (i, 0))] * len(dsums),
+            out_specs=[pl.BlockSpec((blk, cols), lambda i, _: (i, 0))] * scale.shape[0],
+        ),
+        out_shape=[jax.ShapeDtypeStruct((rows, cols), bf16)] * scale.shape[0],
+        compiler_params=pltpu.CompilerParams(vmem_limit_bytes=vmem),
+        name="mixed",
+    )(scale, *dsums)
+
+
+def chip_shift(x, hop):
+    size = lax.axis_size("gy")
+    return lax.ppermute(x, "gy", [(i, (i + 2 * hop) % size) for i in range(size)])
+
+
+def swapped(x):
+    return lax.ppermute(x, "gy", [(i, i ^ 1) for i in range(lax.axis_size("gy"))])
+
+
+def summed(x):
+    for axis in ("gy", "gx"):
+        size = lax.axis_size(axis)
+        hop = 1
+        while hop < size:
+            x += lax.ppermute(x, axis, [(i, i ^ hop) for i in range(size)])
+            hop *= 2
+    return x
 
 
 def body(
@@ -318,21 +364,35 @@
     side = xi_fine.shape[0]
     level_middle, sq_middle = refine(widen(xi_coarse), coef_middle, xi_middle, f32)
     sky, sq_fine = refine(widen(level_middle), coef_fine, xi_fine, bf16)
-    tiles = lax.all_gather(sky, "gy", axis=0)
-    dtiles, lik = facets(
-        tiles, kern_u, kern_v, vis_data, facet_tiles[0], facet_weight[0], facet_count[0]
+    lists, weights, counts = facet_tiles[0], facet_weight[0], facet_count[0]
+    number = lists.shape[0]
+    size = lax.axis_size("gy")
+    chips = size // 2
+    me = lax.axis_index("gy")
+    ids = jnp.arange(size, dtype=jnp.int32)
+    mixing = jnp.sum(
+        weights[:, :, None] * (lists[:, :, None] == ids[None, None, :]).astype(f32), axis=1
     )
+    order = 2 * ((me // 2 + jnp.arange(chips, dtype=jnp.int32)) % chips) + me % 2
+    scale = jnp.concatenate([mixing, swapped(mixing)])[:, order].T
+    mine = [sky] + [chip_shift(sky, hop) for hop in range(1, chips)]
+    tiles = mine + [swapped(tile) for tile in mine]
+    sel = (me // 2 - lists // 2) % chips + jnp.where(lists % 2 == me % 2, 0, chips)
+    dsums, theirs, likelihood = [], [], 0.0
+    for f in range(number):
+        dsum, lik = facet(
+            f, tiles, kern_u, kern_v, vis_data, sel[f], weights[f], counts[f : f + 1]
+        )
+        dsums.append(dsum)
+        theirs.append(swapped(dsum))
+        likelihood += jnp.sum(lik)
+    parts = mixed(dsums + theirs, scale)
+    parts = [parts[0]] + [chip_shift(parts[hop], hop) for hop in range(1, chips)]
     potential = 0.5 * (jnp.sum(xi_coarse * xi_coarse) + jnp.sum(sq_middle) + jnp.sum(sq_fine))
-    potential = (potential + 0.5 * inv_noise * jnp.sum(lik))[None]
-    for axis in ("gy", "gx"):
-        size = lax.axis_size(axis)
-        hop = 1
-        while hop < size:
-            potential += lax.ppermute(potential, axis, [(i, i ^ hop) for i in range(size)])
-            hop *= 2
-    dsky = lax.psum_scatter(dtiles, "gy", scatter_dimension=0, tiled=False)
-    grad_fine, dmiddle = back(dsky, coef_fine, xi_fine)
-    grad_middle, dcoarse = back(dmiddle, coef_middle, xi_middle)
+    potential = summed((potential + 0.5 * inv_noise * likelihood)[None])
+    parts, potential = lax.optimization_barrier((parts, potential))
+    grad_fine, dmiddle = back(parts, coef_fine, xi_fine)
+    grad_middle, dcoarse = back([dmiddle], coef_middle, xi_middle)
     grad_coarse = dcoarse + xi_coarse
     cells = lax.axis_size("gx") * lax.axis_size("gy") * side * side
     return (grad_coarse, grad_middle, grad_fine, potential[0] / cells)

time: 249 us -> 241 us (0.968)
  waiting for transfers between devices: 120 us -> 56.5 us
  starting transfers between devices: 53.8 us -> 106 us
  between operations: 21.6 us -> 8.35 us
  Pallas kernels: 33.5 us -> 42.3 us
  local copies, waits for them, and re-layouts: 4.34 us -> 11.2 us
    ppermute x5 -> x18, starting transfers between devices: 9.37 us -> 60.8 us  [the longest x5 26.9 us: summed(): x += lax.ppermute(x, axis, [(i, i ^ hop) for i in range(size)])]
    reduce_scatter x1 -> x0, waiting for transfers between devices: 47.4 us -> none  [body(): dsky = lax.psum_scatter(dtiles, 'gy', scatter_dimension=0, tiled=False)]
    all_gather x1 -> x0, waiting for transfers between devices: 46.4 us -> none  [body(): tiles = lax.all_gather(sky, 'gy', axis=0)]
    ppermute x5 -> x18, waiting for transfers between devices: 6.92 us -> 37.5 us  [the longest x6 20.2 us: chip_shift(): lax.ppermute(x, 'gy', [(i, (i + 2 * hop) % size) for i in range(size)])]
    pallas_call x3 -> x5, Pallas kernels: 24.3 us -> 33.1 us  [the longest x2 18.8 us: facet(): pl.pallas_call(functools.partial(facet_kernel, blk, len(tiles)), grid_spe...]
    unnamed x8 -> x40, local copies, waits for them, and re-layouts: 0.01 us -> 3.96 us
    ppermute x2, starting transfers between devices: 4.1 us -> 6.86 us  [back(): from_right = lax.ppermute(side[0, 7:9 + rows, 0], 'gy', left)]
    ppermute x2, waiting for transfers between devices: 2.62 us -> 0.01 us  [back(): from_left = lax.ppermute(side[1, 7:9 + rows, 127], 'gy', right)]
  transfers between devices with their start and end apart: 23 -> 34, of which waited for: 16 -> 18; matrix products, arithmetic and copies ran while one was open for 1% -> 3% of each run, Pallas kernels for 0% -> 4%
where the time goes in v2:
time: 241 us; the launch traced here: 238 us
  starting transfers between devices  106 us (44%)
  waiting for transfers between devices  56.5 us (23%)
  Pallas kernels  42.3 us (18%)
  other arithmetic  13.5 us (6%)
  local copies, waits for them, and re-layouts  11.2 us (5%)
  between operations  8.35 us (3%)
    ppermute x5, starting transfers between devices, summed(): x += lax.ppermute(x, axis, [(i, i ^ hop) for i in range(size)])  26.9 us
    ppermute x7, starting transfers between devices, swapped(): lax.ppermute(x, 'gy', [(i, i ^ 1) for i in range(lax.axis_size('gy'))])  25.6 us
    ppermute x6, waiting for transfers between devices, chip_shift(): lax.ppermute(x, 'gy', [(i, (i + 2 * hop) % size) for i in range(size)])  20.2 us
    pallas_call x2, Pallas kernels, facet(): pl.pallas_call(functools.partial(facet_kernel, blk, len(tiles)), grid_spe...  18.8 us
    ppermute x5, waiting for transfers between devices, summed(): x += lax.ppermute(x, axis, [(i, i ^ hop) for i in range(size)])  16 us
    ppermute x4, starting transfers between devices, extended(): after = lax.ppermute(leading, axis, down)  12.8 us
    ppermute x4, waiting for transfers between devices, extended(): after = lax.ppermute(leading, axis, down)  10.5 us
    ppermute x4, starting transfers between devices, extended(): before = lax.ppermute(last, axis, up)  10 us
  transfers between devices with their start and end apart: 34, of which 18 were waited for; matrix products, arithmetic and copies ran while one was open for 3% of the time, Pallas kernels for 4%

profile of v2, /device:TPU:10, one launch (start us, length us, event | category | flops | bytes accessed | tf_op | source)
XLA Modules:
  0.0 238.2 jit_solution(16555778072143622558)
XLA Ops:
  1.3 3.4 %collective-permute-start.1 = (f32[1,128]{1,0:T(1,128)S(1)}, f32[1,128]{1,0:T(1,128)S(1)}, u32[]{:S(2)}, u32[]{:S(2)}) collective-permute-start(f32[1,128]{1,0:T(1,128)S(1)} %get-tuple-element.64), channel_id=1, source_target_pairs={{0,8},{8,16},{16,24},{1,9},{9,17},{17,25},{2,10},{10,18},{18,26},{... | collective-permute-start | bytes 1544 | tf_op jit(solution)/shard_map/ppermute | solution.py:23
  4.7 2.4 %collective-permute-start.2 = (f32[1,128]{1,0:T(1,128)S(1)}, f32[1,128]{1,0:T(1,128)S(1)}, u32[]{:S(2)}, u32[]{:S(2)}) collective-permute-start(f32[1,128]{1,0:T(1,128)S(1)} %get-tuple-element.65), channel_id=1, source_target_pairs={{8,0},{16,8},{24,16},{9,1},{17,9},{25,17},{10,2},{18,10},{26,18},{... | collective-permute-start | bytes 1544 | tf_op jit(solution)/shard_map/ppermute | solution.py:24
  7.2 3.9 %collective-permute-done.2 = f32[1,128]{1,0:T(1,128)S(1)} collective-permute-done((f32[1,128]{1,0:T(1,128)S(1)}, f32[1,128]{1,0:T(1,128)S(1)}, u32[]{:S(2)}, u32[]{:S(2)}) %collective-permute-start.2) | collective-permute-done | bytes 544 | tf_op jit(solution)/shard_map/ppermute | solution.py:24
  13.9 3.6 %collective-permute-start.4 = (f32[130,1]{1,0:T(8,128)S(1)}, f32[130,1]{1,0:T(8,128)S(1)}, u32[]{:S(2)}, u32[]{:S(2)}) collective-permute-start(f32[130,1]{1,0:T(8,128)S(1)} %get-tuple-element.63), channel_id=1, source_target_pairs={{1,0},{2,1},{3,2},{4,3},{5,4},{6,5},{7,6},{9,8},{10,9},{11,10},{12... | collective-permute-start | bytes 1568 | tf_op jit(solution)/shard_map/ppermute | solution.py:24
  21.1 2.9 %refine.2 = (f32[256,256]{1,0:T(8,128)}, f32[8,256]{1,0:T(8,128)}) custom-call(f32[130,130]{1,0:T(8,128)} %pad_maximum_fusion.2.pad_ref, bf16[4,9,128,128]{3,2,1,0:T(8,128)(2,1)} %refs_1_.1, f32[256,256]{1,0:T(8,128)} %refs_2_.1), custom_call_target="tpu_custom_call" | custom-call | tf_op jit(solution)/shard_map/refine/pallas_call | solution.py:91
  24.7 2.5 %collective-permute-start.5 = (f32[1,256]{1,0:T(1,128)S(1)}, f32[1,256]{1,0:T(1,128)S(1)}, u32[]{:S(2)}, u32[]{:S(2)}) collective-permute-start(f32[1,256]{1,0:T(1,128)S(1)} %get-tuple-element.58), channel_id=1, source_target_pairs={{0,8},{8,16},{16,24},{1,9},{9,17},{17,25},{2,10},{10,18},{18,26},{... | collective-permute-start | bytes 3080 | tf_op jit(solution)/shard_map/ppermute | solution.py:23
  27.2 3.3 %collective-permute-start.6 = (f32[1,256]{1,0:T(1,128)S(1)}, f32[1,256]{1,0:T(1,128)S(1)}, u32[]{:S(2)}, u32[]{:S(2)}) collective-permute-start(f32[1,256]{1,0:T(1,128)S(1)} %get-tuple-element.59), channel_id=1, source_target_pairs={{8,0},{16,8},{24,16},{9,1},{17,9},{25,17},{10,2},{18,10},{26,18},{... | collective-permute-start | bytes 3080 | tf_op jit(solution)/shard_map/ppermute | solution.py:24
  30.5 3.0 %collective-permute-done.6 = f32[1,256]{1,0:T(1,128)S(1)} collective-permute-done((f32[1,256]{1,0:T(1,128)S(1)}, f32[1,256]{1,0:T(1,128)S(1)}, u32[]{:S(2)}, u32[]{:S(2)}) %collective-permute-start.6) | collective-permute-done | bytes 1056 | tf_op jit(solution)/shard_map/ppermute | solution.py:24
  34.6 2.2 collective-permute-start.7
  36.9 3.3 %collective-permute-start.8 = (f32[258,1]{1,0:T(8,128)S(1)}, f32[258,1]{1,0:T(8,128)S(1)}, u32[]{:S(2)}, u32[]{:S(2)}) collective-permute-start(f32[258,1]{1,0:T(8,128)S(1)} %get-tuple-element.57), channel_id=1, source_target_pairs={{1,0},{2,1},{3,2},{4,3},{5,4},{6,5},{7,6},{9,8},{10,9},{11,10},{12... | collective-permute-start | bytes 3104 | tf_op jit(solution)/shard_map/ppermute | solution.py:24
  44.7 6.4 %refine.3 = (bf16[512,512]{1,0:T(8,128)(2,1)}, f32[8,512]{1,0:T(8,128)}) custom-call(f32[258,258]{1,0:T(8,128)} %pad_maximum_fusion.pad_ref, bf16[4,9,256,256]{3,2,1,0:T(8,128)(2,1)} %refs_4_.1, f32[512,512]{1,0:T(8,128)} %refs_5_.1), custom_call_target="tpu_custom_call" | custom-call | tf_op jit(solution)/shard_map/refine/pallas_call | solution.py:91
  55.8 9.5 %collective-permute-done.9.refs_1_ = bf16[512,512]{1,0:T(8,128)(2,1)S(1)} collective-permute-done((bf16[512,512]{1,0:T(8,128)(2,1)}, bf16[512,512]{1,0:T(8,128)(2,1)S(1)}, u32[]{:S(2)}, u32[]{:S(2)}) %collective-permute-start.9) | collective-permute-done | bytes 524320 | tf_op jit(solution)/shard_map/ppermute | solution.py:334
  65.2 23.5 %collective-permute-start.13 = (bf16[512,512]{1,0:T(8,128)(2,1)S(1)}, bf16[512,512]{1,0:T(8,128)(2,1)S(1)}, u32[]{:S(2)}, u32[]{:S(2)}) collective-permute-start(bf16[512,512]{1,0:T(8,128)(2,1)S(1)} %collective-permute-done.9.refs_1_), channel_id=1, source_target_pairs={{0,1},{1,0},{2,3},{3,2},{4,5},{5,4},{6,7},{7,6},{8,9},{9,8},{10,11... | collective-permute-start | bytes 1572872 | tf_op jit(solution)/shard_map/ppermute | solution.py:338
  88.7 9.5 %collective-permute-done.10.refs_2_ = bf16[512,512]{1,0:T(8,128)(2,1)S(1)} collective-permute-done((bf16[512,512]{1,0:T(8,128)(2,1)}, bf16[512,512]{1,0:T(8,128)(2,1)S(1)}, u32[]{:S(2)}, u32[]{:S(2)}) %collective-permute-start.10) | collective-permute-done | bytes 524320 | tf_op jit(solution)/shard_map/ppermute | solution.py:334
  103.4 10.0 %facet.3 = (bf16[512,512]{1,0:T(8,128)(2,1)}, f32[8,1024]{1,0:T(8,128)}) custom-call(s32[2]{0:T(128)} %get-tuple-element.68.sel, f32[2]{0:T(128)} %get-tuple-element.66.weights, s32[1]{0:T(128)} %bitcast.8.counts, bf16[512,512]{1,0:T(8,128)(2,1)} %get-tuple-element.28.refs_0_, bf16[512,512]{1,0:T(8,128)(2,1)} %copy-done, bf16[512,512]{1,0:T(8,128)(2,1)} %copy-done.1, ...), custom_call_target="tpu_custom_call" | custom-call | tf_op jit(solution)/shard_map/facet/pallas_call | solution.py:274
  113.9 8.8 %facet.2 = (bf16[512,512]{1,0:T(8,128)(2,1)}, f32[8,1024]{1,0:T(8,128)}) custom-call(s32[2]{0:T(128)} %get-tuple-element.69.sel, f32[2]{0:T(128)} %get-tuple-element.67.weights, s32[1]{0:T(128)} %bitcast.5.counts, bf16[512,512]{1,0:T(8,128)(2,1)} %get-tuple-element.28.refs_0_, bf16[512,512]{1,0:T(8,128)(2,1)} %copy-done, bf16[512,512]{1,0:T(8,128)(2,1)} %copy-done.1, ...), custom_call_target="tpu_custom_call" | custom-call | tf_op jit(solution)/shard_map/facet/pallas_call | solution.py:274
  127.5 5.1 %mixed.1 = (bf16[512,512]{1,0:T(8,128)(2,1)}, bf16[512,512]{1,0:T(8,128)(2,1)}, bf16[512,512]{1,0:T(8,128)(2,1)}, bf16[512,512]{1,0:T(8,128)(2,1)}) custom-call(f32[4,4]{1,0:T(4,128)} %gather_fusion, bf16[512,512]{1,0:T(8,128)(2,1)} %get-tuple-element.29.refs_0_, bf16[512,512]{1,0:T(8,128)(2,1)} %get-tuple-element.30.refs_1_, bf16[512,512]{1,0:T(8,128)(2,1)} %copy-done.9, ...), custom_call_target="tpu_custom_call" | custom-call | tf_op jit(solution)/shard_map/mixed/pallas_call | solution.py:318
  144.6 12.9 %collective-permute-start.22 = (f32[1]{0:T(128)}, f32[1]{0:T(128)}, u32[]{:S(2)}, u32[]{:S(2)}) collective-permute-start(f32[1]{0:T(128)} %add.165), channel_id=1, source_target_pairs={{0,2},{1,3},{2,0},{3,1},{4,6},{5,7},{6,4},{7,5},{8,10},{9,11},{10,... | collective-permute-start | bytes 20 | tf_op jit(solution)/shard_map/ppermute | solution.py:346
  157.5 12.1 %collective-permute-done.22 = f32[1]{0:T(128)} collective-permute-done((f32[1]{0:T(128)}, f32[1]{0:T(128)}, u32[]{:S(2)}, u32[]{:S(2)}) %collective-permute-start.22) | collective-permute-done | bytes 36 | tf_op jit(solution)/shard_map/ppermute | solution.py:346
  170.2 9.2 %collective-permute-start.23 = (f32[1]{0:T(128)}, f32[1]{0:T(128)}, u32[]{:S(2)}, u32[]{:S(2)}) collective-permute-start(f32[1]{0:T(128)} %add.166), channel_id=1, source_target_pairs={{0,4},{1,5},{2,6},{3,7},{4,0},{5,1},{6,2},{7,3},{8,12},{9,13},{10,... | collective-permute-start | bytes 20 | tf_op jit(solution)/shard_map/ppermute | solution.py:346
  179.9 2.4 %collective-permute-start.24 = (f32[1]{0:T(128)}, f32[1]{0:T(128)}, u32[]{:S(2)}, u32[]{:S(2)}) collective-permute-start(f32[1]{0:T(128)} %add.167), channel_id=1, source_target_pairs={{0,8},{8,0},{16,24},{24,16},{1,9},{9,1},{17,25},{25,17},{2,10},{10... | collective-permute-start | bytes 20 | tf_op jit(solution)/shard_map/ppermute | solution.py:346
  185.5 2.3 collective-permute-done.25
  189.7 6.4 %back.2 = (f32[512,512]{1,0:T(8,128)}, f32[272,256]{1,0:T(8,128)}, f32[2,272,128]{2,1,0:T(8,128)}) custom-call(bf16[512,512]{1,0:T(8,128)(2,1)} %get-tuple-element.39.refs_0_, bf16[512,512]{1,0:T(8,128)(2,1)} %copy-done.10, bf16[512,512]{1,0:T(8,128)(2,1)} %copy-done.11, bf16[512,512]{1,0:T(8,128)(2,1)} %copy-done.12, bf16[4,9,256,256]{3,2,1,0:T(8,128)(2,1)} %refs_4_.1, ...), custom_call_target="tpu_custom_call" | custom-call | tf_op jit(solution)/shard_map/back/pallas_call | solution.py:177
  199.3 3.6 %collective-permute-start.27 = (f32[258]{0:T(512)S(1)}, f32[258]{0:T(512)S(1)}, u32[]{:S(2)}, u32[]{:S(2)}) collective-permute-start(f32[258]{0:T(512)S(1)} %get-tuple-element.50), channel_id=1, source_target_pairs={{1,0},{2,1},{3,2},{4,3},{5,4},{6,5},{7,6},{9,8},{10,9},{11,10},{12... | collective-permute-start | bytes 3104 | tf_op jit(solution)/shard_map/ppermute | solution.py:208
  205.1 2.4 %collective-permute-start.28 = (f32[1,256]{1,0:T(1,128)S(1)}, f32[1,256]{1,0:T(1,128)S(1)}, u32[]{:S(2)}, u32[]{:S(2)}) collective-permute-start(f32[1,256]{1,0:T(1,128)S(1)} %get-tuple-element.54), channel_id=1, source_target_pairs={{0,8},{8,16},{16,24},{1,9},{9,17},{17,25},{2,10},{10,18},{18,26},{... | collective-permute-start | bytes 3080 | tf_op jit(solution)/shard_map/ppermute | solution.py:216
  207.5 3.4 %collective-permute-start.29 = (f32[1,256]{1,0:T(1,128)S(1)}, f32[1,256]{1,0:T(1,128)S(1)}, u32[]{:S(2)}, u32[]{:S(2)}) collective-permute-start(f32[1,256]{1,0:T(1,128)S(1)} %get-tuple-element.55), channel_id=1, source_target_pairs={{8,0},{16,8},{24,16},{9,1},{17,9},{25,17},{10,2},{18,10},{26,18},{... | collective-permute-start | bytes 3080 | tf_op jit(solution)/shard_map/ppermute | solution.py:217
  210.9 2.9 %collective-permute-done.29 = f32[1,256]{1,0:T(1,128)S(1)} collective-permute-done((f32[1,256]{1,0:T(1,128)S(1)}, f32[1,256]{1,0:T(1,128)S(1)}, u32[]{:S(2)}, u32[]{:S(2)}) %collective-permute-start.29) | collective-permute-done | bytes 1056 | tf_op jit(solution)/shard_map/ppermute | solution.py:217
  215.6 2.8 %back.3 = (f32[256,256]{1,0:T(8,128)}, f32[144,128]{1,0:T(8,128)}, f32[2,144,128]{2,1,0:T(8,128)}) custom-call(f32[256,256]{1,0:T(8,128)} %fusion.3.refs_0_, bf16[4,9,128,128]{3,2,1,0:T(8,128)(2,1)} %refs_1_.1, f32[256,256]{1,0:T(8,128)} %refs_2_.1), custom_call_target="tpu_custom_call" | custom-call | tf_op jit(solution)/shard_map/back/pallas_call | solution.py:177
  219.5 2.3 collective-permute-start.30
  221.9 3.2 %collective-permute-start.31 = (f32[130]{0:T(256)S(1)}, f32[130]{0:T(256)S(1)}, u32[]{:S(2)}, u32[]{:S(2)}) collective-permute-start(f32[130]{0:T(256)S(1)} %get-tuple-element.53), channel_id=1, source_target_pairs={{1,0},{2,1},{3,2},{4,3},{5,4},{6,5},{7,6},{9,8},{10,9},{11,10},{12... | collective-permute-start | bytes 1568 | tf_op jit(solution)/shard_map/ppermute | solution.py:208
  229.2 3.9 %collective-permute-start.33 = (f32[1,128]{1,0:T(1,128)S(1)}, f32[1,128]{1,0:T(1,128)S(1)}, u32[]{:S(2)}, u32[]{:S(2)}) collective-permute-start(f32[1,128]{1,0:T(1,128)S(1)} %get-tuple-element.61), channel_id=1, source_target_pairs={{8,0},{16,8},{24,16},{9,1},{17,9},{25,17},{10,2},{18,10},{26,18},{... | collective-permute-start | bytes 1544 | tf_op jit(solution)/shard_map/ppermute | solution.py:217
  233.1 2.4 %collective-permute-done.33 = f32[1,128]{1,0:T(1,128)S(1)} collective-permute-done((f32[1,128]{1,0:T(1,128)S(1)}, f32[1,128]{1,0:T(1,128)S(1)}, u32[]{:S(2)}, u32[]{:S(2)}) %collective-permute-start.33) | collective-permute-done | bytes 544 | tf_op jit(solution)/shard_map/ppermute | solution.py:217
  (116 shorter events, 54.3 us)
Async XLA Ops:
  1.3 5.8 %collective-permute-start.1 = (f32[1,128]{1,0:T(1,128)S(1)}, f32[1,128]{1,0:T(1,128)S(1)}, u32[]{:S(2)}, u32[]{:S(2)}) collective-permute-start(f32[1,128]{1,0:T(1,128)S(1)} %get-tuple-element.64), channel_id=1, source_target_pairs={{0,8},{8,16},{16,24},{1,9},{9,17},{17,25},{2,10},{10,18},{18,26},{... | collective-permute-start | bytes 1544 | tf_op jit(solution)/shard_map/ppermute | solution.py:23
  4.7 6.3 %collective-permute-start.2 = (f32[1,128]{1,0:T(1,128)S(1)}, f32[1,128]{1,0:T(1,128)S(1)}, u32[]{:S(2)}, u32[]{:S(2)}) collective-permute-start(f32[1,128]{1,0:T(1,128)S(1)} %get-tuple-element.65), channel_id=1, source_target_pairs={{8,0},{16,8},{24,16},{9,1},{17,9},{25,17},{10,2},{18,10},{26,18},{... | collective-permute-start | bytes 1544 | tf_op jit(solution)/shard_map/ppermute | solution.py:24
  12.0 5.6 %collective-permute-start.3 = (f32[130,1]{1,0:T(8,128)S(1)}, f32[130,1]{1,0:T(8,128)S(1)}, u32[]{:S(2)}, u32[]{:S(2)}) collective-permute-start(f32[130,1]{1,0:T(8,128)S(1)} %get-tuple-element.62), channel_id=1, source_target_pairs={{0,1},{1,2},{2,3},{3,4},{4,5},{5,6},{6,7},{8,9},{9,10},{10,11},{11... | collective-permute-start | bytes 1568 | tf_op jit(solution)/shard_map/ppermute | solution.py:23
  13.9 5.6 %collective-permute-start.4 = (f32[130,1]{1,0:T(8,128)S(1)}, f32[130,1]{1,0:T(8,128)S(1)}, u32[]{:S(2)}, u32[]{:S(2)}) collective-permute-start(f32[130,1]{1,0:T(8,128)S(1)} %get-tuple-element.63), channel_id=1, source_target_pairs={{1,0},{2,1},{3,2},{4,3},{5,4},{6,5},{7,6},{9,8},{10,9},{11,10},{12... | collective-permute-start | bytes 1568 | tf_op jit(solution)/shard_map/ppermute | solution.py:24
  24.7 5.8 %collective-permute-start.5 = (f32[1,256]{1,0:T(1,128)S(1)}, f32[1,256]{1,0:T(1,128)S(1)}, u32[]{:S(2)}, u32[]{:S(2)}) collective-permute-start(f32[1,256]{1,0:T(1,128)S(1)} %get-tuple-element.58), channel_id=1, source_target_pairs={{0,8},{8,16},{16,24},{1,9},{9,17},{17,25},{2,10},{10,18},{18,26},{... | collective-permute-start | bytes 3080 | tf_op jit(solution)/shard_map/ppermute | solution.py:23
  27.2 6.4 %collective-permute-start.6 = (f32[1,256]{1,0:T(1,128)S(1)}, f32[1,256]{1,0:T(1,128)S(1)}, u32[]{:S(2)}, u32[]{:S(2)}) collective-permute-start(f32[1,256]{1,0:T(1,128)S(1)} %get-tuple-element.59), channel_id=1, source_target_pairs={{8,0},{16,8},{24,16},{9,1},{17,9},{25,17},{10,2},{18,10},{26,18},{... | collective-permute-start | bytes 3080 | tf_op jit(solution)/shard_map/ppermute | solution.py:24
  34.6 6.3 %collective-permute-start.7 = (f32[258,1]{1,0:T(8,128)S(1)}, f32[258,1]{1,0:T(8,128)S(1)}, u32[]{:S(2)}, u32[]{:S(2)}) collective-permute-start(f32[258,1]{1,0:T(8,128)S(1)} %get-tuple-element.56), channel_id=1, source_target_pairs={{0,1},{1,2},{2,3},{3,4},{4,5},{5,6},{6,7},{8,9},{9,10},{10,11},{11... | collective-permute-start | bytes 3104 | tf_op jit(solution)/shard_map/ppermute | solution.py:23
  36.9 5.9 %collective-permute-start.8 = (f32[258,1]{1,0:T(8,128)S(1)}, f32[258,1]{1,0:T(8,128)S(1)}, u32[]{:S(2)}, u32[]{:S(2)}) collective-permute-start(f32[258,1]{1,0:T(8,128)S(1)} %get-tuple-element.57), channel_id=1, source_target_pairs={{1,0},{2,1},{3,2},{4,3},{5,4},{6,5},{7,6},{9,8},{10,9},{11,10},{12... | collective-permute-start | bytes 3104 | tf_op jit(solution)/shard_map/ppermute | solution.py:24
  51.0 14.2 %collective-permute-start.9 = (bf16[512,512]{1,0:T(8,128)(2,1)}, bf16[512,512]{1,0:T(8,128)(2,1)S(1)}, u32[]{:S(2)}, u32[]{:S(2)}) collective-permute-start(bf16[512,512]{1,0:T(8,128)(2,1)} %get-tuple-element.28.refs_0_), channel_id=1, source_target_pairs={{0,2},{1,3},{2,4},{3,5},{4,6},{5,7},{6,0},{7,1},{8,10},{9,11},{10,... | collective-permute-start | bytes 1572872 | tf_op jit(solution)/shard_map/ppermute | solution.py:334
  52.6 45.5 %collective-permute-start.10 = (bf16[512,512]{1,0:T(8,128)(2,1)}, bf16[512,512]{1,0:T(8,128)(2,1)S(1)}, u32[]{:S(2)}, u32[]{:S(2)}) collective-permute-start(bf16[512,512]{1,0:T(8,128)(2,1)} %get-tuple-element.28.refs_0_), channel_id=1, source_target_pairs={{0,4},{1,5},{2,6},{3,7},{4,0},{5,1},{6,2},{7,3},{8,12},{9,13},{10,... | collective-permute-start | bytes 1572872 | tf_op jit(solution)/shard_map/ppermute | solution.py:334
  53.6 46.7 %collective-permute-start.11 = (bf16[512,512]{1,0:T(8,128)(2,1)}, bf16[512,512]{1,0:T(8,128)(2,1)S(1)}, u32[]{:S(2)}, u32[]{:S(2)}) collective-permute-start(bf16[512,512]{1,0:T(8,128)(2,1)} %get-tuple-element.28.refs_0_), channel_id=1, source_target_pairs={{0,6},{1,7},{2,0},{3,1},{4,2},{5,3},{6,4},{7,5},{8,14},{9,15},{10,... | collective-permute-start | bytes 1572872 | tf_op jit(solution)/shard_map/ppermute | solution.py:334
  55.7 46.4 %collective-permute-start.12 = (bf16[512,512]{1,0:T(8,128)(2,1)}, bf16[512,512]{1,0:T(8,128)(2,1)S(1)}, u32[]{:S(2)}, u32[]{:S(2)}) collective-permute-start(bf16[512,512]{1,0:T(8,128)(2,1)} %get-tuple-element.28.refs_0_), channel_id=1, source_target_pairs={{0,1},{1,0},{2,3},{3,2},{4,5},{5,4},{6,7},{7,6},{8,9},{9,8},{10,11... | collective-permute-start | bytes 1572872 | tf_op jit(solution)/shard_map/ppermute | solution.py:338
  65.2 36.9 %collective-permute-start.13 = (bf16[512,512]{1,0:T(8,128)(2,1)S(1)}, bf16[512,512]{1,0:T(8,128)(2,1)S(1)}, u32[]{:S(2)}, u32[]{:S(2)}) collective-permute-start(bf16[512,512]{1,0:T(8,128)(2,1)S(1)} %collective-permute-done.9.refs_1_), channel_id=1, source_target_pairs={{0,1},{1,0},{2,3},{3,2},{4,5},{5,4},{6,7},{7,6},{8,9},{9,8},{10,11... | collective-permute-start | bytes 1572872 | tf_op jit(solution)/shard_map/ppermute | solution.py:338
  98.1 4.0 %collective-permute-start.14 = (bf16[512,512]{1,0:T(8,128)(2,1)S(1)}, bf16[512,512]{1,0:T(8,128)(2,1)S(1)}, u32[]{:S(2)}, u32[]{:S(2)}) collective-permute-start(bf16[512,512]{1,0:T(8,128)(2,1)S(1)} %collective-permute-done.10.refs_2_), channel_id=1, source_target_pairs={{0,1},{1,0},{2,3},{3,2},{4,5},{5,4},{6,7},{7,6},{8,9},{9,8},{10,11... | collective-permute-start | bytes 1572872 | tf_op jit(solution)/shard_map/ppermute | solution.py:338
  100.3 1.9 collective-permute-start.15
  113.5 12.5 %collective-permute-start.17 = (bf16[512,512]{1,0:T(8,128)(2,1)}, bf16[512,512]{1,0:T(8,128)(2,1)S(1)}, u32[]{:S(2)}, u32[]{:S(2)}) collective-permute-start(bf16[512,512]{1,0:T(8,128)(2,1)} %get-tuple-element.30.refs_1_), channel_id=1, source_target_pairs={{0,1},{1,0},{2,3},{3,2},{4,5},{5,4},{6,7},{7,6},{8,9},{9,8},{10,11... | collective-permute-start | bytes 1572872 | tf_op jit(solution)/shard_map/ppermute | solution.py:338
  122.8 3.2 %collective-permute-start.16 = (bf16[512,512]{1,0:T(8,128)(2,1)}, bf16[512,512]{1,0:T(8,128)(2,1)S(1)}, u32[]{:S(2)}, u32[]{:S(2)}) collective-permute-start(bf16[512,512]{1,0:T(8,128)(2,1)} %get-tuple-element.29.refs_0_), channel_id=1, source_target_pairs={{0,1},{1,0},{2,3},{3,2},{4,5},{5,4},{6,7},{7,6},{8,9},{9,8},{10,11... | collective-permute-start | bytes 1572872 | tf_op jit(solution)/shard_map/ppermute | solution.py:338
  132.6 55.8 %collective-permute-start.18 = (bf16[512,512]{1,0:T(8,128)(2,1)}, bf16[512,512]{1,0:T(8,128)(2,1)S(1)}, u32[]{:S(2)}, u32[]{:S(2)}) collective-permute-start(bf16[512,512]{1,0:T(8,128)(2,1)} %get-tuple-element.32), channel_id=1, source_target_pairs={{0,2},{1,3},{2,4},{3,5},{4,6},{5,7},{6,0},{7,1},{8,10},{9,11},{10,... | collective-permute-start | bytes 1572872 | tf_op jit(solution)/shard_map/ppermute | solution.py:334
  133.6 54.9 %collective-permute-start.19 = (bf16[512,512]{1,0:T(8,128)(2,1)}, bf16[512,512]{1,0:T(8,128)(2,1)S(1)}, u32[]{:S(2)}, u32[]{:S(2)}) collective-permute-start(bf16[512,512]{1,0:T(8,128)(2,1)} %get-tuple-element.33), channel_id=1, source_target_pairs={{0,4},{1,5},{2,6},{3,7},{4,0},{5,1},{6,2},{7,3},{8,12},{9,13},{10,... | collective-permute-start | bytes 1572872 | tf_op jit(solution)/shard_map/ppermute | solution.py:334
  134.4 54.1 %collective-permute-start.20 = (bf16[512,512]{1,0:T(8,128)(2,1)}, bf16[512,512]{1,0:T(8,128)(2,1)S(1)}, u32[]{:S(2)}, u32[]{:S(2)}) collective-permute-start(bf16[512,512]{1,0:T(8,128)(2,1)} %get-tuple-element.34), channel_id=1, source_target_pairs={{0,6},{1,7},{2,0},{3,1},{4,2},{5,3},{6,4},{7,5},{8,14},{9,15},{10,... | collective-permute-start | bytes 1572872 | tf_op jit(solution)/shard_map/ppermute | solution.py:334
  144.6 25.0 %collective-permute-start.22 = (f32[1]{0:T(128)}, f32[1]{0:T(128)}, u32[]{:S(2)}, u32[]{:S(2)}) collective-permute-start(f32[1]{0:T(128)} %add.165), channel_id=1, source_target_pairs={{0,2},{1,3},{2,0},{3,1},{4,6},{5,7},{6,4},{7,5},{8,10},{9,11},{10,... | collective-permute-start | bytes 20 | tf_op jit(solution)/shard_map/ppermute | solution.py:346
  170.2 9.2 %collective-permute-start.23 = (f32[1]{0:T(128)}, f32[1]{0:T(128)}, u32[]{:S(2)}, u32[]{:S(2)}) collective-permute-start(f32[1]{0:T(128)} %add.166), channel_id=1, source_target_pairs={{0,4},{1,5},{2,6},{3,7},{4,0},{5,1},{6,2},{7,3},{8,12},{9,13},{10,... | collective-permute-start | bytes 20 | tf_op jit(solution)/shard_map/ppermute | solution.py:346
  179.9 3.7 %collective-permute-start.24 = (f32[1]{0:T(128)}, f32[1]{0:T(128)}, u32[]{:S(2)}, u32[]{:S(2)}) collective-permute-start(f32[1]{0:T(128)} %add.167), channel_id=1, source_target_pairs={{0,8},{8,0},{16,24},{24,16},{1,9},{9,1},{17,25},{25,17},{2,10},{10... | collective-permute-start | bytes 20 | tf_op jit(solution)/shard_map/ppermute | solution.py:346
  184.2 3.7 %collective-permute-start.25 = (f32[1]{0:T(128)}, f32[1]{0:T(128)}, u32[]{:S(2)}, u32[]{:S(2)}) collective-permute-start(f32[1]{0:T(128)} %add.168), channel_id=1, source_target_pairs={{0,16},{8,24},{16,0},{24,8},{1,17},{9,25},{17,1},{25,9},{2,18},{10... | collective-permute-start | bytes 20 | tf_op jit(solution)/shard_map/ppermute | solution.py:346
  197.3 5.6 %collective-permute-start.26 = (f32[258]{0:T(512)S(1)}, f32[258]{0:T(512)S(1)}, u32[]{:S(2)}, u32[]{:S(2)}) collective-permute-start(f32[258]{0:T(512)S(1)} %get-tuple-element.51), channel_id=1, source_target_pairs={{0,1},{1,2},{2,3},{3,4},{4,5},{5,6},{6,7},{8,9},{9,10},{10,11},{11... | collective-permute-start | bytes 3104 | tf_op jit(solution)/shard_map/ppermute | solution.py:207
  199.3 4.9 %collective-permute-start.27 = (f32[258]{0:T(512)S(1)}, f32[258]{0:T(512)S(1)}, u32[]{:S(2)}, u32[]{:S(2)}) collective-permute-start(f32[258]{0:T(512)S(1)} %get-tuple-element.50), channel_id=1, source_target_pairs={{1,0},{2,1},{3,2},{4,3},{5,4},{6,5},{7,6},{9,8},{10,9},{11,10},{12... | collective-permute-start | bytes 3104 | tf_op jit(solution)/shard_map/ppermute | solution.py:208
  205.1 5.8 %collective-permute-start.28 = (f32[1,256]{1,0:T(1,128)S(1)}, f32[1,256]{1,0:T(1,128)S(1)}, u32[]{:S(2)}, u32[]{:S(2)}) collective-permute-start(f32[1,256]{1,0:T(1,128)S(1)} %get-tuple-element.54), channel_id=1, source_target_pairs={{0,8},{8,16},{16,24},{1,9},{9,17},{17,25},{2,10},{10,18},{18,26},{... | collective-permute-start | bytes 3080 | tf_op jit(solution)/shard_map/ppermute | solution.py:216
  207.5 6.4 %collective-permute-start.29 = (f32[1,256]{1,0:T(1,128)S(1)}, f32[1,256]{1,0:T(1,128)S(1)}, u32[]{:S(2)}, u32[]{:S(2)}) collective-permute-start(f32[1,256]{1,0:T(1,128)S(1)} %get-tuple-element.55), channel_id=1, source_target_pairs={{8,0},{16,8},{24,16},{9,1},{17,9},{25,17},{10,2},{18,10},{26,18},{... | collective-permute-start | bytes 3080 | tf_op jit(solution)/shard_map/ppermute | solution.py:217
  219.5 5.6 %collective-permute-start.30 = (f32[130]{0:T(256)S(1)}, f32[130]{0:T(256)S(1)}, u32[]{:S(2)}, u32[]{:S(2)}) collective-permute-start(f32[130]{0:T(256)S(1)} %get-tuple-element.52), channel_id=1, source_target_pairs={{0,1},{1,2},{2,3},{3,4},{4,5},{5,6},{6,7},{8,9},{9,10},{10,11},{11... | collective-permute-start | bytes 1568 | tf_op jit(solution)/shard_map/ppermute | solution.py:207
  221.9 4.5 %collective-permute-start.31 = (f32[130]{0:T(256)S(1)}, f32[130]{0:T(256)S(1)}, u32[]{:S(2)}, u32[]{:S(2)}) collective-permute-start(f32[130]{0:T(256)S(1)} %get-tuple-element.53), channel_id=1, source_target_pairs={{1,0},{2,1},{3,2},{4,3},{5,4},{6,5},{7,6},{9,8},{10,9},{11,10},{12... | collective-permute-start | bytes 1568 | tf_op jit(solution)/shard_map/ppermute | solution.py:208
  227.3 5.9 %collective-permute-start.32 = (f32[1,128]{1,0:T(1,128)S(1)}, f32[1,128]{1,0:T(1,128)S(1)}, u32[]{:S(2)}, u32[]{:S(2)}) collective-permute-start(f32[1,128]{1,0:T(1,128)S(1)} %get-tuple-element.60), channel_id=1, source_target_pairs={{0,8},{8,16},{16,24},{1,9},{9,17},{17,25},{2,10},{10,18},{18,26},{... | collective-permute-start | bytes 1544 | tf_op jit(solution)/shard_map/ppermute | solution.py:216
  229.2 6.3 %collective-permute-start.33 = (f32[1,128]{1,0:T(1,128)S(1)}, f32[1,128]{1,0:T(1,128)S(1)}, u32[]{:S(2)}, u32[]{:S(2)}) collective-permute-start(f32[1,128]{1,0:T(1,128)S(1)} %get-tuple-element.61), channel_id=1, source_target_pairs={{8,0},{16,8},{24,16},{9,1},{17,9},{25,17},{10,2},{18,10},{26,18},{... | collective-permute-start | bytes 1544 | tf_op jit(solution)/shard_map/ppermute | solution.py:217
  (22 other events, 257.6 us)

commit v3 on v2

v3 whole, which is shorter than its diff:
```python
import functools

import jax
import jax.numpy as jnp
from jax import lax
from jax.experimental import pallas as pl
from jax.experimental.pallas import tpu as pltpu
from jax.sharding import PartitionSpec as P

inv_noise = 0.125
vmem = 24 * 1024 * 1024
f32 = jnp.float32
bf16 = jnp.bfloat16


def extended(x, sides, width):
    for axis, dim in sides:
        size, length = (lax.axis_size(axis), x.shape[dim])
        up = [(i, (i + 1) % size) for i in range(size - 1)]
        down = [(j, i) for i, j in up]
        last = lax.slice_in_dim(x, length - width, length, axis=dim)
        leading = lax.slice_in_dim(x, 0, width, axis=dim)
        before = lax.ppermute(last, axis, up)
        after = lax.ppermute(leading, axis, down)
        x = jnp.concatenate([before, x, after], axis=dim)
    return x


def widen(field):
    return extended(field, (("gx", 0), ("gy", 1)), 1)


def halves(x):
    high = x.astype(bf16)
    return high, (x - high.astype(f32)).astype(bf16)


def interleaver(cols, transposed):
    shape = (2 * cols, 2 * cols)
    split = lax.broadcasted_iota(jnp.int32, shape, 1 if transposed else 0)
    whole = lax.broadcasted_iota(jnp.int32, shape, 0 if transposed else 1)
    place = jnp.where(split >= cols, 2 * (split - cols) + 1, 2 * split)
    return (place == whole).astype(f32).astype(bf16)


def folded(x):
    rows, cols = x.shape
    x = jnp.sum(x.reshape(rows // 8, 8, cols), axis=0)
    return sum(x[:, i : i + 128] for i in range(0, cols, 128))


def refine_kernel(first, pad_ref, coef_ref, xi_ref, out_ref, sq_ref, win, perm, lhs, mix):
    rows, cols = win.shape[1:]
    for near in range(9):
        r, c = near // 3, near % 3
        win[near] = pad_ref[r : r + rows, c : c + cols]
    perm[...] = interleaver(cols, False)

    def part(i, carry):
        r0 = pl.multiple_of(i * 16, 16)
        total = [jnp.zeros((16, cols), f32) for _ in range(4)]
        for near in range(9):
            w = win[near, pl.ds(r0, 16), :]
            for child in range(4):
                total[child] += coef_ref[child, near, pl.ds(r0, 16), :].astype(f32) * w
        for child in range(4):
            a, b = child // 2, child % 2
            high, low = halves(total[child])
            lhs[pl.ds(2 * a * rows + r0, 16), b * cols : (b + 1) * cols] = high
            lhs[pl.ds((2 * a + 1) * rows + r0, 16), b * cols : (b + 1) * cols] = low
        return carry

    lax.fori_loop(0, rows // 16, part, 0)
    field = jnp.dot(lhs[...], perm[...], preferred_element_type=f32)
    xi = xi_ref[...]
    for tile in range(2 * cols // 128):
        lanes = slice(tile * 128, (tile + 1) * 128)
        for a in range(2):
            mix[tile, pl.ds(a, rows, stride=2), :] = (
                field[2 * a * rows : (2 * a + 1) * rows, lanes]
                + field[(2 * a + 1) * rows : (2 * a + 2) * rows, lanes]
            )
        out_ref[:, lanes] = (mix[tile] + xi[:, lanes]).astype(out_ref.dtype)
    square = folded(xi * xi)
    if first:
        square += folded(win[4] * win[4])
    sq_ref[...] = square


whole = pl.BlockSpec(memory_space=pltpu.VMEM)
scalar = pl.BlockSpec(memory_space=pltpu.SMEM)


def refine(padded, coef, xi, dtype, first):
    rows, cols = coef.shape[2:]
    return pl.pallas_call(
        functools.partial(refine_kernel, first),
        in_specs=[whole] * 3,
        out_specs=[whole] * 2,
        out_shape=[
            jax.ShapeDtypeStruct((2 * rows, 2 * cols), dtype),
            jax.ShapeDtypeStruct((8, 128), f32),
        ],
        scratch_shapes=[
            pltpu.VMEM((9, rows, cols), f32),
            pltpu.VMEM((2 * cols, 2 * cols), bf16),
            pltpu.VMEM((4 * rows, 2 * cols), bf16),
            pltpu.VMEM((2 * cols // 128, 2 * rows, 128), f32),
        ],
        compiler_params=pltpu.CompilerParams(vmem_limit_bytes=vmem),
        name="refine",
    )(padded, coef, xi)


def back_kernel(number, *refs):
    parts = refs[:number]
    coef_ref, xi_ref, grad_ref, main_ref, cols_ref, total_ref, terms, perm, mix, rowed = refs[number:]
    rows, cols = terms.shape[1:]
    perm[...] = interleaver(cols, True)
    g = parts[0][: 2 * rows].astype(f32)
    for part in parts[1:]:
        g += part[: 2 * rows].astype(f32)
    grad_ref[...] = g + xi_ref[...]
    if parts[0].shape[0] > 2 * rows:
        rest = sum(part[2 * rows :, :128].astype(f32) for part in parts)
        total_ref[...] = rest[:8] + rest[8:16] + rest[16:24]
    else:
        total_ref[...] = jnp.zeros_like(total_ref)
    high, low = halves(g)
    split = jnp.dot(high, perm[...], preferred_element_type=f32)
    split += jnp.dot(low, perm[...], preferred_element_type=f32)
    for tile in range(2 * cols // 128):
        mix[tile] = split[:, tile * 128 : (tile + 1) * 128]

    def part(i, carry):
        r0 = pl.multiple_of(i * 16, 16)
        quads = []
        for a in range(2):
            for b in range(2):
                tiles = range(b * cols // 128, (b + 1) * cols // 128)
                lines = [mix[t, pl.ds(2 * r0 + a, 16, stride=2), :] for t in tiles]
                quads.append(jnp.concatenate(lines, axis=1))
        for near in range(9):
            total = jnp.zeros((16, cols), f32)
            for child in range(4):
                total += coef_ref[child, near, pl.ds(r0, 16), :].astype(f32) * quads[child]
            terms[near, pl.ds(r0, 16), :] = total
        return carry

    lax.fori_loop(0, rows // 16, part, 0)
    rowed[...] = jnp.zeros_like(rowed)
    for near in range(9):
        r, c = near // 3, near % 3
        rowed[c, 7 + r : 7 + r + rows, :] += terms[near]
    lane = lax.broadcasted_iota(jnp.int32, (rows + 16, cols), 1)
    from_left = pltpu.roll(rowed[2], 1, 1)
    from_right = pltpu.roll(rowed[0], cols - 1, 1)
    main_ref[...] = (
        rowed[1]
        + jnp.where(lane == 0, 0.0, from_left)
        + jnp.where(lane == cols - 1, 0.0, from_right)
    )
    cols_ref[0] = rowed[0, :, :128]
    cols_ref[1] = rowed[2, :, cols - 128 :]


def back(parts, coef, xi):
    rows, cols = coef.shape[2:]
    grad, main, side, total = pl.pallas_call(
        functools.partial(back_kernel, len(parts)),
        in_specs=[whole] * (len(parts) + 2),
        out_specs=[whole] * 4,
        out_shape=[
            jax.ShapeDtypeStruct((2 * rows, 2 * cols), f32),
            jax.ShapeDtypeStruct((rows + 16, cols), f32),
            jax.ShapeDtypeStruct((2, rows + 16, 128), f32),
            jax.ShapeDtypeStruct((8, 128), f32),
        ],
        scratch_shapes=[
            pltpu.VMEM((9, rows, cols), f32),
            pltpu.VMEM((2 * cols, 2 * cols), bf16),
            pltpu.VMEM((2 * cols // 128, 2 * rows, 128), f32),
            pltpu.VMEM((3, rows + 16, cols), f32),
        ],
        compiler_params=pltpu.CompilerParams(vmem_limit_bytes=vmem),
        name="back",
    )(*parts, coef, xi)
    size = lax.axis_size("gy")
    right = [(i, i + 1) for i in range(size - 1)]
    left = [(j, i) for i, j in right]
    from_left = lax.ppermute(side[1, 7 : 9 + rows, 127], "gy", right)
    from_right = lax.ppermute(side[0, 7 : 9 + rows, 0], "gy", left)
    main = main[7 : 9 + rows]
    ends = jnp.pad(from_left[:, None], ((0, 0), (0, cols - 1))) + jnp.pad(
        from_right[:, None], ((0, 0), (cols - 1, 0))
    )
    size = lax.axis_size("gx")
    down = [(i, i + 1) for i in range(size - 1)]
    up = [(j, i) for i, j in down]
    from_above = lax.ppermute(main[-1:] + ends[-1:], "gx", down)
    from_below = lax.ppermute(main[:1] + ends[:1], "gx", up)
    result = (
        main[1:-1]
        + ends[1:-1]
        + jnp.pad(from_above, ((0, rows - 1), (0, 0)))
        + jnp.pad(from_below, ((rows - 1, 0), (0, 0)))
    )
    return grad, result, total


def facet_kernel(f, blk, number, sel, weights, counts, *refs):
    tiles = refs[:number]
    ku_ref, kv_ref, data_ref, out_ref, lik_ref, sums, dsum = refs[number:]
    slots = sel.shape[1]
    for s in range(slots):
        for i in range(number):

            @pl.when(sel[f, s] == i)
            def _():
                term = weights[f, s] * tiles[i][...].astype(f32)
                if s > 0:
                    term += dsum[...]
                if s < slots - 1:
                    dsum[...] = term
                else:
                    sums[...] = term.astype(bf16)

    lik_ref[...] = jnp.zeros_like(lik_ref)
    for step in range(ku_ref.shape[2] // blk):
        rows = slice(step * blk, (step + 1) * blk)
        count = counts[f] - step * blk

        @pl.when(count > 0)
        def _():
            ku, kv = ku_ref[0, f, rows], kv_ref[0, f]
            amp = jnp.dot(ku, sums[...], preferred_element_type=f32).astype(bf16)
            vis = lax.dot_general(amp, kv, (((1,), (1,)), ((), ())), preferred_element_type=f32)
            live = lax.broadcasted_iota(jnp.int32, vis.shape, 0) < count
            resid = jnp.where(live, vis - data_ref[0, f, rows].astype(f32), 0.0)
            lik_ref[...] += inv_noise * folded(resid * resid)
            dvis = (inv_noise * resid).astype(bf16)
            damp = jnp.dot(dvis, kv, preferred_element_type=f32).astype(bf16)
            part = lax.dot_general(ku, damp, (((0,), (0,)), ((), ())), preferred_element_type=f32)
            if step == 0:
                dsum[...] = part
            else:
                dsum[...] += part

    out_ref[...] = dsum[...].astype(bf16)


def facet(f, tiles, ku, kv, data, sel, weights, counts):
    bins, side = ku.shape[2:]
    blk = 512
    return pl.pallas_call(
        functools.partial(facet_kernel, f, blk, len(tiles)),
        in_specs=[scalar] * 3 + [whole] * (len(tiles) + 3),
        out_specs=[whole] * 2,
        out_shape=[
            jax.ShapeDtypeStruct((side, side), bf16),
            jax.ShapeDtypeStruct((8, 128), f32),
        ],
        scratch_shapes=[pltpu.VMEM((side, side), bf16), pltpu.VMEM((side, side), f32)],
        compiler_params=pltpu.CompilerParams(vmem_limit_bytes=vmem),
        name="facet",
    )(sel, weights, counts, *tiles, ku, kv, data)


def mix_kernel(number, squares, scale, *refs):
    dsums, sums, outs = refs[:number], refs[number : number + squares], refs[number + squares :]
    total = 0.5 * sum(x[...] for x in sums)
    high = total.astype(bf16).astype(f32)
    middle = (total - high).astype(bf16).astype(f32)
    low = total - high - middle
    side = dsums[0].shape[0]
    for d, out in enumerate(outs):
        value = None
        for f, dsum in enumerate(dsums):
            term = scale[d, f] * dsum[...].astype(f32)
            value = term if value is None else value + term
        out[:side] = value.astype(bf16)
        out[side:] = jnp.zeros((32, out.shape[1]), bf16)
        out[side : side + 16, :128] = jnp.concatenate([high, middle]).astype(bf16)
        out[side + 16 :, :128] = jnp.concatenate([low, jnp.zeros_like(low)]).astype(bf16)


def mixed(dsums, scale, sums):
    rows, cols = dsums[0].shape
    return pl.pallas_call(
        functools.partial(mix_kernel, len(dsums), len(sums)),
        in_specs=[scalar] + [whole] * (len(dsums) + len(sums)),
        out_specs=[whole] * scale.shape[0],
        out_shape=[jax.ShapeDtypeStruct((rows + 32, cols), bf16)] * scale.shape[0],
        compiler_params=pltpu.CompilerParams(vmem_limit_bytes=vmem),
        name="mixed",
    )(scale, *dsums, *sums)


def chip_shift(x, hop):
    size = lax.axis_size("gy")
    return lax.ppermute(x, "gy", [(i, (i + 2 * hop) % size) for i in range(size)])


def swapped(x):
    return lax.ppermute(x, "gy", [(i, i ^ 1) for i in range(lax.axis_size("gy"))])


def body(
    xi_coarse,
    xi_middle,
    xi_fine,
    coef_middle,
    coef_fine,
    kern_u,
    kern_v,
    vis_data,
    facet_tiles,
    facet_weight,
    facet_count,
):
    side = xi_fine.shape[0]
    level_middle, sq_middle = refine(widen(xi_coarse), coef_middle, xi_middle, f32, True)
    sky, sq_fine = refine(widen(level_middle), coef_fine, xi_fine, bf16, False)
    lists, weights, counts = facet_tiles[0], facet_weight[0], facet_count[0]
    number = lists.shape[0]
    size = lax.axis_size("gy")
    chips = size // 2
    me = lax.axis_index("gy")
    ids = jnp.arange(size, dtype=jnp.int32)
    mixing = jnp.sum(
        weights[:, :, None] * (lists[:, :, None] == ids[None, None, :]).astype(f32), axis=1
    )
    order = 2 * ((me // 2 + jnp.arange(chips, dtype=jnp.int32)) % chips) + me % 2
    scale = jnp.concatenate([mixing, swapped(mixing)])[:, order].T
    mine = [sky] + [chip_shift(sky, hop) for hop in range(1, chips)]
    tiles = mine + [swapped(tile) for tile in mine]
    sel = (me // 2 - lists // 2) % chips + jnp.where(lists % 2 == me % 2, 0, chips)
    dsums, theirs, sums = [], [], [sq_middle, sq_fine]
    for f in range(number):
        dsum, lik = facet(f, tiles, kern_u, kern_v, vis_data, sel, weights, counts)
        dsums.append(dsum)
        theirs.append(swapped(dsum))
        sums.append(lik)
    parts = mixed(dsums + theirs, scale, sums)
    parts = [parts[0]] + [chip_shift(parts[hop], hop) for hop in range(1, chips)]
    grad_fine, dmiddle, total = back(parts, coef_fine, xi_fine)
    total = jnp.sum(total)[None]
    total += swapped(total)
    dmiddle, total = lax.optimization_barrier((dmiddle, total))
    grad_middle, dcoarse, _ = back([dmiddle], coef_middle, xi_middle)
    size = lax.axis_size("gx")
    hop = 1
    while hop < size:
        total += lax.ppermute(total, "gx", [(i, i ^ hop) for i in range(size)])
        hop *= 2
    grad_coarse = dcoarse + xi_coarse
    cells = lax.axis_size("gx") * lax.axis_size("gy") * side * side
    return (grad_coarse, grad_middle, grad_fine, total[0] / cells)


def solution(mesh):
    placed = (
        P("gx", "gy"),
        P("gx", "gy"),
        P("gx", "gy"),
        P(None, None, "gx", "gy"),
        P(None, None, "gx", "gy"),
        P("gx", "gy", None, None),
        P("gx", "gy", None, None),
        P("gx", "gy", None, None),
        P("gx", "gy", None),
        P("gx", "gy", None),
        P("gx", "gy"),
    )
    return jax.shard_map(
        body,
        mesh=mesh,
        in_specs=placed,
        out_specs=(P("gx", "gy"), P("gx", "gy"), P("gx", "gy"), P()),
        check_vma=False,
    )
```

time: 241 us -> 222 us (0.921)
  waiting for transfers between devices: 56.5 us -> 110 us
  starting transfers between devices: 106 us -> 61.6 us
  Pallas kernels: 42.3 us -> 26.7 us
  other arithmetic: 13.5 us -> 3.85 us
  between operations: 8.35 us -> 4.72 us
    ppermute x6, waiting for transfers between devices: 20.2 us -> 86.7 us  [chip_shift(): lax.ppermute(x, 'gy', [(i, (i + 2 * hop) % size) for i in range(size)])]
    ppermute x5 -> x2, starting transfers between devices: 26.9 us -> 3.37 us  [body(): total += lax.ppermute(total, 'gx', [(i, i ^ hop) for i in range(size)])]
    ppermute x7 -> x8, starting transfers between devices: 25.6 us -> 3.39 us  [swapped(): lax.ppermute(x, 'gy', [(i, i ^ 1) for i in range(lax.axis_size('gy'))])]
    pallas_call x7, Pallas kernels: 42.3 us -> 26.7 us  [the longest x2 15 us: facet(): pl.pallas_call(functools.partial(facet_kernel, f, blk, len(tiles)), in_sp...]
    ppermute x5 -> x2, waiting for transfers between devices: 16 us -> 3.74 us  [body(): total += lax.ppermute(total, 'gx', [(i, i ^ hop) for i in range(size)])]
    unnamed x40 -> x28, local copies, waits for them, and re-layouts: 3.96 us -> 10.7 us
    ppermute x2, waiting for transfers between devices: 5.37 us -> 0.01 us  [back(): from_below = lax.ppermute(main[:1] + ends[:1], 'gx', up)]
    concatenate x4, other arithmetic: 5.36 us -> 2.05 us  [extended(): x = jnp.concatenate([before, x, after], axis=dim)]
  transfers between devices with their start and end apart: 34 -> 32, of which waited for: 18 -> 18; matrix products, arithmetic and copies ran while one was open for 3% -> 1% of each run, Pallas kernels for 4% -> 3%
where the time goes in v3:
time: 222 us; the launch traced here: 220 us
  waiting for transfers between devices  110 us (50%)
  starting transfers between devices  61.6 us (28%)
  Pallas kernels  26.7 us (12%)
  local copies, waits for them, and re-layouts  13 us (6%)
  between operations  4.72 us (2%)
  other arithmetic  3.85 us (2%)
    ppermute x6, waiting for transfers between devices, chip_shift(): lax.ppermute(x, 'gy', [(i, (i + 2 * hop) % size) for i in range(size)])  86.7 us
    pallas_call x2, Pallas kernels, facet(): pl.pallas_call(functools.partial(facet_kernel, f, blk, len(tiles)), in_sp...  15 us
    ppermute x4, starting transfers between devices, extended(): after = lax.ppermute(leading, axis, down)  12.8 us
    unnamed x28, local copies, waits for them, and re-layouts  10.7 us
    ppermute x4, waiting for transfers between devices, extended(): after = lax.ppermute(leading, axis, down)  10.5 us
    ppermute x4, starting transfers between devices, extended(): before = lax.ppermute(last, axis, up)  10 us
    ppermute x6, starting transfers between devices, chip_shift(): lax.ppermute(x, 'gy', [(i, (i + 2 * hop) % size) for i in range(size)])  9.72 us
    ppermute x2, starting transfers between devices, back(): from_right = lax.ppermute(side[0, 7:9 + rows, 0], 'gy', left)  6.69 us
  transfers between devices with their start and end apart: 32, of which 18 were waited for; matrix products, arithmetic and copies ran while one was open for 1% of the time, Pallas kernels for 3%

profile of v3, /device:TPU:10, one launch (start us, length us, event | category | flops | bytes accessed | tf_op | source)
XLA Modules:
  0.0 220.2 jit_solution(6459571625395455106)
XLA Ops:
  1.3 3.4 %collective-permute-start.1 = (f32[1,128]{1,0:T(1,128)S(1)}, f32[1,128]{1,0:T(1,128)S(1)}, u32[]{:S(2)}, u32[]{:S(2)}) collective-permute-start(f32[1,128]{1,0:T(1,128)S(1)} %get-tuple-element.60), channel_id=1, source_target_pairs={{0,8},{8,16},{16,24},{1,9},{9,17},{17,25},{2,10},{10,18},{18,26},{... | collective-permute-start | bytes 1544 | tf_op jit(solution)/shard_map/ppermute | solution.py:23
  4.7 2.4 %collective-permute-start.2 = (f32[1,128]{1,0:T(1,128)S(1)}, f32[1,128]{1,0:T(1,128)S(1)}, u32[]{:S(2)}, u32[]{:S(2)}) collective-permute-start(f32[1,128]{1,0:T(1,128)S(1)} %get-tuple-element.61), channel_id=1, source_target_pairs={{8,0},{16,8},{24,16},{9,1},{17,9},{25,17},{10,2},{18,10},{26,18},{... | collective-permute-start | bytes 1544 | tf_op jit(solution)/shard_map/ppermute | solution.py:24
  7.2 3.9 %collective-permute-done.2 = f32[1,128]{1,0:T(1,128)S(1)} collective-permute-done((f32[1,128]{1,0:T(1,128)S(1)}, f32[1,128]{1,0:T(1,128)S(1)}, u32[]{:S(2)}, u32[]{:S(2)}) %collective-permute-start.2) | collective-permute-done | bytes 544 | tf_op jit(solution)/shard_map/ppermute | solution.py:24
  13.9 3.6 %collective-permute-start.4 = (f32[130,1]{1,0:T(8,128)S(1)}, f32[130,1]{1,0:T(8,128)S(1)}, u32[]{:S(2)}, u32[]{:S(2)}) collective-permute-start(f32[130,1]{1,0:T(8,128)S(1)} %get-tuple-element.59), channel_id=1, source_target_pairs={{1,0},{2,1},{3,2},{4,3},{5,4},{6,5},{7,6},{9,8},{10,9},{11,10},{12... | collective-permute-start | bytes 1568 | tf_op jit(solution)/shard_map/ppermute | solution.py:24
  23.6 2.5 %collective-permute-start.5 = (f32[1,256]{1,0:T(1,128)S(1)}, f32[1,256]{1,0:T(1,128)S(1)}, u32[]{:S(2)}, u32[]{:S(2)}) collective-permute-start(f32[1,256]{1,0:T(1,128)S(1)} %get-tuple-element.54), channel_id=1, source_target_pairs={{0,8},{8,16},{16,24},{1,9},{9,17},{17,25},{2,10},{10,18},{18,26},{... | collective-permute-start | bytes 3080 | tf_op jit(solution)/shard_map/ppermute | solution.py:23
  26.1 3.3 %collective-permute-start.6 = (f32[1,256]{1,0:T(1,128)S(1)}, f32[1,256]{1,0:T(1,128)S(1)}, u32[]{:S(2)}, u32[]{:S(2)}) collective-permute-start(f32[1,256]{1,0:T(1,128)S(1)} %get-tuple-element.55), channel_id=1, source_target_pairs={{8,0},{16,8},{24,16},{9,1},{17,9},{25,17},{10,2},{18,10},{26,18},{... | collective-permute-start | bytes 3080 | tf_op jit(solution)/shard_map/ppermute | solution.py:24
  29.5 3.0 %collective-permute-done.6 = f32[1,256]{1,0:T(1,128)S(1)} collective-permute-done((f32[1,256]{1,0:T(1,128)S(1)}, f32[1,256]{1,0:T(1,128)S(1)}, u32[]{:S(2)}, u32[]{:S(2)}) %collective-permute-start.6) | collective-permute-done | bytes 1056 | tf_op jit(solution)/shard_map/ppermute | solution.py:24
  32.6 2.2 %collective-permute-start.7 = (f32[258,1]{1,0:T(8,128)S(1)}, f32[258,1]{1,0:T(8,128)S(1)}, u32[]{:S(2)}, u32[]{:S(2)}) collective-permute-start(f32[258,1]{1,0:T(8,128)S(1)} %get-tuple-element.52), channel_id=1, source_target_pairs={{0,1},{1,2},{2,3},{3,4},{4,5},{5,6},{6,7},{8,9},{9,10},{10,11},{11... | collective-permute-start | bytes 3104 | tf_op jit(solution)/shard_map/ppermute | solution.py:23
  34.8 3.3 %collective-permute-start.8 = (f32[258,1]{1,0:T(8,128)S(1)}, f32[258,1]{1,0:T(8,128)S(1)}, u32[]{:S(2)}, u32[]{:S(2)}) collective-permute-start(f32[258,1]{1,0:T(8,128)S(1)} %get-tuple-element.53), channel_id=1, source_target_pairs={{1,0},{2,1},{3,2},{4,3},{5,4},{6,5},{7,6},{9,8},{10,9},{11,10},{12... | collective-permute-start | bytes 3104 | tf_op jit(solution)/shard_map/ppermute | solution.py:24
  40.9 2.3 %copy-done = bf16[4,9,256,256]{3,2,1,0:T(8,128)(2,1)S(1)} copy-done((bf16[4,9,256,256]{3,2,1,0:T(8,128)(2,1)S(1)}, bf16[4,9,256,256]{3,2,1,0:T(8,128)(2,1)}, u32[]{:S(2)}) %copy-start) | copy-done | bytes 4718616
  43.3 3.6 %refine.3 = (bf16[512,512]{1,0:T(8,128)(2,1)}, f32[8,128]{1,0:T(8,128)S(1)}) custom-call(f32[258,258]{1,0:T(8,128)S(1)} %pad_maximum_fusion.pad_ref, bf16[4,9,256,256]{3,2,1,0:T(8,128)(2,1)S(1)} %copy-done, f32[512,512]{1,0:T(8,128)S(1)} %copy-done.7), custom_call_target="tpu_custom_call" | custom-call | tf_op jit(solution)/shard_map/refine/pallas_call | solution.py:96
  46.9 3.0 %collective-permute-start.10 = (bf16[512,512]{1,0:T(8,128)(2,1)}, bf16[512,512]{1,0:T(8,128)(2,1)}, u32[]{:S(2)}, u32[]{:S(2)}) collective-permute-start(bf16[512,512]{1,0:T(8,128)(2,1)} %get-tuple-element.26.refs_0_), channel_id=1, source_target_pairs={{0,4},{1,5},{2,6},{3,7},{4,0},{5,1},{6,2},{7,3},{8,12},{9,13},{10,... | collective-permute-start | bytes 1572872 | tf_op jit(solution)/shard_map/ppermute | solution.py:301
  50.0 2.5 %collective-permute-start.9 = (bf16[512,512]{1,0:T(8,128)(2,1)}, bf16[512,512]{1,0:T(8,128)(2,1)}, u32[]{:S(2)}, u32[]{:S(2)}) collective-permute-start(bf16[512,512]{1,0:T(8,128)(2,1)} %get-tuple-element.26.refs_0_), channel_id=1, source_target_pairs={{0,2},{1,3},{2,4},{3,5},{4,6},{5,7},{6,0},{7,1},{8,10},{9,11},{10,... | collective-permute-start | bytes 1572872 | tf_op jit(solution)/shard_map/ppermute | solution.py:301
  52.5 8.7 %collective-permute-done.11.refs_3_ = bf16[512,512]{1,0:T(8,128)(2,1)} collective-permute-done((bf16[512,512]{1,0:T(8,128)(2,1)}, bf16[512,512]{1,0:T(8,128)(2,1)}, u32[]{:S(2)}, u32[]{:S(2)}) %collective-permute-start.11) | collective-permute-done | bytes 524320 | tf_op jit(solution)/shard_map/ppermute | solution.py:301
  61.2 2.4 %collective-permute-start.15 = (bf16[512,512]{1,0:T(8,128)(2,1)}, bf16[512,512]{1,0:T(8,128)(2,1)}, u32[]{:S(2)}, u32[]{:S(2)}) collective-permute-start(bf16[512,512]{1,0:T(8,128)(2,1)} %collective-permute-done.11.refs_3_), channel_id=1, source_target_pairs={{0,1},{1,0},{2,3},{3,2},{4,5},{5,4},{6,7},{7,6},{8,9},{9,8},{10,11... | collective-permute-start | bytes 1572872 | tf_op jit(solution)/shard_map/ppermute | solution.py:305
  63.6 19.4 %collective-permute-done.10.refs_2_ = bf16[512,512]{1,0:T(8,128)(2,1)} collective-permute-done((bf16[512,512]{1,0:T(8,128)(2,1)}, bf16[512,512]{1,0:T(8,128)(2,1)}, u32[]{:S(2)}, u32[]{:S(2)}) %collective-permute-start.10) | collective-permute-done | bytes 524320 | tf_op jit(solution)/shard_map/ppermute | solution.py:301
  83.3 11.0 %collective-permute-done.9.refs_1_ = bf16[512,512]{1,0:T(8,128)(2,1)} collective-permute-done((bf16[512,512]{1,0:T(8,128)(2,1)}, bf16[512,512]{1,0:T(8,128)(2,1)}, u32[]{:S(2)}, u32[]{:S(2)}) %collective-permute-start.9) | collective-permute-done | bytes 524320 | tf_op jit(solution)/shard_map/ppermute | solution.py:301
  100.3 7.4 %facet.3 = (bf16[512,512]{1,0:T(8,128)(2,1)}, f32[8,128]{1,0:T(8,128)S(1)}) custom-call(s32[2,2]{1,0:T(2,128)S(1)} %fusion.9.sel, f32[2,2]{1,0:T(2,128)S(1)} %bitcast.10, s32[2]{0:T(128)S(1)} %bitcast.13, bf16[512,512]{1,0:T(8,128)(2,1)} %get-tuple-element.26.refs_0_, bf16[512,512]{1,0:T(8,128)(2,1)} %collective-permute-done.9.refs_1_, ...), custom_call_target="tpu_custom_call" | custom-call | tf_op jit(solution)/shard_map/facet/pallas_call | solution.py:255
  107.8 7.6 %facet.2 = (bf16[512,512]{1,0:T(8,128)(2,1)}, f32[8,128]{1,0:T(8,128)S(1)}) custom-call(s32[2,2]{1,0:T(2,128)S(1)} %fusion.9.sel, f32[2,2]{1,0:T(2,128)S(1)} %bitcast.11, s32[2]{0:T(128)S(1)} %bitcast.14, bf16[512,512]{1,0:T(8,128)(2,1)} %get-tuple-element.26.refs_0_, bf16[512,512]{1,0:T(8,128)(2,1)} %collective-permute-done.9.refs_1_, ...), custom_call_target="tpu_custom_call" | custom-call | tf_op jit(solution)/shard_map/facet/pallas_call | solution.py:255
  117.9 2.9 %mixed.1 = (bf16[544,512]{1,0:T(8,128)(2,1)S(1)}, bf16[544,512]{1,0:T(8,128)(2,1)S(1)}, bf16[544,512]{1,0:T(8,128)(2,1)S(1)}, bf16[544,512]{1,0:T(8,128)(2,1)S(1)}) custom-call(f32[4,4]{1,0:T(4,128)S(1)} %gather_fusion, bf16[512,512]{1,0:T(8,128)(2,1)} %get-tuple-element.27.refs_0_, bf16[512,512]{1,0:T(8,128)(2,1)} %get-tuple-element.28.refs_1_, ...), custom_call_target="tpu_custom_call" | custom-call | tf_op jit(solution)/shard_map/mixed/pallas_call | solution.py:289
  120.9 2.7 %collective-permute-start.18 = (bf16[544,512]{1,0:T(8,128)(2,1)S(1)}, bf16[544,512]{1,0:T(8,128)(2,1)S(1)}, u32[]{:S(2)}, u32[]{:S(2)}) collective-permute-start(bf16[544,512]{1,0:T(8,128)(2,1)S(1)} %get-tuple-element.34), channel_id=1, source_target_pairs={{0,2},{1,3},{2,4},{3,5},{4,6},{5,7},{6,0},{7,1},{8,10},{9,11},{10,... | collective-permute-start | bytes 1671176 | tf_op jit(solution)/shard_map/ppermute | solution.py:301
  125.1 35.3 %collective-permute-done.18.refs_1_ = bf16[544,512]{1,0:T(8,128)(2,1)S(1)} collective-permute-done((bf16[544,512]{1,0:T(8,128)(2,1)S(1)}, bf16[544,512]{1,0:T(8,128)(2,1)S(1)}, u32[]{:S(2)}, u32[]{:S(2)}) %collective-permute-start.18) | collective-permute-done | bytes 557088 | tf_op jit(solution)/shard_map/ppermute | solution.py:301
  160.4 11.4 %collective-permute-done.19.refs_2_ = bf16[544,512]{1,0:T(8,128)(2,1)S(1)} collective-permute-done((bf16[544,512]{1,0:T(8,128)(2,1)S(1)}, bf16[544,512]{1,0:T(8,128)(2,1)S(1)}, u32[]{:S(2)}, u32[]{:S(2)}) %collective-permute-start.19) | collective-permute-done | bytes 557088 | tf_op jit(solution)/shard_map/ppermute | solution.py:301
  172.6 2.3 %copy-done.1 = bf16[4,9,256,256]{3,2,1,0:T(8,128)(2,1)S(1)} copy-done((bf16[4,9,256,256]{3,2,1,0:T(8,128)(2,1)S(1)}, bf16[4,9,256,256]{3,2,1,0:T(8,128)(2,1)}, u32[]{:S(2)}) %copy-start.1) | copy-done | bytes 4718616
  175.0 2.9 %back.2 = (f32[512,512]{1,0:T(8,128)}, f32[272,256]{1,0:T(8,128)S(1)}, f32[2,272,128]{2,1,0:T(8,128)S(1)}, f32[8,128]{1,0:T(8,128)S(1)}) custom-call(bf16[544,512]{1,0:T(8,128)(2,1)S(1)} %get-tuple-element.33.refs_0_, bf16[544,512]{1,0:T(8,128)(2,1)S(1)} %collective-permute-done.18.refs_1_, bf16[544,512]{1,0:T(8,128)(2,1)S(1)} %collective-permute-done.19.refs_2_, ...), custom_call_target="tpu_custom_call" | custom-call | tf_op jit(solution)/shard_map/back/pallas_call | solution.py:169
  180.2 3.6 %collective-permute-start.22 = (f32[258]{0:T(512)S(1)}, f32[258]{0:T(512)S(1)}, u32[]{:S(2)}, u32[]{:S(2)}) collective-permute-start(f32[258]{0:T(512)S(1)} %get-tuple-element.46), channel_id=1, source_target_pairs={{1,0},{2,1},{3,2},{4,3},{5,4},{6,5},{7,6},{9,8},{10,9},{11,10},{12... | collective-permute-start | bytes 3104 | tf_op jit(solution)/shard_map/ppermute | solution.py:192
  187.2 3.9 %collective-permute-start.24 = (f32[1,256]{1,0:T(1,128)S(1)}, f32[1,256]{1,0:T(1,128)S(1)}, u32[]{:S(2)}, u32[]{:S(2)}) collective-permute-start(f32[1,256]{1,0:T(1,128)S(1)} %get-tuple-element.51), channel_id=1, source_target_pairs={{8,0},{16,8},{24,16},{9,1},{17,9},{25,17},{10,2},{18,10},{26,18},{... | collective-permute-start | bytes 3080 | tf_op jit(solution)/shard_map/ppermute | solution.py:201
  196.0 3.1 %collective-permute-start.27 = (f32[130]{0:T(256)S(1)}, f32[130]{0:T(256)S(1)}, u32[]{:S(2)}, u32[]{:S(2)}) collective-permute-start(f32[130]{0:T(256)S(1)} %get-tuple-element.49), channel_id=1, source_target_pairs={{1,0},{2,1},{3,2},{4,3},{5,4},{6,5},{7,6},{9,8},{10,9},{11,10},{12... | collective-permute-start | bytes 1568 | tf_op jit(solution)/shard_map/ppermute | solution.py:192
  201.1 2.8 %collective-permute-done.26 = f32[130]{0:T(256)S(1)} collective-permute-done((f32[130]{0:T(256)S(1)}, f32[130]{0:T(256)S(1)}, u32[]{:S(2)}, u32[]{:S(2)}) %collective-permute-start.26) | collective-permute-done | bytes 552 | tf_op jit(solution)/shard_map/ppermute | solution.py:191
  204.1 3.1 %collective-permute-start.28 = (f32[1,128]{1,0:T(1,128)S(1)}, f32[1,128]{1,0:T(1,128)S(1)}, u32[]{:S(2)}, u32[]{:S(2)}) collective-permute-start(f32[1,128]{1,0:T(1,128)S(1)} %get-tuple-element.56), channel_id=1, source_target_pairs={{0,8},{8,16},{16,24},{1,9},{9,17},{17,25},{2,10},{10,18},{18,26},{... | collective-permute-start | bytes 1544 | tf_op jit(solution)/shard_map/ppermute | solution.py:200
  207.2 2.7 %collective-permute-start.29 = (f32[1,128]{1,0:T(1,128)S(1)}, f32[1,128]{1,0:T(1,128)S(1)}, u32[]{:S(2)}, u32[]{:S(2)}) collective-permute-start(f32[1,128]{1,0:T(1,128)S(1)} %get-tuple-element.57), channel_id=1, source_target_pairs={{8,0},{16,8},{24,16},{9,1},{17,9},{25,17},{10,2},{18,10},{26,18},{... | collective-permute-start | bytes 1544 | tf_op jit(solution)/shard_map/ppermute | solution.py:201
  211.3 2.2 collective-permute-done.30
  (93 shorter events, 40.6 us)
Async XLA Ops:
  1.3 5.8 %collective-permute-start.1 = (f32[1,128]{1,0:T(1,128)S(1)}, f32[1,128]{1,0:T(1,128)S(1)}, u32[]{:S(2)}, u32[]{:S(2)}) collective-permute-start(f32[1,128]{1,0:T(1,128)S(1)} %get-tuple-element.60), channel_id=1, source_target_pairs={{0,8},{8,16},{16,24},{1,9},{9,17},{17,25},{2,10},{10,18},{18,26},{... | collective-permute-start | bytes 1544 | tf_op jit(solution)/shard_map/ppermute | solution.py:23
  4.7 6.3 %collective-permute-start.2 = (f32[1,128]{1,0:T(1,128)S(1)}, f32[1,128]{1,0:T(1,128)S(1)}, u32[]{:S(2)}, u32[]{:S(2)}) collective-permute-start(f32[1,128]{1,0:T(1,128)S(1)} %get-tuple-element.61), channel_id=1, source_target_pairs={{8,0},{16,8},{24,16},{9,1},{17,9},{25,17},{10,2},{18,10},{26,18},{... | collective-permute-start | bytes 1544 | tf_op jit(solution)/shard_map/ppermute | solution.py:24
  12.0 5.6 %collective-permute-start.3 = (f32[130,1]{1,0:T(8,128)S(1)}, f32[130,1]{1,0:T(8,128)S(1)}, u32[]{:S(2)}, u32[]{:S(2)}) collective-permute-start(f32[130,1]{1,0:T(8,128)S(1)} %get-tuple-element.58), channel_id=1, source_target_pairs={{0,1},{1,2},{2,3},{3,4},{4,5},{5,6},{6,7},{8,9},{9,10},{10,11},{11... | collective-permute-start | bytes 1568 | tf_op jit(solution)/shard_map/ppermute | solution.py:23
  13.9 5.6 %collective-permute-start.4 = (f32[130,1]{1,0:T(8,128)S(1)}, f32[130,1]{1,0:T(8,128)S(1)}, u32[]{:S(2)}, u32[]{:S(2)}) collective-permute-start(f32[130,1]{1,0:T(8,128)S(1)} %get-tuple-element.59), channel_id=1, source_target_pairs={{1,0},{2,1},{3,2},{4,3},{5,4},{6,5},{7,6},{9,8},{10,9},{11,10},{12... | collective-permute-start | bytes 1568 | tf_op jit(solution)/shard_map/ppermute | solution.py:24
  23.6 5.9 %collective-permute-start.5 = (f32[1,256]{1,0:T(1,128)S(1)}, f32[1,256]{1,0:T(1,128)S(1)}, u32[]{:S(2)}, u32[]{:S(2)}) collective-permute-start(f32[1,256]{1,0:T(1,128)S(1)} %get-tuple-element.54), channel_id=1, source_target_pairs={{0,8},{8,16},{16,24},{1,9},{9,17},{17,25},{2,10},{10,18},{18,26},{... | collective-permute-start | bytes 3080 | tf_op jit(solution)/shard_map/ppermute | solution.py:23
  26.1 6.4 %collective-permute-start.6 = (f32[1,256]{1,0:T(1,128)S(1)}, f32[1,256]{1,0:T(1,128)S(1)}, u32[]{:S(2)}, u32[]{:S(2)}) collective-permute-start(f32[1,256]{1,0:T(1,128)S(1)} %get-tuple-element.55), channel_id=1, source_target_pairs={{8,0},{16,8},{24,16},{9,1},{17,9},{25,17},{10,2},{18,10},{26,18},{... | collective-permute-start | bytes 3080 | tf_op jit(solution)/shard_map/ppermute | solution.py:24
  32.6 6.3 %collective-permute-start.7 = (f32[258,1]{1,0:T(8,128)S(1)}, f32[258,1]{1,0:T(8,128)S(1)}, u32[]{:S(2)}, u32[]{:S(2)}) collective-permute-start(f32[258,1]{1,0:T(8,128)S(1)} %get-tuple-element.52), channel_id=1, source_target_pairs={{0,1},{1,2},{2,3},{3,4},{4,5},{5,6},{6,7},{8,9},{9,10},{10,11},{11... | collective-permute-start | bytes 3104 | tf_op jit(solution)/shard_map/ppermute | solution.py:23
  34.8 5.9 %collective-permute-start.8 = (f32[258,1]{1,0:T(8,128)S(1)}, f32[258,1]{1,0:T(8,128)S(1)}, u32[]{:S(2)}, u32[]{:S(2)}) collective-permute-start(f32[258,1]{1,0:T(8,128)S(1)} %get-tuple-element.53), channel_id=1, source_target_pairs={{1,0},{2,1},{3,2},{4,3},{5,4},{6,5},{7,6},{9,8},{10,9},{11,10},{12... | collective-permute-start | bytes 3104 | tf_op jit(solution)/shard_map/ppermute | solution.py:24
  46.9 14.3 %collective-permute-start.11 = (bf16[512,512]{1,0:T(8,128)(2,1)}, bf16[512,512]{1,0:T(8,128)(2,1)}, u32[]{:S(2)}, u32[]{:S(2)}) collective-permute-start(bf16[512,512]{1,0:T(8,128)(2,1)} %get-tuple-element.26.refs_0_), channel_id=1, source_target_pairs={{0,6},{1,7},{2,0},{3,1},{4,2},{5,3},{6,4},{7,5},{8,14},{9,15},{10,... | collective-permute-start | bytes 1572872 | tf_op jit(solution)/shard_map/ppermute | solution.py:301
  46.9 36.1 %collective-permute-start.10 = (bf16[512,512]{1,0:T(8,128)(2,1)}, bf16[512,512]{1,0:T(8,128)(2,1)}, u32[]{:S(2)}, u32[]{:S(2)}) collective-permute-start(bf16[512,512]{1,0:T(8,128)(2,1)} %get-tuple-element.26.refs_0_), channel_id=1, source_target_pairs={{0,4},{1,5},{2,6},{3,7},{4,0},{5,1},{6,2},{7,3},{8,12},{9,13},{10,... | collective-permute-start | bytes 1572872 | tf_op jit(solution)/shard_map/ppermute | solution.py:301
  50.0 44.3 %collective-permute-start.9 = (bf16[512,512]{1,0:T(8,128)(2,1)}, bf16[512,512]{1,0:T(8,128)(2,1)}, u32[]{:S(2)}, u32[]{:S(2)}) collective-permute-start(bf16[512,512]{1,0:T(8,128)(2,1)} %get-tuple-element.26.refs_0_), channel_id=1, source_target_pairs={{0,2},{1,3},{2,4},{3,5},{4,6},{5,7},{6,0},{7,1},{8,10},{9,11},{10,... | collective-permute-start | bytes 1572872 | tf_op jit(solution)/shard_map/ppermute | solution.py:301
  52.5 42.1 %collective-permute-start.12 = (bf16[512,512]{1,0:T(8,128)(2,1)}, bf16[512,512]{1,0:T(8,128)(2,1)}, u32[]{:S(2)}, u32[]{:S(2)}) collective-permute-start(bf16[512,512]{1,0:T(8,128)(2,1)} %get-tuple-element.26.refs_0_), channel_id=1, source_target_pairs={{0,1},{1,0},{2,3},{3,2},{4,5},{5,4},{6,7},{7,6},{8,9},{9,8},{10,11... | collective-permute-start | bytes 1572872 | tf_op jit(solution)/shard_map/ppermute | solution.py:305
  61.2 33.3 %collective-permute-start.15 = (bf16[512,512]{1,0:T(8,128)(2,1)}, bf16[512,512]{1,0:T(8,128)(2,1)}, u32[]{:S(2)}, u32[]{:S(2)}) collective-permute-start(bf16[512,512]{1,0:T(8,128)(2,1)} %collective-permute-done.11.refs_3_), channel_id=1, source_target_pairs={{0,1},{1,0},{2,3},{3,2},{4,5},{5,4},{6,7},{7,6},{8,9},{9,8},{10,11... | collective-permute-start | bytes 1572872 | tf_op jit(solution)/shard_map/ppermute | solution.py:305
  83.0 11.5 %collective-permute-start.14 = (bf16[512,512]{1,0:T(8,128)(2,1)}, bf16[512,512]{1,0:T(8,128)(2,1)}, u32[]{:S(2)}, u32[]{:S(2)}) collective-permute-start(bf16[512,512]{1,0:T(8,128)(2,1)} %collective-permute-done.10.refs_2_), channel_id=1, source_target_pairs={{0,1},{1,0},{2,3},{3,2},{4,5},{5,4},{6,7},{7,6},{8,9},{9,8},{10,11... | collective-permute-start | bytes 1572872 | tf_op jit(solution)/shard_map/ppermute | solution.py:305
  94.3 2.3 %collective-permute-start.13 = (bf16[512,512]{1,0:T(8,128)(2,1)}, bf16[512,512]{1,0:T(8,128)(2,1)}, u32[]{:S(2)}, u32[]{:S(2)}) collective-permute-start(bf16[512,512]{1,0:T(8,128)(2,1)} %collective-permute-done.9.refs_1_), channel_id=1, source_target_pairs={{0,1},{1,0},{2,3},{3,2},{4,5},{5,4},{6,7},{7,6},{8,9},{9,8},{10,11... | collective-permute-start | bytes 1572872 | tf_op jit(solution)/shard_map/ppermute | solution.py:305
  107.7 10.2 %collective-permute-start.17 = (bf16[512,512]{1,0:T(8,128)(2,1)}, bf16[512,512]{1,0:T(8,128)(2,1)}, u32[]{:S(2)}, u32[]{:S(2)}) collective-permute-start(bf16[512,512]{1,0:T(8,128)(2,1)} %get-tuple-element.28.refs_1_), channel_id=1, source_target_pairs={{0,1},{1,0},{2,3},{3,2},{4,5},{5,4},{6,7},{7,6},{8,9},{9,8},{10,11... | collective-permute-start | bytes 1572872 | tf_op jit(solution)/shard_map/ppermute | solution.py:305
  115.4 2.6 %collective-permute-start.16 = (bf16[512,512]{1,0:T(8,128)(2,1)}, bf16[512,512]{1,0:T(8,128)(2,1)S(1)}, u32[]{:S(2)}, u32[]{:S(2)}) collective-permute-start(bf16[512,512]{1,0:T(8,128)(2,1)} %get-tuple-element.27.refs_0_), channel_id=1, source_target_pairs={{0,1},{1,0},{2,3},{3,2},{4,5},{5,4},{6,7},{7,6},{8,9},{9,8},{10,11... | collective-permute-start | bytes 1572872 | tf_op jit(solution)/shard_map/ppermute | solution.py:305
  115.5 1.7 collective-permute-start
  120.9 39.5 %collective-permute-start.18 = (bf16[544,512]{1,0:T(8,128)(2,1)S(1)}, bf16[544,512]{1,0:T(8,128)(2,1)S(1)}, u32[]{:S(2)}, u32[]{:S(2)}) collective-permute-start(bf16[544,512]{1,0:T(8,128)(2,1)S(1)} %get-tuple-element.34), channel_id=1, source_target_pairs={{0,2},{1,3},{2,4},{3,5},{4,6},{5,7},{6,0},{7,1},{8,10},{9,11},{10,... | collective-permute-start | bytes 1671176 | tf_op jit(solution)/shard_map/ppermute | solution.py:301
  123.5 48.2 %collective-permute-start.19 = (bf16[544,512]{1,0:T(8,128)(2,1)S(1)}, bf16[544,512]{1,0:T(8,128)(2,1)S(1)}, u32[]{:S(2)}, u32[]{:S(2)}) collective-permute-start(bf16[544,512]{1,0:T(8,128)(2,1)S(1)} %get-tuple-element.35), channel_id=1, source_target_pairs={{0,4},{1,5},{2,6},{3,7},{4,0},{5,1},{6,2},{7,3},{8,12},{9,13},{10,... | collective-permute-start | bytes 1671176 | tf_op jit(solution)/shard_map/ppermute | solution.py:301
  124.5 48.1 %collective-permute-start.20 = (bf16[544,512]{1,0:T(8,128)(2,1)S(1)}, bf16[544,512]{1,0:T(8,128)(2,1)S(1)}, u32[]{:S(2)}, u32[]{:S(2)}) collective-permute-start(bf16[544,512]{1,0:T(8,128)(2,1)S(1)} %get-tuple-element.36), channel_id=1, source_target_pairs={{0,6},{1,7},{2,0},{3,1},{4,2},{5,3},{6,4},{7,5},{8,14},{9,15},{10,... | collective-permute-start | bytes 1671176 | tf_op jit(solution)/shard_map/ppermute | solution.py:301
  178.1 5.7 %collective-permute-start.21 = (f32[258]{0:T(512)S(1)}, f32[258]{0:T(512)S(1)}, u32[]{:S(2)}, u32[]{:S(2)}) collective-permute-start(f32[258]{0:T(512)S(1)} %get-tuple-element.47), channel_id=1, source_target_pairs={{0,1},{1,2},{2,3},{3,4},{4,5},{5,6},{6,7},{8,9},{9,10},{10,11},{11... | collective-permute-start | bytes 3104 | tf_op jit(solution)/shard_map/ppermute | solution.py:191
  180.2 4.9 %collective-permute-start.22 = (f32[258]{0:T(512)S(1)}, f32[258]{0:T(512)S(1)}, u32[]{:S(2)}, u32[]{:S(2)}) collective-permute-start(f32[258]{0:T(512)S(1)} %get-tuple-element.46), channel_id=1, source_target_pairs={{1,0},{2,1},{3,2},{4,3},{5,4},{6,5},{7,6},{9,8},{10,9},{11,10},{12... | collective-permute-start | bytes 3104 | tf_op jit(solution)/shard_map/ppermute | solution.py:192
  185.3 9.0 %collective-permute-start.23 = (f32[1,256]{1,0:T(1,128)S(1)}, f32[1,256]{1,0:T(1,128)S(1)}, u32[]{:S(2)}, u32[]{:S(2)}) collective-permute-start(f32[1,256]{1,0:T(1,128)S(1)} %get-tuple-element.50), channel_id=1, source_target_pairs={{0,8},{8,16},{16,24},{1,9},{9,17},{17,25},{2,10},{10,18},{18,26},{... | collective-permute-start | bytes 3080 | tf_op jit(solution)/shard_map/ppermute | solution.py:200
  187.2 7.1 %collective-permute-start.24 = (f32[1,256]{1,0:T(1,128)S(1)}, f32[1,256]{1,0:T(1,128)S(1)}, u32[]{:S(2)}, u32[]{:S(2)}) collective-permute-start(f32[1,256]{1,0:T(1,128)S(1)} %get-tuple-element.51), channel_id=1, source_target_pairs={{8,0},{16,8},{24,16},{9,1},{17,9},{25,17},{10,2},{18,10},{26,18},{... | collective-permute-start | bytes 3080 | tf_op jit(solution)/shard_map/ppermute | solution.py:201
  191.8 1.2 collective-permute-start.25
  196.0 5.0 %collective-permute-start.27 = (f32[130]{0:T(256)S(1)}, f32[130]{0:T(256)S(1)}, u32[]{:S(2)}, u32[]{:S(2)}) collective-permute-start(f32[130]{0:T(256)S(1)} %get-tuple-element.49), channel_id=1, source_target_pairs={{1,0},{2,1},{3,2},{4,3},{5,4},{6,5},{7,6},{9,8},{10,9},{11,10},{12... | collective-permute-start | bytes 1568 | tf_op jit(solution)/shard_map/ppermute | solution.py:192
  199.0 4.9 %collective-permute-start.26 = (f32[130]{0:T(256)S(1)}, f32[130]{0:T(256)S(1)}, u32[]{:S(2)}, u32[]{:S(2)}) collective-permute-start(f32[130]{0:T(256)S(1)} %get-tuple-element.48), channel_id=1, source_target_pairs={{0,1},{1,2},{2,3},{3,4},{4,5},{5,6},{6,7},{8,9},{9,10},{10,11},{11... | collective-permute-start | bytes 1568 | tf_op jit(solution)/shard_map/ppermute | solution.py:191
  204.1 14.2 %collective-permute-start.28 = (f32[1,128]{1,0:T(1,128)S(1)}, f32[1,128]{1,0:T(1,128)S(1)}, u32[]{:S(2)}, u32[]{:S(2)}) collective-permute-start(f32[1,128]{1,0:T(1,128)S(1)} %get-tuple-element.56), channel_id=1, source_target_pairs={{0,8},{8,16},{16,24},{1,9},{9,17},{17,25},{2,10},{10,18},{18,26},{... | collective-permute-start | bytes 1544 | tf_op jit(solution)/shard_map/ppermute | solution.py:200
  207.2 11.1 %collective-permute-start.29 = (f32[1,128]{1,0:T(1,128)S(1)}, f32[1,128]{1,0:T(1,128)S(1)}, u32[]{:S(2)}, u32[]{:S(2)}) collective-permute-start(f32[1,128]{1,0:T(1,128)S(1)} %get-tuple-element.57), channel_id=1, source_target_pairs={{8,0},{16,8},{24,16},{9,1},{17,9},{25,17},{10,2},{18,10},{26,18},{... | collective-permute-start | bytes 1544 | tf_op jit(solution)/shard_map/ppermute | solution.py:201
  210.0 3.6 %collective-permute-start.30 = (f32[1]{0:T(128)}, f32[1]{0:T(128)}, u32[]{:S(2)}, u32[]{:S(2)}) collective-permute-start(f32[1]{0:T(128)} %add.149), channel_id=1, source_target_pairs={{0,8},{8,0},{16,24},{24,16},{1,9},{9,1},{17,25},{25,17},{2,10},{10... | collective-permute-start | bytes 20 | tf_op jit(solution)/shard_map/ppermute | solution.py:354
  214.1 3.6 %collective-permute-start.31 = (f32[1]{0:T(128)}, f32[1]{0:T(128)}, u32[]{:S(2)}, u32[]{:S(2)}) collective-permute-start(f32[1]{0:T(128)} %add.157), channel_id=1, source_target_pairs={{0,16},{8,24},{16,0},{24,8},{1,17},{9,25},{17,1},{25,9},{2,18},{10... | collective-permute-start | bytes 20 | tf_op jit(solution)/shard_map/ppermute | solution.py:354
  (14 other events, 316.4 us)

commit v4 on v3

--- a/solution.py
+++ b/solution.py
@@ -13,23 +13,6 @@
 bf16 = jnp.bfloat16
 
 
-def extended(x, sides, width):
-    for axis, dim in sides:
-        size, length = (lax.axis_size(axis), x.shape[dim])
-        up = [(i, (i + 1) % size) for i in range(size - 1)]
-        down = [(j, i) for i, j in up]
-        last = lax.slice_in_dim(x, length - width, length, axis=dim)
-        leading = lax.slice_in_dim(x, 0, width, axis=dim)
-        before = lax.ppermute(last, axis, up)
-        after = lax.ppermute(leading, axis, down)
-        x = jnp.concatenate([before, x, after], axis=dim)
-    return x
-
-
-def widen(field):
-    return extended(field, (("gx", 0), ("gy", 1)), 1)
-
-
 def halves(x):
     high = x.astype(bf16)
     return high, (x - high.astype(f32)).astype(bf16)
@@ -49,13 +32,34 @@
     return sum(x[:, i : i + 128] for i in range(0, cols, 128))
 
 
-def refine_kernel(first, pad_ref, coef_ref, xi_ref, out_ref, sq_ref, win, perm, lhs, mix):
-    rows, cols = win.shape[1:]
-    for near in range(9):
-        r, c = near // 3, near % 3
-        win[near] = pad_ref[r : r + rows, c : c + cols]
-    perm[...] = interleaver(cols, False)
-
+def row_of(ref, i):
+    return ref[i : i + 1, :]
+
+
+def dot_t(x, y, dims):
+    return lax.dot_general(x, y, (dims, ((), ())), preferred_element_type=f32)
+
+
+def moved(x, perm):
+    high, low = halves(x)
+    return jnp.dot(high, perm, preferred_element_type=f32) + jnp.dot(
+        low, perm, preferred_element_type=f32
+    )
+
+
+def ends_placed(first, last, cols):
+    rows = jnp.concatenate([first, first, last, last, jnp.zeros((4, first.shape[1]), f32)])
+    high = rows.astype(bf16).astype(f32)
+    index = lax.broadcasted_iota(jnp.int32, rows.shape, 0)
+    rows = jnp.where(index % 2 == 0, high, rows - high).astype(bf16)
+    shape = (8, cols)
+    index = lax.broadcasted_iota(jnp.int32, shape, 0)
+    lane = lax.broadcasted_iota(jnp.int32, shape, 1)
+    place = ((index < 2) & (lane == 0)) | ((index >= 2) & (index < 4) & (lane == cols - 1))
+    return dot_t(rows, place.astype(f32).astype(bf16), ((0,), (0,)))
+
+
+def weighed(win, coef_ref, perm, lhs, mix, rows, cols):
     def part(i, carry):
         r0 = pl.multiple_of(i * 16, 16)
         total = [jnp.zeros((16, cols), f32) for _ in range(4)]
@@ -72,7 +76,6 @@
 
     lax.fori_loop(0, rows // 16, part, 0)
     field = jnp.dot(lhs[...], perm[...], preferred_element_type=f32)
-    xi = xi_ref[...]
     for tile in range(2 * cols // 128):
         lanes = slice(tile * 128, (tile + 1) * 128)
         for a in range(2):
@@ -80,25 +83,192 @@
                 field[2 * a * rows : (2 * a + 1) * rows, lanes]
                 + field[(2 * a + 1) * rows : (2 * a + 2) * rows, lanes]
             )
-        out_ref[:, lanes] = (mix[tile] + xi[:, lanes]).astype(out_ref.dtype)
-    square = folded(xi * xi)
-    if first:
-        square += folded(win[4] * win[4])
-    sq_ref[...] = square
+
+
+def sky_kernel(
+    wide,
+    above,
+    below,
+    lefts,
+    rights,
+    to_left,
+    to_right,
+    coef_middle,
+    xi_middle,
+    coef_fine,
+    xi_fine,
+    sky_ref,
+    sq_ref,
+    win,
+    perm,
+    lhs,
+    mix,
+    shifted,
+    fine_win,
+    fine_perm,
+    fine_lhs,
+    fine_mix,
+):
+    rows, cols = win.shape[1:]
+    for near in range(9):
+        r, c = near // 3, near % 3
+        win[near] = wide[1 + r : 1 + r + rows, 1 + c : 1 + c + cols]
+    perm[...] = interleaver(cols, False)
+    fine_perm[...] = interleaver(2 * cols, False)
+    weighed(win, coef_middle, perm, lhs, mix, rows, cols)
+
+    def across(message, top):
+        out = []
+        for b in range(2):
+            line = row_of(message, 20 + b)
+            for near in range(9):
+                r, c = near // 3, near % 3
+                line += row_of(message, 9 * b + near) * wide[top + r : top + r + 1, 1 + c : 1 + c + cols]
+            out.append(line)
+        return jnp.concatenate(out, axis=1)
+
+    def along(message, fields):
+        out = []
+        for a in range(2):
+            line = row_of(message, 20 + a)[:, 1 : rows + 3]
+            for near in range(9):
+                r, c = near // 3, near % 3
+                line += row_of(message, 9 * a + near)[:, 1 : rows + 3] * fields[c][:, r : r + rows + 2]
+            out.append(line)
+        inner = jnp.concatenate([line[:, 1 : rows + 1] for line in out], axis=1)
+        return inner, out[1][:, :1], out[0][:, rows + 1 :]
+
+    top, bottom = across(above, 0), across(below, rows + 1)
+    left, top_left, bottom_left = along(
+        lefts, [row_of(lefts, 18), row_of(lefts, 19), row_of(to_left, 18)]
+    )
+    right, top_right, bottom_right = along(
+        rights, [row_of(to_right, 19), row_of(rights, 18), row_of(rights, 19)]
+    )
+    lines = jnp.concatenate([top, bottom, left, right, jnp.zeros((4, 2 * cols), f32)])
+    lines = moved(lines, perm[...])
+    xi = xi_middle[...]
+    last = 8 + 2 * rows
+    for tile in range(2 * cols // 128):
+        lanes = slice(tile * 128, (tile + 1) * 128)
+        shifted[1, 8:last, lanes] = mix[tile] + xi[:, lanes]
+    shifted[1, 7:8, :] = lines[0:1]
+    shifted[1, last : last + 1, :] = lines[1:2]
+    placed = ends_placed(lines[2:3], lines[3:4], 2 * cols)
+    for side, lane, turn, first, final in (
+        (0, 0, 1, top_left, bottom_left),
+        (2, 2 * cols - 1, 2 * cols - 1, top_right, bottom_right),
+    ):
+        turned = pltpu.roll(shifted[1, 8:last, :], turn, 1)
+        here = lax.broadcasted_iota(jnp.int32, turned.shape, 1) == lane
+        shifted[side, 8:last, :] = jnp.where(here, placed, turned)
+        ends = jnp.concatenate([lines[0:2], jnp.zeros((6, 2 * cols), f32)])
+        ends = pltpu.roll(ends, turn, 1)
+        here = lax.broadcasted_iota(jnp.int32, (1, 2 * cols), 1) == lane
+        shifted[side, 7:8, :] = jnp.where(here, first, ends[0:1])
+        shifted[side, last : last + 1, :] = jnp.where(here, final, ends[1:2])
+    for near in range(9):
+        r, c = near // 3, near % 3
+        fine_win[near] = shifted[c, 7 + r : 7 + r + 2 * rows, :]
+    weighed(fine_win, coef_fine, fine_perm, fine_lhs, fine_mix, 2 * rows, 2 * cols)
+    for tile in range(4 * cols // 128):
+        lanes = slice(tile * 128, (tile + 1) * 128)
+        sky_ref[:, lanes] = (fine_mix[tile] + xi_fine[:, lanes]).astype(bf16)
+    sq_ref[...] = (
+        folded(win[4] * win[4]) + folded(xi * xi) + folded(xi_fine[...] * xi_fine[...])
+    )
+
+
+def neighbours(axis):
+    size = lax.axis_size(axis)
+    ahead = [(i, i + 1) for i in range(size - 1)]
+    return ahead, [(j, i) for i, j in ahead]
+
+
+def halo(xi_coarse, xi_middle, coef_middle):
+    rows, cols = xi_coarse.shape
+    down, up = neighbours("gx")
+    right, left = neighbours("gy")
+
+    def edge(a, row, near):
+        return jnp.concatenate(
+            [
+                coef_middle[2 * a : 2 * a + 2, :, row].reshape(18, cols).astype(f32),
+                near,
+                xi_middle[2 * row + a].reshape(cols, 2).T,
+            ]
+        )
+
+    above = lax.ppermute(edge(1, rows - 1, xi_coarse[-2:]), "gx", down)
+    below = lax.ppermute(edge(0, 0, xi_coarse[:2]), "gx", up)
+
+    def inside(b, col, near):
+        return jnp.concatenate(
+            [
+                coef_middle[b::2, :, :, col].reshape(18, rows).astype(f32),
+                near.T,
+                xi_middle[:, 2 * col + b].reshape(rows, 2).T,
+            ]
+        )
+
+    sides = inside(0, 0, xi_coarse[:, :2]), inside(1, cols - 1, xi_coarse[:, -2:])
+    sides = lax.optimization_barrier(sides)
+
+    def edges(b, col, first, side):
+        zero = jnp.zeros((18,), f32)
+        upper = jnp.stack(
+            [
+                jnp.concatenate([zero, above[18, first : first + 2], zero[:2]]),
+                jnp.concatenate(
+                    [
+                        zero[:9],
+                        above[9 * b : 9 * b + 9, col],
+                        above[19, first : first + 2],
+                        zero[:1],
+                        above[20 + b : 21 + b, col],
+                    ]
+                ),
+            ],
+            axis=1,
+        )
+        lower = jnp.stack(
+            [
+                jnp.concatenate(
+                    [
+                        below[9 * b : 9 * b + 9, col],
+                        zero[:9],
+                        below[18, first : first + 2],
+                        below[20 + b : 21 + b, col],
+                        zero[:1],
+                    ]
+                ),
+                jnp.concatenate([zero, below[19, first : first + 2], zero[:2]]),
+            ],
+            axis=1,
+        )
+        return jnp.concatenate([upper, side, lower], axis=1)
+
+    to_left = edges(0, 0, 0, sides[0])
+    to_right = edges(1, cols - 1, cols - 2, sides[1])
+    lefts = lax.ppermute(to_right, "gy", right)
+    rights = lax.ppermute(to_left, "gy", left)
+    tall = jnp.concatenate([above[18:20], xi_coarse, below[18:20]])
+    wide = jnp.concatenate([lefts[18:20].T, tall, rights[18:20].T], axis=1)
+    return wide, above, below, lefts, rights, to_left, to_right
 
 
 whole = pl.BlockSpec(memory_space=pltpu.VMEM)
 scalar = pl.BlockSpec(memory_space=pltpu.SMEM)
 
 
-def refine(padded, coef, xi, dtype, first):
-    rows, cols = coef.shape[2:]
+def sky_of(halos, coef_middle, xi_middle, coef_fine, xi_fine):
+    rows, cols = coef_middle.shape[2:]
     return pl.pallas_call(
-        functools.partial(refine_kernel, first),
-        in_specs=[whole] * 3,
+        sky_kernel,
+        in_specs=[whole] * 11,
         out_specs=[whole] * 2,
         out_shape=[
-            jax.ShapeDtypeStruct((2 * rows, 2 * cols), dtype),
+            jax.ShapeDtypeStruct((4 * rows, 4 * cols), bf16),
             jax.ShapeDtypeStruct((8, 128), f32),
         ],
         scratch_shapes=[
@@ -106,32 +276,18 @@
             pltpu.VMEM((2 * cols, 2 * cols), bf16),
             pltpu.VMEM((4 * rows, 2 * cols), bf16),
             pltpu.VMEM((2 * cols // 128, 2 * rows, 128), f32),
+            pltpu.VMEM((3, 2 * rows + 16, 2 * cols), f32),
+            pltpu.VMEM((9, 2 * rows, 2 * cols), f32),
+            pltpu.VMEM((4 * cols, 4 * cols), bf16),
+            pltpu.VMEM((8 * rows, 4 * cols), bf16),
+            pltpu.VMEM((4 * cols // 128, 4 * rows, 128), f32),
         ],
         compiler_params=pltpu.CompilerParams(vmem_limit_bytes=vmem),
-        name="refine",
-    )(padded, coef, xi)
-
-
-def back_kernel(number, *refs):
-    parts = refs[:number]
-    coef_ref, xi_ref, grad_ref, main_ref, cols_ref, total_ref, terms, perm, mix, rowed = refs[number:]
-    rows, cols = terms.shape[1:]
-    perm[...] = interleaver(cols, True)
-    g = parts[0][: 2 * rows].astype(f32)
-    for part in parts[1:]:
-        g += part[: 2 * rows].astype(f32)
-    grad_ref[...] = g + xi_ref[...]
-    if parts[0].shape[0] > 2 * rows:
-        rest = sum(part[2 * rows :, :128].astype(f32) for part in parts)
-        total_ref[...] = rest[:8] + rest[8:16] + rest[16:24]
-    else:
-        total_ref[...] = jnp.zeros_like(total_ref)
-    high, low = halves(g)
-    split = jnp.dot(high, perm[...], preferred_element_type=f32)
-    split += jnp.dot(low, perm[...], preferred_element_type=f32)
-    for tile in range(2 * cols // 128):
-        mix[tile] = split[:, tile * 128 : (tile + 1) * 128]
-
+        name="sky",
+    )(*halos, coef_middle, xi_middle, coef_fine, xi_fine)
+
+
+def spread(mix, coef_ref, terms, rows, cols):
     def part(i, carry):
         r0 = pl.multiple_of(i * 16, 16)
         quads = []
@@ -148,64 +304,216 @@
         return carry
 
     lax.fori_loop(0, rows // 16, part, 0)
+
+
+def joined(rowed, cols):
+    lane = lax.broadcasted_iota(jnp.int32, rowed.shape[1:], 1)
+    main = (
+        rowed[1]
+        + jnp.where(lane == 0, 0.0, pltpu.roll(rowed[2], 1, 1))
+        + jnp.where(lane == cols - 1, 0.0, pltpu.roll(rowed[0], cols - 1, 1))
+    )
+    lane = lax.broadcasted_iota(jnp.int32, (8, cols), 1)
+    outside = []
+    for c, col in ((0, 0), (2, cols - 1)):
+        pick = (lane == col).astype(f32).astype(bf16)
+        high, low = halves(rowed[c])
+        out = dot_t(pick, high, ((1,), (1,))) + dot_t(pick, low, ((1,), (1,)))
+        outside.append(out[:1])
+    return main, outside[0], outside[1]
+
+
+def adjoint_kernel(number, *refs):
+    parts = refs[:number]
+    (
+        above,
+        below,
+        lefts,
+        rights,
+        coef_middle,
+        coef_fine,
+        xi_fine,
+        grad_ref,
+        middle_ref,
+        coarse_ref,
+        left_ref,
+        right_ref,
+        upper_ref,
+        lower_ref,
+        total_ref,
+        fine_perm,
+        fine_mix,
+        fine_terms,
+        fine_rowed,
+        perm,
+        mix,
+        terms,
+        rowed,
+    ) = refs[number:]
+    rows, cols = terms.shape[1:]
+    fine_perm[...] = interleaver(2 * cols, True)
+    perm[...] = interleaver(cols, True)
+    g = parts[0][: 4 * rows].astype(f32)
+    for part in parts[1:]:
+        g += part[: 4 * rows].astype(f32)
+    grad_ref[...] = g + xi_fine[...]
+    rest = sum(part[4 * rows :, :128].astype(f32) for part in parts)
+    total_ref[...] = rest[:8] + rest[8:16] + rest[16:24]
+    split = moved(g, fine_perm[...])
+    for tile in range(4 * cols // 128):
+        fine_mix[tile] = split[:, tile * 128 : (tile + 1) * 128]
+    spread(fine_mix, coef_fine, fine_terms, 2 * rows, 2 * cols)
+    fine_rowed[...] = jnp.zeros_like(fine_rowed)
+    for near in range(9):
+        r, c = near // 3, near % 3
+        fine_rowed[c, 7 + r : 7 + r + 2 * rows, :] += fine_terms[near]
+    main, left, right = joined(fine_rowed, 2 * cols)
+    last = 8 + 2 * rows
+    inner = main[8:last]
+    middle_ref[...] = inner
+    split = moved(inner, perm[...])
+    for tile in range(2 * cols // 128):
+        mix[tile] = split[:, tile * 128 : (tile + 1) * 128]
+    spread(mix, coef_middle, terms, rows, cols)
+    ring_above, ring_below = main[7:8], main[last : last + 1]
+    lines = [ring_above, ring_below, left[:, 8:last], right[:, 8:last]]
+    lines = moved(jnp.concatenate(lines + [jnp.zeros((4, 2 * cols), f32)]), perm[...])
     rowed[...] = jnp.zeros_like(rowed)
     for near in range(9):
         r, c = near // 3, near % 3
         rowed[c, 7 + r : 7 + r + rows, :] += terms[near]
-    lane = lax.broadcasted_iota(jnp.int32, (rows + 16, cols), 1)
-    from_left = pltpu.roll(rowed[2], 1, 1)
-    from_right = pltpu.roll(rowed[0], cols - 1, 1)
-    main_ref[...] = (
-        rowed[1]
-        + jnp.where(lane == 0, 0.0, from_left)
-        + jnp.where(lane == cols - 1, 0.0, from_right)
-    )
-    cols_ref[0] = rowed[0, :, :128]
-    cols_ref[1] = rowed[2, :, cols - 128 :]
-
-
-def back(parts, coef, xi):
-    rows, cols = coef.shape[2:]
-    grad, main, side, total = pl.pallas_call(
-        functools.partial(back_kernel, len(parts)),
-        in_specs=[whole] * (len(parts) + 2),
-        out_specs=[whole] * 4,
+    for line, message, top in ((0, above, 6), (1, below, 7 + rows)):
+        for near in range(9):
+            r, c = near // 3, near % 3
+            term = row_of(message, near) * lines[line : line + 1, :cols]
+            term += row_of(message, 9 + near) * lines[line : line + 1, cols:]
+            rowed[c, top + r : top + r + 1, :] += term
+
+    def along(line, ends, message):
+        empty = jnp.zeros((1, 1), f32)
+        first = [empty, lines[line : line + 1, :rows], ends[:, last : last + 1]]
+        second = [ends[:, 7:8], lines[line : line + 1, cols : cols + rows], empty]
+        first, second = jnp.concatenate(first, axis=1), jnp.concatenate(second, axis=1)
+        out = []
+        for c in range(3):
+            total = jnp.zeros((1, rows + 4), f32)
+            for r in range(3):
+                near = 3 * r + c
+                term = row_of(message, near)[:, 1 : rows + 3] * first
+                term += row_of(message, 9 + near)[:, 1 : rows + 3] * second
+                pads = [jnp.zeros((1, n), f32) for n in (r, 2 - r) if n]
+                pieces = [term] + pads if r == 0 else pads[:1] + [term] + pads[1:]
+                total += jnp.concatenate(pieces, axis=1)
+            out.append(total)
+        return out
+
+    outer_left = along(2, left, lefts)
+    outer_right = along(3, right, rights)
+    main, near_left, near_right = joined(rowed, cols)
+    coarse_ref[...] = main[8 : 8 + rows] + ends_placed(
+        outer_left[2][:, 2 : rows + 2], outer_right[0][:, 2 : rows + 2], cols
+    )
+    lane = lax.broadcasted_iota(jnp.int32, (1, cols), 1)
+    for ref, first, line in ((upper_ref, 6, ring_above), (lower_ref, 8 + rows, ring_below)):
+        ref[...] = jnp.zeros_like(ref)
+        for i in range(2):
+            at = first - 6 + i
+            ref[i : i + 1, :cols] = (
+                main[first + i : first + i + 1]
+                + jnp.where(lane == 0, outer_left[2][:, at : at + 1], 0.0)
+                + jnp.where(lane == cols - 1, outer_right[0][:, at : at + 1], 0.0)
+            )
+        ref[2:3, :] = line
+    for ref, far, close, beyond, ends in (
+        (left_ref, outer_left[0], outer_left[1], near_left, left),
+        (right_ref, outer_right[2], outer_right[1], near_right, right),
+    ):
+        ref[...] = jnp.zeros_like(ref)
+        ref[0:1, : rows + 4] = far
+        ref[1:2, : rows + 4] = close + beyond[:, 6 : rows + 10]
+        ref[2:3, : 2 * rows + 2] = ends[:, 7 : 2 * rows + 9]
+
+
+def final_kernel(middle, coarse, from_left, from_right, from_above, from_below, xi_middle, xi_coarse, middle_out, coarse_out):
+    rows, cols = coarse.shape
+    middle_out[...] = (
+        middle[...]
+        + xi_middle[...]
+        + ends_placed(from_left[2:3, 1 : 2 * rows + 1], from_right[2:3, 1 : 2 * rows + 1], 2 * cols)
+    )
+    middle_out[:1] += from_above[2:3]
+    middle_out[2 * rows - 1 :] += from_below[2:3]
+    inner = slice(2, rows + 2)
+    outer = ends_placed(from_left[1:2, inner], from_right[1:2, inner], cols)
+    second = ends_placed(from_left[0:1, inner], from_right[0:1, inner], cols)
+    lane = lax.broadcasted_iota(jnp.int32, second.shape, 1)
+    second = jnp.where(lane == 1, pltpu.roll(second, 1, 1), 0.0) + jnp.where(
+        lane == cols - 2, pltpu.roll(second, cols - 1, 1), 0.0
+    )
+    coarse_out[...] = coarse[...] + xi_coarse[...] + outer + second
+    coarse_out[:2] += from_above[0:2, :cols]
+    coarse_out[rows - 2 :] += from_below[0:2, :cols]
+
+
+def adjoint(parts, halos, coef_middle, xi_middle, coef_fine, xi_fine, xi_coarse):
+    rows, cols = coef_middle.shape[2:]
+    _, above, below, lefts, rights, _, _ = halos
+    shape = lambda *dims: jax.ShapeDtypeStruct(dims, f32)
+    long = 2 * rows + 128
+    grad_fine, middle, coarse, to_left, to_right, upper, lower, total = pl.pallas_call(
+        functools.partial(adjoint_kernel, len(parts)),
+        in_specs=[whole] * (len(parts) + 7),
+        out_specs=[whole] * 8,
         out_shape=[
-            jax.ShapeDtypeStruct((2 * rows, 2 * cols), f32),
-            jax.ShapeDtypeStruct((rows + 16, cols), f32),
-            jax.ShapeDtypeStruct((2, rows + 16, 128), f32),
-            jax.ShapeDtypeStruct((8, 128), f32),
+            shape(4 * rows, 4 * cols),
+            shape(2 * rows, 2 * cols),
+            shape(rows, cols),
+            shape(8, long),
+            shape(8, long),
+            shape(8, 2 * cols),
+            shape(8, 2 * cols),
+            shape(8, 128),
         ],
         scratch_shapes=[
-            pltpu.VMEM((9, rows, cols), f32),
+            pltpu.VMEM((4 * cols, 4 * cols), bf16),
+            pltpu.VMEM((4 * cols // 128, 4 * rows, 128), f32),
+            pltpu.VMEM((9, 2 * rows, 2 * cols), f32),
+            pltpu.VMEM((3, 2 * rows + 128, 2 * cols), f32),
             pltpu.VMEM((2 * cols, 2 * cols), bf16),
             pltpu.VMEM((2 * cols // 128, 2 * rows, 128), f32),
-            pltpu.VMEM((3, rows + 16, cols), f32),
+            pltpu.VMEM((9, rows, cols), f32),
+            pltpu.VMEM((3, rows + 128, cols), f32),
         ],
         compiler_params=pltpu.CompilerParams(vmem_limit_bytes=vmem),
-        name="back",
-    )(*parts, coef, xi)
-    size = lax.axis_size("gy")
-    right = [(i, i + 1) for i in range(size - 1)]
-    left = [(j, i) for i, j in right]
-    from_left = lax.ppermute(side[1, 7 : 9 + rows, 127], "gy", right)
-    from_right = lax.ppermute(side[0, 7 : 9 + rows, 0], "gy", left)
-    main = main[7 : 9 + rows]
-    ends = jnp.pad(from_left[:, None], ((0, 0), (0, cols - 1))) + jnp.pad(
-        from_right[:, None], ((0, 0), (cols - 1, 0))
-    )
-    size = lax.axis_size("gx")
-    down = [(i, i + 1) for i in range(size - 1)]
-    up = [(j, i) for i, j in down]
-    from_above = lax.ppermute(main[-1:] + ends[-1:], "gx", down)
-    from_below = lax.ppermute(main[:1] + ends[:1], "gx", up)
-    result = (
-        main[1:-1]
-        + ends[1:-1]
-        + jnp.pad(from_above, ((0, rows - 1), (0, 0)))
-        + jnp.pad(from_below, ((rows - 1, 0), (0, 0)))
-    )
-    return grad, result, total
+        name="adjoint",
+    )(*parts, above, below, lefts, rights, coef_middle, coef_fine, xi_fine)
+    right, left = neighbours("gy")
+    down, up = neighbours("gx")
+    from_left = lax.ppermute(to_right, "gy", right)
+    from_right = lax.ppermute(to_left, "gy", left)
+
+    def corners(rows_out, at, end):
+        first = jnp.stack([from_left[1, at : at + 2], from_left[0, at : at + 2]], axis=1)
+        last = jnp.stack([from_right[0, at : at + 2], from_right[1, at : at + 2]], axis=1)
+        pair = jnp.pad(first, ((0, 0), (0, 2 * cols - 2))) + jnp.pad(
+            last, ((0, 0), (cols - 2, cols))
+        )
+        line = jnp.pad(from_left[2:3, end : end + 1], ((0, 0), (0, 2 * cols - 1))) + jnp.pad(
+            from_right[2:3, end : end + 1], ((0, 0), (2 * cols - 1, 0))
+        )
+        return rows_out + jnp.pad(jnp.concatenate([pair, line]), ((0, 5), (0, 0)))
+
+    from_below = lax.ppermute(corners(upper, 0, 0), "gx", up)
+    from_above = lax.ppermute(corners(lower, rows + 2, 2 * rows + 1), "gx", down)
+    grad_middle, grad_coarse = pl.pallas_call(
+        final_kernel,
+        in_specs=[whole] * 8,
+        out_specs=[whole] * 2,
+        out_shape=[shape(2 * rows, 2 * cols), shape(rows, cols)],
+        compiler_params=pltpu.CompilerParams(vmem_limit_bytes=vmem),
+        name="final",
+    )(middle, coarse, from_left, from_right, from_above, from_below, xi_middle, xi_coarse)
+    return grad_coarse, grad_middle, grad_fine, total
 
 
 def facet_kernel(f, blk, number, sel, weights, counts, *refs):
@@ -319,8 +627,8 @@
     facet_count,
 ):
     side = xi_fine.shape[0]
-    level_middle, sq_middle = refine(widen(xi_coarse), coef_middle, xi_middle, f32, True)
-    sky, sq_fine = refine(widen(level_middle), coef_fine, xi_fine, bf16, False)
+    halos = halo(xi_coarse, xi_middle, coef_middle)
+    sky, squares = sky_of(halos, coef_middle, xi_middle, coef_fine, xi_fine)
     lists, weights, counts = facet_tiles[0], facet_weight[0], facet_count[0]
     number = lists.shape[0]
     size = lax.axis_size("gy")
@@ -335,7 +643,7 @@
     mine = [sky] + [chip_shift(sky, hop) for hop in range(1, chips)]
     tiles = mine + [swapped(tile) for tile in mine]
     sel = (me // 2 - lists // 2) % chips + jnp.where(lists % 2 == me % 2, 0, chips)
-    dsums, theirs, sums = [], [], [sq_middle, sq_fine]
+    dsums, theirs, sums = [], [], [squares]
     for f in range(number):
         dsum, lik = facet(f, tiles, kern_u, kern_v, vis_data, sel, weights, counts)
         dsums.append(dsum)
@@ -343,17 +651,16 @@
         sums.append(lik)
     parts = mixed(dsums + theirs, scale, sums)
     parts = [parts[0]] + [chip_shift(parts[hop], hop) for hop in range(1, chips)]
-    grad_fine, dmiddle, total = back(parts, coef_fine, xi_fine)
+    grad_coarse, grad_middle, grad_fine, total = adjoint(
+        parts, halos, coef_middle, xi_middle, coef_fine, xi_fine, xi_coarse
+    )
     total = jnp.sum(total)[None]
     total += swapped(total)
-    dmiddle, total = lax.optimization_barrier((dmiddle, total))
-    grad_middle, dcoarse, _ = back([dmiddle], coef_middle, xi_middle)
     size = lax.axis_size("gx")
     hop = 1
     while hop < size:
         total += lax.ppermute(total, "gx", [(i, i ^ hop) for i in range(size)])
         hop *= 2
-    grad_coarse = dcoarse + xi_coarse
     cells = lax.axis_size("gx") * lax.axis_size("gy") * side * side
     return (grad_coarse, grad_middle, grad_fine, total[0] / cells)
 

time: 222 us -> 215 us (0.968)
  starting transfers between devices: 61.6 us -> 36.5 us
  local copies, waits for them, and re-layouts: 13 us -> 33.9 us
  waiting for transfers between devices: 110 us -> 101 us
  other arithmetic: 3.85 us -> 7.44 us
    ppermute x16 -> x8, starting transfers between devices: 45.1 us -> 22.5 us  [the longest x1 4.3 us: halo(): above = lax.ppermute(edge(1, rows - 1, xi_coarse[-2:]), 'gx', down)]
    ppermute x16 -> x8, waiting for transfers between devices: 15.4 us -> 3.51 us  [the longest x1 2.56 us: halo(): lefts = lax.ppermute(to_right, 'gy', right)]
    unnamed x28 -> x72, local copies, waits for them, and re-layouts: 10.7 us -> 21.9 us
    slice x6 -> x12, local copies, waits for them, and re-layouts: 1.34 us -> 5.49 us  [the longest x1 1.19 us: inside(): xi_middle[:, 2 * col + b].reshape(rows, 2)]
    concatenate x0 -> x6, local copies, waits for them, and re-layouts: none -> 3.08 us  [the longest x2 1.46 us: edges(): jnp.concatenate([zero[:9], above[9 * b:9 * b + 9, col], above[19, first:f...]
    convert_element_type x0 -> x2, other arithmetic: none -> 2.79 us  [the longest x1 1.95 us: inside(): coef_middle[b::2, :, :, col].reshape(18, rows).astype(f32)]
    ppermute x6, waiting for transfers between devices: 86.7 us -> 89.2 us  [chip_shift(): lax.ppermute(x, 'gy', [(i, (i + 2 * hop) % size) for i in range(size)])]
    another operation x0 -> x29, local copies, waits for them, and re-layouts: none -> 2.47 us  [the longest x5 0.44 us: corners(): jnp.stack([from_left[1, at:at + 2], from_left[0, at:at + 2]], axis=1)]
  transfers between devices with their start and end apart: 32 -> 24, of which waited for: 18 -> 12; matrix products, arithmetic and copies ran while one was open for 1% -> 6% of each run, Pallas kernels for 3% -> 4%
where the time goes in v4:
time: 215 us; the launch traced here: 212 us
  waiting for transfers between devices  101 us (47%)
  starting transfers between devices  36.5 us (17%)
  local copies, waits for them, and re-layouts  33.9 us (16%)
  Pallas kernels  27.6 us (13%)
  other arithmetic  7.44 us (3%)
  between operations  4.84 us (2%)
    ppermute x6, waiting for transfers between devices, chip_shift(): lax.ppermute(x, 'gy', [(i, (i + 2 * hop) % size) for i in range(size)])  89.2 us
    unnamed x72, local copies, waits for them, and re-layouts  21.9 us
    pallas_call x2, Pallas kernels, facet(): pl.pallas_call(functools.partial(facet_kernel, f, blk, len(tiles)), in_sp...  15.1 us
    ppermute x6, starting transfers between devices, chip_shift(): lax.ppermute(x, 'gy', [(i, (i + 2 * hop) % size) for i in range(size)])  10 us
    ppermute x2, waiting for transfers between devices, body(): total += lax.ppermute(total, 'gx', [(i, i ^ hop) for i in range(size)])  4.66 us
    pallas_call x1, Pallas kernels, sky_of(): pl.pallas_call(sky_kernel, in_specs=[whole] * 11, out_specs=[whole] * 2,...  4.38 us
  transfers between devices with their start and end apart: 24, of which 12 were waited for; matrix products, arithmetic and copies ran while one was open for 6% of the time, Pallas kernels for 4%

profile of v4, /device:TPU:10, one launch (start us, length us, event | category | flops | bytes accessed | tf_op | source)
XLA Modules:
  0.0 211.8 jit_solution(4728929369551682572)
XLA Ops:
  3.2 2.4 %collective-permute-start.2 = (f32[22,128]{1,0:T(8,128)S(1)}, f32[22,128]{1,0:T(8,128)S(1)}, u32[]{:S(2)}, u32[]{:S(2)}) collective-permute-start(f32[22,128]{1,0:T(8,128)S(1)} %pad_maximum_fusion.4), channel_id=1, source_target_pairs={{8,0},{16,8},{24,16},{9,1},{17,9},{25,17},{10,2},{18,10},{26,18},{... | collective-permute-start | bytes 33800 | tf_op jit(solution)/shard_map/ppermute | solution.py:203
  5.9 4.3 %collective-permute-start.1 = (f32[22,128]{1,0:T(8,128)S(1)}, f32[22,128]{1,0:T(8,128)S(1)}, u32[]{:S(2)}, u32[]{:S(2)}) collective-permute-start(f32[22,128]{1,0:T(8,128)S(1)} %pad_maximum_fusion.1), channel_id=1, source_target_pairs={{0,8},{8,16},{16,24},{1,9},{9,17},{17,25},{2,10},{10,18},{18,26},{... | collective-permute-start | bytes 33800 | tf_op jit(solution)/shard_map/ppermute | solution.py:202
  11.4 2.0 convert_reduce_fusion
  17.9 1.9 collective-permute-start.4
  21.8 2.4 %collective-permute-start.3 = (f32[22,132]{1,0:T(8,128)S(1)}, f32[22,132]{1,0:T(8,128)S(1)}, u32[]{:S(2)}, u32[]{:S(2)}) collective-permute-start(f32[22,132]{1,0:T(8,128)S(1)} %concatenate.66.to_right), channel_id=1, source_target_pairs={{0,1},{1,2},{2,3},{3,4},{4,5},{5,6},{6,7},{8,9},{9,10},{10,11},{11... | collective-permute-start | bytes 34856 | tf_op jit(solution)/shard_map/ppermute | solution.py:253
  24.3 2.6 %collective-permute-done.3.lefts.refs_6_ = f32[22,132]{1,0:T(8,128)S(1)} collective-permute-done((f32[22,132]{1,0:T(8,128)S(1)}, f32[22,132]{1,0:T(8,128)S(1)}, u32[]{:S(2)}, u32[]{:S(2)}) %collective-permute-start.3) | collective-permute-done | bytes 11648 | tf_op jit(solution)/shard_map/ppermute | solution.py:253
  27.7 2.3 %copy-done = bf16[4,9,256,256]{3,2,1,0:T(8,128)(2,1)S(1)} copy-done((bf16[4,9,256,256]{3,2,1,0:T(8,128)(2,1)S(1)}, bf16[4,9,256,256]{3,2,1,0:T(8,128)(2,1)}, u32[]{:S(2)}) %copy-start) | copy-done | bytes 4718616
  34.9 4.4 %sky.1 = (bf16[512,512]{1,0:T(8,128)(2,1)}, f32[8,128]{1,0:T(8,128)S(1)}) custom-call(f32[132,132]{1,0:T(8,128)S(1)} %pad_maximum_fusion.wide, f32[22,128]{1,0:T(8,128)S(1)} %copy-done.14, f32[22,128]{1,0:T(8,128)S(1)} %collective-permute-done.2.below.refs_5_, f32[22,132]{1,0:T(8,128)S(1)} %copy-done.20, f32[22,132]{1,0:T(8,128)S(1)} %copy-done.17, ...), custom_call_target="tpu_custom_call" | custom-call | tf_op jit(solution)/shard_map/sky/pallas_call | solution.py:266
  39.9 3.0 %collective-permute-start.6 = (bf16[512,512]{1,0:T(8,128)(2,1)}, bf16[512,512]{1,0:T(8,128)(2,1)}, u32[]{:S(2)}, u32[]{:S(2)}) collective-permute-start(bf16[512,512]{1,0:T(8,128)(2,1)} %get-tuple-element.28.refs_0_), channel_id=1, source_target_pairs={{0,4},{1,5},{2,6},{3,7},{4,0},{5,1},{6,2},{7,3},{8,12},{9,13},{10,... | collective-permute-start | bytes 1572872 | tf_op jit(solution)/shard_map/ppermute | solution.py:609
  42.9 2.5 %collective-permute-start.5 = (bf16[512,512]{1,0:T(8,128)(2,1)}, bf16[512,512]{1,0:T(8,128)(2,1)}, u32[]{:S(2)}, u32[]{:S(2)}) collective-permute-start(bf16[512,512]{1,0:T(8,128)(2,1)} %get-tuple-element.28.refs_0_), channel_id=1, source_target_pairs={{0,2},{1,3},{2,4},{3,5},{4,6},{5,7},{6,0},{7,1},{8,10},{9,11},{10,... | collective-permute-start | bytes 1572872 | tf_op jit(solution)/shard_map/ppermute | solution.py:609
  45.4 32.1 %collective-permute-done.7.refs_3_ = bf16[512,512]{1,0:T(8,128)(2,1)} collective-permute-done((bf16[512,512]{1,0:T(8,128)(2,1)}, bf16[512,512]{1,0:T(8,128)(2,1)}, u32[]{:S(2)}, u32[]{:S(2)}) %collective-permute-start.7) | collective-permute-done | bytes 524320 | tf_op jit(solution)/shard_map/ppermute | solution.py:609
  78.0 9.2 %collective-permute-done.5.refs_1_ = bf16[512,512]{1,0:T(8,128)(2,1)} collective-permute-done((bf16[512,512]{1,0:T(8,128)(2,1)}, bf16[512,512]{1,0:T(8,128)(2,1)}, u32[]{:S(2)}, u32[]{:S(2)}) %collective-permute-start.5) | collective-permute-done | bytes 524320 | tf_op jit(solution)/shard_map/ppermute | solution.py:609
  87.9 1.5 collective-permute-done.9.refs_5_
  89.5 2.2 %copy-done.2 = bf16[1,2,1024,1024]{3,2,1,0:T(8,128)(2,1)S(1)} copy-done((bf16[1,2,1024,1024]{3,2,1,0:T(8,128)(2,1)S(1)}, bf16[1,2,1024,1024]{3,2,1,0:T(8,128)(2,1)}, u32[]{:S(2)}) %copy-start.2) | copy-done | bytes 4194328
  91.7 1.6 copy-done.5
  93.9 7.4 %facet.3 = (bf16[512,512]{1,0:T(8,128)(2,1)}, f32[8,128]{1,0:T(8,128)S(1)}) custom-call(s32[2,2]{1,0:T(2,128)S(1)} %fusion.5.sel, f32[2,2]{1,0:T(2,128)S(1)} %bitcast.66, s32[2]{0:T(128)S(1)} %bitcast.69, bf16[512,512]{1,0:T(8,128)(2,1)} %get-tuple-element.28.refs_0_, bf16[512,512]{1,0:T(8,128)(2,1)} %collective-permute-done.5.refs_1_, ...), custom_call_target="tpu_custom_call" | custom-call | tf_op jit(solution)/shard_map/facet/pallas_call | solution.py:563
  101.5 7.6 %facet.2 = (bf16[512,512]{1,0:T(8,128)(2,1)}, f32[8,128]{1,0:T(8,128)S(1)}) custom-call(s32[2,2]{1,0:T(2,128)S(1)} %fusion.5.sel, f32[2,2]{1,0:T(2,128)S(1)} %bitcast.67, s32[2]{0:T(128)S(1)} %bitcast.70, bf16[512,512]{1,0:T(8,128)(2,1)} %get-tuple-element.28.refs_0_, bf16[512,512]{1,0:T(8,128)(2,1)} %collective-permute-done.5.refs_1_, ...), custom_call_target="tpu_custom_call" | custom-call | tf_op jit(solution)/shard_map/facet/pallas_call | solution.py:563
  116.2 3.1 %mixed.1 = (bf16[544,512]{1,0:T(8,128)(2,1)S(1)}, bf16[544,512]{1,0:T(8,128)(2,1)S(1)}, bf16[544,512]{1,0:T(8,128)(2,1)S(1)}, bf16[544,512]{1,0:T(8,128)(2,1)S(1)}) custom-call(f32[4,4]{1,0:T(4,128)S(1)} %gather_fusion, bf16[512,512]{1,0:T(8,128)(2,1)} %get-tuple-element.29.refs_0_, bf16[512,512]{1,0:T(8,128)(2,1)} %get-tuple-element.30.refs_1_, ...), custom_call_target="tpu_custom_call" | custom-call | tf_op jit(solution)/shard_map/mixed/pallas_call | solution.py:597
  119.3 2.4 %collective-permute-start.14 = (bf16[544,512]{1,0:T(8,128)(2,1)S(1)}, bf16[544,512]{1,0:T(8,128)(2,1)S(1)}, u32[]{:S(2)}, u32[]{:S(2)}) collective-permute-start(bf16[544,512]{1,0:T(8,128)(2,1)S(1)} %get-tuple-element.35), channel_id=1, source_target_pairs={{0,2},{1,3},{2,4},{3,5},{4,6},{5,7},{6,0},{7,1},{8,10},{9,11},{10,... | collective-permute-start | bytes 1671176 | tf_op jit(solution)/shard_map/ppermute | solution.py:609
  121.7 2.1 collective-permute-start.15
  123.8 34.7 %collective-permute-done.14.refs_1_ = bf16[544,512]{1,0:T(8,128)(2,1)S(1)} collective-permute-done((bf16[544,512]{1,0:T(8,128)(2,1)S(1)}, bf16[544,512]{1,0:T(8,128)(2,1)S(1)}, u32[]{:S(2)}, u32[]{:S(2)}) %collective-permute-start.14) | collective-permute-done | bytes 557088 | tf_op jit(solution)/shard_map/ppermute | solution.py:609
  158.5 11.1 %collective-permute-done.15.refs_2_ = bf16[544,512]{1,0:T(8,128)(2,1)S(1)} collective-permute-done((bf16[544,512]{1,0:T(8,128)(2,1)S(1)}, bf16[544,512]{1,0:T(8,128)(2,1)S(1)}, u32[]{:S(2)}, u32[]{:S(2)}) %collective-permute-start.15) | collective-permute-done | bytes 557088 | tf_op jit(solution)/shard_map/ppermute | solution.py:609
  169.7 2.0 collective-permute-done.16.refs_3_
  171.7 2.3 %copy-done.1 = bf16[4,9,256,256]{3,2,1,0:T(8,128)(2,1)S(1)} copy-done((bf16[4,9,256,256]{3,2,1,0:T(8,128)(2,1)S(1)}, bf16[4,9,256,256]{3,2,1,0:T(8,128)(2,1)}, u32[]{:S(2)}) %copy-start.1) | copy-done | bytes 4718616
  176.2 4.0 %adjoint.1 = (f32[512,512]{1,0:T(8,128)}, f32[256,256]{1,0:T(8,128)S(1)}, f32[128,128]{1,0:T(8,128)S(1)}, f32[8,384]{1,0:T(8,128)S(1)}, f32[8,384]{1,0:T(8,128)S...) custom-call(bf16[544,512]{1,0:T(8,128)(2,1)S(1)} %get-tuple-element.34.refs_0_, ...), custom_call_target="tpu_custom_call" | custom-call | tf_op jit(solution)/shard_map/adjoint/pallas_call | solution.py:463
  180.2 1.9 collective-permute-start.17
  182.2 3.6 %collective-permute-start.18 = (f32[8,384]{1,0:T(8,128)S(1)}, f32[8,384]{1,0:T(8,128)S(1)}, u32[]{:S(2)}, u32[]{:S(2)}) collective-permute-start(f32[8,384]{1,0:T(8,128)S(1)} %get-tuple-element.41), channel_id=1, source_target_pairs={{1,0},{2,1},{3,2},{4,3},{5,4},{6,5},{7,6},{9,8},{10,9},{11,10},{12... | collective-permute-start | bytes 36872 | tf_op jit(solution)/shard_map/ppermute | solution.py:493
  190.3 2.5 %collective-permute-start.19 = (f32[8,256]{1,0:T(8,128)S(1)}, f32[8,256]{1,0:T(8,128)S(1)}, u32[]{:S(2)}, u32[]{:S(2)}) collective-permute-start(f32[8,256]{1,0:T(8,128)S(1)} %fusion.1), channel_id=1, source_target_pairs={{0,8},{8,16},{16,24},{1,9},{9,17},{17,25},{2,10},{10,18},{18,26},{... | collective-permute-start | bytes 24584 | tf_op jit(solution)/shard_map/ppermute | solution.py:507
  194.2 3.3 %collective-permute-start.20 = (f32[8,256]{1,0:T(8,128)S(1)}, f32[8,256]{1,0:T(8,128)S(1)}, u32[]{:S(2)}, u32[]{:S(2)}) collective-permute-start(f32[8,256]{1,0:T(8,128)S(1)} %fusion), channel_id=1, source_target_pairs={{8,0},{16,8},{24,16},{9,1},{17,9},{25,17},{10,2},{18,10},{26,18},{... | collective-permute-start | bytes 24584 | tf_op jit(solution)/shard_map/ppermute | solution.py:506
  202.2 2.3 %collective-permute-done.22 = f32[1]{0:T(128)} collective-permute-done((f32[1]{0:T(128)}, f32[1]{0:T(128)}, u32[]{:S(2)}, u32[]{:S(2)}) %collective-permute-start.22) | collective-permute-done | bytes 36 | tf_op jit(solution)/shard_map/ppermute | solution.py:662
  205.2 1.4 collective-permute-start.23
  206.6 2.3 %collective-permute-done.23 = f32[1]{0:T(128)} collective-permute-done((f32[1]{0:T(128)}, f32[1]{0:T(128)}, u32[]{:S(2)}, u32[]{:S(2)}) %collective-permute-start.23) | collective-permute-done | bytes 36 | tf_op jit(solution)/shard_map/ppermute | solution.py:662
  (172 shorter events, 38.2 us)
Async XLA Ops:
  0.6 12.8 %copy-start.9 = (f32[128,128]{1,0:T(8,128)S(1)}, f32[128,128]{1,0:T(8,128)}, u32[]{:S(2)}) copy-start(f32[128,128]{1,0:T(8,128)} %xi_coarse.1) | copy-start | bytes 196612
  3.2 10.9 %collective-permute-start.2 = (f32[22,128]{1,0:T(8,128)S(1)}, f32[22,128]{1,0:T(8,128)S(1)}, u32[]{:S(2)}, u32[]{:S(2)}) collective-permute-start(f32[22,128]{1,0:T(8,128)S(1)} %pad_maximum_fusion.4), channel_id=1, source_target_pairs={{8,0},{16,8},{24,16},{9,1},{17,9},{25,17},{10,2},{18,10},{26,18},{... | collective-permute-start | bytes 33800 | tf_op jit(solution)/shard_map/ppermute | solution.py:203
  5.9 9.9 %collective-permute-start.1 = (f32[22,128]{1,0:T(8,128)S(1)}, f32[22,128]{1,0:T(8,128)S(1)}, u32[]{:S(2)}, u32[]{:S(2)}) collective-permute-start(f32[22,128]{1,0:T(8,128)S(1)} %pad_maximum_fusion.1), channel_id=1, source_target_pairs={{0,8},{8,16},{16,24},{1,9},{9,17},{17,25},{2,10},{10,18},{18,26},{... | collective-permute-start | bytes 33800 | tf_op jit(solution)/shard_map/ppermute | solution.py:202
  11.4 16.2 %copy-start.3 = (bf16[4,9,128,128]{3,2,1,0:T(8,128)(2,1)S(1)}, bf16[4,9,128,128]{3,2,1,0:T(8,128)(2,1)}, u32[]{:S(2)}) copy-start(bf16[4,9,128,128]{3,2,1,0:T(8,128)(2,1)} %refs_8_.5) | copy-start | bytes 3538948
  11.4 16.2 %copy-start.8 = (f32[256,256]{1,0:T(8,128)S(1)}, f32[256,256]{1,0:T(8,128)}, u32[]{:S(2)}) copy-start(f32[256,256]{1,0:T(8,128)} %xi_middle.3) | copy-start | bytes 786436
  15.8 11.2 %copy-start.13 = (f32[22,128]{1,0:T(8,128)}, f32[22,128]{1,0:T(8,128)S(1)}, u32[]{:S(2)}) copy-start(f32[22,128]{1,0:T(8,128)S(1)} %collective-permute-done.1.above.refs_4_) | copy-start | bytes 33796
  17.9 6.3 %collective-permute-start.4 = (f32[22,132]{1,0:T(8,128)S(1)}, f32[22,132]{1,0:T(8,128)S(1)}, u32[]{:S(2)}, u32[]{:S(2)}) collective-permute-start(f32[22,132]{1,0:T(8,128)S(1)} %concatenate.72.to_left), channel_id=1, source_target_pairs={{1,0},{2,1},{3,2},{4,3},{5,4},{6,5},{7,6},{9,8},{10,9},{11,10},{12... | collective-permute-start | bytes 34856 | tf_op jit(solution)/shard_map/ppermute | solution.py:254
  21.8 5.1 %collective-permute-start.3 = (f32[22,132]{1,0:T(8,128)S(1)}, f32[22,132]{1,0:T(8,128)S(1)}, u32[]{:S(2)}, u32[]{:S(2)}) collective-permute-start(f32[22,132]{1,0:T(8,128)S(1)} %concatenate.66.to_right), channel_id=1, source_target_pairs={{0,1},{1,2},{2,3},{3,4},{4,5},{5,6},{6,7},{8,9},{9,10},{10,11},{11... | collective-permute-start | bytes 34856 | tf_op jit(solution)/shard_map/ppermute | solution.py:253
  34.9 54.6 %copy-start.4 = (bf16[1,2,1024,512]{3,2,1,0:T(8,128)(2,1)S(1)}, bf16[1,2,1024,512]{3,2,1,0:T(8,128)(2,1)}, u32[]{:S(2)}) copy-start(bf16[1,2,1024,512]{3,2,1,0:T(8,128)(2,1)} %refs_8_.4) | copy-start | bytes 6291460
  34.9 54.6 %copy-start.26 = (f32[1,2,2]{2,1,0:T(2,128)S(1)}, f32[1,2,2]{2,1,0:T(2,128)}, u32[]{:S(2)}) copy-start(f32[1,2,2]{2,1,0:T(2,128)} %param.20) | copy-start | bytes 52
  39.9 37.6 %collective-permute-start.7 = (bf16[512,512]{1,0:T(8,128)(2,1)}, bf16[512,512]{1,0:T(8,128)(2,1)}, u32[]{:S(2)}, u32[]{:S(2)}) collective-permute-start(bf16[512,512]{1,0:T(8,128)(2,1)} %get-tuple-element.28.refs_0_), channel_id=1, source_target_pairs={{0,6},{1,7},{2,0},{3,1},{4,2},{5,3},{6,4},{7,5},{8,14},{9,15},{10,... | collective-permute-start | bytes 1572872 | tf_op jit(solution)/shard_map/ppermute | solution.py:609
  39.9 37.7 %collective-permute-start.6 = (bf16[512,512]{1,0:T(8,128)(2,1)}, bf16[512,512]{1,0:T(8,128)(2,1)}, u32[]{:S(2)}, u32[]{:S(2)}) collective-permute-start(bf16[512,512]{1,0:T(8,128)(2,1)} %get-tuple-element.28.refs_0_), channel_id=1, source_target_pairs={{0,4},{1,5},{2,6},{3,7},{4,0},{5,1},{6,2},{7,3},{8,12},{9,13},{10,... | collective-permute-start | bytes 1572872 | tf_op jit(solution)/shard_map/ppermute | solution.py:609
  42.9 44.3 %collective-permute-start.5 = (bf16[512,512]{1,0:T(8,128)(2,1)}, bf16[512,512]{1,0:T(8,128)(2,1)}, u32[]{:S(2)}, u32[]{:S(2)}) collective-permute-start(bf16[512,512]{1,0:T(8,128)(2,1)} %get-tuple-element.28.refs_0_), channel_id=1, source_target_pairs={{0,2},{1,3},{2,4},{3,5},{4,6},{5,7},{6,0},{7,1},{8,10},{9,11},{10,... | collective-permute-start | bytes 1572872 | tf_op jit(solution)/shard_map/ppermute | solution.py:609
  45.4 42.5 %collective-permute-start.8 = (bf16[512,512]{1,0:T(8,128)(2,1)}, bf16[512,512]{1,0:T(8,128)(2,1)}, u32[]{:S(2)}, u32[]{:S(2)}) collective-permute-start(bf16[512,512]{1,0:T(8,128)(2,1)} %get-tuple-element.28.refs_0_), channel_id=1, source_target_pairs={{0,1},{1,0},{2,3},{3,2},{4,5},{5,4},{6,7},{7,6},{8,9},{9,8},{10,11... | collective-permute-start | bytes 1572872 | tf_op jit(solution)/shard_map/ppermute | solution.py:613
  77.5 10.4 %collective-permute-start.11 = (bf16[512,512]{1,0:T(8,128)(2,1)}, bf16[512,512]{1,0:T(8,128)(2,1)}, u32[]{:S(2)}, u32[]{:S(2)}) collective-permute-start(bf16[512,512]{1,0:T(8,128)(2,1)} %collective-permute-done.7.refs_3_), channel_id=1, source_target_pairs={{0,1},{1,0},{2,3},{3,2},{4,5},{5,4},{6,7},{7,6},{8,9},{9,8},{10,11... | collective-permute-start | bytes 1572872 | tf_op jit(solution)/shard_map/ppermute | solution.py:613
  77.5 10.4 %collective-permute-start.10 = (bf16[512,512]{1,0:T(8,128)(2,1)}, bf16[512,512]{1,0:T(8,128)(2,1)}, u32[]{:S(2)}, u32[]{:S(2)}) collective-permute-start(bf16[512,512]{1,0:T(8,128)(2,1)} %collective-permute-done.6.refs_2_), channel_id=1, source_target_pairs={{0,1},{1,0},{2,3},{3,2},{4,5},{5,4},{6,7},{7,6},{8,9},{9,8},{10,11... | collective-permute-start | bytes 1572872 | tf_op jit(solution)/shard_map/ppermute | solution.py:613
  87.2 2.3 %collective-permute-start.9 = (bf16[512,512]{1,0:T(8,128)(2,1)}, bf16[512,512]{1,0:T(8,128)(2,1)}, u32[]{:S(2)}, u32[]{:S(2)}) collective-permute-start(bf16[512,512]{1,0:T(8,128)(2,1)} %collective-permute-done.5.refs_1_), channel_id=1, source_target_pairs={{0,1},{1,0},{2,3},{3,2},{4,5},{5,4},{6,7},{7,6},{8,9},{9,8},{10,11... | collective-permute-start | bytes 1572872 | tf_op jit(solution)/shard_map/ppermute | solution.py:613
  101.3 11.0 %collective-permute-start.13 = (bf16[512,512]{1,0:T(8,128)(2,1)}, bf16[512,512]{1,0:T(8,128)(2,1)}, u32[]{:S(2)}, u32[]{:S(2)}) collective-permute-start(bf16[512,512]{1,0:T(8,128)(2,1)} %get-tuple-element.30.refs_1_), channel_id=1, source_target_pairs={{0,1},{1,0},{2,3},{3,2},{4,5},{5,4},{6,7},{7,6},{8,9},{9,8},{10,11... | collective-permute-start | bytes 1572872 | tf_op jit(solution)/shard_map/ppermute | solution.py:613
  109.8 61.9 %copy-start.7 = (f32[512,512]{1,0:T(8,128)S(1)}, f32[512,512]{1,0:T(8,128)}, u32[]{:S(2)}) copy-start(f32[512,512]{1,0:T(8,128)} %refs_10_.5) | copy-start | bytes 3145732
  109.8 2.6 %collective-permute-start.12 = (bf16[512,512]{1,0:T(8,128)(2,1)}, bf16[512,512]{1,0:T(8,128)(2,1)S(1)}, u32[]{:S(2)}, u32[]{:S(2)}) collective-permute-start(bf16[512,512]{1,0:T(8,128)(2,1)} %get-tuple-element.29.refs_0_), channel_id=1, source_target_pairs={{0,1},{1,0},{2,3},{3,2},{4,5},{5,4},{6,7},{7,6},{8,9},{9,8},{10,11... | collective-permute-start | bytes 1572872 | tf_op jit(solution)/shard_map/ppermute | solution.py:613
  110.3 1.4 collective-permute-start
  119.3 39.3 %collective-permute-start.14 = (bf16[544,512]{1,0:T(8,128)(2,1)S(1)}, bf16[544,512]{1,0:T(8,128)(2,1)S(1)}, u32[]{:S(2)}, u32[]{:S(2)}) collective-permute-start(bf16[544,512]{1,0:T(8,128)(2,1)S(1)} %get-tuple-element.35), channel_id=1, source_target_pairs={{0,2},{1,3},{2,4},{3,5},{4,6},{5,7},{6,0},{7,1},{8,10},{9,11},{10,... | collective-permute-start | bytes 1671176 | tf_op jit(solution)/shard_map/ppermute | solution.py:609
  121.7 48.0 %collective-permute-start.15 = (bf16[544,512]{1,0:T(8,128)(2,1)S(1)}, bf16[544,512]{1,0:T(8,128)(2,1)S(1)}, u32[]{:S(2)}, u32[]{:S(2)}) collective-permute-start(bf16[544,512]{1,0:T(8,128)(2,1)S(1)} %get-tuple-element.36), channel_id=1, source_target_pairs={{0,4},{1,5},{2,6},{3,7},{4,0},{5,1},{6,2},{7,3},{8,12},{9,13},{10,... | collective-permute-start | bytes 1671176 | tf_op jit(solution)/shard_map/ppermute | solution.py:609
  123.8 47.9 %collective-permute-start.16 = (bf16[544,512]{1,0:T(8,128)(2,1)S(1)}, bf16[544,512]{1,0:T(8,128)(2,1)S(1)}, u32[]{:S(2)}, u32[]{:S(2)}) collective-permute-start(bf16[544,512]{1,0:T(8,128)(2,1)S(1)} %get-tuple-element.37), channel_id=1, source_target_pairs={{0,6},{1,7},{2,0},{3,1},{4,2},{5,3},{6,4},{7,5},{8,14},{9,15},{10,... | collective-permute-start | bytes 1671176 | tf_op jit(solution)/shard_map/ppermute | solution.py:609
  176.2 33.4 %copy-start.10 = (f32[128,128]{1,0:T(8,128)S(1)}, f32[128,128]{1,0:T(8,128)}, u32[]{:S(2)}) copy-start(f32[128,128]{1,0:T(8,128)} %xi_coarse.1) | copy-start | bytes 196612
  180.2 5.6 %collective-permute-start.17 = (f32[8,384]{1,0:T(8,128)S(1)}, f32[8,384]{1,0:T(8,128)S(1)}, u32[]{:S(2)}, u32[]{:S(2)}) collective-permute-start(f32[8,384]{1,0:T(8,128)S(1)} %get-tuple-element.40), channel_id=1, source_target_pairs={{0,1},{1,2},{2,3},{3,4},{4,5},{5,6},{6,7},{8,9},{9,10},{10,11},{11... | collective-permute-start | bytes 36872 | tf_op jit(solution)/shard_map/ppermute | solution.py:492
  182.2 5.0 %collective-permute-start.18 = (f32[8,384]{1,0:T(8,128)S(1)}, f32[8,384]{1,0:T(8,128)S(1)}, u32[]{:S(2)}, u32[]{:S(2)}) collective-permute-start(f32[8,384]{1,0:T(8,128)S(1)} %get-tuple-element.41), channel_id=1, source_target_pairs={{1,0},{2,1},{3,2},{4,3},{5,4},{6,5},{7,6},{9,8},{10,9},{11,10},{12... | collective-permute-start | bytes 36872 | tf_op jit(solution)/shard_map/ppermute | solution.py:493
  190.3 19.3 %collective-permute-start.19 = (f32[8,256]{1,0:T(8,128)S(1)}, f32[8,256]{1,0:T(8,128)S(1)}, u32[]{:S(2)}, u32[]{:S(2)}) collective-permute-start(f32[8,256]{1,0:T(8,128)S(1)} %fusion.1), channel_id=1, source_target_pairs={{0,8},{8,16},{16,24},{1,9},{9,17},{17,25},{2,10},{10,18},{18,26},{... | collective-permute-start | bytes 24584 | tf_op jit(solution)/shard_map/ppermute | solution.py:507
  194.2 15.3 %collective-permute-start.20 = (f32[8,256]{1,0:T(8,128)S(1)}, f32[8,256]{1,0:T(8,128)S(1)}, u32[]{:S(2)}, u32[]{:S(2)}) collective-permute-start(f32[8,256]{1,0:T(8,128)S(1)} %fusion), channel_id=1, source_target_pairs={{8,0},{16,8},{24,16},{9,1},{17,9},{25,17},{10,2},{18,10},{26,18},{... | collective-permute-start | bytes 24584 | tf_op jit(solution)/shard_map/ppermute | solution.py:506
  198.2 1.4 collective-permute-start.21
  200.9 3.7 %collective-permute-start.22 = (f32[1]{0:T(128)}, f32[1]{0:T(128)}, u32[]{:S(2)}, u32[]{:S(2)}) collective-permute-start(f32[1]{0:T(128)} %add.132), channel_id=1, source_target_pairs={{0,8},{8,0},{16,24},{24,16},{1,9},{9,1},{17,25},{25,17},{2,10},{10... | collective-permute-start | bytes 20 | tf_op jit(solution)/shard_map/ppermute | solution.py:662
  205.2 3.7 %collective-permute-start.23 = (f32[1]{0:T(128)}, f32[1]{0:T(128)}, u32[]{:S(2)}, u32[]{:S(2)}) collective-permute-start(f32[1]{0:T(128)} %add.133), channel_id=1, source_target_pairs={{0,16},{8,24},{16,0},{24,8},{1,17},{9,25},{17,1},{25,9},{2,18},{10... | collective-permute-start | bytes 20 | tf_op jit(solution)/shard_map/ppermute | solution.py:662
  (27 other events, 55.8 us)

commit v5 on v4

v5 whole, which is shorter than its diff:
```python
import functools

import jax
import jax.numpy as jnp
from jax import lax
from jax.experimental import pallas as pl
from jax.experimental.pallas import tpu as pltpu
from jax.sharding import PartitionSpec as P

inv_noise = 0.125
vmem = 32 * 1024 * 1024
f32 = jnp.float32
bf16 = jnp.bfloat16


def halves(x):
    high = x.astype(bf16)
    return high, (x - high.astype(f32)).astype(bf16)


def interleaver(cols, transposed):
    shape = (2 * cols, 2 * cols)
    split = lax.broadcasted_iota(jnp.int32, shape, 1 if transposed else 0)
    whole = lax.broadcasted_iota(jnp.int32, shape, 0 if transposed else 1)
    place = jnp.where(split >= cols, 2 * (split - cols) + 1, 2 * split)
    return (place == whole).astype(f32).astype(bf16)


def folded(x):
    rows, cols = x.shape
    x = jnp.sum(x.reshape(rows // 8, 8, cols), axis=0)
    return sum(x[:, i : i + 128] for i in range(0, cols, 128))


def row_of(ref, i):
    return ref[i : i + 1, :]


def dot_t(x, y, dims):
    return lax.dot_general(x, y, (dims, ((), ())), preferred_element_type=f32)


def moved(x, perm):
    high, low = halves(x)
    return jnp.dot(high, perm, preferred_element_type=f32) + jnp.dot(
        low, perm, preferred_element_type=f32
    )


def ends_placed(first, last, cols):
    rows = jnp.concatenate([first, first, last, last, jnp.zeros((4, first.shape[1]), f32)])
    high = rows.astype(bf16).astype(f32)
    index = lax.broadcasted_iota(jnp.int32, rows.shape, 0)
    rows = jnp.where(index % 2 == 0, high, rows - high).astype(bf16)
    shape = (8, cols)
    index = lax.broadcasted_iota(jnp.int32, shape, 0)
    lane = lax.broadcasted_iota(jnp.int32, shape, 1)
    place = ((index < 2) & (lane == 0)) | ((index >= 2) & (index < 4) & (lane == cols - 1))
    return dot_t(rows, place.astype(f32).astype(bf16), ((0,), (0,)))


def weighed(win, coef_ref, perm, lhs, mix, rows, cols):
    def part(i, carry):
        r0 = pl.multiple_of(i * 16, 16)
        total = [jnp.zeros((16, cols), f32) for _ in range(4)]
        for near in range(9):
            w = win[near, pl.ds(r0, 16), :]
            for child in range(4):
                total[child] += coef_ref[child, near, pl.ds(r0, 16), :].astype(f32) * w
        for child in range(4):
            a, b = child // 2, child % 2
            high, low = halves(total[child])
            lhs[pl.ds(2 * a * rows + r0, 16), b * cols : (b + 1) * cols] = high
            lhs[pl.ds((2 * a + 1) * rows + r0, 16), b * cols : (b + 1) * cols] = low
        return carry

    lax.fori_loop(0, rows // 16, part, 0)
    field = jnp.dot(lhs[...], perm[...], preferred_element_type=f32)
    for tile in range(2 * cols // 128):
        lanes = slice(tile * 128, (tile + 1) * 128)
        for a in range(2):
            mix[tile, pl.ds(a, rows, stride=2), :] = (
                field[2 * a * rows : (2 * a + 1) * rows, lanes]
                + field[(2 * a + 1) * rows : (2 * a + 2) * rows, lanes]
            )


def fetched(pairs, sems):
    copies = [pltpu.make_async_copy(src, dst, sems.at[i]) for i, (src, dst) in enumerate(pairs)]
    for copy in copies:
        copy.start()
    return copies


def columns_beside(field, left, right):
    rows, cols = field.shape[1:]
    placed = ends_placed(left, right, cols)
    lane = lax.broadcasted_iota(jnp.int32, (rows, cols), 1)
    here = field[1]
    field[0] = jnp.where(lane == 0, placed, pltpu.roll(here, 1, 1))
    field[2] = jnp.where(lane == cols - 1, placed, pltpu.roll(here, cols - 1, 1))


def sky_kernel(*refs):
    sources, (sky_ref, sq_ref), held, rest = refs[:11], refs[11:13], refs[13:24], refs[24:]
    win, perm, lhs, mix, near_coarse, shifted, fine_win, fine_perm, fine_lhs, fine_mix, sems = rest
    copies = fetched(zip(sources, held), sems)
    xi_coarse, above, below, lefts, rights, to_left, to_right = held[:7]
    coef_middle, xi_middle, coef_fine, xi_fine = held[7:]
    rows, cols = win.shape[1:]
    perm[...] = interleaver(cols, False)
    fine_perm[...] = interleaver(2 * cols, False)
    near_coarse[...] = jnp.zeros_like(near_coarse)
    for copy in copies[:8]:
        copy.wait()
    near_coarse[1, 6:8] = above[18:20]
    near_coarse[1, 8 : 8 + rows] = xi_coarse[...]
    near_coarse[1, 8 + rows : 10 + rows] = below[18:20]
    pad = jnp.zeros((1, 6), f32)
    beside = [
        jnp.concatenate([pad, row_of(x, i)[:, : rows + 4], pad], axis=1)
        for x, i in ((lefts, 19), (rights, 18))
    ]
    columns_beside(near_coarse, *beside)
    for near in range(9):
        r, c = near // 3, near % 3
        win[near] = near_coarse[c, 7 + r : 7 + r + rows]
    weighed(win, coef_middle, perm, lhs, mix, rows, cols)

    def across(message, top):
        out = []
        for b in range(2):
            line = row_of(message, 20 + b)
            for near in range(9):
                r, c = near // 3, near % 3
                line += row_of(message, 9 * b + near) * near_coarse[c, top + r : top + r + 1]
            out.append(line)
        return jnp.concatenate(out, axis=1)

    def along(message, fields):
        out = []
        for a in range(2):
            line = row_of(message, 20 + a)[:, 1 : rows + 3]
            for near in range(9):
                r, c = near // 3, near % 3
                line += row_of(message, 9 * a + near)[:, 1 : rows + 3] * fields[c][:, r : r + rows + 2]
            out.append(line)
        inner = jnp.concatenate([line[:, 1 : rows + 1] for line in out], axis=1)
        return inner, out[1][:, :1], out[0][:, rows + 1 :]

    top, bottom = across(above, 6), across(below, rows + 7)
    left, top_left, bottom_left = along(
        lefts, [row_of(lefts, 18), row_of(lefts, 19), row_of(to_left, 18)]
    )
    right, top_right, bottom_right = along(
        rights, [row_of(to_right, 19), row_of(rights, 18), row_of(rights, 19)]
    )
    lines = jnp.concatenate([top, bottom, left, right, jnp.zeros((4, 2 * cols), f32)])
    lines = moved(lines, perm[...])
    copies[8].wait()
    xi = xi_middle[...]
    last = 8 + 2 * rows
    shifted[1] = jnp.zeros(shifted.shape[1:], f32)
    for tile in range(2 * cols // 128):
        lanes = slice(tile * 128, (tile + 1) * 128)
        shifted[1, 8:last, lanes] = mix[tile] + xi[:, lanes]
    shifted[1, 7:8, :] = lines[0:1]
    shifted[1, last : last + 1, :] = lines[1:2]
    pad = jnp.zeros((1, 7), f32)
    beside = [
        jnp.concatenate([pad, first, line, final, pad], axis=1)
        for first, line, final in (
            (top_left, lines[2:3], bottom_left),
            (top_right, lines[3:4], bottom_right),
        )
    ]
    columns_beside(shifted, *beside)
    for near in range(9):
        r, c = near // 3, near % 3
        fine_win[near] = shifted[c, 7 + r : 7 + r + 2 * rows, :]
    copies[9].wait()
    weighed(fine_win, coef_fine, fine_perm, fine_lhs, fine_mix, 2 * rows, 2 * cols)
    copies[10].wait()
    for tile in range(4 * cols // 128):
        lanes = slice(tile * 128, (tile + 1) * 128)
        sky_ref[:, lanes] = (fine_mix[tile] + xi_fine[:, lanes]).astype(bf16)
    sq_ref[...] = (
        folded(win[4] * win[4]) + folded(xi * xi) + folded(xi_fine[...] * xi_fine[...])
    )


def sides_kernel(above, below, left_side, right_side, to_left, to_right):
    rows, cols = left_side.shape[1], above.shape[1]
    for out, side, b, col, first in (
        (to_left, left_side, 0, 0, 0),
        (to_right, right_side, 1, cols - 1, cols - 2),
    ):
        out[...] = jnp.zeros_like(out)
        out[:, 2 : rows + 2] = side[...]
        out[9:18, 1:2] = above[9 * b : 9 * b + 9, col : col + 1]
        out[21:22, 1:2] = above[20 + b : 21 + b, col : col + 1]
        out[0:9, rows + 2 : rows + 3] = below[9 * b : 9 * b + 9, col : col + 1]
        out[20:21, rows + 2 : rows + 3] = below[20 + b : 21 + b, col : col + 1]
        for k in range(2):
            at = slice(first + k, first + k + 1)
            for i in range(2):
                out[18 + k : 19 + k, i : i + 1] = above[18 + i : 19 + i, at]
                lane = rows + 2 + i
                out[18 + k : 19 + k, lane : lane + 1] = below[18 + i : 19 + i, at]


def neighbours(axis):
    size = lax.axis_size(axis)
    ahead = [(i, i + 1) for i in range(size - 1)]
    return ahead, [(j, i) for i, j in ahead]


def halo(xi_coarse, xi_middle, coef_middle, extra):
    rows, cols = xi_coarse.shape
    down, up = neighbours("gx")
    right, left = neighbours("gy")

    def edge(a, row, near):
        return jnp.concatenate(
            [
                coef_middle[2 * a : 2 * a + 2, :, row].reshape(18, cols).astype(f32),
                near,
                xi_middle[2 * row + a].reshape(cols, 2).T,
            ]
        )

    above = lax.ppermute(edge(1, rows - 1, xi_coarse[-2:]), "gx", down)
    below = lax.ppermute(edge(0, 0, xi_coarse[:2]), "gx", up)

    def inside(b, col, near):
        return jnp.concatenate(
            [
                coef_middle[b::2, :, :, col].reshape(18, rows).astype(f32),
                near.T,
                xi_middle[:, 2 * col + b].reshape(rows, 2).T,
            ]
        )

    sides = inside(0, 0, xi_coarse[:, :2]), inside(1, cols - 1, xi_coarse[:, -2:])
    sides, extra = lax.optimization_barrier((sides, extra))

    to_left, to_right = pl.pallas_call(
        sides_kernel,
        in_specs=[whole] * 4,
        out_specs=[whole] * 2,
        out_shape=[jax.ShapeDtypeStruct((22, rows + 4), f32)] * 2,
        name="sides",
    )(above, below, *sides)
    lefts = lax.ppermute(to_right, "gy", right)
    rights = lax.ppermute(to_left, "gy", left)
    return (above, below, lefts, rights, to_left, to_right), extra


whole = pl.BlockSpec(memory_space=pltpu.VMEM)
scalar = pl.BlockSpec(memory_space=pltpu.SMEM)
anywhere = pl.BlockSpec(memory_space=pl.ANY)


def sky_of(halos, xi_coarse, coef_middle, xi_middle, coef_fine, xi_fine):
    rows, cols = coef_middle.shape[2:]
    operands = (xi_coarse, *halos, coef_middle, xi_middle, coef_fine, xi_fine)
    return pl.pallas_call(
        sky_kernel,
        in_specs=[anywhere] * 11,
        out_specs=[whole] * 2,
        out_shape=[
            jax.ShapeDtypeStruct((4 * rows, 4 * cols), bf16),
            jax.ShapeDtypeStruct((8, 128), f32),
        ],
        scratch_shapes=[pltpu.VMEM(x.shape, x.dtype) for x in operands]
        + [
            pltpu.VMEM((9, rows, cols), f32),
            pltpu.VMEM((2 * cols, 2 * cols), bf16),
            pltpu.VMEM((4 * rows, 2 * cols), bf16),
            pltpu.VMEM((2 * cols // 128, 2 * rows, 128), f32),
            pltpu.VMEM((3, rows + 16, cols), f32),
            pltpu.VMEM((3, 2 * rows + 16, 2 * cols), f32),
            pltpu.VMEM((9, 2 * rows, 2 * cols), f32),
            pltpu.VMEM((4 * cols, 4 * cols), bf16),
            pltpu.VMEM((8 * rows, 4 * cols), bf16),
            pltpu.VMEM((4 * cols // 128, 4 * rows, 128), f32),
            pltpu.SemaphoreType.DMA((11,)),
        ],
        compiler_params=pltpu.CompilerParams(vmem_limit_bytes=vmem),
        name="sky",
    )(*operands)


def spread(mix, coef_ref, terms, rows, cols):
    def part(i, carry):
        r0 = pl.multiple_of(i * 16, 16)
        quads = []
        for a in range(2):
            for b in range(2):
                tiles = range(b * cols // 128, (b + 1) * cols // 128)
                lines = [mix[t, pl.ds(2 * r0 + a, 16, stride=2), :] for t in tiles]
                quads.append(jnp.concatenate(lines, axis=1))
        for near in range(9):
            total = jnp.zeros((16, cols), f32)
            for child in range(4):
                total += coef_ref[child, near, pl.ds(r0, 16), :].astype(f32) * quads[child]
            terms[near, pl.ds(r0, 16), :] = total
        return carry

    lax.fori_loop(0, rows // 16, part, 0)


def joined(rowed, cols):
    lane = lax.broadcasted_iota(jnp.int32, rowed.shape[1:], 1)
    main = (
        rowed[1]
        + jnp.where(lane == 0, 0.0, pltpu.roll(rowed[2], 1, 1))
        + jnp.where(lane == cols - 1, 0.0, pltpu.roll(rowed[0], cols - 1, 1))
    )
    lane = lax.broadcasted_iota(jnp.int32, (8, cols), 1)
    outside = []
    for c, col in ((0, 0), (2, cols - 1)):
        pick = (lane == col).astype(f32).astype(bf16)
        high, low = halves(rowed[c])
        out = dot_t(pick, high, ((1,), (1,))) + dot_t(pick, low, ((1,), (1,)))
        outside.append(out[:1])
    return main, outside[0], outside[1]


def adjoint_kernel(number, *refs):
    parts, sources, outs = refs[:number], refs[number : number + 9], refs[number + 9 : number + 17]
    held, rest = refs[number + 17 : number + 26], refs[number + 26 :]
    grad_ref, middle_ref, coarse_ref, left_ref, right_ref, upper_ref, lower_ref, total_ref = outs
    fine_perm, fine_mix, fine_terms, fine_rowed, perm, mix, terms, rowed, sems = rest
    copies = fetched(zip(sources, held), sems)
    xi_fine, coef_fine, coef_middle, above, below, lefts, rights, xi_middle, xi_coarse = held
    rows, cols = terms.shape[1:]
    fine_perm[...] = interleaver(2 * cols, True)
    perm[...] = interleaver(cols, True)
    g = parts[0][: 4 * rows].astype(f32)
    for part in parts[1:]:
        g += part[: 4 * rows].astype(f32)
    copies[0].wait()
    grad_ref[...] = g + xi_fine[...]
    tail = sum(part[4 * rows :, :128].astype(f32) for part in parts)
    total_ref[...] = tail[:8] + tail[8:16] + tail[16:24]
    split = moved(g, fine_perm[...])
    for tile in range(4 * cols // 128):
        fine_mix[tile] = split[:, tile * 128 : (tile + 1) * 128]
    copies[1].wait()
    spread(fine_mix, coef_fine, fine_terms, 2 * rows, 2 * cols)
    fine_rowed[...] = jnp.zeros_like(fine_rowed)
    for near in range(9):
        r, c = near // 3, near % 3
        fine_rowed[c, 7 + r : 7 + r + 2 * rows, :] += fine_terms[near]
    main, left, right = joined(fine_rowed, 2 * cols)
    last = 8 + 2 * rows
    inner = main[8:last]
    for copy in copies[2:]:
        copy.wait()
    middle_ref[...] = inner + xi_middle[...]
    split = moved(inner, perm[...])
    for tile in range(2 * cols // 128):
        mix[tile] = split[:, tile * 128 : (tile + 1) * 128]
    spread(mix, coef_middle, terms, rows, cols)
    ring_above, ring_below = main[7:8], main[last : last + 1]
    lines = [ring_above, ring_below, left[:, 8:last], right[:, 8:last]]
    lines = moved(jnp.concatenate(lines + [jnp.zeros((4, 2 * cols), f32)]), perm[...])
    rowed[...] = jnp.zeros_like(rowed)
    for near in range(9):
        r, c = near // 3, near % 3
        rowed[c, 7 + r : 7 + r + rows, :] += terms[near]
    for line, message, top in ((0, above, 6), (1, below, 7 + rows)):
        for near in range(9):
            r, c = near // 3, near % 3
            term = row_of(message, near) * lines[line : line + 1, :cols]
            term += row_of(message, 9 + near) * lines[line : line + 1, cols:]
            rowed[c, top + r : top + r + 1, :] += term

    def along(line, ends, message):
        empty = jnp.zeros((1, 1), f32)
        first = [empty, lines[line : line + 1, :rows], ends[:, last : last + 1]]
        second = [ends[:, 7:8], lines[line : line + 1, cols : cols + rows], empty]
        first, second = jnp.concatenate(first, axis=1), jnp.concatenate(second, axis=1)
        out = []
        for c in range(3):
            total = jnp.zeros((1, rows + 4), f32)
            for r in range(3):
                near = 3 * r + c
                term = row_of(message, near)[:, 1 : rows + 3] * first
                term += row_of(message, 9 + near)[:, 1 : rows + 3] * second
                pads = [jnp.zeros((1, n), f32) for n in (r, 2 - r) if n]
                pieces = [term] + pads if r == 0 else pads[:1] + [term] + pads[1:]
                total += jnp.concatenate(pieces, axis=1)
            out.append(total)
        return out

    outer_left = along(2, left, lefts)
    outer_right = along(3, right, rights)
    main, near_left, near_right = joined(rowed, cols)
    coarse_ref[...] = (
        main[8 : 8 + rows]
        + xi_coarse[...]
        + ends_placed(outer_left[2][:, 2 : rows + 2], outer_right[0][:, 2 : rows + 2], cols)
    )
    lane = lax.broadcasted_iota(jnp.int32, (1, cols), 1)
    for ref, first, line in ((upper_ref, 6, ring_above), (lower_ref, 8 + rows, ring_below)):
        ref[...] = jnp.zeros_like(ref)
        for i in range(2):
            at = first - 6 + i
            ref[i : i + 1, :cols] = (
                main[first + i : first + i + 1]
                + jnp.where(lane == 0, outer_left[2][:, at : at + 1], 0.0)
                + jnp.where(lane == cols - 1, outer_right[0][:, at : at + 1], 0.0)
            )
        ref[2:3, :] = line
    for ref, far, close, beyond, ends in (
        (left_ref, outer_left[0], outer_left[1], near_left, left),
        (right_ref, outer_right[2], outer_right[1], near_right, right),
    ):
        ref[...] = jnp.zeros_like(ref)
        ref[0:1, : rows + 4] = far
        ref[1:2, : rows + 4] = close + beyond[:, 6 : rows + 10]
        ref[2:3, : 2 * rows + 2] = ends[:, 7 : 2 * rows + 9]


def corners_kernel(upper, lower, from_left, from_right, total, other, upper_out, lower_out, total_out):
    rows, cols = lower.shape[1] // 2, lower.shape[1] // 2
    for ref, out, at, end in ((upper, upper_out, 0, 0), (lower, lower_out, rows + 2, 2 * rows + 1)):
        out[...] = ref[...]
        for i in range(2):
            here = slice(at + i, at + i + 1)
            out[i : i + 1, 0:1] += from_left[1:2, here]
            out[i : i + 1, 1:2] += from_left[0:1, here]
            out[i : i + 1, cols - 2 : cols - 1] += from_right[0:1, here]
            out[i : i + 1, cols - 1 : cols] += from_right[1:2, here]
        out[2:3, 0:1] += from_left[2:3, end : end + 1]
        out[2:3, 2 * cols - 1 :] += from_right[2:3, end : end + 1]
    total_out[...] = total[...] + other[...]


def final_kernel(
    cells,
    middle,
    coarse,
    from_left,
    from_right,
    from_above,
    from_below,
    total,
    other,
    middle_out,
    coarse_out,
    total_out,
):
    rows, cols = coarse.shape
    middle_out[...] = middle[...] + ends_placed(
        from_left[2:3, 1 : 2 * rows + 1], from_right[2:3, 1 : 2 * rows + 1], 2 * cols
    )
    middle_out[:1] += from_above[2:3]
    middle_out[2 * rows - 1 :] += from_below[2:3]
    inner = slice(2, rows + 2)
    outer = ends_placed(from_left[1:2, inner], from_right[1:2, inner], cols)
    second = ends_placed(from_left[0:1, inner], from_right[0:1, inner], cols)
    lane = lax.broadcasted_iota(jnp.int32, second.shape, 1)
    second = jnp.where(lane == 1, pltpu.roll(second, 1, 1), 0.0) + jnp.where(
        lane == cols - 2, pltpu.roll(second, cols - 1, 1), 0.0
    )
    coarse_out[...] = coarse[...] + outer + second
    coarse_out[:2] += from_above[0:2, :cols]
    coarse_out[rows - 2 :] += from_below[0:2, :cols]
    both = total[...] + other[...]
    both = jnp.sum(jnp.sum(both, axis=1, keepdims=True), axis=0, keepdims=True)
    total_out[...] = both * (1.0 / cells)


def adjoint(parts, halos, coef_middle, xi_middle, coef_fine, xi_fine, xi_coarse):
    rows, cols = coef_middle.shape[2:]
    above, below, lefts, rights, _, _ = halos
    shape = lambda *dims: jax.ShapeDtypeStruct(dims, f32)
    long = 2 * rows + 128
    operands = (
        xi_fine,
        coef_fine,
        coef_middle,
        above,
        below,
        lefts,
        rights,
        xi_middle,
        xi_coarse,
    )
    grad_fine, middle, coarse, to_left, to_right, upper, lower, total = pl.pallas_call(
        functools.partial(adjoint_kernel, len(parts)),
        in_specs=[whole] * len(parts) + [anywhere] * 9,
        out_specs=[whole] * 8,
        out_shape=[
            shape(4 * rows, 4 * cols),
            shape(2 * rows, 2 * cols),
            shape(rows, cols),
            shape(8, long),
            shape(8, long),
            shape(8, 2 * cols),
            shape(8, 2 * cols),
            shape(8, 128),
        ],
        scratch_shapes=[pltpu.VMEM(x.shape, x.dtype) for x in operands]
        + [
            pltpu.VMEM((4 * cols, 4 * cols), bf16),
            pltpu.VMEM((4 * cols // 128, 4 * rows, 128), f32),
            pltpu.VMEM((9, 2 * rows, 2 * cols), f32),
            pltpu.VMEM((3, 2 * rows + 128, 2 * cols), f32),
            pltpu.VMEM((2 * cols, 2 * cols), bf16),
            pltpu.VMEM((2 * cols // 128, 2 * rows, 128), f32),
            pltpu.VMEM((9, rows, cols), f32),
            pltpu.VMEM((3, rows + 128, cols), f32),
            pltpu.SemaphoreType.DMA((9,)),
        ],
        compiler_params=pltpu.CompilerParams(vmem_limit_bytes=vmem),
        name="adjoint",
    )(*parts, *operands)
    right, left = neighbours("gy")
    down, up = neighbours("gx")
    from_left = lax.ppermute(to_right, "gy", right)
    from_right = lax.ppermute(to_left, "gy", left)

    size = lax.axis_size("gx")
    hops = [1 << i for i in range(size.bit_length()) if 1 << i < size]

    def across(x, hop):
        return lax.ppermute(x, "gx", [(i, i ^ hop) for i in range(size)])

    other = across(total, hops[0])
    upper, lower, total = pl.pallas_call(
        corners_kernel,
        in_specs=[whole] * 6,
        out_specs=[whole] * 3,
        out_shape=[shape(8, 2 * cols), shape(8, 2 * cols), shape(8, 128)],
        name="corners",
    )(upper, lower, from_left, from_right, total, other)
    from_below = lax.ppermute(upper, "gx", up)
    from_above = lax.ppermute(lower, "gx", down)
    for hop in hops[1:-1]:
        total += across(total, hop)
    other = across(total, hops[-1])
    cells = size * lax.axis_size("gy") * 16 * rows * cols
    grad_middle, grad_coarse, total = pl.pallas_call(
        functools.partial(final_kernel, cells),
        in_specs=[whole] * 8,
        out_specs=[whole] * 3,
        out_shape=[shape(2 * rows, 2 * cols), shape(rows, cols), shape(1, 1)],
        compiler_params=pltpu.CompilerParams(vmem_limit_bytes=vmem),
        name="final",
    )(middle, coarse, from_left, from_right, from_above, from_below, total, other)
    return grad_coarse, grad_middle, grad_fine, total.reshape(())


def in_three(x):
    high = x.astype(bf16).astype(f32)
    middle = (x - high).astype(bf16).astype(f32)
    return jnp.concatenate([high, middle, x - high - middle, jnp.zeros_like(x)]).astype(bf16)


def from_three(x):
    x = x.astype(f32)
    return x[:8] + x[8:16] + x[16:24]


def facets_kernel(blk, ints, weights, *refs):
    number, slots = weights.shape
    tiles, rest = refs[:-14], refs[-14:]
    ku_hbm, kv_hbm, data_hbm, squares, out_ref = rest[:5]
    held, ku, kv, data, sums, dsum, total, sems, tile_sems = rest[5:]
    bins, side = ku.shape[1:]

    def inputs(f):
        for s in range(slots):
            for i, tile in enumerate(tiles):

                @pl.when(ints[f, s] == i)
                def _():
                    pltpu.make_async_copy(tile, held.at[f, s], tile_sems.at[f, s]).start()

        pairs = ((ku_hbm, ku), (kv_hbm, kv), (data_hbm, data))
        copies = [
            pltpu.make_async_copy(src.at[0, f], dst.at[f], sems.at[f, i])
            for i, (src, dst) in enumerate(pairs)
        ]
        for copy in copies:
            copy.start()
        return copies

    def work(f, step):
        rows = slice(step * blk, (step + 1) * blk)
        count = ints[f, slots] - step * blk

        @pl.when(count > 0)
        def _():
            amp = jnp.dot(ku[f, rows], sums[...], preferred_element_type=f32).astype(bf16)
            vis = dot_t(amp, kv[f], ((1,), (1,)))
            live = lax.broadcasted_iota(jnp.int32, vis.shape, 0) < count
            resid = jnp.where(live, vis - data[f, rows].astype(f32), 0.0)
            total[...] += 0.5 * inv_noise * folded(resid * resid)
            dvis = (inv_noise * resid).astype(bf16)
            damp = jnp.dot(dvis, kv[f], preferred_element_type=f32).astype(bf16)
            part = dot_t(ku[f, rows], damp, ((0,), (0,)))
            if step == 0:
                dsum[...] = part
            else:
                dsum[...] += part

    copies = [inputs(0)]
    total[...] = 0.5 * squares[...]
    for f in range(number):
        for s in range(slots):
            pltpu.make_async_copy(tiles[0], held.at[f, s], tile_sems.at[f, s]).wait()
        copies[f][0].wait()
        if f + 1 < number:
            copies.append(inputs(f + 1))
        mixture = weights[f, 0] * held[f, 0].astype(f32)
        for s in range(1, slots):
            mixture += weights[f, s] * held[f, s].astype(f32)
        sums[...] = mixture.astype(bf16)
        copies[f][1].wait()
        copies[f][2].wait()
        for step in range(bins // blk):
            work(f, step)
        out_ref[f * side : (f + 1) * side] = dsum[...].astype(bf16)
    out_ref[number * side :] = jnp.zeros((32, side), bf16)
    out_ref[number * side :, :128] = in_three(total[...])


def facets(tiles, ku, kv, data, ints, weights, squares):
    number, bins, side = ku.shape[1:]
    slots = weights.shape[1]
    return pl.pallas_call(
        functools.partial(facets_kernel, 512),
        in_specs=[scalar] * 2 + [anywhere] * (len(tiles) + 3) + [whole],
        out_specs=whole,
        out_shape=jax.ShapeDtypeStruct((number * side + 32, side), bf16),
        scratch_shapes=[
            pltpu.VMEM((number, slots, side, side), bf16),
            pltpu.VMEM((number, bins, side), bf16),
            pltpu.VMEM((number, bins, side), bf16),
            pltpu.VMEM((number, bins, bins), bf16),
            pltpu.VMEM((side, side), bf16),
            pltpu.VMEM((side, side), f32),
            pltpu.VMEM((8, 128), f32),
            pltpu.SemaphoreType.DMA((number, 3)),
            pltpu.SemaphoreType.DMA((number, slots)),
        ],
        compiler_params=pltpu.CompilerParams(vmem_limit_bytes=vmem),
        name="facets",
    )(ints, weights, *tiles, ku, kv, data, squares)


def mix_kernel(scale, mine, theirs, *outs):
    side = outs[0].shape[1]
    number = mine.shape[0] // side
    total = in_three(from_three(mine[number * side :, :128]) + from_three(theirs[number * side :, :128]))
    for d, out in enumerate(outs):
        value = None
        for f in range(2 * number):
            ref, at = (mine, f) if f < number else (theirs, f - number)
            term = scale[d, f] * ref[at * side : (at + 1) * side].astype(f32)
            value = term if value is None else value + term
        out[:side] = value.astype(bf16)
        out[side:] = jnp.zeros((32, side), bf16)
        out[side:, :128] = total


def mixed(mine, theirs, scale):
    side = mine.shape[1]
    return pl.pallas_call(
        mix_kernel,
        in_specs=[scalar, whole, whole],
        out_specs=[whole] * scale.shape[0],
        out_shape=[jax.ShapeDtypeStruct((side + 32, side), bf16)] * scale.shape[0],
        compiler_params=pltpu.CompilerParams(vmem_limit_bytes=vmem),
        name="mixed",
    )(scale, mine, theirs)


def chip_shift(x, hop):
    size = lax.axis_size("gy")
    return lax.ppermute(x, "gy", [(i, (i + 2 * hop) % size) for i in range(size)])


def swapped(x):
    return lax.ppermute(x, "gy", [(i, i ^ 1) for i in range(lax.axis_size("gy"))])


def body(
    xi_coarse,
    xi_middle,
    xi_fine,
    coef_middle,
    coef_fine,
    kern_u,
    kern_v,
    vis_data,
    facet_tiles,
    facet_weight,
    facet_count,
):
    lists, weights, counts = facet_tiles[0], facet_weight[0], facet_count[0]
    size = lax.axis_size("gy")
    chips = size // 2
    me = lax.axis_index("gy")
    ids = jnp.arange(size, dtype=jnp.int32)
    mixing = jnp.sum(
        weights[:, :, None] * (lists[:, :, None] == ids[None, None, :]).astype(f32), axis=1
    )
    order = 2 * ((me // 2 + jnp.arange(chips, dtype=jnp.int32)) % chips) + me % 2
    scale = jnp.concatenate([mixing, swapped(mixing)])[:, order].T
    sel = (me // 2 - lists // 2) % chips + jnp.where(lists % 2 == me % 2, 0, chips)
    ints = jnp.concatenate([sel, counts[:, None]], axis=1)
    halos, (scale, ints, weights) = halo(
        xi_coarse, xi_middle, coef_middle, (scale, ints, weights)
    )
    sky, squares = sky_of(halos, xi_coarse, coef_middle, xi_middle, coef_fine, xi_fine)
    mine = [sky] + [chip_shift(sky, hop) for hop in range(1, chips)]
    tiles = mine + [swapped(tile) for tile in mine]
    dsums = facets(tiles, kern_u, kern_v, vis_data, ints, weights, squares)
    parts = mixed(dsums, swapped(dsums), scale)
    parts = [parts[0]] + [chip_shift(parts[hop], hop) for hop in range(1, chips)]
    return adjoint(parts, halos, coef_middle, xi_middle, coef_fine, xi_fine, xi_coarse)


def solution(mesh):
    placed = (
        P("gx", "gy"),
        P("gx", "gy"),
        P("gx", "gy"),
        P(None, None, "gx", "gy"),
        P(None, None, "gx", "gy"),
        P("gx", "gy", None, None),
        P("gx", "gy", None, None),
        P("gx", "gy", None, None),
        P("gx", "gy", None),
        P("gx", "gy", None),
        P("gx", "gy"),
    )
    return jax.shard_map(
        body,
        mesh=mesh,
        in_specs=placed,
        out_specs=(P("gx", "gy"), P("gx", "gy"), P("gx", "gy"), P()),
        check_vma=False,
    )
```

time: 215 us -> 188 us (0.87)
  local copies, waits for them, and re-layouts: 33.9 us -> 16.6 us
  Pallas kernels: 27.6 us -> 22 us
  starting transfers between devices: 36.5 us -> 41.5 us
  between operations: 4.84 us -> 1.07 us
  other arithmetic: 7.44 us -> 5.05 us
    unnamed x72 -> x60, local copies, waits for them, and re-layouts: 21.9 us -> 12.2 us
    pallas_call x5 -> x6, Pallas kernels: 23.5 us -> 16.8 us  [the longest x1 6.14 us: facets(): pl.pallas_call(functools.partial(facets_kernel, 512), in_specs=[scalar] *...]
    ppermute x6, starting transfers between devices: 10 us -> 13.3 us  [chip_shift(): lax.ppermute(x, 'gy', [(i, (i + 2 * hop) % size) for i in range(size)])]
    concatenate x6 -> x0, local copies, waits for them, and re-layouts: 3.08 us -> none  [the longest x2 1.46 us: edges(): jnp.concatenate([zero[:9], above[9 * b:9 * b + 9, col], above[19, first:f...]
    ppermute x8 -> x6, starting transfers between devices: 1.24 us -> 4.31 us  [swapped(): lax.ppermute(x, 'gy', [(i, i ^ 1) for i in range(lax.axis_size('gy'))])]
    add x6 -> x0, other arithmetic: 2.9 us -> none  [the longest x2 2.72 us: corners(): jnp.pad(from_left[2:3, end:end + 1], ((0, 0), (0, 2 * cols - 1)))]
    ppermute x4, waiting for transfers between devices: 4.67 us -> 7.4 us  [the longest x2 7.4 us: across(): return lax.ppermute(x, 'gx', [(i, i ^ hop) for i in range(size)])]
    slice x8 -> x0, local copies, waits for them, and re-layouts: 2.72 us -> none  [the longest x1 0.61 us: corners(): from_left[2:3, end:end + 1]]
  transfers between devices with their start and end apart: 24 -> 22, of which waited for: 12 -> 11; matrix products, arithmetic and copies ran while one was open for 6% -> 5% of each run, Pallas kernels for 4% -> 0%
where the time goes in v5:
time: 188 us; the launch traced here: 187 us
  waiting for transfers between devices  101 us (54%)
  starting transfers between devices  41.5 us (22%)
  Pallas kernels  22 us (12%)
  local copies, waits for them, and re-layouts  16.6 us (9%)
  other arithmetic  5.05 us (3%)
    ppermute x6, waiting for transfers between devices, chip_shift(): lax.ppermute(x, 'gy', [(i, (i + 2 * hop) % size) for i in range(size)])  87.3 us
    ppermute x6, starting transfers between devices, chip_shift(): lax.ppermute(x, 'gy', [(i, (i + 2 * hop) % size) for i in range(size)])  13.3 us
    unnamed x60, local copies, waits for them, and re-layouts  12.2 us
    ppermute x2, waiting for transfers between devices, across(): return lax.ppermute(x, 'gx', [(i, i ^ hop) for i in range(size)])  7.4 us
    pallas_call x1, Pallas kernels, facets(): pl.pallas_call(functools.partial(facets_kernel, 512), in_specs=[scalar] *...  6.14 us
    pallas_call x1, Pallas kernels, adjoint(): pl.pallas_call(functools.partial(adjoint_kernel, len(parts)), in_specs=[w...  5.13 us
    pallas_call x1, Pallas kernels, sky_of(): pl.pallas_call(sky_kernel, in_specs=[anywhere] * 11, out_specs=[whole] *...  4.57 us
    ppermute x6, starting transfers between devices, swapped(): lax.ppermute(x, 'gy', [(i, i ^ 1) for i in range(lax.axis_size('gy'))])  4.31 us
  transfers between devices with their start and end apart: 22, of which 11 were waited for; matrix products, arithmetic and copies ran while one was open for 5% of the time, Pallas kernels for 0%

profile of v5, /device:TPU:10, one launch (start us, length us, event | category | flops | bytes accessed | tf_op | source)
XLA Modules:
  0.0 186.7 jit_solution(12517404530080269075)
XLA Ops:
  4.1 2.4 %collective-permute-start.2 = (f32[22,128]{1,0:T(8,128)S(1)}, f32[22,128]{1,0:T(8,128)S(1)}, u32[]{:S(2)}, u32[]{:S(2)}) collective-permute-start(f32[22,128]{1,0:T(8,128)S(1)} %pad_maximum_fusion.3), channel_id=1, source_target_pairs={{8,0},{16,8},{24,16},{9,1},{17,9},{25,17},{10,2},{18,10},{26,18},{... | collective-permute-start | bytes 33800 | tf_op jit(solution)/shard_map/ppermute | solution.py:233
  6.8 4.3 %collective-permute-start.1 = (f32[22,128]{1,0:T(8,128)S(1)}, f32[22,128]{1,0:T(8,128)S(1)}, u32[]{:S(2)}, u32[]{:S(2)}) collective-permute-start(f32[22,128]{1,0:T(8,128)S(1)} %pad_maximum_fusion.2), channel_id=1, source_target_pairs={{0,8},{8,16},{16,24},{1,9},{9,17},{17,25},{2,10},{10,18},{18,26},{... | collective-permute-start | bytes 33800 | tf_op jit(solution)/shard_map/ppermute | solution.py:232
  13.2 1.8 convert_reduce_fusion
  19.9 1.9 %collective-permute-start.3 = (f32[22,132]{1,0:T(8,128)}, f32[22,132]{1,0:T(8,128)S(1)}, u32[]{:S(2)}, u32[]{:S(2)}) collective-permute-start(f32[22,132]{1,0:T(8,128)} %get-tuple-element.36.refs_6_), channel_id=1, source_target_pairs={{0,1},{1,2},{2,3},{3,4},{4,5},{5,6},{6,7},{8,9},{9,10},{10,11},{11... | collective-permute-start | bytes 34856 | tf_op jit(solution)/shard_map/ppermute | solution.py:254
  21.8 3.6 %collective-permute-start.4 = (f32[22,132]{1,0:T(8,128)}, f32[22,132]{1,0:T(8,128)S(1)}, u32[]{:S(2)}, u32[]{:S(2)}) collective-permute-start(f32[22,132]{1,0:T(8,128)} %get-tuple-element.37.refs_5_), channel_id=1, source_target_pairs={{1,0},{2,1},{3,2},{4,3},{5,4},{6,5},{7,6},{9,8},{10,9},{11,10},{12... | collective-permute-start | bytes 34856 | tf_op jit(solution)/shard_map/ppermute | solution.py:255
  25.5 1.7 collective-permute-done.4.refs_4_.refs_10_
  27.2 2.3 %copy-done = bf16[4,9,256,256]{3,2,1,0:T(8,128)(2,1)S(1)} copy-done((bf16[4,9,256,256]{3,2,1,0:T(8,128)(2,1)S(1)}, bf16[4,9,256,256]{3,2,1,0:T(8,128)(2,1)}, u32[]{:S(2)}) %copy-start) | copy-done | bytes 4718616
  32.4 4.6 %sky.1 = (bf16[512,512]{1,0:T(8,128)(2,1)S(1)}, f32[8,128]{1,0:T(8,128)S(1)}) custom-call(f32[128,128]{1,0:T(8,128)S(1)} %copy-done.7, f32[22,128]{1,0:T(8,128)S(1)} %copy-done.12, f32[22,128]{1,0:T(8,128)S(1)} %copy-done.9, f32[22,132]{1,0:T(8,128)S(1)} %collective-permute-done.3.refs_3_.refs_9_, f32[22,132]{1,0:T(8,128)S(1)} %collective-permute-done.4.refs_4_.refs_10_, ...), custom_call_target="tpu_custom_call" | custom-call | tf_op jit(solution)/shard_map/sky/pallas_call | solution.py:267
  37.1 3.0 %collective-permute-start.6 = (bf16[512,512]{1,0:T(8,128)(2,1)S(1)}, bf16[512,512]{1,0:T(8,128)(2,1)S(1)}, u32[]{:S(2)}, u32[]{:S(2)}) collective-permute-start(bf16[512,512]{1,0:T(8,128)(2,1)S(1)} %get-tuple-element.38.refs_0_), channel_id=1, source_target_pairs={{0,4},{1,5},{2,6},{3,7},{4,0},{5,1},{6,2},{7,3},{8,12},{9,13},{10,... | collective-permute-start | bytes 1572872 | tf_op jit(solution)/shard_map/ppermute | solution.py:686
  40.1 2.5 %collective-permute-start.5 = (bf16[512,512]{1,0:T(8,128)(2,1)S(1)}, bf16[512,512]{1,0:T(8,128)(2,1)S(1)}, u32[]{:S(2)}, u32[]{:S(2)}) collective-permute-start(bf16[512,512]{1,0:T(8,128)(2,1)S(1)} %get-tuple-element.38.refs_0_), channel_id=1, source_target_pairs={{0,2},{1,3},{2,4},{3,5},{4,6},{5,7},{6,0},{7,1},{8,10},{9,11},{10,... | collective-permute-start | bytes 1572872 | tf_op jit(solution)/shard_map/ppermute | solution.py:686
  42.6 8.6 %collective-permute-done.7.refs_3_ = bf16[512,512]{1,0:T(8,128)(2,1)S(1)} collective-permute-done((bf16[512,512]{1,0:T(8,128)(2,1)S(1)}, bf16[512,512]{1,0:T(8,128)(2,1)S(1)}, u32[]{:S(2)}, u32[]{:S(2)}) %collective-permute-start.7) | collective-permute-done | bytes 524320 | tf_op jit(solution)/shard_map/ppermute | solution.py:686
  51.2 1.8 collective-permute-start.11
  52.9 19.8 %collective-permute-done.6.refs_2_ = bf16[512,512]{1,0:T(8,128)(2,1)S(1)} collective-permute-done((bf16[512,512]{1,0:T(8,128)(2,1)S(1)}, bf16[512,512]{1,0:T(8,128)(2,1)S(1)}, u32[]{:S(2)}, u32[]{:S(2)}) %collective-permute-start.6) | collective-permute-done | bytes 524320 | tf_op jit(solution)/shard_map/ppermute | solution.py:686
  72.9 11.0 %collective-permute-done.5.refs_1_ = bf16[512,512]{1,0:T(8,128)(2,1)S(1)} collective-permute-done((bf16[512,512]{1,0:T(8,128)(2,1)S(1)}, bf16[512,512]{1,0:T(8,128)(2,1)S(1)}, u32[]{:S(2)}, u32[]{:S(2)}) %collective-permute-start.5) | collective-permute-done | bytes 524320 | tf_op jit(solution)/shard_map/ppermute | solution.py:686
  84.2 1.7 collective-permute-done.9.refs_5_
  85.9 1.7 copy-done.6
  87.6 6.1 %facets.1.mine = bf16[1056,512]{1,0:T(8,128)(2,1)S(1)} custom-call(s32[2,3]{1,0:T(2,128)S(1)} %pad_add_fusion.ints, f32[2,2]{1,0:T(2,128)S(1)} %bitcast.16, bf16[512,512]{1,0:T(8,128)(2,1)S(1)} %get-tuple-element.38.refs_0_, bf16[512,512]{1,0:T(8,128)(2,1)S(1)} %collective-permute-done.5.refs_1_, bf16[512,512]{1,0:T(8,128)(2,1)S(1)} %collective-permute-done.6.refs_2_, ...), custom_call_target="tpu_custom_call" | custom-call | tf_op jit(solution)/shard_map/facets/pallas_call | solution.py:636
  93.8 2.2 %collective-permute-start.12 = (bf16[1056,512]{1,0:T(8,128)(2,1)S(1)}, bf16[1056,512]{1,0:T(8,128)(2,1)S(1)}, u32[]{:S(2)}, u32[]{:S(2)}) collective-permute-start(bf16[1056,512]{1,0:T(8,128)(2,1)S(1)} %facets.1.mine), channel_id=1, source_target_pairs={{0,1},{1,0},{2,3},{3,2},{4,5},{5,4},{6,7},{7,6},{8,9},{9,8},{10,11... | collective-permute-start | bytes 3244040 | tf_op jit(solution)/shard_map/ppermute | solution.py:690
  96.0 2.3 %collective-permute-done.12.theirs = bf16[1056,512]{1,0:T(8,128)(2,1)S(1)} collective-permute-done((bf16[1056,512]{1,0:T(8,128)(2,1)S(1)}, bf16[1056,512]{1,0:T(8,128)(2,1)S(1)}, u32[]{:S(2)}, u32[]{:S(2)}) %collective-permute-start.12) | collective-permute-done | bytes 1081376 | tf_op jit(solution)/shard_map/ppermute | solution.py:690
  98.3 2.2 %mixed.1 = (bf16[544,512]{1,0:T(8,128)(2,1)S(1)}, bf16[544,512]{1,0:T(8,128)(2,1)S(1)}, bf16[544,512]{1,0:T(8,128)(2,1)S(1)}, bf16[544,512]{1,0:T(8,128)(2,1)S(1)}) custom-call(f32[4,4]{1,0:T(4,128)S(1)} %gather_fusion, bf16[1056,512]{1,0:T(8,128)(2,1)S(1)} %facets.1.mine, bf16[1056,512]{1,0:T(8,128)(2,1)S(1)} %collective-permute-done.12.theirs), custom_call_target="tpu_custom_call" | custom-call | tf_op jit(solution)/shard_map/mixed/pallas_call | solution.py:674
  100.5 4.4 %collective-permute-start.13 = (bf16[544,512]{1,0:T(8,128)(2,1)S(1)}, bf16[544,512]{1,0:T(8,128)(2,1)S(1)}, u32[]{:S(2)}, u32[]{:S(2)}) collective-permute-start(bf16[544,512]{1,0:T(8,128)(2,1)S(1)} %get-tuple-element.41), channel_id=1, source_target_pairs={{0,2},{1,3},{2,4},{3,5},{4,6},{5,7},{6,0},{7,1},{8,10},{9,11},{10,... | collective-permute-start | bytes 1671176 | tf_op jit(solution)/shard_map/ppermute | solution.py:686
  104.9 3.4 %collective-permute-start.14 = (bf16[544,512]{1,0:T(8,128)(2,1)S(1)}, bf16[544,512]{1,0:T(8,128)(2,1)S(1)}, u32[]{:S(2)}, u32[]{:S(2)}) collective-permute-start(bf16[544,512]{1,0:T(8,128)(2,1)S(1)} %get-tuple-element.42), channel_id=1, source_target_pairs={{0,4},{1,5},{2,6},{3,7},{4,0},{5,1},{6,2},{7,3},{8,12},{9,13},{10,... | collective-permute-start | bytes 1671176 | tf_op jit(solution)/shard_map/ppermute | solution.py:686
  108.3 11.1 %collective-permute-done.13.refs_1_ = bf16[544,512]{1,0:T(8,128)(2,1)S(1)} collective-permute-done((bf16[544,512]{1,0:T(8,128)(2,1)S(1)}, bf16[544,512]{1,0:T(8,128)(2,1)S(1)}, u32[]{:S(2)}, u32[]{:S(2)}) %collective-permute-start.13) | collective-permute-done | bytes 557088 | tf_op jit(solution)/shard_map/ppermute | solution.py:686
  119.3 33.7 %collective-permute-done.14.refs_2_ = bf16[544,512]{1,0:T(8,128)(2,1)S(1)} collective-permute-done((bf16[544,512]{1,0:T(8,128)(2,1)S(1)}, bf16[544,512]{1,0:T(8,128)(2,1)S(1)}, u32[]{:S(2)}, u32[]{:S(2)}) %collective-permute-start.14) | collective-permute-done | bytes 557088 | tf_op jit(solution)/shard_map/ppermute | solution.py:686
  153.1 3.0 %collective-permute-done.15.refs_3_ = bf16[544,512]{1,0:T(8,128)(2,1)S(1)} collective-permute-done((bf16[544,512]{1,0:T(8,128)(2,1)S(1)}, bf16[544,512]{1,0:T(8,128)(2,1)S(1)}, u32[]{:S(2)}, u32[]{:S(2)}) %collective-permute-start.15) | collective-permute-done | bytes 557088 | tf_op jit(solution)/shard_map/ppermute | solution.py:686
  156.2 5.1 %adjoint.1 = (f32[512,512]{1,0:T(8,128)}, f32[256,256]{1,0:T(8,128)S(1)}, f32[128,128]{1,0:T(8,128)S(1)}, f32[8,384]{1,0:T(8,128)S(1)}, f32[8,384]{1,0:T(8,128)S...) custom-call(bf16[544,512]{1,0:T(8,128)(2,1)S(1)} %get-tuple-element.40.refs_0_, ...), custom_call_target="tpu_custom_call" | custom-call | tf_op jit(solution)/shard_map/adjoint/pallas_call | solution.py:493
  162.5 1.9 %collective-permute-start.16 = (f32[8,384]{1,0:T(8,128)S(1)}, f32[8,384]{1,0:T(8,128)S(1)}, u32[]{:S(2)}, u32[]{:S(2)}) collective-permute-start(f32[8,384]{1,0:T(8,128)S(1)} %get-tuple-element.46), channel_id=1, source_target_pairs={{0,1},{1,2},{2,3},{3,4},{4,5},{5,6},{6,7},{8,9},{9,10},{10,11},{11... | collective-permute-start | bytes 36872 | tf_op jit(solution)/shard_map/ppermute | solution.py:524
  164.4 3.6 %collective-permute-start.17 = (f32[8,384]{1,0:T(8,128)S(1)}, f32[8,384]{1,0:T(8,128)S(1)}, u32[]{:S(2)}, u32[]{:S(2)}) collective-permute-start(f32[8,384]{1,0:T(8,128)S(1)} %get-tuple-element.47), channel_id=1, source_target_pairs={{1,0},{2,1},{3,2},{4,3},{5,4},{6,5},{7,6},{9,8},{10,9},{11,10},{12... | collective-permute-start | bytes 36872 | tf_op jit(solution)/shard_map/ppermute | solution.py:525
  168.1 3.6 %collective-permute-done.18.other = f32[8,128]{1,0:T(8,128)S(1)} collective-permute-done((f32[8,128]{1,0:T(8,128)S(1)}, f32[8,128]{1,0:T(8,128)S(1)}, u32[]{:S(2)}, u32[]{:S(2)}) %collective-permute-start.18) | collective-permute-done | bytes 4128 | tf_op jit(solution)/shard_map/ppermute | solution.py:531
  173.8 2.5 %collective-permute-start.19 = (f32[8,256]{1,0:T(8,128)}, f32[8,256]{1,0:T(8,128)S(1)}, u32[]{:S(2)}, u32[]{:S(2)}) collective-permute-start(f32[8,256]{1,0:T(8,128)} %get-tuple-element.51), channel_id=1, source_target_pairs={{0,8},{8,16},{16,24},{1,9},{9,17},{17,25},{2,10},{10,18},{18,26},{... | collective-permute-start | bytes 24584 | tf_op jit(solution)/shard_map/ppermute | solution.py:542
  176.3 3.3 %collective-permute-start.20 = (f32[8,256]{1,0:T(8,128)}, f32[8,256]{1,0:T(8,128)S(1)}, u32[]{:S(2)}, u32[]{:S(2)}) collective-permute-start(f32[8,256]{1,0:T(8,128)} %get-tuple-element.52), channel_id=1, source_target_pairs={{8,0},{16,8},{24,16},{9,1},{17,9},{25,17},{10,2},{18,10},{26,18},{... | collective-permute-start | bytes 24584 | tf_op jit(solution)/shard_map/ppermute | solution.py:541
  179.7 3.8 %collective-permute-done.21.other = f32[8,128]{1,0:T(8,128)S(1)} collective-permute-done((f32[8,128]{1,0:T(8,128)}, f32[8,128]{1,0:T(8,128)S(1)}, u32[]{:S(2)}, u32[]{:S(2)}) %collective-permute-start.21) | collective-permute-done | bytes 4128 | tf_op jit(solution)/shard_map/ppermute | solution.py:531
  (110 shorter events, 20.3 us)
Async XLA Ops:
  1.6 15.0 %collective-permute-start = (f32[2,8]{0,1:T(8,128)S(1)}, f32[2,8]{0,1:T(8,128)S(1)}, u32[]{:S(2)}, u32[]{:S(2)}) collective-permute-start(f32[2,8]{0,1:T(8,128)S(1)} %copy.30), channel_id=1, source_target_pairs={{0,1},{1,0},{2,3},{3,2},{4,5},{5,4},{6,7},{7,6},{8,9},{9,8},{10,11... | collective-permute-start | bytes 200 | tf_op jit(solution)/shard_map/ppermute | solution.py:690
  4.1 13.1 %collective-permute-start.2 = (f32[22,128]{1,0:T(8,128)S(1)}, f32[22,128]{1,0:T(8,128)S(1)}, u32[]{:S(2)}, u32[]{:S(2)}) collective-permute-start(f32[22,128]{1,0:T(8,128)S(1)} %pad_maximum_fusion.3), channel_id=1, source_target_pairs={{8,0},{16,8},{24,16},{9,1},{17,9},{25,17},{10,2},{18,10},{26,18},{... | collective-permute-start | bytes 33800 | tf_op jit(solution)/shard_map/ppermute | solution.py:233
  6.7 20.5 %copy-start.4 = (f32[256,256]{1,0:T(8,128)S(1)}, f32[256,256]{1,0:T(8,128)}, u32[]{:S(2)}) copy-start(f32[256,256]{1,0:T(8,128)} %refs_11_.1) | copy-start | bytes 786436
  6.8 10.4 %collective-permute-start.1 = (f32[22,128]{1,0:T(8,128)S(1)}, f32[22,128]{1,0:T(8,128)S(1)}, u32[]{:S(2)}, u32[]{:S(2)}) collective-permute-start(f32[22,128]{1,0:T(8,128)S(1)} %pad_maximum_fusion.2), channel_id=1, source_target_pairs={{0,8},{8,16},{16,24},{1,9},{9,17},{17,25},{2,10},{10,18},{18,26},{... | collective-permute-start | bytes 33800 | tf_op jit(solution)/shard_map/ppermute | solution.py:232
  11.8 15.3 %copy-start.1 = (bf16[4,9,128,128]{3,2,1,0:T(8,128)(2,1)S(1)}, bf16[4,9,128,128]{3,2,1,0:T(8,128)(2,1)}, u32[]{:S(2)}) copy-start(bf16[4,9,128,128]{3,2,1,0:T(8,128)(2,1)} %refs_6_.1) | copy-start | bytes 3538948
  11.9 15.3 %copy-start.3 = (f32[512,512]{1,0:T(8,128)S(1)}, f32[512,512]{1,0:T(8,128)}, u32[]{:S(2)}) copy-start(f32[512,512]{1,0:T(8,128)} %refs_4_.1) | copy-start | bytes 3145732
  19.9 5.6 %collective-permute-start.3 = (f32[22,132]{1,0:T(8,128)}, f32[22,132]{1,0:T(8,128)S(1)}, u32[]{:S(2)}, u32[]{:S(2)}) collective-permute-start(f32[22,132]{1,0:T(8,128)} %get-tuple-element.36.refs_6_), channel_id=1, source_target_pairs={{0,1},{1,2},{2,3},{3,4},{4,5},{5,6},{6,7},{8,9},{9,10},{10,11},{11... | collective-permute-start | bytes 34856 | tf_op jit(solution)/shard_map/ppermute | solution.py:254
  21.8 64.1 %copy-start.24 = (f32[1,2,2]{2,1,0:T(2,128)S(1)}, f32[1,2,2]{2,1,0:T(2,128)}, u32[]{:S(2)}) copy-start(f32[1,2,2]{2,1,0:T(2,128)} %param.20) | copy-start | bytes 52
  21.8 5.4 %collective-permute-start.4 = (f32[22,132]{1,0:T(8,128)}, f32[22,132]{1,0:T(8,128)S(1)}, u32[]{:S(2)}, u32[]{:S(2)}) collective-permute-start(f32[22,132]{1,0:T(8,128)} %get-tuple-element.37.refs_5_), channel_id=1, source_target_pairs={{1,0},{2,1},{3,2},{4,3},{5,4},{6,5},{7,6},{9,8},{10,9},{11,10},{12... | collective-permute-start | bytes 34856 | tf_op jit(solution)/shard_map/ppermute | solution.py:255
  32.4 53.5 %copy-start.2 = (bf16[1,2,1024,1024]{3,2,1,0:T(8,128)(2,1)S(1)}, bf16[1,2,1024,1024]{3,2,1,0:T(8,128)(2,1)}, u32[]{:S(2)}) copy-start(bf16[1,2,1024,1024]{3,2,1,0:T(8,128)(2,1)} %refs_10_.3) | copy-start | bytes 12582916
  32.4 53.5 %copy-start.5 = (bf16[1,2,1024,512]{3,2,1,0:T(8,128)(2,1)S(1)}, bf16[1,2,1024,512]{3,2,1,0:T(8,128)(2,1)}, u32[]{:S(2)}) copy-start(bf16[1,2,1024,512]{3,2,1,0:T(8,128)(2,1)} %refs_8_.3) | copy-start | bytes 6291460
  37.0 14.2 %collective-permute-start.7 = (bf16[512,512]{1,0:T(8,128)(2,1)S(1)}, bf16[512,512]{1,0:T(8,128)(2,1)S(1)}, u32[]{:S(2)}, u32[]{:S(2)}) collective-permute-start(bf16[512,512]{1,0:T(8,128)(2,1)S(1)} %get-tuple-element.38.refs_0_), channel_id=1, source_target_pairs={{0,6},{1,7},{2,0},{3,1},{4,2},{5,3},{6,4},{7,5},{8,14},{9,15},{10,... | collective-permute-start | bytes 1572872 | tf_op jit(solution)/shard_map/ppermute | solution.py:686
  37.1 35.7 %collective-permute-start.6 = (bf16[512,512]{1,0:T(8,128)(2,1)S(1)}, bf16[512,512]{1,0:T(8,128)(2,1)S(1)}, u32[]{:S(2)}, u32[]{:S(2)}) collective-permute-start(bf16[512,512]{1,0:T(8,128)(2,1)S(1)} %get-tuple-element.38.refs_0_), channel_id=1, source_target_pairs={{0,4},{1,5},{2,6},{3,7},{4,0},{5,1},{6,2},{7,3},{8,12},{9,13},{10,... | collective-permute-start | bytes 1572872 | tf_op jit(solution)/shard_map/ppermute | solution.py:686
  40.1 43.9 %collective-permute-start.5 = (bf16[512,512]{1,0:T(8,128)(2,1)S(1)}, bf16[512,512]{1,0:T(8,128)(2,1)S(1)}, u32[]{:S(2)}, u32[]{:S(2)}) collective-permute-start(bf16[512,512]{1,0:T(8,128)(2,1)S(1)} %get-tuple-element.38.refs_0_), channel_id=1, source_target_pairs={{0,2},{1,3},{2,4},{3,5},{4,6},{5,7},{6,0},{7,1},{8,10},{9,11},{10,... | collective-permute-start | bytes 1572872 | tf_op jit(solution)/shard_map/ppermute | solution.py:686
  42.6 41.6 %collective-permute-start.8 = (bf16[512,512]{1,0:T(8,128)(2,1)S(1)}, bf16[512,512]{1,0:T(8,128)(2,1)S(1)}, u32[]{:S(2)}, u32[]{:S(2)}) collective-permute-start(bf16[512,512]{1,0:T(8,128)(2,1)S(1)} %get-tuple-element.38.refs_0_), channel_id=1, source_target_pairs={{0,1},{1,0},{2,3},{3,2},{4,5},{5,4},{6,7},{7,6},{8,9},{9,8},{10,11... | collective-permute-start | bytes 1572872 | tf_op jit(solution)/shard_map/ppermute | solution.py:690
  51.2 33.0 %collective-permute-start.11 = (bf16[512,512]{1,0:T(8,128)(2,1)S(1)}, bf16[512,512]{1,0:T(8,128)(2,1)S(1)}, u32[]{:S(2)}, u32[]{:S(2)}) collective-permute-start(bf16[512,512]{1,0:T(8,128)(2,1)S(1)} %collective-permute-done.7.refs_3_), channel_id=1, source_target_pairs={{0,1},{1,0},{2,3},{3,2},{4,5},{5,4},{6,7},{7,6},{8,9},{9,8},{10,11... | collective-permute-start | bytes 1572872 | tf_op jit(solution)/shard_map/ppermute | solution.py:690
  72.7 11.4 %collective-permute-start.10 = (bf16[512,512]{1,0:T(8,128)(2,1)S(1)}, bf16[512,512]{1,0:T(8,128)(2,1)S(1)}, u32[]{:S(2)}, u32[]{:S(2)}) collective-permute-start(bf16[512,512]{1,0:T(8,128)(2,1)S(1)} %collective-permute-done.6.refs_2_), channel_id=1, source_target_pairs={{0,1},{1,0},{2,3},{3,2},{4,5},{5,4},{6,7},{7,6},{8,9},{9,8},{10,11... | collective-permute-start | bytes 1572872 | tf_op jit(solution)/shard_map/ppermute | solution.py:690
  84.0 1.9 %collective-permute-start.9 = (bf16[512,512]{1,0:T(8,128)(2,1)S(1)}, bf16[512,512]{1,0:T(8,128)(2,1)S(1)}, u32[]{:S(2)}, u32[]{:S(2)}) collective-permute-start(bf16[512,512]{1,0:T(8,128)(2,1)S(1)} %collective-permute-done.5.refs_1_), channel_id=1, source_target_pairs={{0,1},{1,0},{2,3},{3,2},{4,5},{5,4},{6,7},{7,6},{8,9},{9,8},{10,11... | collective-permute-start | bytes 1572872 | tf_op jit(solution)/shard_map/ppermute | solution.py:690
  85.9 70.3 %slice-start = ((s8[4718592]{0:T(1024)(128)(4,1)}), s8[4194304]{0:T(1024)(128)(4,1)S(1)}, s32[]{:S(2)}) async-start(s8[4718592]{0:T(1024)(128)(4,1)} %bitcast.13), calls=%async_computation | async-start | bytes 8388608
  87.6 68.5 %slice-start.1 = ((s8[4718592]{0:T(1024)(128)(4,1)}), s8[524288]{0:T(1024)(128)(4,1)S(1)}, s32[]{:S(2)}) async-start(s8[4718592]{0:T(1024)(128)(4,1)} %bitcast.13), calls=%async_computation.1 | async-start | bytes 1048576
  93.8 62.4 %copy-start.10 = (f32[22,128]{1,0:T(8,128)S(1)}, f32[22,128]{1,0:T(8,128)}, u32[]{:S(2)}) copy-start(f32[22,128]{1,0:T(8,128)} %copy-done.8) | copy-start | bytes 33796
  93.8 62.4 %copy-start.13 = (f32[22,128]{1,0:T(8,128)S(1)}, f32[22,128]{1,0:T(8,128)}, u32[]{:S(2)}) copy-start(f32[22,128]{1,0:T(8,128)} %copy-done.11) | copy-start | bytes 33796
  93.8 4.5 %collective-permute-start.12 = (bf16[1056,512]{1,0:T(8,128)(2,1)S(1)}, bf16[1056,512]{1,0:T(8,128)(2,1)S(1)}, u32[]{:S(2)}, u32[]{:S(2)}) collective-permute-start(bf16[1056,512]{1,0:T(8,128)(2,1)S(1)} %facets.1.mine), channel_id=1, source_target_pairs={{0,1},{1,0},{2,3},{3,2},{4,5},{5,4},{6,7},{7,6},{8,9},{9,8},{10,11... | collective-permute-start | bytes 3244040 | tf_op jit(solution)/shard_map/ppermute | solution.py:690
  100.5 18.9 %collective-permute-start.13 = (bf16[544,512]{1,0:T(8,128)(2,1)S(1)}, bf16[544,512]{1,0:T(8,128)(2,1)S(1)}, u32[]{:S(2)}, u32[]{:S(2)}) collective-permute-start(bf16[544,512]{1,0:T(8,128)(2,1)S(1)} %get-tuple-element.41), channel_id=1, source_target_pairs={{0,2},{1,3},{2,4},{3,5},{4,6},{5,7},{6,0},{7,1},{8,10},{9,11},{10,... | collective-permute-start | bytes 1671176 | tf_op jit(solution)/shard_map/ppermute | solution.py:686
  104.9 48.2 %collective-permute-start.14 = (bf16[544,512]{1,0:T(8,128)(2,1)S(1)}, bf16[544,512]{1,0:T(8,128)(2,1)S(1)}, u32[]{:S(2)}, u32[]{:S(2)}) collective-permute-start(bf16[544,512]{1,0:T(8,128)(2,1)S(1)} %get-tuple-element.42), channel_id=1, source_target_pairs={{0,4},{1,5},{2,6},{3,7},{4,0},{5,1},{6,2},{7,3},{8,12},{9,13},{10,... | collective-permute-start | bytes 1671176 | tf_op jit(solution)/shard_map/ppermute | solution.py:686
  108.2 47.9 %collective-permute-start.15 = (bf16[544,512]{1,0:T(8,128)(2,1)S(1)}, bf16[544,512]{1,0:T(8,128)(2,1)S(1)}, u32[]{:S(2)}, u32[]{:S(2)}) collective-permute-start(bf16[544,512]{1,0:T(8,128)(2,1)S(1)} %get-tuple-element.43), channel_id=1, source_target_pairs={{0,6},{1,7},{2,0},{3,1},{4,2},{5,3},{6,4},{7,5},{8,14},{9,15},{10,... | collective-permute-start | bytes 1671176 | tf_op jit(solution)/shard_map/ppermute | solution.py:686
  162.5 9.2 %collective-permute-start.16 = (f32[8,384]{1,0:T(8,128)S(1)}, f32[8,384]{1,0:T(8,128)S(1)}, u32[]{:S(2)}, u32[]{:S(2)}) collective-permute-start(f32[8,384]{1,0:T(8,128)S(1)} %get-tuple-element.46), channel_id=1, source_target_pairs={{0,1},{1,2},{2,3},{3,4},{4,5},{5,6},{6,7},{8,9},{9,10},{10,11},{11... | collective-permute-start | bytes 36872 | tf_op jit(solution)/shard_map/ppermute | solution.py:524
  164.4 7.3 %collective-permute-start.17 = (f32[8,384]{1,0:T(8,128)S(1)}, f32[8,384]{1,0:T(8,128)S(1)}, u32[]{:S(2)}, u32[]{:S(2)}) collective-permute-start(f32[8,384]{1,0:T(8,128)S(1)} %get-tuple-element.47), channel_id=1, source_target_pairs={{1,0},{2,1},{3,2},{4,3},{5,4},{6,5},{7,6},{9,8},{10,9},{11,10},{12... | collective-permute-start | bytes 36872 | tf_op jit(solution)/shard_map/ppermute | solution.py:525
  168.0 3.7 %collective-permute-start.18 = (f32[8,128]{1,0:T(8,128)S(1)}, f32[8,128]{1,0:T(8,128)S(1)}, u32[]{:S(2)}, u32[]{:S(2)}) collective-permute-start(f32[8,128]{1,0:T(8,128)S(1)} %get-tuple-element.50.total), channel_id=1, source_target_pairs={{0,8},{8,0},{16,24},{24,16},{1,9},{9,1},{17,25},{25,17},{2,10},{10... | collective-permute-start | bytes 12296 | tf_op jit(solution)/shard_map/ppermute | solution.py:531
  173.8 9.7 %collective-permute-start.19 = (f32[8,256]{1,0:T(8,128)}, f32[8,256]{1,0:T(8,128)S(1)}, u32[]{:S(2)}, u32[]{:S(2)}) collective-permute-start(f32[8,256]{1,0:T(8,128)} %get-tuple-element.51), channel_id=1, source_target_pairs={{0,8},{8,16},{16,24},{1,9},{9,17},{17,25},{2,10},{10,18},{18,26},{... | collective-permute-start | bytes 24584 | tf_op jit(solution)/shard_map/ppermute | solution.py:542
  176.3 7.2 %collective-permute-start.20 = (f32[8,256]{1,0:T(8,128)}, f32[8,256]{1,0:T(8,128)S(1)}, u32[]{:S(2)}, u32[]{:S(2)}) collective-permute-start(f32[8,256]{1,0:T(8,128)} %get-tuple-element.52), channel_id=1, source_target_pairs={{8,0},{16,8},{24,16},{9,1},{17,9},{25,17},{10,2},{18,10},{26,18},{... | collective-permute-start | bytes 24584 | tf_op jit(solution)/shard_map/ppermute | solution.py:541
  179.6 3.9 %collective-permute-start.21 = (f32[8,128]{1,0:T(8,128)}, f32[8,128]{1,0:T(8,128)S(1)}, u32[]{:S(2)}, u32[]{:S(2)}) collective-permute-start(f32[8,128]{1,0:T(8,128)} %get-tuple-element.53.total), channel_id=1, source_target_pairs={{0,16},{8,24},{16,0},{24,8},{1,17},{9,25},{17,1},{25,9},{2,18},{10... | collective-permute-start | bytes 12296 | tf_op jit(solution)/shard_map/ppermute | solution.py:531
  (19 other events, 51.4 us)

commit v6 on v5

--- a/solution.py
+++ b/solution.py
@@ -8,6 +8,8 @@
 from jax.sharding import PartitionSpec as P
 
 inv_noise = 0.125
+long_work = pl.CostEstimate(flops=40_000_000_000, transcendentals=0, bytes_accessed=64_000_000)
+border = 8
 vmem = 32 * 1024 * 1024
 f32 = jnp.float32
 bf16 = jnp.bfloat16
@@ -101,18 +103,72 @@
     field[2] = jnp.where(lane == cols - 1, placed, pltpu.roll(here, cols - 1, 1))
 
 
-def sky_kernel(*refs):
-    sources, (sky_ref, sq_ref), held, rest = refs[:11], refs[11:13], refs[13:24], refs[24:]
-    win, perm, lhs, mix, near_coarse, shifted, fine_win, fine_perm, fine_lhs, fine_mix, sems = rest
-    copies = fetched(zip(sources, held), sems)
-    xi_coarse, above, below, lefts, rights, to_left, to_right = held[:7]
+def strips_of(tile, out):
+    rows, cols = tile.shape
+    first, last = tile[: 2 * border].astype(f32), tile[rows - 2 * border :].astype(f32)
+    out[: 2 * border] = jnp.concatenate([first[:border], last[border:]]).astype(bf16)
+    index = lax.broadcasted_iota(jnp.int32, (2 * border, cols), 0)
+    lane = lax.broadcasted_iota(jnp.int32, (2 * border, cols), 1)
+    pick = lane == jnp.where(index < border, index, index + cols - 2 * border)
+    pick = pick.astype(f32).astype(bf16)
+    out[2 * border : 4 * border] = dot_t(pick, tile[...], ((1,), (1,))).astype(bf16)
+
+
+def columns_of(strip):
+    index = lax.broadcasted_iota(jnp.int32, (2 * border, 128), 0)
+    lane = lax.broadcasted_iota(jnp.int32, (2 * border, 128), 1)
+    out = []
+    for place in (
+        (index < border) & (lane == index),
+        (index >= border) & (lane == index + 128 - 2 * border),
+    ):
+        out.append(dot_t(strip, place.astype(f32).astype(bf16), ((0,), (0,))))
+    return out
+
+
+def stretch(out, side, over, under, b, lane, first):
+    rows = side.shape[1]
+    out[...] = jnp.zeros_like(out)
+    out[:, 2 : rows + 2] = side[...]
+    out[9:18, 1:2] = over[9 * b : 9 * b + 9, lane : lane + 1]
+    out[21:22, 1:2] = over[20 + b : 21 + b, lane : lane + 1]
+    out[0:9, rows + 2 : rows + 3] = under[9 * b : 9 * b + 9, lane : lane + 1]
+    out[20:21, rows + 2 : rows + 3] = under[20 + b : 21 + b, lane : lane + 1]
+    for k in range(2):
+        at = slice(first + k, first + k + 1)
+        for i in range(2):
+            out[18 + k : 19 + k, i : i + 1] = over[18 + i : 19 + i, at]
+            end = rows + 2 + i
+            out[18 + k : 19 + k, end : end + 1] = under[18 + i : 19 + i, at]
+
+
+def sky_kernel(alone, *refs):
+    count = 5 if alone else 11
+    sources, refs = refs[:count], refs[count:]
+    outs, refs = (refs[:1], refs[1:]) if alone else (refs[:5], refs[5:])
+    held, rest = refs[:11], refs[11:]
+    win, perm, lhs, mix, near_coarse, shifted, fine_win, fine_perm, fine_lhs, fine_mix = rest[:10]
+    lefts, rights, to_left, to_right, sems = rest[10:]
+    sky_ref = outs[0]
+    if alone:
+        for ref in held[1:7]:
+            ref[...] = jnp.zeros_like(ref)
+        copies = fetched(zip(sources, (held[0],) + tuple(held[7:])), sems)
+    else:
+        copies = fetched(zip(sources, held), sems)
+    xi_coarse, over, under, left_in, right_in, left_side, right_side = held[:7]
     coef_middle, xi_middle, coef_fine, xi_fine = held[7:]
     rows, cols = win.shape[1:]
     perm[...] = interleaver(cols, False)
     fine_perm[...] = interleaver(2 * cols, False)
     near_coarse[...] = jnp.zeros_like(near_coarse)
-    for copy in copies[:8]:
+    for copy in copies[:-3]:
         copy.wait()
+    above, below = over[:, 2 : cols + 2], under[:, 2 : cols + 2]
+    stretch(lefts, left_in, over, under, 1, 1, 0)
+    stretch(rights, right_in, over, under, 0, cols + 2, cols + 2)
+    stretch(to_left, left_side, over, under, 0, 2, 2)
+    stretch(to_right, right_side, over, under, 1, cols + 1, cols)
     near_coarse[1, 6:8] = above[18:20]
     near_coarse[1, 8 : 8 + rows] = xi_coarse[...]
     near_coarse[1, 8 + rows : 10 + rows] = below[18:20]
@@ -157,7 +213,7 @@
     )
     lines = jnp.concatenate([top, bottom, left, right, jnp.zeros((4, 2 * cols), f32)])
     lines = moved(lines, perm[...])
-    copies[8].wait()
+    copies[-3].wait()
     xi = xi_middle[...]
     last = 8 + 2 * rows
     shifted[1] = jnp.zeros(shifted.shape[1:], f32)
@@ -178,35 +234,27 @@
     for near in range(9):
         r, c = near // 3, near % 3
         fine_win[near] = shifted[c, 7 + r : 7 + r + 2 * rows, :]
-    copies[9].wait()
+    copies[-2].wait()
     weighed(fine_win, coef_fine, fine_perm, fine_lhs, fine_mix, 2 * rows, 2 * cols)
-    copies[10].wait()
+    copies[-1].wait()
     for tile in range(4 * cols // 128):
         lanes = slice(tile * 128, (tile + 1) * 128)
         sky_ref[:, lanes] = (fine_mix[tile] + xi_fine[:, lanes]).astype(bf16)
+    if alone:
+        return
+    strips_ref, sq_ref, lefts_ref, rights_ref = outs[1:]
+    lefts_ref[...] = lefts[...]
+    rights_ref[...] = rights[...]
+    strips_of(sky_ref, strips_ref)
     sq_ref[...] = (
         folded(win[4] * win[4]) + folded(xi * xi) + folded(xi_fine[...] * xi_fine[...])
     )
 
 
-def sides_kernel(above, below, left_side, right_side, to_left, to_right):
-    rows, cols = left_side.shape[1], above.shape[1]
-    for out, side, b, col, first in (
-        (to_left, left_side, 0, 0, 0),
-        (to_right, right_side, 1, cols - 1, cols - 2),
-    ):
-        out[...] = jnp.zeros_like(out)
-        out[:, 2 : rows + 2] = side[...]
-        out[9:18, 1:2] = above[9 * b : 9 * b + 9, col : col + 1]
-        out[21:22, 1:2] = above[20 + b : 21 + b, col : col + 1]
-        out[0:9, rows + 2 : rows + 3] = below[9 * b : 9 * b + 9, col : col + 1]
-        out[20:21, rows + 2 : rows + 3] = below[20 + b : 21 + b, col : col + 1]
-        for k in range(2):
-            at = slice(first + k, first + k + 1)
-            for i in range(2):
-                out[18 + k : 19 + k, i : i + 1] = above[18 + i : 19 + i, at]
-                lane = rows + 2 + i
-                out[18 + k : 19 + k, lane : lane + 1] = below[18 + i : 19 + i, at]
+def sides_kernel(left_in, right_in, first_side, last_side, to_above, to_below):
+    rows = left_in.shape[1]
+    stretch(to_above, first_side, left_in, right_in, 0, 0, 0)
+    stretch(to_below, last_side, left_in, right_in, 1, rows - 1, rows - 2)
 
 
 def neighbours(axis):
@@ -215,10 +263,23 @@
     return ahead, [(j, i) for i, j in ahead]
 
 
-def halo(xi_coarse, xi_middle, coef_middle, extra):
+def halo_sides(xi_coarse, xi_middle, coef_middle):
     rows, cols = xi_coarse.shape
-    down, up = neighbours("gx")
-    right, left = neighbours("gy")
+
+    def inside(b, col, near):
+        return jnp.concatenate(
+            [
+                coef_middle[b::2, :, :, col].reshape(18, rows).astype(f32),
+                near.T,
+                xi_middle[:, 2 * col + b].reshape(rows, 2).T,
+            ]
+        )
+
+    return inside(0, 0, xi_coarse[:, :2]), inside(1, cols - 1, xi_coarse[:, -2:])
+
+
+def halo_rows(xi_coarse, xi_middle, coef_middle, left_in, right_in):
+    rows, cols = xi_coarse.shape
 
     def edge(a, row, near):
         return jnp.concatenate(
@@ -229,50 +290,43 @@
             ]
         )
 
-    above = lax.ppermute(edge(1, rows - 1, xi_coarse[-2:]), "gx", down)
-    below = lax.ppermute(edge(0, 0, xi_coarse[:2]), "gx", up)
-
-    def inside(b, col, near):
-        return jnp.concatenate(
-            [
-                coef_middle[b::2, :, :, col].reshape(18, rows).astype(f32),
-                near.T,
-                xi_middle[:, 2 * col + b].reshape(rows, 2).T,
-            ]
-        )
-
-    sides = inside(0, 0, xi_coarse[:, :2]), inside(1, cols - 1, xi_coarse[:, -2:])
-    sides, extra = lax.optimization_barrier((sides, extra))
-
-    to_left, to_right = pl.pallas_call(
+    to_above, to_below = pl.pallas_call(
         sides_kernel,
         in_specs=[whole] * 4,
         out_specs=[whole] * 2,
-        out_shape=[jax.ShapeDtypeStruct((22, rows + 4), f32)] * 2,
+        out_shape=[jax.ShapeDtypeStruct((22, cols + 4), f32)] * 2,
+        cost_estimate=long_work,
         name="sides",
-    )(above, below, *sides)
-    lefts = lax.ppermute(to_right, "gy", right)
-    rights = lax.ppermute(to_left, "gy", left)
-    return (above, below, lefts, rights, to_left, to_right), extra
+    )(left_in, right_in, edge(0, 0, xi_coarse[:2]), edge(1, rows - 1, xi_coarse[-2:]))
+    down, up = neighbours("gx")
+    return lax.ppermute(to_below, "gx", down), lax.ppermute(to_above, "gx", up)
 
 
 whole = pl.BlockSpec(memory_space=pltpu.VMEM)
 scalar = pl.BlockSpec(memory_space=pltpu.SMEM)
-anywhere = pl.BlockSpec(memory_space=pl.ANY)
+anywhere = pl.BlockSpec(memory_space=pltpu.HBM)
 
 
 def sky_of(halos, xi_coarse, coef_middle, xi_middle, coef_fine, xi_fine):
     rows, cols = coef_middle.shape[2:]
-    operands = (xi_coarse, *halos, coef_middle, xi_middle, coef_fine, xi_fine)
+    alone = halos is None
+    given = (coef_middle, xi_middle, coef_fine, xi_fine)
+    operands = (xi_coarse, *given) if alone else (xi_coarse, *halos, *given)
+    message = [(22, cols + 4)] * 2 + [(22, rows)] * 4
     return pl.pallas_call(
-        sky_kernel,
-        in_specs=[anywhere] * 11,
-        out_specs=[whole] * 2,
+        functools.partial(sky_kernel, alone),
+        in_specs=[anywhere] * len(operands),
+        out_specs=[whole] * (1 if alone else 5),
         out_shape=[
             jax.ShapeDtypeStruct((4 * rows, 4 * cols), bf16),
+            jax.ShapeDtypeStruct((4 * border, 4 * cols), bf16),
             jax.ShapeDtypeStruct((8, 128), f32),
-        ],
-        scratch_shapes=[pltpu.VMEM(x.shape, x.dtype) for x in operands]
+            jax.ShapeDtypeStruct((22, rows + 4), f32),
+            jax.ShapeDtypeStruct((22, rows + 4), f32),
+        ][: 1 if alone else 5],
+        scratch_shapes=[pltpu.VMEM(xi_coarse.shape, f32)]
+        + [pltpu.VMEM(shape, f32) for shape in message]
+        + [pltpu.VMEM(x.shape, x.dtype) for x in given]
         + [
             pltpu.VMEM((9, rows, cols), f32),
             pltpu.VMEM((2 * cols, 2 * cols), bf16),
@@ -284,9 +338,10 @@
             pltpu.VMEM((4 * cols, 4 * cols), bf16),
             pltpu.VMEM((8 * rows, 4 * cols), bf16),
             pltpu.VMEM((4 * cols // 128, 4 * rows, 128), f32),
+            *[pltpu.VMEM((22, rows + 4), f32) for _ in range(4)],
             pltpu.SemaphoreType.DMA((11,)),
         ],
-        compiler_params=pltpu.CompilerParams(vmem_limit_bytes=vmem),
+        compiler_params=pltpu.CompilerParams(vmem_limit_bytes=60 * 1024 * 1024),
         name="sky",
     )(*operands)
 
@@ -327,27 +382,45 @@
     return main, outside[0], outside[1]
 
 
-def adjoint_kernel(number, *refs):
-    parts, sources, outs = refs[:number], refs[number : number + 9], refs[number + 9 : number + 17]
-    held, rest = refs[number + 17 : number + 26], refs[number + 26 :]
-    grad_ref, middle_ref, coarse_ref, left_ref, right_ref, upper_ref, lower_ref, total_ref = outs
-    fine_perm, fine_mix, fine_terms, fine_rowed, perm, mix, terms, rowed, sems = rest
+def adjoint_kernel(edge, number, *refs):
+    count = 6 if edge else 9
+    parts, sources = refs[:number], refs[number : number + count]
+    outs, refs = refs[number + count :][: 5 if edge else 3], refs[number + count :][5 if edge else 3 :]
+    held, rest = refs[:count], refs[count:]
+    fine_perm, fine_mix, fine_terms, fine_rowed, perm, mix, terms, rowed, full, sems, out_sem = rest
     copies = fetched(zip(sources, held), sems)
-    xi_fine, coef_fine, coef_middle, above, below, lefts, rights, xi_middle, xi_coarse = held
+    coef_fine, coef_middle, over, under, lefts, rights = held[:6]
+    if edge:
+        left_ref, right_ref, upper_ref, lower_ref, total_ref = outs
+    else:
+        grad_ref, middle_ref, coarse_ref = outs
+        xi_fine, xi_middle, xi_coarse = held[6:]
     rows, cols = terms.shape[1:]
     fine_perm[...] = interleaver(2 * cols, True)
     perm[...] = interleaver(cols, True)
-    g = parts[0][: 4 * rows].astype(f32)
+    g = parts[0][...].astype(f32)
     for part in parts[1:]:
-        g += part[: 4 * rows].astype(f32)
-    copies[0].wait()
-    grad_ref[...] = g + xi_fine[...]
-    tail = sum(part[4 * rows :, :128].astype(f32) for part in parts)
-    total_ref[...] = tail[:8] + tail[8:16] + tail[16:24]
+        g += part[...].astype(f32)
+    if edge:
+        tail = g[4 * border :, :128]
+        total_ref[...] = tail[:8] + tail[8:16] + tail[16:24]
+        high, low = halves(g[2 * border : 4 * border])
+        left, right = [x + y for x, y in zip(columns_of(high), columns_of(low))]
+        full[...] = jnp.zeros_like(full)
+        full[:, :128] = left
+        full[:, 4 * cols - 128 :] = right
+        full[:border] = g[:border]
+        full[4 * rows - border :] = g[border : 2 * border]
+        g = full[...]
+    else:
+        copies[6].wait()
+        full[...] = g + xi_fine[...]
+        leaving = pltpu.make_async_copy(full, grad_ref, out_sem)
+        leaving.start()
     split = moved(g, fine_perm[...])
     for tile in range(4 * cols // 128):
         fine_mix[tile] = split[:, tile * 128 : (tile + 1) * 128]
-    copies[1].wait()
+    copies[0].wait()
     spread(fine_mix, coef_fine, fine_terms, 2 * rows, 2 * cols)
     fine_rowed[...] = jnp.zeros_like(fine_rowed)
     for near in range(9):
@@ -356,9 +429,11 @@
     main, left, right = joined(fine_rowed, 2 * cols)
     last = 8 + 2 * rows
     inner = main[8:last]
-    for copy in copies[2:]:
+    for copy in copies[1:6] + copies[7:]:
         copy.wait()
-    middle_ref[...] = inner + xi_middle[...]
+    above, below = over[:, 2 : cols + 2], under[:, 2 : cols + 2]
+    if not edge:
+        middle_ref[...] = inner + xi_middle[...]
     split = moved(inner, perm[...])
     for tile in range(2 * cols // 128):
         mix[tile] = split[:, tile * 128 : (tile + 1) * 128]
@@ -398,44 +473,58 @@
     outer_left = along(2, left, lefts)
     outer_right = along(3, right, rights)
     main, near_left, near_right = joined(rowed, cols)
-    coarse_ref[...] = (
-        main[8 : 8 + rows]
-        + xi_coarse[...]
-        + ends_placed(outer_left[2][:, 2 : rows + 2], outer_right[0][:, 2 : rows + 2], cols)
-    )
-    lane = lax.broadcasted_iota(jnp.int32, (1, cols), 1)
-    for ref, first, line in ((upper_ref, 6, ring_above), (lower_ref, 8 + rows, ring_below)):
-        ref[...] = jnp.zeros_like(ref)
-        for i in range(2):
-            at = first - 6 + i
-            ref[i : i + 1, :cols] = (
-                main[first + i : first + i + 1]
-                + jnp.where(lane == 0, outer_left[2][:, at : at + 1], 0.0)
-                + jnp.where(lane == cols - 1, outer_right[0][:, at : at + 1], 0.0)
-            )
-        ref[2:3, :] = line
+    if not edge:
+        coarse_ref[...] = (
+            main[8 : 8 + rows]
+            + xi_coarse[...]
+            + ends_placed(outer_left[2][:, 2 : rows + 2], outer_right[0][:, 2 : rows + 2], cols)
+        )
+        leaving.wait()
+        return
+    sides = []
     for ref, far, close, beyond, ends in (
         (left_ref, outer_left[0], outer_left[1], near_left, left),
         (right_ref, outer_right[2], outer_right[1], near_right, right),
     ):
+        close += beyond[:, 6 : rows + 10]
+        ends = ends[:, 7 : 2 * rows + 9]
         ref[...] = jnp.zeros_like(ref)
         ref[0:1, : rows + 4] = far
-        ref[1:2, : rows + 4] = close + beyond[:, 6 : rows + 10]
-        ref[2:3, : 2 * rows + 2] = ends[:, 7 : 2 * rows + 9]
-
-
-def corners_kernel(upper, lower, from_left, from_right, total, other, upper_out, lower_out, total_out):
-    rows, cols = lower.shape[1] // 2, lower.shape[1] // 2
-    for ref, out, at, end in ((upper, upper_out, 0, 0), (lower, lower_out, rows + 2, 2 * rows + 1)):
+        ref[1:2, : rows + 4] = close
+        ref[2:3, : 2 * rows + 2] = ends
+        sides.append((far, close, ends))
+    lane = lax.broadcasted_iota(jnp.int32, (1, cols), 1)
+    (far_left, close_left, ends_left), (far_right, close_right, ends_right) = sides
+    for ref, first, line, end in (
+        (upper_ref, 6, ring_above, 0),
+        (lower_ref, 8 + rows, ring_below, 2 * rows + 1),
+    ):
+        ref[...] = jnp.zeros_like(ref)
+        for i in range(2):
+            at = slice(first - 6 + i, first - 5 + i)
+            inner = (
+                main[first + i : first + i + 1]
+                + jnp.where(lane == 0, outer_left[2][:, at], 0.0)
+                + jnp.where(lane == cols - 1, outer_right[0][:, at], 0.0)
+            )
+            pieces = [far_left[:, at], close_left[:, at], inner, close_right[:, at], far_right[:, at]]
+            ref[i : i + 1, : cols + 4] = jnp.concatenate(pieces, axis=1)
+        pieces = [ends_left[:, end : end + 1], line, ends_right[:, end : end + 1]]
+        ref[2:3, : 2 * cols + 2] = jnp.concatenate(pieces, axis=1)
+
+
+def corners_kernel(rows, cols, left, right, from_above, from_below, total, other, left_out, right_out, total_out):
+    for ref, out, far, close, end in (
+        (left, left_out, 0, 1, 0),
+        (right, right_out, cols + 3, cols + 2, 2 * cols + 1),
+    ):
         out[...] = ref[...]
-        for i in range(2):
-            here = slice(at + i, at + i + 1)
-            out[i : i + 1, 0:1] += from_left[1:2, here]
-            out[i : i + 1, 1:2] += from_left[0:1, here]
-            out[i : i + 1, cols - 2 : cols - 1] += from_right[0:1, here]
-            out[i : i + 1, cols - 1 : cols] += from_right[1:2, here]
-        out[2:3, 0:1] += from_left[2:3, end : end + 1]
-        out[2:3, 2 * cols - 1 :] += from_right[2:3, end : end + 1]
+        for rows_in, first, line in ((from_above, 2, 1), (from_below, rows, 2 * rows)):
+            for i in range(2):
+                at = slice(first + i, first + i + 1)
+                out[0:1, at] += rows_in[i : i + 1, far : far + 1]
+                out[1:2, at] += rows_in[i : i + 1, close : close + 1]
+            out[2:3, line : line + 1] += rows_in[2:3, end : end + 1]
     total_out[...] = total[...] + other[...]
 
 
@@ -457,8 +546,9 @@
     middle_out[...] = middle[...] + ends_placed(
         from_left[2:3, 1 : 2 * rows + 1], from_right[2:3, 1 : 2 * rows + 1], 2 * cols
     )
-    middle_out[:1] += from_above[2:3]
-    middle_out[2 * rows - 1 :] += from_below[2:3]
+    line = slice(1, 2 * cols + 1)
+    middle_out[:1] += from_above[2:3, line]
+    middle_out[2 * rows - 1 :] += from_below[2:3, line]
     inner = slice(2, rows + 2)
     outer = ends_placed(from_left[1:2, inner], from_right[1:2, inner], cols)
     second = ends_placed(from_left[0:1, inner], from_right[0:1, inner], cols)
@@ -467,43 +557,33 @@
         lane == cols - 2, pltpu.roll(second, cols - 1, 1), 0.0
     )
     coarse_out[...] = coarse[...] + outer + second
-    coarse_out[:2] += from_above[0:2, :cols]
-    coarse_out[rows - 2 :] += from_below[0:2, :cols]
+    line = slice(2, cols + 2)
+    coarse_out[:2] += from_above[0:2, line]
+    coarse_out[rows - 2 :] += from_below[0:2, line]
     both = total[...] + other[...]
     both = jnp.sum(jnp.sum(both, axis=1, keepdims=True), axis=0, keepdims=True)
     total_out[...] = both * (1.0 / cells)
 
 
-def adjoint(parts, halos, coef_middle, xi_middle, coef_fine, xi_fine, xi_coarse):
-    rows, cols = coef_middle.shape[2:]
-    above, below, lefts, rights, _, _ = halos
-    shape = lambda *dims: jax.ShapeDtypeStruct(dims, f32)
-    long = 2 * rows + 128
-    operands = (
-        xi_fine,
-        coef_fine,
-        coef_middle,
-        above,
-        below,
-        lefts,
-        rights,
-        xi_middle,
-        xi_coarse,
-    )
-    grad_fine, middle, coarse, to_left, to_right, upper, lower, total = pl.pallas_call(
-        functools.partial(adjoint_kernel, len(parts)),
-        in_specs=[whole] * len(parts) + [anywhere] * 9,
-        out_specs=[whole] * 8,
-        out_shape=[
-            shape(4 * rows, 4 * cols),
-            shape(2 * rows, 2 * cols),
-            shape(rows, cols),
-            shape(8, long),
-            shape(8, long),
-            shape(8, 2 * cols),
-            shape(8, 2 * cols),
-            shape(8, 128),
-        ],
+def shape(*dims):
+    return jax.ShapeDtypeStruct(dims, f32)
+
+
+def adjoint(edge, parts, sides, fields):
+    rows, cols = fields[1].shape[2:]
+    xi_coarse, coef_middle, xi_middle, coef_fine, xi_fine = fields
+    wide = 2 * rows + 128
+    operands = (coef_fine, coef_middle, *sides)
+    if edge:
+        outs = [shape(8, wide)] * 2 + [shape(8, 2 * cols + 128)] * 2 + [shape(8, 128)]
+    else:
+        operands += (xi_fine, xi_middle, xi_coarse)
+        outs = [shape(4 * rows, 4 * cols), shape(2 * rows, 2 * cols), shape(rows, cols)]
+    return pl.pallas_call(
+        functools.partial(adjoint_kernel, edge, len(parts)),
+        in_specs=[whole] * len(parts) + [anywhere] * len(operands),
+        out_specs=[whole] * len(outs) if edge else [anywhere, whole, whole],
+        out_shape=outs,
         scratch_shapes=[pltpu.VMEM(x.shape, x.dtype) for x in operands]
         + [
             pltpu.VMEM((4 * cols, 4 * cols), bf16),
@@ -514,45 +594,14 @@
             pltpu.VMEM((2 * cols // 128, 2 * rows, 128), f32),
             pltpu.VMEM((9, rows, cols), f32),
             pltpu.VMEM((3, rows + 128, cols), f32),
-            pltpu.SemaphoreType.DMA((9,)),
+            pltpu.VMEM((4 * rows, 4 * cols), f32),
+            pltpu.SemaphoreType.DMA((len(operands),)),
+            pltpu.SemaphoreType.DMA,
         ],
         compiler_params=pltpu.CompilerParams(vmem_limit_bytes=vmem),
+        cost_estimate=long_work if edge else None,
         name="adjoint",
     )(*parts, *operands)
-    right, left = neighbours("gy")
-    down, up = neighbours("gx")
-    from_left = lax.ppermute(to_right, "gy", right)
-    from_right = lax.ppermute(to_left, "gy", left)
-
-    size = lax.axis_size("gx")
-    hops = [1 << i for i in range(size.bit_length()) if 1 << i < size]
-
-    def across(x, hop):
-        return lax.ppermute(x, "gx", [(i, i ^ hop) for i in range(size)])
-
-    other = across(total, hops[0])
-    upper, lower, total = pl.pallas_call(
-        corners_kernel,
-        in_specs=[whole] * 6,
-        out_specs=[whole] * 3,
-        out_shape=[shape(8, 2 * cols), shape(8, 2 * cols), shape(8, 128)],
-        name="corners",
-    )(upper, lower, from_left, from_right, total, other)
-    from_below = lax.ppermute(upper, "gx", up)
-    from_above = lax.ppermute(lower, "gx", down)
-    for hop in hops[1:-1]:
-        total += across(total, hop)
-    other = across(total, hops[-1])
-    cells = size * lax.axis_size("gy") * 16 * rows * cols
-    grad_middle, grad_coarse, total = pl.pallas_call(
-        functools.partial(final_kernel, cells),
-        in_specs=[whole] * 8,
-        out_specs=[whole] * 3,
-        out_shape=[shape(2 * rows, 2 * cols), shape(rows, cols), shape(1, 1)],
-        compiler_params=pltpu.CompilerParams(vmem_limit_bytes=vmem),
-        name="final",
-    )(middle, coarse, from_left, from_right, from_above, from_below, total, other)
-    return grad_coarse, grad_middle, grad_fine, total.reshape(())
 
 
 def in_three(x):
@@ -566,11 +615,11 @@
     return x[:8] + x[8:16] + x[16:24]
 
 
-def facets_kernel(blk, ints, weights, *refs):
+def facets_kernel(blk, early, chips, ints, weights, *refs):
     number, slots = weights.shape
-    tiles, rest = refs[:-14], refs[-14:]
+    tiles, strips, rest = refs[: 2 * chips], refs[2 * chips : 2 * chips + 2], refs[2 * chips + 2 :]
     ku_hbm, kv_hbm, data_hbm, squares, out_ref = rest[:5]
-    held, ku, kv, data, sums, dsum, total, sems, tile_sems = rest[5:]
+    held, held_strips, ku, kv, data, sums, dsum, total, sems, tile_sems, strip_sems = rest[5:]
     bins, side = ku.shape[1:]
 
     def inputs(f):
@@ -580,6 +629,13 @@
                 @pl.when(ints[f, s] == i)
                 def _():
                     pltpu.make_async_copy(tile, held.at[f, s], tile_sems.at[f, s]).start()
+                    hop = i % chips
+                    if 1 <= hop <= early:
+                        height = 4 * border
+                        strip = strips[i // chips].at[(hop - 1) * height : hop * height]
+                        pltpu.make_async_copy(
+                            strip, held_strips.at[f, s], strip_sems.at[f, s]
+                        ).start()
 
         pairs = ((ku_hbm, ku), (kv_hbm, kv), (data_hbm, data))
         copies = [
@@ -589,6 +645,29 @@
         for copy in copies:
             copy.start()
         return copies
+
+    def patch(f, s):
+        hop = lax.rem(ints[f, s], chips)
+
+        @pl.when((hop >= 1) & (hop <= early))
+        def _():
+            strip = strips[0].at[: 4 * border]
+            pltpu.make_async_copy(strip, held_strips.at[f, s], strip_sems.at[f, s]).wait()
+            tile, strip = held.at[f, s], held_strips.at[f, s]
+            lines = strip[: 2 * border].astype(f32)
+            top, bottom = tile[: 2 * border].astype(f32), tile[side - 2 * border :].astype(f32)
+            tile[: 2 * border] = jnp.concatenate([lines[:border], top[border:]]).astype(bf16)
+            tile[side - 2 * border :] = jnp.concatenate([bottom[:border], lines[border:]]).astype(
+                bf16
+            )
+            lane = lax.broadcasted_iota(jnp.int32, (side, 128), 1)
+            left, right = columns_of(strip[2 * border :])
+            for cells, inside, start in (
+                (left, lane < border, 0),
+                (right, lane >= 128 - border, side - 128),
+            ):
+                here = tile[:, start : start + 128].astype(f32)
+                tile[:, start : start + 128] = jnp.where(inside, cells, here).astype(bf16)
 
     def work(f, step):
         rows = slice(step * blk, (step + 1) * blk)
@@ -614,6 +693,7 @@
     for f in range(number):
         for s in range(slots):
             pltpu.make_async_copy(tiles[0], held.at[f, s], tile_sems.at[f, s]).wait()
+            patch(f, s)
         copies[f][0].wait()
         if f + 1 < number:
             copies.append(inputs(f + 1))
@@ -630,16 +710,19 @@
     out_ref[number * side :, :128] = in_three(total[...])
 
 
-def facets(tiles, ku, kv, data, ints, weights, squares):
+def facets(tiles, strips, ku, kv, data, ints, weights, squares):
     number, bins, side = ku.shape[1:]
     slots = weights.shape[1]
     return pl.pallas_call(
-        functools.partial(facets_kernel, 512),
-        in_specs=[scalar] * 2 + [anywhere] * (len(tiles) + 3) + [whole],
+        functools.partial(
+            facets_kernel, 512, strips[0].shape[0] // (4 * border), len(tiles) // 2
+        ),
+        in_specs=[scalar] * 2 + [anywhere] * (len(tiles) + len(strips) + 3) + [whole],
         out_specs=whole,
         out_shape=jax.ShapeDtypeStruct((number * side + 32, side), bf16),
         scratch_shapes=[
             pltpu.VMEM((number, slots, side, side), bf16),
+            pltpu.VMEM((number, slots, 4 * border, side), bf16),
             pltpu.VMEM((number, bins, side), bf16),
             pltpu.VMEM((number, bins, side), bf16),
             pltpu.VMEM((number, bins, bins), bf16),
@@ -648,34 +731,53 @@
             pltpu.VMEM((8, 128), f32),
             pltpu.SemaphoreType.DMA((number, 3)),
             pltpu.SemaphoreType.DMA((number, slots)),
+            pltpu.SemaphoreType.DMA((number, slots)),
         ],
-        compiler_params=pltpu.CompilerParams(vmem_limit_bytes=vmem),
+        compiler_params=pltpu.CompilerParams(vmem_limit_bytes=60 * 1024 * 1024),
         name="facets",
-    )(ints, weights, *tiles, ku, kv, data, squares)
+    )(ints, weights, *tiles, *strips, ku, kv, data, squares)
 
 
 def mix_kernel(scale, mine, theirs, *outs):
     side = outs[0].shape[1]
     number = mine.shape[0] // side
-    total = in_three(from_three(mine[number * side :, :128]) + from_three(theirs[number * side :, :128]))
     for d, out in enumerate(outs):
         value = None
         for f in range(2 * number):
             ref, at = (mine, f) if f < number else (theirs, f - number)
             term = scale[d, f] * ref[at * side : (at + 1) * side].astype(f32)
             value = term if value is None else value + term
-        out[:side] = value.astype(bf16)
-        out[side:] = jnp.zeros((32, side), bf16)
-        out[side:, :128] = total
-
-
-def mixed(mine, theirs, scale):
+        out[...] = value.astype(bf16)
+
+
+def mix_strips_kernel(scale, mine, theirs, *refs):
+    outs, strips = refs[:-1], refs[-1]
+    side = outs[0].shape[1]
+    number = mine.shape[0] // side
+    for f in range(2 * number):
+        ref, at = (mine, f) if f < number else (theirs, f - number)
+        strips_of(ref.at[at * side : (at + 1) * side], strips.at[f])
+    total = from_three(mine[number * side :, :128]) + from_three(theirs[number * side :, :128])
+    for d, out in enumerate(outs):
+        value = None
+        for f in range(2 * number):
+            term = scale[d, f] * strips[f].astype(f32)
+            value = term if value is None else value + term
+        out[: 4 * border] = value.astype(bf16)
+        out[4 * border :] = jnp.zeros((32, side), bf16)
+        out[4 * border :, :128] = in_three(total)
+
+
+def mixed(mine, theirs, scale, strips):
     side = mine.shape[1]
+    rows = 4 * border + 32 if strips else side
+    kept = [pltpu.VMEM((scale.shape[1], 4 * border, side), bf16)] if strips else []
     return pl.pallas_call(
-        mix_kernel,
+        mix_strips_kernel if strips else mix_kernel,
         in_specs=[scalar, whole, whole],
         out_specs=[whole] * scale.shape[0],
-        out_shape=[jax.ShapeDtypeStruct((side + 32, side), bf16)] * scale.shape[0],
+        out_shape=[jax.ShapeDtypeStruct((rows, side), bf16)] * scale.shape[0],
+        scratch_shapes=kept,
         compiler_params=pltpu.CompilerParams(vmem_limit_bytes=vmem),
         name="mixed",
     )(scale, mine, theirs)
@@ -715,16 +817,74 @@
     scale = jnp.concatenate([mixing, swapped(mixing)])[:, order].T
     sel = (me // 2 - lists // 2) % chips + jnp.where(lists % 2 == me % 2, 0, chips)
     ints = jnp.concatenate([sel, counts[:, None]], axis=1)
-    halos, (scale, ints, weights) = halo(
-        xi_coarse, xi_middle, coef_middle, (scale, ints, weights)
-    )
-    sky, squares = sky_of(halos, xi_coarse, coef_middle, xi_middle, coef_fine, xi_fine)
-    mine = [sky] + [chip_shift(sky, hop) for hop in range(1, chips)]
+    fields = (xi_coarse, coef_middle, xi_middle, coef_fine, xi_fine)
+    right, left = neighbours("gy")
+    down, up = neighbours("gx")
+    sides = halo_sides(xi_coarse, xi_middle, coef_middle)
+    left_in = lax.ppermute(sides[1], "gy", right)
+    right_in = lax.ppermute(sides[0], "gy", left)
+    (first,) = sky_of(None, *fields)
+    first, left_in, right_in, around = lax.optimization_barrier(
+        (first, left_in, right_in, (xi_coarse, xi_middle, coef_middle))
+    )
+    hops = range(1, chips)
+    early = range(1, min(3, chips))
+    mine = {hop: chip_shift(first, hop) for hop in early}
+    above, below = halo_rows(*around, left_in, right_in)
+    sky, strips, squares, lefts, rights = sky_of((above, below, left_in, right_in, *sides), *fields)
+    strips = jnp.concatenate([chip_shift(strips, hop) for hop in early])
+    sky, strips, mine, scale, ints, weights = lax.optimization_barrier(
+        (sky, strips, mine, scale, ints, weights)
+    )
+    for hop in hops[len(early) :]:
+        mine[hop] = chip_shift(sky, hop)
+    mine = [sky] + [mine[hop] for hop in hops]
     tiles = mine + [swapped(tile) for tile in mine]
-    dsums = facets(tiles, kern_u, kern_v, vis_data, ints, weights, squares)
-    parts = mixed(dsums, swapped(dsums), scale)
-    parts = [parts[0]] + [chip_shift(parts[hop], hop) for hop in range(1, chips)]
-    return adjoint(parts, halos, coef_middle, xi_middle, coef_fine, xi_fine, xi_coarse)
+    strips = [strips, swapped(strips)]
+    dsums = facets(tiles, strips, kern_u, kern_v, vis_data, ints, weights, squares)
+    theirs = swapped(dsums)
+    strips = mixed(dsums, theirs, scale, True)
+    strips, dsums, theirs = lax.optimization_barrier((strips, dsums, theirs))
+    edges = [strips[0]] + [chip_shift(strips[hop], hop) for hop in hops]
+    parts = mixed(dsums, theirs, scale, False)
+    edges, parts = lax.optimization_barrier((edges, parts))
+    parts = [parts[0]] + [chip_shift(parts[hop], hop) for hop in hops]
+    around = (above, below, lefts, rights)
+    to_left, to_right, upper, lower, total = adjoint(True, edges, around, fields)
+    size = lax.axis_size("gx")
+    steps = [1 << i for i in range(size.bit_length()) if 1 << i < size]
+
+    def across(x, hop):
+        return lax.ppermute(x, "gx", [(i, i ^ hop) for i in range(size)])
+
+    from_below = lax.ppermute(upper, "gx", up)
+    from_above = lax.ppermute(lower, "gx", down)
+    other = across(total, steps[0])
+    rows, cols = xi_coarse.shape
+    to_left, to_right, total = pl.pallas_call(
+        functools.partial(corners_kernel, rows, cols),
+        in_specs=[whole] * 6,
+        out_specs=[whole] * 3,
+        out_shape=[shape(*to_left.shape), shape(*to_right.shape), shape(8, 128)],
+        name="corners",
+    )(to_left, to_right, from_above, from_below, total, other)
+    for hop in steps[1:-1]:
+        total += across(total, hop)
+    other = across(total, steps[-1])
+    parts, to_left, to_right = lax.optimization_barrier((parts, to_left, to_right))
+    from_left = lax.ppermute(to_right, "gy", right)
+    from_right = lax.ppermute(to_left, "gy", left)
+    grad_fine, middle, coarse = adjoint(False, parts, around, fields)
+    cells = size * lax.axis_size("gy") * 16 * rows * cols
+    grad_middle, grad_coarse, total = pl.pallas_call(
+        functools.partial(final_kernel, cells),
+        in_specs=[whole] * 8,
+        out_specs=[whole] * 3,
+        out_shape=[shape(2 * rows, 2 * cols), shape(rows, cols), shape(1, 1)],
+        compiler_params=pltpu.CompilerParams(vmem_limit_bytes=vmem),
+        name="final",
+    )(middle, coarse, from_left, from_right, from_above, from_below, total, other)
+    return grad_coarse, grad_middle, grad_fine, total.reshape(())
 
 
 def solution(mesh):

time: 188 us -> 167 us (0.89)
  waiting for transfers between devices: 101 us -> 60.1 us
  Pallas kernels: 22 us -> 41.2 us
  local copies, waits for them, and re-layouts: 16.6 us -> 14.1 us
    ppermute x6 -> x11, waiting for transfers between devices: 87.3 us -> 48.1 us  [chip_shift(): lax.ppermute(x, 'gy', [(i, (i + 2 * hop) % size) for i in range(size)])]
    pallas_call x7 -> x10, Pallas kernels: 22 us -> 41.2 us  [the longest x2 11.7 us: sky_of(): pl.pallas_call(functools.partial(sky_kernel, alone), in_specs=[anywhere]...]
    ppermute x2, waiting for transfers between devices: 7.4 us -> 0.01 us  [across(): return lax.ppermute(x, 'gx', [(i, i ^ hop) for i in range(size)])]
    ppermute x8, waiting for transfers between devices: 1.72 us -> 7.57 us  [the longest x1 3.81 us: body(): from_below = lax.ppermute(upper, 'gx', up)]
    ppermute x6 -> x11, starting transfers between devices: 13.3 us -> 17.5 us  [chip_shift(): lax.ppermute(x, 'gy', [(i, (i + 2 * hop) % size) for i in range(size)])]
    ppermute x6 -> x7, starting transfers between devices: 4.31 us -> 1.1 us  [swapped(): lax.ppermute(x, 'gy', [(i, i ^ 1) for i in range(lax.axis_size('gy'))])]
    unnamed x60 -> x78, local copies, waits for them, and re-layouts: 12.2 us -> 9.8 us
    ppermute x6 -> x7, waiting for transfers between devices: 4.05 us -> 4.41 us  [swapped(): lax.ppermute(x, 'gy', [(i, i ^ 1) for i in range(lax.axis_size('gy'))])]
  transfers between devices with their start and end apart: 22 -> 28, of which waited for: 11 -> 11; matrix products, arithmetic and copies ran while one was open for 5% -> 5% of each run, Pallas kernels for 0% -> 17%
where the time goes in v6:
time: 167 us; the launch traced here: 165 us
  waiting for transfers between devices  60.1 us (36%)
  starting transfers between devices  43.1 us (26%)
  Pallas kernels  41.2 us (25%)
  local copies, waits for them, and re-layouts  14.1 us (8%)
  other arithmetic  4.94 us (3%)
    ppermute x11, waiting for transfers between devices, chip_shift(): lax.ppermute(x, 'gy', [(i, (i + 2 * hop) % size) for i in range(size)])  48.1 us
    ppermute x11, starting transfers between devices, chip_shift(): lax.ppermute(x, 'gy', [(i, (i + 2 * hop) % size) for i in range(size)])  17.5 us
    pallas_call x2, Pallas kernels, sky_of(): pl.pallas_call(functools.partial(sky_kernel, alone), in_specs=[anywhere]...  11.7 us
    pallas_call x1, Pallas kernels, facets(): pl.pallas_call(functools.partial(facets_kernel, 512, strips[0].shape[0] /...  11.1 us
    pallas_call x2, Pallas kernels, adjoint(): pl.pallas_call(functools.partial(adjoint_kernel, edge, len(parts)), in_sp...  10.7 us
    unnamed x78, local copies, waits for them, and re-layouts  9.8 us
    ppermute x7, waiting for transfers between devices, swapped(): lax.ppermute(x, 'gy', [(i, i ^ 1) for i in range(lax.axis_size('gy'))])  4.41 us
    ppermute x1, waiting for transfers between devices, body(): from_below = lax.ppermute(upper, 'gx', up)  3.81 us
  transfers between devices with their start and end apart: 28, of which 11 were waited for; matrix products, arithmetic and copies ran while one was open for 5% of the time, Pallas kernels for 17%

profile of v6, /device:TPU:10, one launch (start us, length us, event | category | flops | bytes accessed | tf_op | source)
XLA Modules:
  0.0 164.8 jit_solution(2917291321515758673)
XLA Ops:
  2.7 1.8 %convert_reduce_fusion = (f32[2,9,128]{2,1,0:T(8,128)S(1)}, f32[2,9,128]{2,1,0:T(8,128)S(1)}) fusion(bf16[4,9,128,128]{3,2,1,0:T(8,128)(2,1)} %refs_5_.3), kind=kLoop, calls=%fused_computation.1 | loop fusion | flops 4608 | bytes 27648 | tf_op jit(solution)/shard_map/convert_element_type | solution.py:272
  5.0 2.4 %collective-permute-start = (f32[22,128]{1,0:T(8,128)S(1)}, f32[22,128]{1,0:T(8,128)S(1)}, u32[]{:S(2)}, u32[]{:S(2)}) collective-permute-start(f32[22,128]{1,0:T(8,128)S(1)} %pad_maximum_fusion.1.refs_6_), channel_id=1, source_target_pairs={{0,1},{1,2},{2,3},{3,4},{4,5},{5,6},{6,7},{8,9},{9,10},{10,11},{11... | collective-permute-start | bytes 33800 | tf_op jit(solution)/shard_map/ppermute | solution.py:824
  7.8 3.1 %collective-permute-start.1 = (f32[22,128]{1,0:T(8,128)S(1)}, f32[22,128]{1,0:T(8,128)S(1)}, u32[]{:S(2)}, u32[]{:S(2)}) collective-permute-start(f32[22,128]{1,0:T(8,128)S(1)} %pad_maximum_fusion.2.refs_5_), channel_id=1, source_target_pairs={{1,0},{2,1},{3,2},{4,3},{5,4},{6,5},{7,6},{9,8},{10,9},{11,10},{12... | collective-permute-start | bytes 33800 | tf_op jit(solution)/shard_map/ppermute | solution.py:825
  11.1 5.8 %sky.2 = bf16[512,512]{1,0:T(8,128)(2,1)} custom-call(f32[128,128]{1,0:T(8,128)} %refs_12_.3, bf16[4,9,128,128]{3,2,1,0:T(8,128)(2,1)} %refs_5_.3, f32[256,256]{1,0:T(8,128)} %refs_11_.3, bf16[4,9,256,256]{3,2,1,0:T(8,128)(2,1)} %refs_4_.5, f32[512,512]{1,0:T(8,128)} %refs_10_.5), custom_call_target="tpu_custom_call" | custom-call | tf_op jit(solution)/shard_map/sky/pallas_call | solution.py:316
  17.0 2.7 %collective-permute-start.7 = (bf16[512,512]{1,0:T(8,128)(2,1)}, bf16[512,512]{1,0:T(8,128)(2,1)S(1)}, u32[]{:S(2)}, u32[]{:S(2)}) collective-permute-start(bf16[512,512]{1,0:T(8,128)(2,1)} %sky.2), channel_id=1, source_target_pairs={{0,4},{1,5},{2,6},{3,7},{4,0},{5,1},{6,2},{7,3},{8,12},{9,13},{10,... | collective-permute-start | bytes 1572872 | tf_op jit(solution)/shard_map/ppermute | solution.py:788
  24.5 3.4 %collective-permute-start.2 = (f32[22,132]{1,0:T(8,128)}, f32[22,132]{1,0:T(8,128)S(1)}, u32[]{:S(2)}, u32[]{:S(2)}) collective-permute-start(f32[22,132]{1,0:T(8,128)} %get-tuple-element.71), channel_id=1, source_target_pairs={{0,8},{8,16},{16,24},{1,9},{9,17},{17,25},{2,10},{10,18},{18,26},{... | collective-permute-start | bytes 34856 | tf_op jit(solution)/shard_map/ppermute | solution.py:302
  27.9 2.4 %collective-permute-start.3 = (f32[22,132]{1,0:T(8,128)}, f32[22,132]{1,0:T(8,128)S(1)}, u32[]{:S(2)}, u32[]{:S(2)}) collective-permute-start(f32[22,132]{1,0:T(8,128)} %get-tuple-element.72), channel_id=1, source_target_pairs={{8,0},{16,8},{24,16},{9,1},{17,9},{25,17},{10,2},{18,10},{26,18},{... | collective-permute-start | bytes 34856 | tf_op jit(solution)/shard_map/ppermute | solution.py:302
  30.9 3.7 %collective-permute-done.3.refs_2_.refs_7_ = f32[22,132]{1,0:T(8,128)S(1)} collective-permute-done((f32[22,132]{1,0:T(8,128)}, f32[22,132]{1,0:T(8,128)S(1)}, u32[]{:S(2)}, u32[]{:S(2)}) %collective-permute-start.3) | collective-permute-done | bytes 11648 | tf_op jit(solution)/shard_map/ppermute | solution.py:302
  35.3 5.9 %sky.3 = (bf16[512,512]{1,0:T(8,128)(2,1)}, bf16[32,512]{1,0:T(8,128)(2,1)}, f32[8,128]{1,0:T(8,128)}, f32[22,132]{1,0:T(8,128)}, f32[22,132]{1,0:T(8,128)}) custom-call(f32[128,128]{1,0:T(8,128)} %refs_12_.3, f32[22,132]{1,0:T(8,128)} %copy-done.8, f32[22,132]{1,0:T(8,128)} %copy-done.10, f32[22,128]{1,0:T(8,128)} %copy-done.33, f32[22,128]{1,0:T(8,128)} %copy-done.34, ...), custom_call_target="tpu_custom_call" | custom-call | tf_op jit(solution)/shard_map/sky/pallas_call | solution.py:316
  41.2 2.9 %collective-permute-start.5 = (bf16[32,512]{1,0:T(8,128)(2,1)}, bf16[32,512]{1,0:T(8,128)(2,1)S(1)}, u32[]{:S(2)}, u32[]{:S(2)}) collective-permute-start(bf16[32,512]{1,0:T(8,128)(2,1)} %get-tuple-element.74), channel_id=1, source_target_pairs={{0,4},{1,5},{2,6},{3,7},{4,0},{5,1},{6,2},{7,3},{8,12},{9,13},{10,... | collective-permute-start | bytes 98312 | tf_op jit(solution)/shard_map/ppermute | solution.py:788
  45.4 9.3 %collective-permute-done.5 = bf16[32,512]{1,0:T(8,128)(2,1)S(1)} collective-permute-done((bf16[32,512]{1,0:T(8,128)(2,1)}, bf16[32,512]{1,0:T(8,128)(2,1)S(1)}, u32[]{:S(2)}, u32[]{:S(2)}) %collective-permute-start.5) | collective-permute-done | bytes 32800 | tf_op jit(solution)/shard_map/ppermute | solution.py:788
  55.2 1.9 %collective-permute-start.9 = (bf16[512,512]{1,0:T(8,128)(2,1)}, bf16[512,512]{1,0:T(8,128)(2,1)S(1)}, u32[]{:S(2)}, u32[]{:S(2)}) collective-permute-start(bf16[512,512]{1,0:T(8,128)(2,1)} %get-tuple-element.79.refs_0_), channel_id=1, source_target_pairs={{0,6},{1,7},{2,0},{3,1},{4,2},{5,3},{6,4},{7,5},{8,14},{9,15},{10,... | collective-permute-start | bytes 1572872 | tf_op jit(solution)/shard_map/ppermute | solution.py:788
  57.6 11.7 %collective-permute-done.9.refs_3_ = bf16[512,512]{1,0:T(8,128)(2,1)S(1)} collective-permute-done((bf16[512,512]{1,0:T(8,128)(2,1)}, bf16[512,512]{1,0:T(8,128)(2,1)S(1)}, u32[]{:S(2)}, u32[]{:S(2)}) %collective-permute-start.9) | collective-permute-done | bytes 524320 | tf_op jit(solution)/shard_map/ppermute | solution.py:788
  69.8 1.5 collective-permute-done.14.refs_9_
  72.6 11.1 %facets.1.mine = bf16[1056,512]{1,0:T(8,128)(2,1)} custom-call(s32[2,3]{1,0:T(2,128)} %pad_add_fusion.ints, f32[2,2]{1,0:T(2,128)} %bitcast.21, bf16[512,512]{1,0:T(8,128)(2,1)} %get-tuple-element.79.refs_0_, bf16[512,512]{1,0:T(8,128)(2,1)} %copy-done.23, bf16[512,512]{1,0:T(8,128)(2,1)} %copy-done.22, bf16[512,512]{1,0:T(8,128)(2,1)} %copy-done.24, ...), custom_call_target="tpu_custom_call" | custom-call | tf_op jit(solution)/shard_map/facets/pallas_call | solution.py:716
  83.8 2.9 %collective-permute-done.15.theirs = bf16[1056,512]{1,0:T(8,128)(2,1)S(1)} collective-permute-done((bf16[1056,512]{1,0:T(8,128)(2,1)}, bf16[1056,512]{1,0:T(8,128)(2,1)S(1)}, u32[]{:S(2)}, u32[]{:S(2)}) %collective-permute-start.15) | collective-permute-done | bytes 1081376 | tf_op jit(solution)/shard_map/ppermute | solution.py:792
  89.2 3.7 %collective-permute-start.16 = (bf16[64,512]{1,0:T(8,128)(2,1)S(1)}, bf16[64,512]{1,0:T(8,128)(2,1)S(1)}, u32[]{:S(2)}, u32[]{:S(2)}) collective-permute-start(bf16[64,512]{1,0:T(8,128)(2,1)S(1)} %get-tuple-element.89), channel_id=1, source_target_pairs={{0,2},{1,3},{2,4},{3,5},{4,6},{5,7},{6,0},{7,1},{8,10},{9,11},{10,... | collective-permute-start | bytes 196616 | tf_op jit(solution)/shard_map/ppermute | solution.py:788
  92.9 1.9 %collective-permute-start.17 = (bf16[64,512]{1,0:T(8,128)(2,1)S(1)}, bf16[64,512]{1,0:T(8,128)(2,1)S(1)}, u32[]{:S(2)}, u32[]{:S(2)}) collective-permute-start(bf16[64,512]{1,0:T(8,128)(2,1)S(1)} %get-tuple-element.90), channel_id=1, source_target_pairs={{0,4},{1,5},{2,6},{3,7},{4,0},{5,1},{6,2},{7,3},{8,12},{9,13},{10,... | collective-permute-start | bytes 196616 | tf_op jit(solution)/shard_map/ppermute | solution.py:788
  94.9 2.5 %mixed.3 = (bf16[512,512]{1,0:T(8,128)(2,1)S(1)}, bf16[512,512]{1,0:T(8,128)(2,1)}, bf16[512,512]{1,0:T(8,128)(2,1)}, bf16[512,512]{1,0:T(8,128)(2,1)}) custom-call(f32[4,4]{1,0:T(4,128)S(1)} %gather_fusion, bf16[1056,512]{1,0:T(8,128)(2,1)S(1)} %copy-done.3, bf16[1056,512]{1,0:T(8,128)(2,1)S(1)} %collective-permute-done.15.theirs), custom_call_target="tpu_custom_call" | custom-call | tf_op jit(solution)/shard_map/mixed/pallas_call | solution.py:775
  97.4 1.8 %collective-permute-done.17.refs_2_ = bf16[64,512]{1,0:T(8,128)(2,1)S(1)} collective-permute-done((bf16[64,512]{1,0:T(8,128)(2,1)S(1)}, bf16[64,512]{1,0:T(8,128)(2,1)S(1)}, u32[]{:S(2)}, u32[]{:S(2)}) %collective-permute-start.17) | collective-permute-done | bytes 65568 | tf_op jit(solution)/shard_map/ppermute | solution.py:788
  100.6 2.9 %collective-permute-start.20 = (bf16[512,512]{1,0:T(8,128)(2,1)}, bf16[512,512]{1,0:T(8,128)(2,1)}, u32[]{:S(2)}, u32[]{:S(2)}) collective-permute-start(bf16[512,512]{1,0:T(8,128)(2,1)} %get-tuple-element.100), channel_id=1, source_target_pairs={{0,4},{1,5},{2,6},{3,7},{4,0},{5,1},{6,2},{7,3},{8,12},{9,13},{10,... | collective-permute-start | bytes 1572872 | tf_op jit(solution)/shard_map/ppermute | solution.py:788
  104.4 2.3 %copy-done = bf16[4,9,256,256]{3,2,1,0:T(8,128)(2,1)S(1)} copy-done((bf16[4,9,256,256]{3,2,1,0:T(8,128)(2,1)S(1)}, bf16[4,9,256,256]{3,2,1,0:T(8,128)(2,1)}, u32[]{:S(2)}) %copy-start) | copy-done | bytes 4718616
  106.7 4.4 %adjoint.2 = (f32[8,384]{1,0:T(8,128)S(1)}, f32[8,384]{1,0:T(8,128)S(1)}, f32[8,384]{1,0:T(8,128)S(1)}, f32[8,384]{1,0:T(8,128)S(1)}, f32[8,128]{1,0:T(8,128)S(1)}) custom-call(bf16[64,512]{1,0:T(8,128)(2,1)S(1)} %get-tuple-element.102.refs_0_, bf16[64,512]{1,0:T(8,128)(2,1)S(1)} %collective-permute-done.16.refs_1_, ...), custom_call_target="tpu_custom_call" | custom-call | flops 40000000000 | bytes 64000000 | tf_op jit(solution)/shard_map/adjoint/pallas_call | solution.py:582
  113.2 3.2 %collective-permute-start.22 = (f32[8,384]{1,0:T(8,128)S(1)}, f32[8,384]{1,0:T(8,128)S(1)}, u32[]{:S(2)}, u32[]{:S(2)}) collective-permute-start(f32[8,384]{1,0:T(8,128)S(1)} %get-tuple-element.110), channel_id=1, source_target_pairs={{0,8},{8,16},{16,24},{1,9},{9,17},{17,25},{2,10},{10,18},{18,26},{... | collective-permute-start | bytes 36872 | tf_op jit(solution)/shard_map/ppermute | solution.py:861
  116.4 2.6 %collective-permute-start.23 = (f32[8,384]{1,0:T(8,128)S(1)}, f32[8,384]{1,0:T(8,128)S(1)}, u32[]{:S(2)}, u32[]{:S(2)}) collective-permute-start(f32[8,384]{1,0:T(8,128)S(1)} %get-tuple-element.111), channel_id=1, source_target_pairs={{8,0},{16,8},{24,16},{9,1},{17,9},{25,17},{10,2},{18,10},{26,18},{... | collective-permute-start | bytes 36872 | tf_op jit(solution)/shard_map/ppermute | solution.py:860
  119.1 3.8 %collective-permute-done.23.from_below = f32[8,384]{1,0:T(8,128)S(1)} collective-permute-done((f32[8,384]{1,0:T(8,128)S(1)}, f32[8,384]{1,0:T(8,128)S(1)}, u32[]{:S(2)}, u32[]{:S(2)}) %collective-permute-start.23) | collective-permute-done | bytes 12320 | tf_op jit(solution)/shard_map/ppermute | solution.py:860
  124.9 20.9 %collective-permute-done.20.refs_2_ = bf16[512,512]{1,0:T(8,128)(2,1)} collective-permute-done((bf16[512,512]{1,0:T(8,128)(2,1)}, bf16[512,512]{1,0:T(8,128)(2,1)}, u32[]{:S(2)}, u32[]{:S(2)}) %collective-permute-start.20) | collective-permute-done | bytes 524320 | tf_op jit(solution)/shard_map/ppermute | solution.py:788
  145.9 2.7 %collective-permute-done.21.refs_3_ = bf16[512,512]{1,0:T(8,128)(2,1)} collective-permute-done((bf16[512,512]{1,0:T(8,128)(2,1)}, bf16[512,512]{1,0:T(8,128)(2,1)}, u32[]{:S(2)}, u32[]{:S(2)}) %collective-permute-start.21) | collective-permute-done | bytes 524320 | tf_op jit(solution)/shard_map/ppermute | solution.py:788
  148.5 1.9 %collective-permute-start.25 = (f32[8,384]{1,0:T(8,128)}, f32[8,384]{1,0:T(8,128)S(1)}, u32[]{:S(2)}, u32[]{:S(2)}) collective-permute-start(f32[8,384]{1,0:T(8,128)} %get-tuple-element.121), channel_id=1, source_target_pairs={{0,1},{1,2},{2,3},{3,4},{4,5},{5,6},{6,7},{8,9},{9,10},{10,11},{11... | collective-permute-start | bytes 36872 | tf_op jit(solution)/shard_map/ppermute | solution.py:875
  150.4 3.6 %collective-permute-start.26 = (f32[8,384]{1,0:T(8,128)}, f32[8,384]{1,0:T(8,128)S(1)}, u32[]{:S(2)}, u32[]{:S(2)}) collective-permute-start(f32[8,384]{1,0:T(8,128)} %get-tuple-element.122), channel_id=1, source_target_pairs={{1,0},{2,1},{3,2},{4,3},{5,4},{6,5},{7,6},{9,8},{10,9},{11,10},{12... | collective-permute-start | bytes 36872 | tf_op jit(solution)/shard_map/ppermute | solution.py:876
  155.0 2.3 %copy-done.1 = bf16[4,9,256,256]{3,2,1,0:T(8,128)(2,1)S(1)} copy-done((bf16[4,9,256,256]{3,2,1,0:T(8,128)(2,1)S(1)}, bf16[4,9,256,256]{3,2,1,0:T(8,128)(2,1)}, u32[]{:S(2)}) %copy-start.1) | copy-done | bytes 4718616
  157.3 6.3 %adjoint.3 = (f32[512,512]{1,0:T(8,128)}, f32[256,256]{1,0:T(8,128)S(1)}, f32[128,128]{1,0:T(8,128)S(1)}) custom-call(bf16[512,512]{1,0:T(8,128)(2,1)S(1)} %get-tuple-element.115.refs_0_, bf16[512,512]{1,0:T(8,128)(2,1)} %collective-permute-done.19.refs_1_, bf16[512,512]{1,0:T(8,128)(2,1)} %collective-permute-done.20.refs_2_, ...), custom_call_target="tpu_custom_call" | custom-call | tf_op jit(solution)/shard_map/adjoint/pallas_call | solution.py:582
  (143 shorter events, 23.9 us)
Async XLA Ops:
  1.6 43.2 %collective-permute-start.8 = (f32[2,8]{0,1:T(8,128)S(1)}, f32[2,8]{0,1:T(8,128)S(1)}, u32[]{:S(2)}, u32[]{:S(2)}) collective-permute-start(f32[2,8]{0,1:T(8,128)S(1)} %copy.32), channel_id=1, source_target_pairs={{0,1},{1,0},{2,3},{3,2},{4,5},{5,4},{6,7},{7,6},{8,9},{9,8},{10,11... | collective-permute-start | bytes 200 | tf_op jit(solution)/shard_map/ppermute | solution.py:792
  5.0 11.9 %collective-permute-start = (f32[22,128]{1,0:T(8,128)S(1)}, f32[22,128]{1,0:T(8,128)S(1)}, u32[]{:S(2)}, u32[]{:S(2)}) collective-permute-start(f32[22,128]{1,0:T(8,128)S(1)} %pad_maximum_fusion.1.refs_6_), channel_id=1, source_target_pairs={{0,1},{1,2},{2,3},{3,4},{4,5},{5,6},{6,7},{8,9},{9,10},{10,11},{11... | collective-permute-start | bytes 33800 | tf_op jit(solution)/shard_map/ppermute | solution.py:824
  7.8 9.2 %collective-permute-start.1 = (f32[22,128]{1,0:T(8,128)S(1)}, f32[22,128]{1,0:T(8,128)S(1)}, u32[]{:S(2)}, u32[]{:S(2)}) collective-permute-start(f32[22,128]{1,0:T(8,128)S(1)} %pad_maximum_fusion.2.refs_5_), channel_id=1, source_target_pairs={{1,0},{2,1},{3,2},{4,3},{5,4},{6,5},{7,6},{9,8},{10,9},{11,10},{12... | collective-permute-start | bytes 33800 | tf_op jit(solution)/shard_map/ppermute | solution.py:825
  17.0 38.2 %collective-permute-start.7 = (bf16[512,512]{1,0:T(8,128)(2,1)}, bf16[512,512]{1,0:T(8,128)(2,1)S(1)}, u32[]{:S(2)}, u32[]{:S(2)}) collective-permute-start(bf16[512,512]{1,0:T(8,128)(2,1)} %sky.2), channel_id=1, source_target_pairs={{0,4},{1,5},{2,6},{3,7},{4,0},{5,1},{6,2},{7,3},{8,12},{9,13},{10,... | collective-permute-start | bytes 1572872 | tf_op jit(solution)/shard_map/ppermute | solution.py:788
  19.6 35.5 %collective-permute-start.6 = (bf16[512,512]{1,0:T(8,128)(2,1)}, bf16[512,512]{1,0:T(8,128)(2,1)S(1)}, u32[]{:S(2)}, u32[]{:S(2)}) collective-permute-start(bf16[512,512]{1,0:T(8,128)(2,1)} %sky.2), channel_id=1, source_target_pairs={{0,2},{1,3},{2,4},{3,5},{4,6},{5,7},{6,0},{7,1},{8,10},{9,11},{10,... | collective-permute-start | bytes 1572872 | tf_op jit(solution)/shard_map/ppermute | solution.py:788
  24.5 6.5 %collective-permute-start.2 = (f32[22,132]{1,0:T(8,128)}, f32[22,132]{1,0:T(8,128)S(1)}, u32[]{:S(2)}, u32[]{:S(2)}) collective-permute-start(f32[22,132]{1,0:T(8,128)} %get-tuple-element.71), channel_id=1, source_target_pairs={{0,8},{8,16},{16,24},{1,9},{9,17},{17,25},{2,10},{10,18},{18,26},{... | collective-permute-start | bytes 34856 | tf_op jit(solution)/shard_map/ppermute | solution.py:302
  27.9 6.8 %collective-permute-start.3 = (f32[22,132]{1,0:T(8,128)}, f32[22,132]{1,0:T(8,128)S(1)}, u32[]{:S(2)}, u32[]{:S(2)}) collective-permute-start(f32[22,132]{1,0:T(8,128)} %get-tuple-element.72), channel_id=1, source_target_pairs={{8,0},{16,8},{24,16},{9,1},{17,9},{25,17},{10,2},{18,10},{26,18},{... | collective-permute-start | bytes 34856 | tf_op jit(solution)/shard_map/ppermute | solution.py:302
  41.2 13.5 %collective-permute-start.5 = (bf16[32,512]{1,0:T(8,128)(2,1)}, bf16[32,512]{1,0:T(8,128)(2,1)S(1)}, u32[]{:S(2)}, u32[]{:S(2)}) collective-permute-start(bf16[32,512]{1,0:T(8,128)(2,1)} %get-tuple-element.74), channel_id=1, source_target_pairs={{0,4},{1,5},{2,6},{3,7},{4,0},{5,1},{6,2},{7,3},{8,12},{9,13},{10,... | collective-permute-start | bytes 98312 | tf_op jit(solution)/shard_map/ppermute | solution.py:788
  44.1 11.0 %collective-permute-start.4 = (bf16[32,512]{1,0:T(8,128)(2,1)}, bf16[32,512]{1,0:T(8,128)(2,1)S(1)}, u32[]{:S(2)}, u32[]{:S(2)}) collective-permute-start(bf16[32,512]{1,0:T(8,128)(2,1)} %get-tuple-element.74), channel_id=1, source_target_pairs={{0,2},{1,3},{2,4},{3,5},{4,6},{5,7},{6,0},{7,1},{8,10},{9,11},{10,... | collective-permute-start | bytes 98312 | tf_op jit(solution)/shard_map/ppermute | solution.py:788
  55.1 17.1 %copy-start.29 = (bf16[64,512]{1,0:T(8,128)(2,1)}, bf16[64,512]{1,0:T(8,128)(2,1)S(1)}, u32[]{:S(2)}) copy-start(bf16[64,512]{1,0:T(8,128)(2,1)S(1)} %pad_maximum_fusion.refs_8_) | copy-start | bytes 196612
  55.2 14.1 %collective-permute-start.9 = (bf16[512,512]{1,0:T(8,128)(2,1)}, bf16[512,512]{1,0:T(8,128)(2,1)S(1)}, u32[]{:S(2)}, u32[]{:S(2)}) collective-permute-start(bf16[512,512]{1,0:T(8,128)(2,1)} %get-tuple-element.79.refs_0_), channel_id=1, source_target_pairs={{0,6},{1,7},{2,0},{3,1},{4,2},{5,3},{6,4},{7,5},{8,14},{9,15},{10,... | collective-permute-start | bytes 1572872 | tf_op jit(solution)/shard_map/ppermute | solution.py:788
  57.1 14.2 %collective-permute-start.10 = (bf16[512,512]{1,0:T(8,128)(2,1)}, bf16[512,512]{1,0:T(8,128)(2,1)S(1)}, u32[]{:S(2)}, u32[]{:S(2)}) collective-permute-start(bf16[512,512]{1,0:T(8,128)(2,1)} %get-tuple-element.79.refs_0_), channel_id=1, source_target_pairs={{0,1},{1,0},{2,3},{3,2},{4,5},{5,4},{6,7},{7,6},{8,9},{9,8},{10,11... | collective-permute-start | bytes 1572872 | tf_op jit(solution)/shard_map/ppermute | solution.py:792
  57.1 14.2 %collective-permute-start.11 = (bf16[512,512]{1,0:T(8,128)(2,1)S(1)}, bf16[512,512]{1,0:T(8,128)(2,1)S(1)}, u32[]{:S(2)}, u32[]{:S(2)}) collective-permute-start(bf16[512,512]{1,0:T(8,128)(2,1)S(1)} %collective-permute-done.6.refs_1_), channel_id=1, source_target_pairs={{0,1},{1,0},{2,3},{3,2},{4,5},{5,4},{6,7},{7,6},{8,9},{9,8},{10,11... | collective-permute-start | bytes 1572872 | tf_op jit(solution)/shard_map/ppermute | solution.py:792
  57.6 13.7 %collective-permute-start.12 = (bf16[512,512]{1,0:T(8,128)(2,1)S(1)}, bf16[512,512]{1,0:T(8,128)(2,1)S(1)}, u32[]{:S(2)}, u32[]{:S(2)}) collective-permute-start(bf16[512,512]{1,0:T(8,128)(2,1)S(1)} %collective-permute-done.7.refs_2_), channel_id=1, source_target_pairs={{0,1},{1,0},{2,3},{3,2},{4,5},{5,4},{6,7},{7,6},{8,9},{9,8},{10,11... | collective-permute-start | bytes 1572872 | tf_op jit(solution)/shard_map/ppermute | solution.py:792
  69.3 2.1 %collective-permute-start.13 = (bf16[512,512]{1,0:T(8,128)(2,1)S(1)}, bf16[512,512]{1,0:T(8,128)(2,1)S(1)}, u32[]{:S(2)}, u32[]{:S(2)}) collective-permute-start(bf16[512,512]{1,0:T(8,128)(2,1)S(1)} %collective-permute-done.9.refs_3_), channel_id=1, source_target_pairs={{0,1},{1,0},{2,3},{3,2},{4,5},{5,4},{6,7},{7,6},{8,9},{9,8},{10,11... | collective-permute-start | bytes 1572872 | tf_op jit(solution)/shard_map/ppermute | solution.py:792
  69.3 2.0 %collective-permute-start.14 = (bf16[64,512]{1,0:T(8,128)(2,1)S(1)}, bf16[64,512]{1,0:T(8,128)(2,1)S(1)}, u32[]{:S(2)}, u32[]{:S(2)}) collective-permute-start(bf16[64,512]{1,0:T(8,128)(2,1)S(1)} %pad_maximum_fusion.refs_8_), channel_id=1, source_target_pairs={{0,1},{1,0},{2,3},{3,2},{4,5},{5,4},{6,7},{7,6},{8,9},{9,8},{10,11... | collective-permute-start | bytes 196616 | tf_op jit(solution)/shard_map/ppermute | solution.py:792
  83.7 3.0 %collective-permute-start.15 = (bf16[1056,512]{1,0:T(8,128)(2,1)}, bf16[1056,512]{1,0:T(8,128)(2,1)S(1)}, u32[]{:S(2)}, u32[]{:S(2)}) collective-permute-start(bf16[1056,512]{1,0:T(8,128)(2,1)} %facets.1.mine), channel_id=1, source_target_pairs={{0,1},{1,0},{2,3},{3,2},{4,5},{5,4},{6,7},{7,6},{8,9},{9,8},{10,11... | collective-permute-start | bytes 3244040 | tf_op jit(solution)/shard_map/ppermute | solution.py:792
  89.2 8.2 %collective-permute-start.16 = (bf16[64,512]{1,0:T(8,128)(2,1)S(1)}, bf16[64,512]{1,0:T(8,128)(2,1)S(1)}, u32[]{:S(2)}, u32[]{:S(2)}) collective-permute-start(bf16[64,512]{1,0:T(8,128)(2,1)S(1)} %get-tuple-element.89), channel_id=1, source_target_pairs={{0,2},{1,3},{2,4},{3,5},{4,6},{5,7},{6,0},{7,1},{8,10},{9,11},{10,... | collective-permute-start | bytes 196616 | tf_op jit(solution)/shard_map/ppermute | solution.py:788
  92.9 6.3 %collective-permute-start.17 = (bf16[64,512]{1,0:T(8,128)(2,1)S(1)}, bf16[64,512]{1,0:T(8,128)(2,1)S(1)}, u32[]{:S(2)}, u32[]{:S(2)}) collective-permute-start(bf16[64,512]{1,0:T(8,128)(2,1)S(1)} %get-tuple-element.90), channel_id=1, source_target_pairs={{0,4},{1,5},{2,6},{3,7},{4,0},{5,1},{6,2},{7,3},{8,12},{9,13},{10,... | collective-permute-start | bytes 196616 | tf_op jit(solution)/shard_map/ppermute | solution.py:788
  94.9 5.7 %collective-permute-start.18 = (bf16[64,512]{1,0:T(8,128)(2,1)S(1)}, bf16[64,512]{1,0:T(8,128)(2,1)S(1)}, u32[]{:S(2)}, u32[]{:S(2)}) collective-permute-start(bf16[64,512]{1,0:T(8,128)(2,1)S(1)} %get-tuple-element.91), channel_id=1, source_target_pairs={{0,6},{1,7},{2,0},{3,1},{4,2},{5,3},{6,4},{7,5},{8,14},{9,15},{10,... | collective-permute-start | bytes 196616 | tf_op jit(solution)/shard_map/ppermute | solution.py:788
  100.6 24.4 %collective-permute-start.19 = (bf16[512,512]{1,0:T(8,128)(2,1)}, bf16[512,512]{1,0:T(8,128)(2,1)}, u32[]{:S(2)}, u32[]{:S(2)}) collective-permute-start(bf16[512,512]{1,0:T(8,128)(2,1)} %get-tuple-element.99), channel_id=1, source_target_pairs={{0,2},{1,3},{2,4},{3,5},{4,6},{5,7},{6,0},{7,1},{8,10},{9,11},{10,... | collective-permute-start | bytes 1572872 | tf_op jit(solution)/shard_map/ppermute | solution.py:788
  100.6 45.3 %collective-permute-start.20 = (bf16[512,512]{1,0:T(8,128)(2,1)}, bf16[512,512]{1,0:T(8,128)(2,1)}, u32[]{:S(2)}, u32[]{:S(2)}) collective-permute-start(bf16[512,512]{1,0:T(8,128)(2,1)} %get-tuple-element.100), channel_id=1, source_target_pairs={{0,4},{1,5},{2,6},{3,7},{4,0},{5,1},{6,2},{7,3},{8,12},{9,13},{10,... | collective-permute-start | bytes 1572872 | tf_op jit(solution)/shard_map/ppermute | solution.py:788
  103.5 45.0 %collective-permute-start.21 = (bf16[512,512]{1,0:T(8,128)(2,1)}, bf16[512,512]{1,0:T(8,128)(2,1)}, u32[]{:S(2)}, u32[]{:S(2)}) collective-permute-start(bf16[512,512]{1,0:T(8,128)(2,1)} %get-tuple-element.101), channel_id=1, source_target_pairs={{0,6},{1,7},{2,0},{3,1},{4,2},{5,3},{6,4},{7,5},{8,14},{9,15},{10,... | collective-permute-start | bytes 1572872 | tf_op jit(solution)/shard_map/ppermute | solution.py:788
  106.7 48.2 %copy-start.4 = (f32[512,512]{1,0:T(8,128)S(1)}, f32[512,512]{1,0:T(8,128)}, u32[]{:S(2)}) copy-start(f32[512,512]{1,0:T(8,128)} %refs_10_.5) | copy-start | bytes 3145732
  106.7 48.2 %copy-start.5 = (f32[256,256]{1,0:T(8,128)S(1)}, f32[256,256]{1,0:T(8,128)}, u32[]{:S(2)}) copy-start(f32[256,256]{1,0:T(8,128)} %refs_11_.3) | copy-start | bytes 786436
  106.7 48.2 %copy-start.7 = (f32[128,128]{1,0:T(8,128)S(1)}, f32[128,128]{1,0:T(8,128)}, u32[]{:S(2)}) copy-start(f32[128,128]{1,0:T(8,128)} %refs_12_.3) | copy-start | bytes 196612
  112.3 4.1 %collective-permute-start.24 = (f32[8,128]{1,0:T(8,128)S(1)}, f32[8,128]{1,0:T(8,128)S(1)}, u32[]{:S(2)}, u32[]{:S(2)}) collective-permute-start(f32[8,128]{1,0:T(8,128)S(1)} %get-tuple-element.112.total), channel_id=1, source_target_pairs={{0,8},{8,0},{16,24},{24,16},{1,9},{9,1},{17,25},{25,17},{2,10},{10... | collective-permute-start | bytes 12296 | tf_op jit(solution)/shard_map/ppermute | solution.py:858
  113.2 5.9 %collective-permute-start.22 = (f32[8,384]{1,0:T(8,128)S(1)}, f32[8,384]{1,0:T(8,128)S(1)}, u32[]{:S(2)}, u32[]{:S(2)}) collective-permute-start(f32[8,384]{1,0:T(8,128)S(1)} %get-tuple-element.110), channel_id=1, source_target_pairs={{0,8},{8,16},{16,24},{1,9},{9,17},{17,25},{2,10},{10,18},{18,26},{... | collective-permute-start | bytes 36872 | tf_op jit(solution)/shard_map/ppermute | solution.py:861
  116.4 6.5 %collective-permute-start.23 = (f32[8,384]{1,0:T(8,128)S(1)}, f32[8,384]{1,0:T(8,128)S(1)}, u32[]{:S(2)}, u32[]{:S(2)}) collective-permute-start(f32[8,384]{1,0:T(8,128)S(1)} %get-tuple-element.111), channel_id=1, source_target_pairs={{8,0},{16,8},{24,16},{9,1},{17,9},{25,17},{10,2},{18,10},{26,18},{... | collective-permute-start | bytes 36872 | tf_op jit(solution)/shard_map/ppermute | solution.py:860
  148.5 15.1 %collective-permute-start.25 = (f32[8,384]{1,0:T(8,128)}, f32[8,384]{1,0:T(8,128)S(1)}, u32[]{:S(2)}, u32[]{:S(2)}) collective-permute-start(f32[8,384]{1,0:T(8,128)} %get-tuple-element.121), channel_id=1, source_target_pairs={{0,1},{1,2},{2,3},{3,4},{4,5},{5,6},{6,7},{8,9},{9,10},{10,11},{11... | collective-permute-start | bytes 36872 | tf_op jit(solution)/shard_map/ppermute | solution.py:875
  150.4 13.2 %collective-permute-start.26 = (f32[8,384]{1,0:T(8,128)}, f32[8,384]{1,0:T(8,128)S(1)}, u32[]{:S(2)}, u32[]{:S(2)}) collective-permute-start(f32[8,384]{1,0:T(8,128)} %get-tuple-element.122), channel_id=1, source_target_pairs={{1,0},{2,1},{3,2},{4,3},{5,4},{6,5},{7,6},{9,8},{10,9},{11,10},{12... | collective-permute-start | bytes 36872 | tf_op jit(solution)/shard_map/ppermute | solution.py:876
  154.1 9.6 %collective-permute-start.27 = (f32[8,128]{1,0:T(8,128)}, f32[8,128]{1,0:T(8,128)S(1)}, u32[]{:S(2)}, u32[]{:S(2)}) collective-permute-start(f32[8,128]{1,0:T(8,128)} %get-tuple-element.123.total), channel_id=1, source_target_pairs={{0,16},{8,24},{16,0},{24,8},{1,17},{9,25},{17,1},{25,9},{2,18},{10... | collective-permute-start | bytes 12296 | tf_op jit(solution)/shard_map/ppermute | solution.py:858
  (34 other events, 228.5 us)

commit v7 on v6

--- a/solution.py
+++ b/solution.py
@@ -61,7 +61,7 @@
     return dot_t(rows, place.astype(f32).astype(bf16), ((0,), (0,)))
 
 
-def weighed(win, coef_ref, perm, lhs, mix, rows, cols):
+def weighed(win, coef_ref, perm, lhs, mix, rows, cols, chunks=()):
     def part(i, carry):
         r0 = pl.multiple_of(i * 16, 16)
         total = [jnp.zeros((16, cols), f32) for _ in range(4)]
@@ -76,7 +76,7 @@
             lhs[pl.ds((2 * a + 1) * rows + r0, 16), b * cols : (b + 1) * cols] = low
         return carry
 
-    lax.fori_loop(0, rows // 16, part, 0)
+    in_chunks(part, rows, chunks)
     field = jnp.dot(lhs[...], perm[...], preferred_element_type=f32)
     for tile in range(2 * cols // 128):
         lanes = slice(tile * 128, (tile + 1) * 128)
@@ -87,11 +87,32 @@
             )
 
 
-def fetched(pairs, sems):
-    copies = [pltpu.make_async_copy(src, dst, sems.at[i]) for i, (src, dst) in enumerate(pairs)]
+def fetched(pairs, sems, first=0):
+    copies = [
+        pltpu.make_async_copy(src, dst, sems.at[first + i]) for i, (src, dst) in enumerate(pairs)
+    ]
     for copy in copies:
         copy.start()
     return copies
+
+
+def chunked(source, target, sems):
+    number, rows = sems.shape[0], source.shape[2] // sems.shape[0]
+    copies = []
+    for i in range(number):
+        at = slice(i * rows, (i + 1) * rows)
+        copies.append(pltpu.make_async_copy(source.at[:, :, at], target.at[:, :, at], sems.at[i]))
+        copies[i].start()
+    return copies
+
+
+def in_chunks(part, rows, chunks):
+    steps = rows // 16
+    if not chunks:
+        lax.fori_loop(0, steps, part, 0)
+    for i, copy in enumerate(chunks):
+        copy.wait()
+        lax.fori_loop(i * steps // len(chunks), (i + 1) * steps // len(chunks), part, 0)
 
 
 def columns_beside(field, left, right):
@@ -148,27 +169,34 @@
     outs, refs = (refs[:1], refs[1:]) if alone else (refs[:5], refs[5:])
     held, rest = refs[:11], refs[11:]
     win, perm, lhs, mix, near_coarse, shifted, fine_win, fine_perm, fine_lhs, fine_mix = rest[:10]
-    lefts, rights, to_left, to_right, sems = rest[10:]
+    lefts, rights, to_left, to_right, sems, chunk_sems = rest[10:]
     sky_ref = outs[0]
     if alone:
         for ref in held[1:7]:
             ref[...] = jnp.zeros_like(ref)
-        copies = fetched(zip(sources, (held[0],) + tuple(held[7:])), sems)
+        held_here = (held[0], *held[7:])
     else:
-        copies = fetched(zip(sources, held), sems)
+        held_here = held
+    copies = fetched(zip(sources[:-2], held_here[:-2]), sems)
+    chunks = chunked(sources[-2], held_here[-2], chunk_sems)
+    copies += fetched(zip(sources[-1:], held_here[-1:]), sems, len(copies))
     xi_coarse, over, under, left_in, right_in, left_side, right_side = held[:7]
     coef_middle, xi_middle, coef_fine, xi_fine = held[7:]
     rows, cols = win.shape[1:]
     perm[...] = interleaver(cols, False)
     fine_perm[...] = interleaver(2 * cols, False)
     near_coarse[...] = jnp.zeros_like(near_coarse)
-    for copy in copies[:-3]:
+    for copy in copies[:-2]:
         copy.wait()
     above, below = over[:, 2 : cols + 2], under[:, 2 : cols + 2]
-    stretch(lefts, left_in, over, under, 1, 1, 0)
-    stretch(rights, right_in, over, under, 0, cols + 2, cols + 2)
-    stretch(to_left, left_side, over, under, 0, 2, 2)
-    stretch(to_right, right_side, over, under, 1, cols + 1, cols)
+    if alone:
+        for ref in (lefts, rights):
+            ref[...] = jnp.zeros_like(ref)
+    else:
+        stretch(lefts, left_in, over, under, 1, 1, 0)
+        stretch(rights, right_in, over, under, 0, cols + 2, cols + 2)
+        stretch(to_left, left_side, over, under, 0, 2, 2)
+        stretch(to_right, right_side, over, under, 1, cols + 1, cols)
     near_coarse[1, 6:8] = above[18:20]
     near_coarse[1, 8 : 8 + rows] = xi_coarse[...]
     near_coarse[1, 8 + rows : 10 + rows] = below[18:20]
@@ -204,16 +232,21 @@
         inner = jnp.concatenate([line[:, 1 : rows + 1] for line in out], axis=1)
         return inner, out[1][:, :1], out[0][:, rows + 1 :]
 
-    top, bottom = across(above, 6), across(below, rows + 7)
-    left, top_left, bottom_left = along(
-        lefts, [row_of(lefts, 18), row_of(lefts, 19), row_of(to_left, 18)]
-    )
-    right, top_right, bottom_right = along(
-        rights, [row_of(to_right, 19), row_of(rights, 18), row_of(rights, 19)]
-    )
+    if alone:
+        empty = jnp.zeros((1, 1), f32)
+        top = bottom = left = right = jnp.zeros((1, 2 * cols), f32)
+        top_left = bottom_left = top_right = bottom_right = empty
+    else:
+        top, bottom = across(above, 6), across(below, rows + 7)
+        left, top_left, bottom_left = along(
+            lefts, [row_of(lefts, 18), row_of(lefts, 19), row_of(to_left, 18)]
+        )
+        right, top_right, bottom_right = along(
+            rights, [row_of(to_right, 19), row_of(rights, 18), row_of(rights, 19)]
+        )
     lines = jnp.concatenate([top, bottom, left, right, jnp.zeros((4, 2 * cols), f32)])
     lines = moved(lines, perm[...])
-    copies[-3].wait()
+    copies[-2].wait()
     xi = xi_middle[...]
     last = 8 + 2 * rows
     shifted[1] = jnp.zeros(shifted.shape[1:], f32)
@@ -234,8 +267,7 @@
     for near in range(9):
         r, c = near // 3, near % 3
         fine_win[near] = shifted[c, 7 + r : 7 + r + 2 * rows, :]
-    copies[-2].wait()
-    weighed(fine_win, coef_fine, fine_perm, fine_lhs, fine_mix, 2 * rows, 2 * cols)
+    weighed(fine_win, coef_fine, fine_perm, fine_lhs, fine_mix, 2 * rows, 2 * cols, chunks)
     copies[-1].wait()
     for tile in range(4 * cols // 128):
         lanes = slice(tile * 128, (tile + 1) * 128)
@@ -340,13 +372,14 @@
             pltpu.VMEM((4 * cols // 128, 4 * rows, 128), f32),
             *[pltpu.VMEM((22, rows + 4), f32) for _ in range(4)],
             pltpu.SemaphoreType.DMA((11,)),
+            pltpu.SemaphoreType.DMA((4,)),
         ],
         compiler_params=pltpu.CompilerParams(vmem_limit_bytes=60 * 1024 * 1024),
         name="sky",
     )(*operands)
 
 
-def spread(mix, coef_ref, terms, rows, cols):
+def spread(mix, coef_ref, terms, rows, cols, chunks=()):
     def part(i, carry):
         r0 = pl.multiple_of(i * 16, 16)
         quads = []
@@ -362,7 +395,7 @@
             terms[near, pl.ds(r0, 16), :] = total
         return carry
 
-    lax.fori_loop(0, rows // 16, part, 0)
+    in_chunks(part, rows, chunks)
 
 
 def joined(rowed, cols):
@@ -382,22 +415,28 @@
     return main, outside[0], outside[1]
 
 
-def adjoint_kernel(edge, number, *refs):
-    count = 6 if edge else 9
-    parts, sources = refs[:number], refs[number : number + count]
-    outs, refs = refs[number + count :][: 5 if edge else 3], refs[number + count :][5 if edge else 3 :]
-    held, rest = refs[:count], refs[count:]
-    fine_perm, fine_mix, fine_terms, fine_rowed, perm, mix, terms, rowed, full, sems, out_sem = rest
-    copies = fetched(zip(sources, held), sems)
+def adjoint_kernel(edge, number, cells, *refs):
+    count = 6 if edge else 15
+    written = 5 if edge else 4
+    count += number
+    sources, outs, refs = refs[:count], refs[count : count + written], refs[count + written :]
+    parts, held, rest = refs[:number], refs[number:count], refs[count:]
+    fine_perm, fine_mix, fine_terms, fine_rowed, perm, mix, terms, rowed, full, sems, chunk_sems, out_sem = rest
+    arriving = fetched(zip(sources[:number], parts), sems)
+    chunks = chunked(sources[number], held[0], chunk_sems)
+    copies = [None] + fetched(zip(sources[number + 1 :], held[1:]), sems, number)
     coef_fine, coef_middle, over, under, lefts, rights = held[:6]
     if edge:
         left_ref, right_ref, upper_ref, lower_ref, total_ref = outs
     else:
-        grad_ref, middle_ref, coarse_ref = outs
-        xi_fine, xi_middle, xi_coarse = held[6:]
+        grad_ref, middle_ref, coarse_ref, total_ref = outs
+        xi_fine, xi_middle, xi_coarse, from_left, from_right, from_above, from_below = held[6:13]
+        total, other = held[13:]
     rows, cols = terms.shape[1:]
     fine_perm[...] = interleaver(2 * cols, True)
     perm[...] = interleaver(cols, True)
+    for copy in arriving:
+        copy.wait()
     g = parts[0][...].astype(f32)
     for part in parts[1:]:
         g += part[...].astype(f32)
@@ -420,8 +459,7 @@
     split = moved(g, fine_perm[...])
     for tile in range(4 * cols // 128):
         fine_mix[tile] = split[:, tile * 128 : (tile + 1) * 128]
-    copies[0].wait()
-    spread(fine_mix, coef_fine, fine_terms, 2 * rows, 2 * cols)
+    spread(fine_mix, coef_fine, fine_terms, 2 * rows, 2 * cols, chunks)
     fine_rowed[...] = jnp.zeros_like(fine_rowed)
     for near in range(9):
         r, c = near // 3, near % 3
@@ -433,7 +471,14 @@
         copy.wait()
     above, below = over[:, 2 : cols + 2], under[:, 2 : cols + 2]
     if not edge:
-        middle_ref[...] = inner + xi_middle[...]
+        line = slice(1, 2 * rows + 1)
+        middle_ref[...] = (
+            inner
+            + xi_middle[...]
+            + ends_placed(from_left[2:3, line], from_right[2:3, line], 2 * cols)
+        )
+        middle_ref[:1] += from_above[2:3, 1 : 2 * cols + 1]
+        middle_ref[2 * rows - 1 :] += from_below[2:3, 1 : 2 * cols + 1]
     split = moved(inner, perm[...])
     for tile in range(2 * cols // 128):
         mix[tile] = split[:, tile * 128 : (tile + 1) * 128]
@@ -474,11 +519,22 @@
     outer_right = along(3, right, rights)
     main, near_left, near_right = joined(rowed, cols)
     if not edge:
+        line = slice(2, rows + 2)
+        first = outer_left[2][:, line] + from_left[1:2, line]
+        last = outer_right[0][:, line] + from_right[1:2, line]
+        second = ends_placed(from_left[0:1, line], from_right[0:1, line], cols)
+        lane = lax.broadcasted_iota(jnp.int32, second.shape, 1)
+        second = jnp.where(lane == 1, pltpu.roll(second, 1, 1), 0.0) + jnp.where(
+            lane == cols - 2, pltpu.roll(second, cols - 1, 1), 0.0
+        )
         coarse_ref[...] = (
-            main[8 : 8 + rows]
-            + xi_coarse[...]
-            + ends_placed(outer_left[2][:, 2 : rows + 2], outer_right[0][:, 2 : rows + 2], cols)
+            main[8 : 8 + rows] + xi_coarse[...] + ends_placed(first, last, cols) + second
         )
+        coarse_ref[:2] += from_above[0:2, 2 : cols + 2]
+        coarse_ref[rows - 2 :] += from_below[0:2, 2 : cols + 2]
+        both = total[...] + other[...]
+        both = jnp.sum(jnp.sum(both, axis=1, keepdims=True), axis=0, keepdims=True)
+        total_ref[...] = both * (1.0 / cells)
         leaving.wait()
         return
     sides = []
@@ -528,48 +584,11 @@
     total_out[...] = total[...] + other[...]
 
 
-def final_kernel(
-    cells,
-    middle,
-    coarse,
-    from_left,
-    from_right,
-    from_above,
-    from_below,
-    total,
-    other,
-    middle_out,
-    coarse_out,
-    total_out,
-):
-    rows, cols = coarse.shape
-    middle_out[...] = middle[...] + ends_placed(
-        from_left[2:3, 1 : 2 * rows + 1], from_right[2:3, 1 : 2 * rows + 1], 2 * cols
-    )
-    line = slice(1, 2 * cols + 1)
-    middle_out[:1] += from_above[2:3, line]
-    middle_out[2 * rows - 1 :] += from_below[2:3, line]
-    inner = slice(2, rows + 2)
-    outer = ends_placed(from_left[1:2, inner], from_right[1:2, inner], cols)
-    second = ends_placed(from_left[0:1, inner], from_right[0:1, inner], cols)
-    lane = lax.broadcasted_iota(jnp.int32, second.shape, 1)
-    second = jnp.where(lane == 1, pltpu.roll(second, 1, 1), 0.0) + jnp.where(
-        lane == cols - 2, pltpu.roll(second, cols - 1, 1), 0.0
-    )
-    coarse_out[...] = coarse[...] + outer + second
-    line = slice(2, cols + 2)
-    coarse_out[:2] += from_above[0:2, line]
-    coarse_out[rows - 2 :] += from_below[0:2, line]
-    both = total[...] + other[...]
-    both = jnp.sum(jnp.sum(both, axis=1, keepdims=True), axis=0, keepdims=True)
-    total_out[...] = both * (1.0 / cells)
-
-
 def shape(*dims):
     return jax.ShapeDtypeStruct(dims, f32)
 
 
-def adjoint(edge, parts, sides, fields):
+def adjoint(edge, parts, sides, fields, arrived=(), cells=0):
     rows, cols = fields[1].shape[2:]
     xi_coarse, coef_middle, xi_middle, coef_fine, xi_fine = fields
     wide = 2 * rows + 128
@@ -577,14 +596,15 @@
     if edge:
         outs = [shape(8, wide)] * 2 + [shape(8, 2 * cols + 128)] * 2 + [shape(8, 128)]
     else:
-        operands += (xi_fine, xi_middle, xi_coarse)
+        operands += (xi_fine, xi_middle, xi_coarse, *arrived)
         outs = [shape(4 * rows, 4 * cols), shape(2 * rows, 2 * cols), shape(rows, cols)]
+        outs += [shape(1, 1)]
     return pl.pallas_call(
-        functools.partial(adjoint_kernel, edge, len(parts)),
-        in_specs=[whole] * len(parts) + [anywhere] * len(operands),
-        out_specs=[whole] * len(outs) if edge else [anywhere, whole, whole],
+        functools.partial(adjoint_kernel, edge, len(parts), cells),
+        in_specs=[anywhere] * (len(parts) + len(operands)),
+        out_specs=[whole] * 5 if edge else [anywhere, whole, whole, whole],
         out_shape=outs,
-        scratch_shapes=[pltpu.VMEM(x.shape, x.dtype) for x in operands]
+        scratch_shapes=[pltpu.VMEM(x.shape, x.dtype) for x in (*parts, *operands)]
         + [
             pltpu.VMEM((4 * cols, 4 * cols), bf16),
             pltpu.VMEM((4 * cols // 128, 4 * rows, 128), f32),
@@ -595,10 +615,11 @@
             pltpu.VMEM((9, rows, cols), f32),
             pltpu.VMEM((3, rows + 128, cols), f32),
             pltpu.VMEM((4 * rows, 4 * cols), f32),
-            pltpu.SemaphoreType.DMA((len(operands),)),
+            pltpu.SemaphoreType.DMA((len(parts) + len(operands),)),
+            pltpu.SemaphoreType.DMA((4,)),
             pltpu.SemaphoreType.DMA,
         ],
-        compiler_params=pltpu.CompilerParams(vmem_limit_bytes=vmem),
+        compiler_params=pltpu.CompilerParams(vmem_limit_bytes=60 * 1024 * 1024),
         cost_estimate=long_work if edge else None,
         name="adjoint",
     )(*parts, *operands)
@@ -733,7 +754,7 @@
             pltpu.SemaphoreType.DMA((number, slots)),
             pltpu.SemaphoreType.DMA((number, slots)),
         ],
-        compiler_params=pltpu.CompilerParams(vmem_limit_bytes=60 * 1024 * 1024),
+        compiler_params=pltpu.CompilerParams(vmem_limit_bytes=44 * 1024 * 1024),
         name="facets",
     )(ints, weights, *tiles, *strips, ku, kv, data, squares)
 
@@ -805,7 +826,23 @@
     facet_weight,
     facet_count,
 ):
-    lists, weights, counts = facet_tiles[0], facet_weight[0], facet_count[0]
+    fields = (xi_coarse, coef_middle, xi_middle, coef_fine, xi_fine)
+    right, left = neighbours("gy")
+    down, up = neighbours("gx")
+    sides = halo_sides(xi_coarse, xi_middle, coef_middle)
+    left_in = lax.ppermute(sides[1], "gy", right)
+    right_in = lax.ppermute(sides[0], "gy", left)
+    (first,) = sky_of(None, *fields)
+    first, left_in, right_in, around, listed = lax.optimization_barrier(
+        (
+            first,
+            left_in,
+            right_in,
+            (xi_coarse, xi_middle, coef_middle),
+            (facet_tiles[0], facet_weight[0], facet_count[0]),
+        )
+    )
+    lists, weights, counts = listed
     size = lax.axis_size("gy")
     chips = size // 2
     me = lax.axis_index("gy")
@@ -817,27 +854,17 @@
     scale = jnp.concatenate([mixing, swapped(mixing)])[:, order].T
     sel = (me // 2 - lists // 2) % chips + jnp.where(lists % 2 == me % 2, 0, chips)
     ints = jnp.concatenate([sel, counts[:, None]], axis=1)
-    fields = (xi_coarse, coef_middle, xi_middle, coef_fine, xi_fine)
-    right, left = neighbours("gy")
-    down, up = neighbours("gx")
-    sides = halo_sides(xi_coarse, xi_middle, coef_middle)
-    left_in = lax.ppermute(sides[1], "gy", right)
-    right_in = lax.ppermute(sides[0], "gy", left)
-    (first,) = sky_of(None, *fields)
-    first, left_in, right_in, around = lax.optimization_barrier(
-        (first, left_in, right_in, (xi_coarse, xi_middle, coef_middle))
-    )
     hops = range(1, chips)
     early = range(1, min(3, chips))
     mine = {hop: chip_shift(first, hop) for hop in early}
     above, below = halo_rows(*around, left_in, right_in)
     sky, strips, squares, lefts, rights = sky_of((above, below, left_in, right_in, *sides), *fields)
     strips = jnp.concatenate([chip_shift(strips, hop) for hop in early])
-    sky, strips, mine, scale, ints, weights = lax.optimization_barrier(
-        (sky, strips, mine, scale, ints, weights)
+    late = {hop: chip_shift(sky, hop) for hop in hops[len(early) :]}
+    strips, mine, scale, ints, weights = lax.optimization_barrier(
+        (strips, mine, scale, ints, weights)
     )
-    for hop in hops[len(early) :]:
-        mine[hop] = chip_shift(sky, hop)
+    mine |= late
     mine = [sky] + [mine[hop] for hop in hops]
     tiles = mine + [swapped(tile) for tile in mine]
     strips = [strips, swapped(strips)]
@@ -847,7 +874,7 @@
     strips, dsums, theirs = lax.optimization_barrier((strips, dsums, theirs))
     edges = [strips[0]] + [chip_shift(strips[hop], hop) for hop in hops]
     parts = mixed(dsums, theirs, scale, False)
-    edges, parts = lax.optimization_barrier((edges, parts))
+    edges, _ = lax.optimization_barrier((edges, parts))
     parts = [parts[0]] + [chip_shift(parts[hop], hop) for hop in hops]
     around = (above, below, lefts, rights)
     to_left, to_right, upper, lower, total = adjoint(True, edges, around, fields)
@@ -871,19 +898,16 @@
     for hop in steps[1:-1]:
         total += across(total, hop)
     other = across(total, steps[-1])
-    parts, to_left, to_right = lax.optimization_barrier((parts, to_left, to_right))
     from_left = lax.ppermute(to_right, "gy", right)
     from_right = lax.ppermute(to_left, "gy", left)
-    grad_fine, middle, coarse = adjoint(False, parts, around, fields)
+    parts, from_left, from_right, other = lax.optimization_barrier(
+        (parts, from_left, from_right, other)
+    )
     cells = size * lax.axis_size("gy") * 16 * rows * cols
-    grad_middle, grad_coarse, total = pl.pallas_call(
-        functools.partial(final_kernel, cells),
-        in_specs=[whole] * 8,
-        out_specs=[whole] * 3,
-        out_shape=[shape(2 * rows, 2 * cols), shape(rows, cols), shape(1, 1)],
-        compiler_params=pltpu.CompilerParams(vmem_limit_bytes=vmem),
-        name="final",
-    )(middle, coarse, from_left, from_right, from_above, from_below, total, other)
+    arrived = (from_left, from_right, from_above, from_below, total, other)
+    grad_fine, grad_middle, grad_coarse, total = adjoint(
+        False, parts, around, fields, arrived, cells
+    )
     return grad_coarse, grad_middle, grad_fine, total.reshape(())
 
 

time: 167 us -> 155 us (0.928)
  waiting for transfers between devices: 60.1 us -> 53.9 us
  starting transfers between devices: 43.1 us -> 38.9 us
  local copies, waits for them, and re-layouts: 14.1 us -> 11.8 us
    ppermute x11, waiting for transfers between devices: 48.1 us -> 31.5 us  [chip_shift(): lax.ppermute(x, 'gy', [(i, (i + 2 * hop) % size) for i in range(size)])]
    ppermute x1, waiting for transfers between devices: 0.01 us -> 5.73 us  [body(): from_left = lax.ppermute(to_right, 'gy', right)]
    ppermute x2, waiting for transfers between devices: 0.01 us -> 2.44 us  [across(): return lax.ppermute(x, 'gx', [(i, i ^ hop) for i in range(size)])]
    unnamed x78 -> x58, local copies, waits for them, and re-layouts: 9.8 us -> 7.53 us
    ppermute x1, starting transfers between devices: 3.64 us -> 1.91 us  [body(): from_right = lax.ppermute(to_left, 'gy', left)]
    ppermute x2, starting transfers between devices: 1.76 us -> 0.07 us  [across(): return lax.ppermute(x, 'gx', [(i, i ^ hop) for i in range(size)])]
    pallas_call x3 -> x2, Pallas kernels: 11.8 us -> 13 us  [adjoint(): pl.pallas_call(functools.partial(adjoint_kernel, edge, len(parts), cells)...]
  transfers between devices with their start and end apart: 28 -> 28, of which waited for: 11 -> 14; matrix products, arithmetic and copies ran while one was open for 5% -> 3% of each run, Pallas kernels for 17% -> 15%
where the time goes in v7:
time: 155 us; the launch traced here: 152 us
  waiting for transfers between devices  53.9 us (35%)
  Pallas kernels  42.8 us (28%)
  starting transfers between devices  38.9 us (25%)
  local copies, waits for them, and re-layouts  11.8 us (8%)
  other arithmetic  3.66 us (2%)
    ppermute x11, waiting for transfers between devices, chip_shift(): lax.ppermute(x, 'gy', [(i, (i + 2 * hop) % size) for i in range(size)])  31.5 us
    ppermute x11, starting transfers between devices, chip_shift(): lax.ppermute(x, 'gy', [(i, (i + 2 * hop) % size) for i in range(size)])  17.2 us
    pallas_call x2, Pallas kernels, adjoint(): pl.pallas_call(functools.partial(adjoint_kernel, edge, len(parts), cells)...  13 us
    pallas_call x2, Pallas kernels, sky_of(): pl.pallas_call(functools.partial(sky_kernel, alone), in_specs=[anywhere]...  12.4 us
    pallas_call x1, Pallas kernels, facets(): pl.pallas_call(functools.partial(facets_kernel, 512, strips[0].shape[0] /...  11.1 us
    unnamed x58, local copies, waits for them, and re-layouts  7.53 us
    ppermute x1, waiting for transfers between devices, body(): from_left = lax.ppermute(to_right, 'gy', right)  5.73 us
    ppermute x7, waiting for transfers between devices, swapped(): lax.ppermute(x, 'gy', [(i, i ^ 1) for i in range(lax.axis_size('gy'))])  5.55 us
  transfers between devices with their start and end apart: 28, of which 14 were waited for; matrix products, arithmetic and copies ran while one was open for 3% of the time, Pallas kernels for 15%

profile of v7, /device:TPU:10, one launch (start us, length us, event | category | flops | bytes accessed | tf_op | source)
XLA Modules:
  0.0 152.4 jit_solution(5051906759793593718)
XLA Ops:
  1.8 1.8 %convert_reduce_fusion = (f32[2,9,128]{2,1,0:T(8,128)S(1)}, f32[2,9,128]{2,1,0:T(8,128)S(1)}) fusion(bf16[4,9,128,128]{3,2,1,0:T(8,128)(2,1)} %refs_5_.3), kind=kLoop, calls=%fused_computation.1 | loop fusion | flops 4608 | bytes 27648 | tf_op jit(solution)/shard_map/convert_element_type | solution.py:304
  4.1 1.9 %collective-permute-start = (f32[22,128]{1,0:T(8,128)S(1)}, f32[22,128]{1,0:T(8,128)S(1)}, u32[]{:S(2)}, u32[]{:S(2)}) collective-permute-start(f32[22,128]{1,0:T(8,128)S(1)} %pad_maximum_fusion.1.refs_6_), channel_id=1, source_target_pairs={{0,1},{1,2},{2,3},{3,4},{4,5},{5,6},{6,7},{8,9},{9,10},{10,11},{11... | collective-permute-start | bytes 33800 | tf_op jit(solution)/shard_map/ppermute | solution.py:833
  6.4 3.6 %collective-permute-start.1 = (f32[22,128]{1,0:T(8,128)S(1)}, f32[22,128]{1,0:T(8,128)S(1)}, u32[]{:S(2)}, u32[]{:S(2)}) collective-permute-start(f32[22,128]{1,0:T(8,128)S(1)} %pad_maximum_fusion.2.refs_5_), channel_id=1, source_target_pairs={{1,0},{2,1},{3,2},{4,3},{5,4},{6,5},{7,6},{9,8},{10,9},{11,10},{12... | collective-permute-start | bytes 33800 | tf_op jit(solution)/shard_map/ppermute | solution.py:834
  10.1 6.0 %sky.2 = bf16[512,512]{1,0:T(8,128)(2,1)} custom-call(f32[128,128]{1,0:T(8,128)} %refs_12_.3, bf16[4,9,128,128]{3,2,1,0:T(8,128)(2,1)} %refs_5_.3, f32[256,256]{1,0:T(8,128)} %refs_11_.3, bf16[4,9,256,256]{3,2,1,0:T(8,128)(2,1)} %refs_4_.5, f32[512,512]{1,0:T(8,128)} %refs_10_.5), custom_call_target="tpu_custom_call" | custom-call | tf_op jit(solution)/shard_map/sky/pallas_call | solution.py:348
  16.1 2.7 %collective-permute-start.7 = (bf16[512,512]{1,0:T(8,128)(2,1)}, bf16[512,512]{1,0:T(8,128)(2,1)S(1)}, u32[]{:S(2)}, u32[]{:S(2)}) collective-permute-start(bf16[512,512]{1,0:T(8,128)(2,1)} %sky.2), channel_id=1, source_target_pairs={{0,4},{1,5},{2,6},{3,7},{4,0},{5,1},{6,2},{7,3},{8,12},{9,13},{10,... | collective-permute-start | bytes 1572872 | tf_op jit(solution)/shard_map/ppermute | solution.py:809
  22.2 1.5 sides.1
  23.7 3.4 %collective-permute-start.2 = (f32[22,132]{1,0:T(8,128)}, f32[22,132]{1,0:T(8,128)S(1)}, u32[]{:S(2)}, u32[]{:S(2)}) collective-permute-start(f32[22,132]{1,0:T(8,128)} %get-tuple-element.68), channel_id=1, source_target_pairs={{0,8},{8,16},{16,24},{1,9},{9,17},{17,25},{2,10},{10,18},{18,26},{... | collective-permute-start | bytes 34856 | tf_op jit(solution)/shard_map/ppermute | solution.py:334
  27.1 2.4 %collective-permute-start.3 = (f32[22,132]{1,0:T(8,128)}, f32[22,132]{1,0:T(8,128)S(1)}, u32[]{:S(2)}, u32[]{:S(2)}) collective-permute-start(f32[22,132]{1,0:T(8,128)} %get-tuple-element.69), channel_id=1, source_target_pairs={{8,0},{16,8},{24,16},{9,1},{17,9},{25,17},{10,2},{18,10},{26,18},{... | collective-permute-start | bytes 34856 | tf_op jit(solution)/shard_map/ppermute | solution.py:334
  29.8 4.1 %collective-permute-done.3.refs_2_.refs_7_ = f32[22,132]{1,0:T(8,128)S(1)} collective-permute-done((f32[22,132]{1,0:T(8,128)}, f32[22,132]{1,0:T(8,128)S(1)}, u32[]{:S(2)}, u32[]{:S(2)}) %collective-permute-start.3) | collective-permute-done | bytes 11648 | tf_op jit(solution)/shard_map/ppermute | solution.py:334
  34.5 6.5 %sky.3 = (bf16[512,512]{1,0:T(8,128)(2,1)}, bf16[32,512]{1,0:T(8,128)(2,1)}, f32[8,128]{1,0:T(8,128)}, f32[22,132]{1,0:T(8,128)}, f32[22,132]{1,0:T(8,128)}) custom-call(f32[128,128]{1,0:T(8,128)} %refs_12_.3, f32[22,132]{1,0:T(8,128)} %copy-done.11, f32[22,132]{1,0:T(8,128)} %copy-done.12, f32[22,128]{1,0:T(8,128)} %copy-done.17, f32[22,128]{1,0:T(8,128)} %copy-done.18, ...), custom_call_target="tpu_custom_call" | custom-call | tf_op jit(solution)/shard_map/sky/pallas_call | solution.py:348
  41.0 2.1 %collective-permute-start.9 = (bf16[512,512]{1,0:T(8,128)(2,1)}, bf16[512,512]{1,0:T(8,128)(2,1)}, u32[]{:S(2)}, u32[]{:S(2)}) collective-permute-start(bf16[512,512]{1,0:T(8,128)(2,1)} %get-tuple-element.78.refs_0_), channel_id=1, source_target_pairs={{0,6},{1,7},{2,0},{3,1},{4,2},{5,3},{6,4},{7,5},{8,14},{9,15},{10,... | collective-permute-start | bytes 1572872 | tf_op jit(solution)/shard_map/ppermute | solution.py:809
  43.9 2.9 %collective-permute-start.4 = (bf16[32,512]{1,0:T(8,128)(2,1)}, bf16[32,512]{1,0:T(8,128)(2,1)S(1)}, u32[]{:S(2)}, u32[]{:S(2)}) collective-permute-start(bf16[32,512]{1,0:T(8,128)(2,1)} %get-tuple-element.70), channel_id=1, source_target_pairs={{0,2},{1,3},{2,4},{3,5},{4,6},{5,7},{6,0},{7,1},{8,10},{9,11},{10,... | collective-permute-start | bytes 98312 | tf_op jit(solution)/shard_map/ppermute | solution.py:809
  47.5 17.2 %collective-permute-done.5 = bf16[32,512]{1,0:T(8,128)(2,1)S(1)} collective-permute-done((bf16[32,512]{1,0:T(8,128)(2,1)}, bf16[32,512]{1,0:T(8,128)(2,1)S(1)}, u32[]{:S(2)}, u32[]{:S(2)}) %collective-permute-start.5) | collective-permute-done | bytes 32800 | tf_op jit(solution)/shard_map/ppermute | solution.py:809
  66.8 2.1 %collective-permute-done.14.refs_9_ = bf16[64,512]{1,0:T(8,128)(2,1)S(1)} collective-permute-done((bf16[64,512]{1,0:T(8,128)(2,1)S(1)}, bf16[64,512]{1,0:T(8,128)(2,1)S(1)}, u32[]{:S(2)}, u32[]{:S(2)}) %collective-permute-start.14) | collective-permute-done | bytes 65568 | tf_op jit(solution)/shard_map/ppermute | solution.py:813
  69.0 1.6 %copy-done.1 = bf16[1,2,1024,512]{3,2,1,0:T(8,128)(2,1)S(1)} copy-done((bf16[1,2,1024,512]{3,2,1,0:T(8,128)(2,1)S(1)}, bf16[1,2,1024,512]{3,2,1,0:T(8,128)(2,1)}, u32[]{:S(2)}) %copy-start.1) | copy-done | bytes 2097176
  72.3 11.1 %facets.1.mine = bf16[1056,512]{1,0:T(8,128)(2,1)S(1)} custom-call(s32[2,3]{1,0:T(2,128)S(1)} %pad_add_fusion.ints, f32[2,2]{1,0:T(2,128)S(1)} %bitcast.14, bf16[512,512]{1,0:T(8,128)(2,1)S(1)} %copy-done.2, bf16[512,512]{1,0:T(8,128)(2,1)S(1)} %collective-permute-done.6.refs_1_, bf16[512,512]{1,0:T(8,128)(2,1)S(1)} %collective-permute-done.7.refs_2_, ...), custom_call_target="tpu_custom_call" | custom-call | tf_op jit(solution)/shard_map/facets/pallas_call | solution.py:737
  83.6 2.7 %collective-permute-done.15.theirs = bf16[1056,512]{1,0:T(8,128)(2,1)S(1)} collective-permute-done((bf16[1056,512]{1,0:T(8,128)(2,1)S(1)}, bf16[1056,512]{1,0:T(8,128)(2,1)S(1)}, u32[]{:S(2)}, u32[]{:S(2)}) %collective-permute-start.15) | collective-permute-done | bytes 1081376 | tf_op jit(solution)/shard_map/ppermute | solution.py:813
  88.1 2.0 %collective-permute-start.19 = (bf16[64,512]{1,0:T(8,128)(2,1)S(1)}, bf16[64,512]{1,0:T(8,128)(2,1)S(1)}, u32[]{:S(2)}, u32[]{:S(2)}) collective-permute-start(bf16[64,512]{1,0:T(8,128)(2,1)S(1)} %get-tuple-element.94), channel_id=1, source_target_pairs={{0,2},{1,3},{2,4},{3,5},{4,6},{5,7},{6,0},{7,1},{8,10},{9,11},{10,... | collective-permute-start | bytes 196616 | tf_op jit(solution)/shard_map/ppermute | solution.py:809
  91.2 1.9 %collective-permute-start.21 = (bf16[64,512]{1,0:T(8,128)(2,1)S(1)}, bf16[64,512]{1,0:T(8,128)(2,1)S(1)}, u32[]{:S(2)}, u32[]{:S(2)}) collective-permute-start(bf16[64,512]{1,0:T(8,128)(2,1)S(1)} %get-tuple-element.96), channel_id=1, source_target_pairs={{0,6},{1,7},{2,0},{3,1},{4,2},{5,3},{6,4},{7,5},{8,14},{9,15},{10,... | collective-permute-start | bytes 196616 | tf_op jit(solution)/shard_map/ppermute | solution.py:809
  93.0 2.1 %mixed.3 = (bf16[512,512]{1,0:T(8,128)(2,1)S(1)}, bf16[512,512]{1,0:T(8,128)(2,1)S(1)}, bf16[512,512]{1,0:T(8,128)(2,1)S(1)}, bf16[512,512]{1,0:T(8,128)(2,1)S(1)}) custom-call(f32[4,4]{1,0:T(4,128)S(1)} %gather_fusion, bf16[1056,512]{1,0:T(8,128)(2,1)S(1)} %facets.1.mine, bf16[1056,512]{1,0:T(8,128)(2,1)S(1)} %collective-permute-done.15.theirs), custom_call_target="tpu_custom_call" | custom-call | tf_op jit(solution)/shard_map/mixed/pallas_call | solution.py:796
  96.1 3.7 %collective-permute-start.17 = (bf16[512,512]{1,0:T(8,128)(2,1)S(1)}, bf16[512,512]{1,0:T(8,128)(2,1)S(1)}, u32[]{:S(2)}, u32[]{:S(2)}) collective-permute-start(bf16[512,512]{1,0:T(8,128)(2,1)S(1)} %get-tuple-element.91), channel_id=1, source_target_pairs={{0,4},{1,5},{2,6},{3,7},{4,0},{5,1},{6,2},{7,3},{8,12},{9,13},{10,... | collective-permute-start | bytes 1572872 | tf_op jit(solution)/shard_map/ppermute | solution.py:809
  100.4 5.6 %adjoint.2 = (f32[8,384]{1,0:T(8,128)}, f32[8,384]{1,0:T(8,128)}, f32[8,384]{1,0:T(8,128)}, f32[8,384]{1,0:T(8,128)}, f32[8,128]{1,0:T(8,128)}) custom-call(bf16[64,512]{1,0:T(8,128)(2,1)} %copy-done.6, bf16[64,512]{1,0:T(8,128)(2,1)} %copy-done.24, bf16[64,512]{1,0:T(8,128)(2,1)} %copy-done.25, bf16[64,512]{1,0:T(8,128)(2,1)} %copy-done.26, ...), custom_call_target="tpu_custom_call" | custom-call | flops 40000000000 | bytes 64000000 | tf_op jit(solution)/shard_map/adjoint/pallas_call | solution.py:602
  106.1 3.3 %collective-permute-start.22 = (f32[8,384]{1,0:T(8,128)}, f32[8,384]{1,0:T(8,128)S(1)}, u32[]{:S(2)}, u32[]{:S(2)}) collective-permute-start(f32[8,384]{1,0:T(8,128)} %get-tuple-element.105), channel_id=1, source_target_pairs={{0,8},{8,16},{16,24},{1,9},{9,17},{17,25},{2,10},{10,18},{18,26},{... | collective-permute-start | bytes 36872 | tf_op jit(solution)/shard_map/ppermute | solution.py:888
  109.9 2.1 %collective-permute-start.23 = (f32[8,384]{1,0:T(8,128)}, f32[8,384]{1,0:T(8,128)S(1)}, u32[]{:S(2)}, u32[]{:S(2)}) collective-permute-start(f32[8,384]{1,0:T(8,128)} %get-tuple-element.106), channel_id=1, source_target_pairs={{8,0},{16,8},{24,16},{9,1},{17,9},{25,17},{10,2},{18,10},{26,18},{... | collective-permute-start | bytes 36872 | tf_op jit(solution)/shard_map/ppermute | solution.py:887
  112.0 4.6 %collective-permute-done.23.from_below.refs_16_ = f32[8,384]{1,0:T(8,128)S(1)} collective-permute-done((f32[8,384]{1,0:T(8,128)}, f32[8,384]{1,0:T(8,128)S(1)}, u32[]{:S(2)}, u32[]{:S(2)}) %collective-permute-start.23) | collective-permute-done | bytes 12320 | tf_op jit(solution)/shard_map/ppermute | solution.py:887
  118.7 1.9 %collective-permute-start.25 = (f32[8,384]{1,0:T(8,128)}, f32[8,384]{1,0:T(8,128)S(1)}, u32[]{:S(2)}, u32[]{:S(2)}) collective-permute-start(f32[8,384]{1,0:T(8,128)} %get-tuple-element.108), channel_id=1, source_target_pairs={{0,1},{1,2},{2,3},{3,4},{4,5},{5,6},{6,7},{8,9},{9,10},{10,11},{11... | collective-permute-start | bytes 36872 | tf_op jit(solution)/shard_map/ppermute | solution.py:901
  120.6 1.9 %collective-permute-done.27.refs_18_ = f32[8,128]{1,0:T(8,128)S(1)} collective-permute-done((f32[8,128]{1,0:T(8,128)}, f32[8,128]{1,0:T(8,128)S(1)}, u32[]{:S(2)}, u32[]{:S(2)}) %collective-permute-start.27) | collective-permute-done | bytes 4128 | tf_op jit(solution)/shard_map/ppermute | solution.py:885
  122.5 1.9 %collective-permute-start.26 = (f32[8,384]{1,0:T(8,128)}, f32[8,384]{1,0:T(8,128)S(1)}, u32[]{:S(2)}, u32[]{:S(2)}) collective-permute-start(f32[8,384]{1,0:T(8,128)} %get-tuple-element.109), channel_id=1, source_target_pairs={{1,0},{2,1},{3,2},{4,3},{5,4},{6,5},{7,6},{9,8},{10,9},{11,10},{12... | collective-permute-start | bytes 36872 | tf_op jit(solution)/shard_map/ppermute | solution.py:902
  124.4 5.7 %collective-permute-done.25.refs_13_ = f32[8,384]{1,0:T(8,128)S(1)} collective-permute-done((f32[8,384]{1,0:T(8,128)}, f32[8,384]{1,0:T(8,128)S(1)}, u32[]{:S(2)}, u32[]{:S(2)}) %collective-permute-start.25) | collective-permute-done | bytes 12320 | tf_op jit(solution)/shard_map/ppermute | solution.py:901
  130.2 11.0 %collective-permute-done.17.refs_2_ = bf16[512,512]{1,0:T(8,128)(2,1)S(1)} collective-permute-done((bf16[512,512]{1,0:T(8,128)(2,1)S(1)}, bf16[512,512]{1,0:T(8,128)(2,1)S(1)}, u32[]{:S(2)}, u32[]{:S(2)}) %collective-permute-start.17) | collective-permute-done | bytes 524320 | tf_op jit(solution)/shard_map/ppermute | solution.py:809
  141.2 2.8 %collective-permute-done.18.refs_3_ = bf16[512,512]{1,0:T(8,128)(2,1)S(1)} collective-permute-done((bf16[512,512]{1,0:T(8,128)(2,1)S(1)}, bf16[512,512]{1,0:T(8,128)(2,1)S(1)}, u32[]{:S(2)}, u32[]{:S(2)}) %collective-permute-start.18) | collective-permute-done | bytes 524320 | tf_op jit(solution)/shard_map/ppermute | solution.py:809
  144.9 7.3 %adjoint.3 = (f32[512,512]{1,0:T(8,128)}, f32[256,256]{1,0:T(8,128)}, f32[128,128]{1,0:T(8,128)}, f32[1,1]{1,0:T(1,128)}) custom-call(bf16[512,512]{1,0:T(8,128)(2,1)} %copy-done.3, bf16[512,512]{1,0:T(8,128)(2,1)} %copy-done.8, bf16[512,512]{1,0:T(8,128)(2,1)} %copy-done.9, bf16[512,512]{1,0:T(8,128)(2,1)} %copy-done.10, bf16[4,9,256,256]{3,2,1,0:T(8,128)(2,1)} %refs_4_.5, ...), custom_call_target="tpu_custom_call" | custom-call | tf_op jit(solution)/shard_map/adjoint/pallas_call | solution.py:602
  (122 shorter events, 19.7 us)
Async XLA Ops:
  4.1 12.0 %collective-permute-start = (f32[22,128]{1,0:T(8,128)S(1)}, f32[22,128]{1,0:T(8,128)S(1)}, u32[]{:S(2)}, u32[]{:S(2)}) collective-permute-start(f32[22,128]{1,0:T(8,128)S(1)} %pad_maximum_fusion.1.refs_6_), channel_id=1, source_target_pairs={{0,1},{1,2},{2,3},{3,4},{4,5},{5,6},{6,7},{8,9},{9,10},{10,11},{11... | collective-permute-start | bytes 33800 | tf_op jit(solution)/shard_map/ppermute | solution.py:833
  6.4 9.7 %collective-permute-start.1 = (f32[22,128]{1,0:T(8,128)S(1)}, f32[22,128]{1,0:T(8,128)S(1)}, u32[]{:S(2)}, u32[]{:S(2)}) collective-permute-start(f32[22,128]{1,0:T(8,128)S(1)} %pad_maximum_fusion.2.refs_5_), channel_id=1, source_target_pairs={{1,0},{2,1},{3,2},{4,3},{5,4},{6,5},{7,6},{9,8},{10,9},{11,10},{12... | collective-permute-start | bytes 33800 | tf_op jit(solution)/shard_map/ppermute | solution.py:834
  16.1 48.9 %collective-permute-start.7 = (bf16[512,512]{1,0:T(8,128)(2,1)}, bf16[512,512]{1,0:T(8,128)(2,1)S(1)}, u32[]{:S(2)}, u32[]{:S(2)}) collective-permute-start(bf16[512,512]{1,0:T(8,128)(2,1)} %sky.2), channel_id=1, source_target_pairs={{0,4},{1,5},{2,6},{3,7},{4,0},{5,1},{6,2},{7,3},{8,12},{9,13},{10,... | collective-permute-start | bytes 1572872 | tf_op jit(solution)/shard_map/ppermute | solution.py:809
  18.8 46.3 %collective-permute-start.6 = (bf16[512,512]{1,0:T(8,128)(2,1)}, bf16[512,512]{1,0:T(8,128)(2,1)S(1)}, u32[]{:S(2)}, u32[]{:S(2)}) collective-permute-start(bf16[512,512]{1,0:T(8,128)(2,1)} %sky.2), channel_id=1, source_target_pairs={{0,2},{1,3},{2,4},{3,5},{4,6},{5,7},{6,0},{7,1},{8,10},{9,11},{10,... | collective-permute-start | bytes 1572872 | tf_op jit(solution)/shard_map/ppermute | solution.py:809
  23.7 6.1 %collective-permute-start.2 = (f32[22,132]{1,0:T(8,128)}, f32[22,132]{1,0:T(8,128)S(1)}, u32[]{:S(2)}, u32[]{:S(2)}) collective-permute-start(f32[22,132]{1,0:T(8,128)} %get-tuple-element.68), channel_id=1, source_target_pairs={{0,8},{8,16},{16,24},{1,9},{9,17},{17,25},{2,10},{10,18},{18,26},{... | collective-permute-start | bytes 34856 | tf_op jit(solution)/shard_map/ppermute | solution.py:334
  27.1 6.8 %collective-permute-start.3 = (f32[22,132]{1,0:T(8,128)}, f32[22,132]{1,0:T(8,128)S(1)}, u32[]{:S(2)}, u32[]{:S(2)}) collective-permute-start(f32[22,132]{1,0:T(8,128)} %get-tuple-element.69), channel_id=1, source_target_pairs={{8,0},{16,8},{24,16},{9,1},{17,9},{25,17},{10,2},{18,10},{26,18},{... | collective-permute-start | bytes 34856 | tf_op jit(solution)/shard_map/ppermute | solution.py:334
  29.8 14.2 %collective-permute-start.8 = (f32[2,8]{0,1:T(8,128)S(1)}, f32[2,8]{0,1:T(8,128)S(1)}, u32[]{:S(2)}, u32[]{:S(2)}) collective-permute-start(f32[2,8]{0,1:T(8,128)S(1)} %copy.32), channel_id=1, source_target_pairs={{0,1},{1,0},{2,3},{3,2},{4,5},{5,4},{6,7},{7,6},{8,9},{9,8},{10,11... | collective-permute-start | bytes 200 | tf_op jit(solution)/shard_map/ppermute | solution.py:813
  34.5 34.5 %copy-start = (bf16[1,2,1024,512]{3,2,1,0:T(8,128)(2,1)S(1)}, bf16[1,2,1024,512]{3,2,1,0:T(8,128)(2,1)}, u32[]{:S(2)}) copy-start(bf16[1,2,1024,512]{3,2,1,0:T(8,128)(2,1)} %refs_10_.4) | copy-start | bytes 6291460
  41.0 24.7 %collective-permute-start.9 = (bf16[512,512]{1,0:T(8,128)(2,1)}, bf16[512,512]{1,0:T(8,128)(2,1)}, u32[]{:S(2)}, u32[]{:S(2)}) collective-permute-start(bf16[512,512]{1,0:T(8,128)(2,1)} %get-tuple-element.78.refs_0_), channel_id=1, source_target_pairs={{0,6},{1,7},{2,0},{3,1},{4,2},{5,3},{6,4},{7,5},{8,14},{9,15},{10,... | collective-permute-start | bytes 1572872 | tf_op jit(solution)/shard_map/ppermute | solution.py:809
  43.1 21.5 %collective-permute-start.5 = (bf16[32,512]{1,0:T(8,128)(2,1)}, bf16[32,512]{1,0:T(8,128)(2,1)S(1)}, u32[]{:S(2)}, u32[]{:S(2)}) collective-permute-start(bf16[32,512]{1,0:T(8,128)(2,1)} %get-tuple-element.70), channel_id=1, source_target_pairs={{0,4},{1,5},{2,6},{3,7},{4,0},{5,1},{6,2},{7,3},{8,12},{9,13},{10,... | collective-permute-start | bytes 98312 | tf_op jit(solution)/shard_map/ppermute | solution.py:809
  43.9 21.1 %collective-permute-start.4 = (bf16[32,512]{1,0:T(8,128)(2,1)}, bf16[32,512]{1,0:T(8,128)(2,1)S(1)}, u32[]{:S(2)}, u32[]{:S(2)}) collective-permute-start(bf16[32,512]{1,0:T(8,128)(2,1)} %get-tuple-element.70), channel_id=1, source_target_pairs={{0,2},{1,3},{2,4},{3,5},{4,6},{5,7},{6,0},{7,1},{8,10},{9,11},{10,... | collective-permute-start | bytes 98312 | tf_op jit(solution)/shard_map/ppermute | solution.py:809
  64.7 2.1 %collective-permute-start.10 = (bf16[512,512]{1,0:T(8,128)(2,1)}, bf16[512,512]{1,0:T(8,128)(2,1)S(1)}, u32[]{:S(2)}, u32[]{:S(2)}) collective-permute-start(bf16[512,512]{1,0:T(8,128)(2,1)} %get-tuple-element.78.refs_0_), channel_id=1, source_target_pairs={{0,1},{1,0},{2,3},{3,2},{4,5},{5,4},{6,7},{7,6},{8,9},{9,8},{10,11... | collective-permute-start | bytes 1572872 | tf_op jit(solution)/shard_map/ppermute | solution.py:813
  65.0 3.9 %collective-permute-start.11 = (bf16[512,512]{1,0:T(8,128)(2,1)S(1)}, bf16[512,512]{1,0:T(8,128)(2,1)S(1)}, u32[]{:S(2)}, u32[]{:S(2)}) collective-permute-start(bf16[512,512]{1,0:T(8,128)(2,1)S(1)} %collective-permute-done.6.refs_1_), channel_id=1, source_target_pairs={{0,1},{1,0},{2,3},{3,2},{4,5},{5,4},{6,7},{7,6},{8,9},{9,8},{10,11... | collective-permute-start | bytes 1572872 | tf_op jit(solution)/shard_map/ppermute | solution.py:813
  65.3 3.7 %collective-permute-start.12 = (bf16[512,512]{1,0:T(8,128)(2,1)S(1)}, bf16[512,512]{1,0:T(8,128)(2,1)S(1)}, u32[]{:S(2)}, u32[]{:S(2)}) collective-permute-start(bf16[512,512]{1,0:T(8,128)(2,1)S(1)} %collective-permute-done.7.refs_2_), channel_id=1, source_target_pairs={{0,1},{1,0},{2,3},{3,2},{4,5},{5,4},{6,7},{7,6},{8,9},{9,8},{10,11... | collective-permute-start | bytes 1572872 | tf_op jit(solution)/shard_map/ppermute | solution.py:813
  65.7 3.4 %collective-permute-start.13 = (bf16[512,512]{1,0:T(8,128)(2,1)}, bf16[512,512]{1,0:T(8,128)(2,1)S(1)}, u32[]{:S(2)}, u32[]{:S(2)}) collective-permute-start(bf16[512,512]{1,0:T(8,128)(2,1)} %collective-permute-done.9.refs_3_), channel_id=1, source_target_pairs={{0,1},{1,0},{2,3},{3,2},{4,5},{5,4},{6,7},{7,6},{8,9},{9,8},{10,11... | collective-permute-start | bytes 1572872 | tf_op jit(solution)/shard_map/ppermute | solution.py:813
  65.8 3.1 %collective-permute-start.14 = (bf16[64,512]{1,0:T(8,128)(2,1)S(1)}, bf16[64,512]{1,0:T(8,128)(2,1)S(1)}, u32[]{:S(2)}, u32[]{:S(2)}) collective-permute-start(bf16[64,512]{1,0:T(8,128)(2,1)S(1)} %pad_maximum_fusion.refs_8_), channel_id=1, source_target_pairs={{0,1},{1,0},{2,3},{3,2},{4,5},{5,4},{6,7},{7,6},{8,9},{9,8},{10,11... | collective-permute-start | bytes 196616 | tf_op jit(solution)/shard_map/ppermute | solution.py:813
  83.5 2.8 %collective-permute-start.15 = (bf16[1056,512]{1,0:T(8,128)(2,1)S(1)}, bf16[1056,512]{1,0:T(8,128)(2,1)S(1)}, u32[]{:S(2)}, u32[]{:S(2)}) collective-permute-start(bf16[1056,512]{1,0:T(8,128)(2,1)S(1)} %facets.1.mine), channel_id=1, source_target_pairs={{0,1},{1,0},{2,3},{3,2},{4,5},{5,4},{6,7},{7,6},{8,9},{9,8},{10,11... | collective-permute-start | bytes 3244040 | tf_op jit(solution)/shard_map/ppermute | solution.py:813
  88.1 11.6 %collective-permute-start.19 = (bf16[64,512]{1,0:T(8,128)(2,1)S(1)}, bf16[64,512]{1,0:T(8,128)(2,1)S(1)}, u32[]{:S(2)}, u32[]{:S(2)}) collective-permute-start(bf16[64,512]{1,0:T(8,128)(2,1)S(1)} %get-tuple-element.94), channel_id=1, source_target_pairs={{0,2},{1,3},{2,4},{3,5},{4,6},{5,7},{6,0},{7,1},{8,10},{9,11},{10,... | collective-permute-start | bytes 196616 | tf_op jit(solution)/shard_map/ppermute | solution.py:809
  90.1 9.7 %collective-permute-start.20 = (bf16[64,512]{1,0:T(8,128)(2,1)S(1)}, bf16[64,512]{1,0:T(8,128)(2,1)S(1)}, u32[]{:S(2)}, u32[]{:S(2)}) collective-permute-start(bf16[64,512]{1,0:T(8,128)(2,1)S(1)} %get-tuple-element.95), channel_id=1, source_target_pairs={{0,4},{1,5},{2,6},{3,7},{4,0},{5,1},{6,2},{7,3},{8,12},{9,13},{10,... | collective-permute-start | bytes 196616 | tf_op jit(solution)/shard_map/ppermute | solution.py:809
  91.2 8.6 %collective-permute-start.21 = (bf16[64,512]{1,0:T(8,128)(2,1)S(1)}, bf16[64,512]{1,0:T(8,128)(2,1)S(1)}, u32[]{:S(2)}, u32[]{:S(2)}) collective-permute-start(bf16[64,512]{1,0:T(8,128)(2,1)S(1)} %get-tuple-element.96), channel_id=1, source_target_pairs={{0,6},{1,7},{2,0},{3,1},{4,2},{5,3},{6,4},{7,5},{8,14},{9,15},{10,... | collective-permute-start | bytes 196616 | tf_op jit(solution)/shard_map/ppermute | solution.py:809
  96.0 34.2 %collective-permute-start.16 = (bf16[512,512]{1,0:T(8,128)(2,1)S(1)}, bf16[512,512]{1,0:T(8,128)(2,1)S(1)}, u32[]{:S(2)}, u32[]{:S(2)}) collective-permute-start(bf16[512,512]{1,0:T(8,128)(2,1)S(1)} %get-tuple-element.90), channel_id=1, source_target_pairs={{0,2},{1,3},{2,4},{3,5},{4,6},{5,7},{6,0},{7,1},{8,10},{9,11},{10,... | collective-permute-start | bytes 1572872 | tf_op jit(solution)/shard_map/ppermute | solution.py:809
  96.1 45.1 %collective-permute-start.17 = (bf16[512,512]{1,0:T(8,128)(2,1)S(1)}, bf16[512,512]{1,0:T(8,128)(2,1)S(1)}, u32[]{:S(2)}, u32[]{:S(2)}) collective-permute-start(bf16[512,512]{1,0:T(8,128)(2,1)S(1)} %get-tuple-element.91), channel_id=1, source_target_pairs={{0,4},{1,5},{2,6},{3,7},{4,0},{5,1},{6,2},{7,3},{8,12},{9,13},{10,... | collective-permute-start | bytes 1572872 | tf_op jit(solution)/shard_map/ppermute | solution.py:809
  99.8 44.3 %collective-permute-start.18 = (bf16[512,512]{1,0:T(8,128)(2,1)S(1)}, bf16[512,512]{1,0:T(8,128)(2,1)S(1)}, u32[]{:S(2)}, u32[]{:S(2)}) collective-permute-start(bf16[512,512]{1,0:T(8,128)(2,1)S(1)} %get-tuple-element.92), channel_id=1, source_target_pairs={{0,6},{1,7},{2,0},{3,1},{4,2},{5,3},{6,4},{7,5},{8,14},{9,15},{10,... | collective-permute-start | bytes 1572872 | tf_op jit(solution)/shard_map/ppermute | solution.py:809
  106.1 3.9 %collective-permute-start.24 = (f32[8,128]{1,0:T(8,128)}, f32[8,128]{1,0:T(8,128)S(1)}, u32[]{:S(2)}, u32[]{:S(2)}) collective-permute-start(f32[8,128]{1,0:T(8,128)} %get-tuple-element.107.total), channel_id=1, source_target_pairs={{0,8},{8,0},{16,24},{24,16},{1,9},{9,1},{17,25},{25,17},{2,10},{10... | collective-permute-start | bytes 12296 | tf_op jit(solution)/shard_map/ppermute | solution.py:885
  106.1 5.9 %collective-permute-start.22 = (f32[8,384]{1,0:T(8,128)}, f32[8,384]{1,0:T(8,128)S(1)}, u32[]{:S(2)}, u32[]{:S(2)}) collective-permute-start(f32[8,384]{1,0:T(8,128)} %get-tuple-element.105), channel_id=1, source_target_pairs={{0,8},{8,16},{16,24},{1,9},{9,17},{17,25},{2,10},{10,18},{18,26},{... | collective-permute-start | bytes 36872 | tf_op jit(solution)/shard_map/ppermute | solution.py:888
  109.9 6.7 %collective-permute-start.23 = (f32[8,384]{1,0:T(8,128)}, f32[8,384]{1,0:T(8,128)S(1)}, u32[]{:S(2)}, u32[]{:S(2)}) collective-permute-start(f32[8,384]{1,0:T(8,128)} %get-tuple-element.106), channel_id=1, source_target_pairs={{8,0},{16,8},{24,16},{9,1},{17,9},{25,17},{10,2},{18,10},{26,18},{... | collective-permute-start | bytes 36872 | tf_op jit(solution)/shard_map/ppermute | solution.py:887
  118.7 3.8 %collective-permute-start.27 = (f32[8,128]{1,0:T(8,128)}, f32[8,128]{1,0:T(8,128)S(1)}, u32[]{:S(2)}, u32[]{:S(2)}) collective-permute-start(f32[8,128]{1,0:T(8,128)} %get-tuple-element.110.refs_17_), channel_id=1, source_target_pairs={{0,16},{8,24},{16,0},{24,8},{1,17},{9,25},{17,1},{25,9},{2,18},{10... | collective-permute-start | bytes 12296 | tf_op jit(solution)/shard_map/ppermute | solution.py:885
  118.7 11.5 %collective-permute-start.25 = (f32[8,384]{1,0:T(8,128)}, f32[8,384]{1,0:T(8,128)S(1)}, u32[]{:S(2)}, u32[]{:S(2)}) collective-permute-start(f32[8,384]{1,0:T(8,128)} %get-tuple-element.108), channel_id=1, source_target_pairs={{0,1},{1,2},{2,3},{3,4},{4,5},{5,6},{6,7},{8,9},{9,10},{10,11},{11... | collective-permute-start | bytes 36872 | tf_op jit(solution)/shard_map/ppermute | solution.py:901
  122.5 21.6 %copy-start.21 = (f32[8,128]{1,0:T(8,128)}, f32[8,128]{1,0:T(8,128)S(1)}, u32[]{:S(2)}) copy-start(f32[8,128]{1,0:T(8,128)S(1)} %collective-permute-done.27.refs_18_) | copy-start | bytes 12292
  122.5 7.7 %collective-permute-start.26 = (f32[8,384]{1,0:T(8,128)}, f32[8,384]{1,0:T(8,128)S(1)}, u32[]{:S(2)}, u32[]{:S(2)}) collective-permute-start(f32[8,384]{1,0:T(8,128)} %get-tuple-element.109), channel_id=1, source_target_pairs={{1,0},{2,1},{3,2},{4,3},{5,4},{6,5},{7,6},{9,8},{10,9},{11,10},{12... | collective-permute-start | bytes 36872 | tf_op jit(solution)/shard_map/ppermute | solution.py:902
  130.2 13.9 %copy-start.19 = (f32[8,384]{1,0:T(8,128)}, f32[8,384]{1,0:T(8,128)S(1)}, u32[]{:S(2)}) copy-start(f32[8,384]{1,0:T(8,128)S(1)} %collective-permute-done.25.refs_13_) | copy-start | bytes 36868
  130.2 13.9 %copy-start.20 = (f32[8,384]{1,0:T(8,128)}, f32[8,384]{1,0:T(8,128)S(1)}, u32[]{:S(2)}) copy-start(f32[8,384]{1,0:T(8,128)S(1)} %collective-permute-done.26.refs_14_) | copy-start | bytes 36868
  (24 other events, 100.0 us)

commit v8 on v7

--- a/solution.py
+++ b/solution.py
@@ -392,10 +392,23 @@
             total = jnp.zeros((16, cols), f32)
             for child in range(4):
                 total += coef_ref[child, near, pl.ds(r0, 16), :].astype(f32) * quads[child]
-            terms[near, pl.ds(r0, 16), :] = total
+            terms[near, pl.ds(16 + r0, 16), :] = total
         return carry
 
     in_chunks(part, rows, chunks)
+
+
+def row_sums(terms, rowed):
+    rows = terms.shape[1] - 32
+    for near in range(9):
+        terms[near, :16] = jnp.zeros((16, terms.shape[2]), f32)
+        terms[near, rows + 16 :] = jnp.zeros((16, terms.shape[2]), f32)
+    for c in range(3):
+        total = terms[c, 9 : rows + 25]
+        for r in (1, 2):
+            total += terms[3 * r + c, 9 - r : rows + 25 - r]
+        rowed[c, : rows + 16] = total
+        rowed[c, rows + 16 :] = jnp.zeros((rowed.shape[1] - rows - 16, rowed.shape[2]), f32)
 
 
 def joined(rowed, cols):
@@ -432,7 +445,7 @@
         grad_ref, middle_ref, coarse_ref, total_ref = outs
         xi_fine, xi_middle, xi_coarse, from_left, from_right, from_above, from_below = held[6:13]
         total, other = held[13:]
-    rows, cols = terms.shape[1:]
+    rows, cols = terms.shape[1] - 32, terms.shape[2]
     fine_perm[...] = interleaver(2 * cols, True)
     perm[...] = interleaver(cols, True)
     for copy in arriving:
@@ -460,10 +473,7 @@
     for tile in range(4 * cols // 128):
         fine_mix[tile] = split[:, tile * 128 : (tile + 1) * 128]
     spread(fine_mix, coef_fine, fine_terms, 2 * rows, 2 * cols, chunks)
-    fine_rowed[...] = jnp.zeros_like(fine_rowed)
-    for near in range(9):
-        r, c = near // 3, near % 3
-        fine_rowed[c, 7 + r : 7 + r + 2 * rows, :] += fine_terms[near]
+    row_sums(fine_terms, fine_rowed)
     main, left, right = joined(fine_rowed, 2 * cols)
     last = 8 + 2 * rows
     inner = main[8:last]
@@ -486,10 +496,7 @@
     ring_above, ring_below = main[7:8], main[last : last + 1]
     lines = [ring_above, ring_below, left[:, 8:last], right[:, 8:last]]
     lines = moved(jnp.concatenate(lines + [jnp.zeros((4, 2 * cols), f32)]), perm[...])
-    rowed[...] = jnp.zeros_like(rowed)
-    for near in range(9):
-        r, c = near // 3, near % 3
-        rowed[c, 7 + r : 7 + r + rows, :] += terms[near]
+    row_sums(terms, rowed)
     for line, message, top in ((0, above, 6), (1, below, 7 + rows)):
         for near in range(9):
             r, c = near // 3, near % 3
@@ -608,11 +615,11 @@
         + [
             pltpu.VMEM((4 * cols, 4 * cols), bf16),
             pltpu.VMEM((4 * cols // 128, 4 * rows, 128), f32),
-            pltpu.VMEM((9, 2 * rows, 2 * cols), f32),
+            pltpu.VMEM((9, 2 * rows + 32, 2 * cols), f32),
             pltpu.VMEM((3, 2 * rows + 128, 2 * cols), f32),
             pltpu.VMEM((2 * cols, 2 * cols), bf16),
             pltpu.VMEM((2 * cols // 128, 2 * rows, 128), f32),
-            pltpu.VMEM((9, rows, cols), f32),
+            pltpu.VMEM((9, rows + 32, cols), f32),
             pltpu.VMEM((3, rows + 128, cols), f32),
             pltpu.VMEM((4 * rows, 4 * cols), f32),
             pltpu.SemaphoreType.DMA((len(parts) + len(operands),)),
@@ -636,9 +643,11 @@
     return x[:8] + x[8:16] + x[16:24]
 
 
-def facets_kernel(blk, early, chips, ints, weights, *refs):
+def facets_kernel(blk, given, ints, weights, *refs):
     number, slots = weights.shape
-    tiles, strips, rest = refs[: 2 * chips], refs[2 * chips : 2 * chips + 2], refs[2 * chips + 2 :]
+    tiles, strips, rest = refs[:given], refs[given : given + 2], refs[given + 2 :]
+    height = 4 * border
+    kinds = strips[0].shape[0] // height
     ku_hbm, kv_hbm, data_hbm, squares, out_ref = rest[:5]
     held, held_strips, ku, kv, data, sums, dsum, total, sems, tile_sems, strip_sems = rest[5:]
     bins, side = ku.shape[1:]
@@ -650,13 +659,14 @@
                 @pl.when(ints[f, s] == i)
                 def _():
                     pltpu.make_async_copy(tile, held.at[f, s], tile_sems.at[f, s]).start()
-                    hop = i % chips
-                    if 1 <= hop <= early:
-                        height = 4 * border
-                        strip = strips[i // chips].at[(hop - 1) * height : hop * height]
-                        pltpu.make_async_copy(
-                            strip, held_strips.at[f, s], strip_sems.at[f, s]
-                        ).start()
+
+            for i in range(2 * kinds):
+
+                @pl.when(ints[f, slots + 1 + s] == i + 1)
+                def _():
+                    first = i % kinds * height
+                    strip = strips[i // kinds].at[first : first + height]
+                    pltpu.make_async_copy(strip, held_strips.at[f, s], strip_sems.at[f, s]).start()
 
         pairs = ((ku_hbm, ku), (kv_hbm, kv), (data_hbm, data))
         copies = [
@@ -668,11 +678,9 @@
         return copies
 
     def patch(f, s):
-        hop = lax.rem(ints[f, s], chips)
-
-        @pl.when((hop >= 1) & (hop <= early))
+        @pl.when(ints[f, slots + 1 + s] > 0)
         def _():
-            strip = strips[0].at[: 4 * border]
+            strip = strips[0].at[:height]
             pltpu.make_async_copy(strip, held_strips.at[f, s], strip_sems.at[f, s]).wait()
             tile, strip = held.at[f, s], held_strips.at[f, s]
             lines = strip[: 2 * border].astype(f32)
@@ -735,9 +743,7 @@
     number, bins, side = ku.shape[1:]
     slots = weights.shape[1]
     return pl.pallas_call(
-        functools.partial(
-            facets_kernel, 512, strips[0].shape[0] // (4 * border), len(tiles) // 2
-        ),
+        functools.partial(facets_kernel, 512, len(tiles)),
         in_specs=[scalar] * 2 + [anywhere] * (len(tiles) + len(strips) + 3) + [whole],
         out_specs=whole,
         out_shape=jax.ShapeDtypeStruct((number * side + 32, side), bf16),
@@ -807,6 +813,14 @@
 def chip_shift(x, hop):
     size = lax.axis_size("gy")
     return lax.ppermute(x, "gy", [(i, (i + 2 * hop) % size) for i in range(size)])
+
+
+def by_chips(x, pairs):
+    return lax.ppermute(x, "gy", [(2 * a + c, 2 * b + c) for a, b in pairs for c in range(2)])
+
+
+def paired(x, bits):
+    return by_chips(x, [(i, i ^ bits) for i in range(lax.axis_size("gy") // 2)])
 
 
 def swapped(x):
@@ -852,22 +866,39 @@
     )
     order = 2 * ((me // 2 + jnp.arange(chips, dtype=jnp.int32)) % chips) + me % 2
     scale = jnp.concatenate([mixing, swapped(mixing)])[:, order].T
-    sel = (me // 2 - lists // 2) % chips + jnp.where(lists % 2 == me % 2, 0, chips)
-    ints = jnp.concatenate([sel, counts[:, None]], axis=1)
     hops = range(1, chips)
-    early = range(1, min(3, chips))
-    mine = {hop: chip_shift(first, hop) for hop in early}
+    chip, other_core = me // 2, jnp.where(lists % 2 == me % 2, 0, 1)
+    if chips == 4:
+        mine = {1: paired(first, 1), 2: paired(first, 2)}
+    else:
+        mine = {hop: chip_shift(first, hop) for hop in range(1, min(3, chips))}
     above, below = halo_rows(*around, left_in, right_in)
     sky, strips, squares, lefts, rights = sky_of((above, below, left_in, right_in, *sides), *fields)
-    strips = jnp.concatenate([chip_shift(strips, hop) for hop in early])
-    late = {hop: chip_shift(sky, hop) for hop in hops[len(early) :]}
-    strips, mine, scale, ints, weights = lax.optimization_barrier(
-        (strips, mine, scale, ints, weights)
+    if chips == 4:
+        strips = [paired(strips, hop) for hop in hops]
+        away = chip ^ (lists // 2)
+        place = jnp.where((away == 3) & ((chip == 0) | (chip == 3)), 4, away)
+        kind = away
+    else:
+        strips = [chip_shift(strips, hop) for hop in mine]
+        place = away = (chip - lists // 2) % chips
+        kind = jnp.where(away <= len(mine), away, 0)
+    kinds = len(strips)
+    strips = jnp.concatenate(strips)
+    sky, strips, mine, scale, weights = lax.optimization_barrier(
+        (sky, strips, mine, scale, weights)
     )
-    mine |= late
-    mine = [sky] + [mine[hop] for hop in hops]
+    if chips == 4:
+        mine[3] = by_chips(sky, ((1, 2), (2, 1)))
+        mine[4] = by_chips(mine[2], ((2, 3), (1, 0)))
+    else:
+        mine |= {hop: chip_shift(sky, hop) for hop in hops[len(mine) :]}
+    mine = [sky] + [mine[hop] for hop in sorted(mine)]
     tiles = mine + [swapped(tile) for tile in mine]
     strips = [strips, swapped(strips)]
+    place += len(mine) * other_core
+    kind = jnp.where(kind > 0, kind + kinds * other_core, 0)
+    ints = jnp.concatenate([place, counts[:, None], kind], axis=1)
     dsums = facets(tiles, strips, kern_u, kern_v, vis_data, ints, weights, squares)
     theirs = swapped(dsums)
     strips = mixed(dsums, theirs, scale, True)

time: 155 us -> 148 us (0.955)
  waiting for transfers between devices: 53.9 us -> 45.5 us
  starting transfers between devices: 38.9 us -> 41.3 us
    ppermute x11 -> x6, waiting for transfers between devices: 31.5 us -> 13.4 us  [chip_shift(): lax.ppermute(x, 'gy', [(i, (i + 2 * hop) % size) for i in range(size)])]
    ppermute x0 -> x7, starting transfers between devices: none -> 11.3 us  [by_chips(): lax.ppermute(x, 'gy', [(2 * a + c, 2 * b + c) for a, b in pairs for c in...]
    ppermute x11 -> x6, starting transfers between devices: 17.2 us -> 7 us  [chip_shift(): lax.ppermute(x, 'gy', [(i, (i + 2 * hop) % size) for i in range(size)])]
    ppermute x0 -> x7, waiting for transfers between devices: none -> 9.77 us  [by_chips(): lax.ppermute(x, 'gy', [(2 * a + c, 2 * b + c) for a, b in pairs for c in...]
    unnamed x58 -> x56, local copies, waits for them, and re-layouts: 7.53 us -> 5.96 us
    ppermute x7 -> x8, waiting for transfers between devices: 5.55 us -> 5.57 us  [swapped(): lax.ppermute(x, 'gy', [(i, i ^ 1) for i in range(lax.axis_size('gy'))])]
  transfers between devices with their start and end apart: 28 -> 31, of which waited for: 14 -> 14; matrix products, arithmetic and copies ran while one was open for 3% -> 3% of each run, Pallas kernels for 15% -> 16%
where the time goes in v8:
time: 148 us; the launch traced here: 145 us
  waiting for transfers between devices  45.5 us (31%)
  Pallas kernels  43.1 us (29%)
  starting transfers between devices  41.3 us (28%)
  local copies, waits for them, and re-layouts  10.3 us (7%)
  other arithmetic  3.66 us (2%)
    ppermute x6, waiting for transfers between devices, chip_shift(): lax.ppermute(x, 'gy', [(i, (i + 2 * hop) % size) for i in range(size)])  13.4 us
    pallas_call x2, Pallas kernels, adjoint(): pl.pallas_call(functools.partial(adjoint_kernel, edge, len(parts), cells)...  12.8 us
    pallas_call x2, Pallas kernels, sky_of(): pl.pallas_call(functools.partial(sky_kernel, alone), in_specs=[anywhere]...  12.5 us
    pallas_call x1, Pallas kernels, facets(): pl.pallas_call(functools.partial(facets_kernel, 512, len(tiles)), in_spec...  11.5 us
    ppermute x7, starting transfers between devices, by_chips(): lax.ppermute(x, 'gy', [(2 * a + c, 2 * b + c) for a, b in pairs for c in...  11.3 us
    ppermute x7, waiting for transfers between devices, by_chips(): lax.ppermute(x, 'gy', [(2 * a + c, 2 * b + c) for a, b in pairs for c in...  9.77 us
    ppermute x6, starting transfers between devices, chip_shift(): lax.ppermute(x, 'gy', [(i, (i + 2 * hop) % size) for i in range(size)])  7 us
    unnamed x56, local copies, waits for them, and re-layouts  5.96 us
  transfers between devices with their start and end apart: 31, of which 14 were waited for; matrix products, arithmetic and copies ran while one was open for 3% of the time, Pallas kernels for 16%

profile of v8, /device:TPU:10, one launch (start us, length us, event | category | flops | bytes accessed | tf_op | source)
XLA Modules:
  0.0 145.1 jit_solution(9638681889818185371)
XLA Ops:
  1.8 1.8 %convert_reduce_fusion = (f32[2,9,128]{2,1,0:T(8,128)S(1)}, f32[2,9,128]{2,1,0:T(8,128)S(1)}) fusion(bf16[4,9,128,128]{3,2,1,0:T(8,128)(2,1)} %refs_5_.3), kind=kLoop, calls=%fused_computation.1 | loop fusion | flops 4608 | bytes 27648 | tf_op jit(solution)/shard_map/convert_element_type | solution.py:304
  4.1 1.9 %collective-permute-start = (f32[22,128]{1,0:T(8,128)S(1)}, f32[22,128]{1,0:T(8,128)S(1)}, u32[]{:S(2)}, u32[]{:S(2)}) collective-permute-start(f32[22,128]{1,0:T(8,128)S(1)} %pad_maximum_fusion.1.refs_6_), channel_id=1, source_target_pairs={{0,1},{1,2},{2,3},{3,4},{4,5},{5,6},{6,7},{8,9},{9,10},{10,11},{11... | collective-permute-start | bytes 33800 | tf_op jit(solution)/shard_map/ppermute | solution.py:847
  6.4 3.6 %collective-permute-start.1 = (f32[22,128]{1,0:T(8,128)S(1)}, f32[22,128]{1,0:T(8,128)S(1)}, u32[]{:S(2)}, u32[]{:S(2)}) collective-permute-start(f32[22,128]{1,0:T(8,128)S(1)} %pad_maximum_fusion.2.refs_5_), channel_id=1, source_target_pairs={{1,0},{2,1},{3,2},{4,3},{5,4},{6,5},{7,6},{9,8},{10,9},{11,10},{12... | collective-permute-start | bytes 33800 | tf_op jit(solution)/shard_map/ppermute | solution.py:848
  10.1 6.0 %sky.2 = bf16[512,512]{1,0:T(8,128)(2,1)} custom-call(f32[128,128]{1,0:T(8,128)} %refs_12_.3, bf16[4,9,128,128]{3,2,1,0:T(8,128)(2,1)} %refs_5_.3, f32[256,256]{1,0:T(8,128)} %refs_11_.1, bf16[4,9,256,256]{3,2,1,0:T(8,128)(2,1)} %refs_4_.5, f32[512,512]{1,0:T(8,128)} %refs_10_.3), custom_call_target="tpu_custom_call" | custom-call | tf_op jit(solution)/shard_map/sky/pallas_call | solution.py:348
  16.1 2.7 %collective-permute-start.8 = (bf16[512,512]{1,0:T(8,128)(2,1)}, bf16[512,512]{1,0:T(8,128)(2,1)S(1)}, u32[]{:S(2)}, u32[]{:S(2)}) collective-permute-start(bf16[512,512]{1,0:T(8,128)(2,1)} %sky.2), channel_id=1, source_target_pairs={{0,4},{1,5},{2,6},{3,7},{4,0},{5,1},{6,2},{7,3},{8,12},{9,13},{10,... | collective-permute-start | bytes 1572872 | tf_op jit(solution)/shard_map/ppermute | solution.py:819
  24.1 3.4 %collective-permute-start.2 = (f32[22,132]{1,0:T(8,128)}, f32[22,132]{1,0:T(8,128)S(1)}, u32[]{:S(2)}, u32[]{:S(2)}) collective-permute-start(f32[22,132]{1,0:T(8,128)} %get-tuple-element.68), channel_id=1, source_target_pairs={{0,8},{8,16},{16,24},{1,9},{9,17},{17,25},{2,10},{10,18},{18,26},{... | collective-permute-start | bytes 34856 | tf_op jit(solution)/shard_map/ppermute | solution.py:334
  27.5 2.4 %collective-permute-start.3 = (f32[22,132]{1,0:T(8,128)}, f32[22,132]{1,0:T(8,128)S(1)}, u32[]{:S(2)}, u32[]{:S(2)}) collective-permute-start(f32[22,132]{1,0:T(8,128)} %get-tuple-element.69), channel_id=1, source_target_pairs={{8,0},{16,8},{24,16},{9,1},{17,9},{25,17},{10,2},{18,10},{26,18},{... | collective-permute-start | bytes 34856 | tf_op jit(solution)/shard_map/ppermute | solution.py:334
  30.2 4.2 %collective-permute-done.3.refs_2_.refs_7_ = f32[22,132]{1,0:T(8,128)S(1)} collective-permute-done((f32[22,132]{1,0:T(8,128)}, f32[22,132]{1,0:T(8,128)S(1)}, u32[]{:S(2)}, u32[]{:S(2)}) %collective-permute-start.3) | collective-permute-done | bytes 11648 | tf_op jit(solution)/shard_map/ppermute | solution.py:334
  34.9 6.5 %sky.3 = (bf16[512,512]{1,0:T(8,128)(2,1)}, bf16[32,512]{1,0:T(8,128)(2,1)}, f32[8,128]{1,0:T(8,128)}, f32[22,132]{1,0:T(8,128)}, f32[22,132]{1,0:T(8,128)}) custom-call(f32[128,128]{1,0:T(8,128)} %refs_12_.3, f32[22,132]{1,0:T(8,128)} %copy-done.10, f32[22,132]{1,0:T(8,128)} %copy-done.11, f32[22,128]{1,0:T(8,128)} %copy-done.16, f32[22,128]{1,0:T(8,128)} %copy-done.17, ...), custom_call_target="tpu_custom_call" | custom-call | tf_op jit(solution)/shard_map/sky/pallas_call | solution.py:348
  41.9 3.5 %collective-permute-start.5 = (bf16[32,512]{1,0:T(8,128)(2,1)}, bf16[32,512]{1,0:T(8,128)(2,1)S(1)}, u32[]{:S(2)}, u32[]{:S(2)}) collective-permute-start(bf16[32,512]{1,0:T(8,128)(2,1)} %get-tuple-element.71), channel_id=1, source_target_pairs={{0,4},{1,5},{2,6},{3,7},{4,0},{5,1},{6,2},{7,3},{8,12},{9,13},{10,... | collective-permute-start | bytes 98312 | tf_op jit(solution)/shard_map/ppermute | solution.py:819
  46.1 1.8 %collective-permute-done.5 = bf16[32,512]{1,0:T(8,128)(2,1)S(1)} collective-permute-done((bf16[32,512]{1,0:T(8,128)(2,1)}, bf16[32,512]{1,0:T(8,128)(2,1)S(1)}, u32[]{:S(2)}, u32[]{:S(2)}) %collective-permute-start.5) | collective-permute-done | bytes 32800 | tf_op jit(solution)/shard_map/ppermute | solution.py:819
  47.9 1.7 %collective-permute-done.4 = bf16[32,512]{1,0:T(8,128)(2,1)S(1)} collective-permute-done((bf16[32,512]{1,0:T(8,128)(2,1)}, bf16[32,512]{1,0:T(8,128)(2,1)S(1)}, u32[]{:S(2)}, u32[]{:S(2)}) %collective-permute-start.4) | collective-permute-done | bytes 32800 | tf_op jit(solution)/shard_map/ppermute | solution.py:819
  49.6 1.9 %collective-permute-start.10 = (bf16[512,512]{1,0:T(8,128)(2,1)}, bf16[512,512]{1,0:T(8,128)(2,1)}, u32[]{:S(2)}, u32[]{:S(2)}) collective-permute-start(bf16[512,512]{1,0:T(8,128)(2,1)} %get-tuple-element.78.refs_0_), channel_id=1, source_target_pairs={{2,4},{3,5},{4,2},{5,3},{10,12},{11,13},{12,10},{13,11},{18,20},{1... | collective-permute-start | bytes 1572872 | tf_op jit(solution)/shard_map/ppermute | solution.py:819
  51.5 2.3 %collective-permute-start.11 = (bf16[512,512]{1,0:T(8,128)(2,1)S(1)}, bf16[512,512]{1,0:T(8,128)(2,1)}, u32[]{:S(2)}, u32[]{:S(2)}) collective-permute-start(bf16[512,512]{1,0:T(8,128)(2,1)S(1)} %collective-permute-done.8.refs_2_), channel_id=1, source_target_pairs={{4,6},{5,7},{2,0},{3,1},{12,14},{13,15},{10,8},{11,9},{20,22},{21,... | collective-permute-start | bytes 1572872 | tf_op jit(solution)/shard_map/ppermute | solution.py:819
  55.3 6.3 %collective-permute-done.10.refs_3_ = bf16[512,512]{1,0:T(8,128)(2,1)} collective-permute-done((bf16[512,512]{1,0:T(8,128)(2,1)}, bf16[512,512]{1,0:T(8,128)(2,1)}, u32[]{:S(2)}, u32[]{:S(2)}) %collective-permute-start.10) | collective-permute-done | bytes 524320 | tf_op jit(solution)/shard_map/ppermute | solution.py:819
  66.2 11.5 %facets.1.mine = bf16[1056,512]{1,0:T(8,128)(2,1)S(1)} custom-call(s32[2,5]{1,0:T(2,128)S(1)} %pad_add_fusion.ints, f32[2,2]{1,0:T(2,128)S(1)} %bitcast.14, bf16[512,512]{1,0:T(8,128)(2,1)S(1)} %copy-done.1, bf16[512,512]{1,0:T(8,128)(2,1)S(1)} %collective-permute-done.7.refs_1_, bf16[512,512]{1,0:T(8,128)(2,1)S(1)} %collective-permute-done.8.refs_2_, ...), custom_call_target="tpu_custom_call" | custom-call | tf_op jit(solution)/shard_map/facets/pallas_call | solution.py:745
  77.7 2.7 %collective-permute-done.18.theirs = bf16[1056,512]{1,0:T(8,128)(2,1)S(1)} collective-permute-done((bf16[1056,512]{1,0:T(8,128)(2,1)S(1)}, bf16[1056,512]{1,0:T(8,128)(2,1)S(1)}, u32[]{:S(2)}, u32[]{:S(2)}) %collective-permute-start.18) | collective-permute-done | bytes 1081376 | tf_op jit(solution)/shard_map/ppermute | solution.py:827
  82.6 2.7 %collective-permute-start.23 = (bf16[64,512]{1,0:T(8,128)(2,1)S(1)}, bf16[64,512]{1,0:T(8,128)(2,1)S(1)}, u32[]{:S(2)}, u32[]{:S(2)}) collective-permute-start(bf16[64,512]{1,0:T(8,128)(2,1)S(1)} %get-tuple-element.95), channel_id=1, source_target_pairs={{0,4},{1,5},{2,6},{3,7},{4,0},{5,1},{6,2},{7,3},{8,12},{9,13},{10,... | collective-permute-start | bytes 196616 | tf_op jit(solution)/shard_map/ppermute | solution.py:815
  85.3 2.1 %mixed.3 = (bf16[512,512]{1,0:T(8,128)(2,1)S(1)}, bf16[512,512]{1,0:T(8,128)(2,1)S(1)}, bf16[512,512]{1,0:T(8,128)(2,1)S(1)}, bf16[512,512]{1,0:T(8,128)(2,1)S(1)}) custom-call(f32[4,4]{1,0:T(4,128)S(1)} %gather_fusion, bf16[1056,512]{1,0:T(8,128)(2,1)S(1)} %facets.1.mine, bf16[1056,512]{1,0:T(8,128)(2,1)S(1)} %collective-permute-done.18.theirs), custom_call_target="tpu_custom_call" | custom-call | tf_op jit(solution)/shard_map/mixed/pallas_call | solution.py:802
  88.2 2.0 %collective-permute-start.19 = (bf16[512,512]{1,0:T(8,128)(2,1)S(1)}, bf16[512,512]{1,0:T(8,128)(2,1)S(1)}, u32[]{:S(2)}, u32[]{:S(2)}) collective-permute-start(bf16[512,512]{1,0:T(8,128)(2,1)S(1)} %get-tuple-element.90), channel_id=1, source_target_pairs={{0,2},{1,3},{2,4},{3,5},{4,6},{5,7},{6,0},{7,1},{8,10},{9,11},{10,... | collective-permute-start | bytes 1572872 | tf_op jit(solution)/shard_map/ppermute | solution.py:815
  90.2 2.0 %collective-permute-start.20 = (bf16[512,512]{1,0:T(8,128)(2,1)S(1)}, bf16[512,512]{1,0:T(8,128)(2,1)S(1)}, u32[]{:S(2)}, u32[]{:S(2)}) collective-permute-start(bf16[512,512]{1,0:T(8,128)(2,1)S(1)} %get-tuple-element.91), channel_id=1, source_target_pairs={{0,4},{1,5},{2,6},{3,7},{4,0},{5,1},{6,2},{7,3},{8,12},{9,13},{10,... | collective-permute-start | bytes 1572872 | tf_op jit(solution)/shard_map/ppermute | solution.py:815
  92.9 5.6 %adjoint.2 = (f32[8,384]{1,0:T(8,128)}, f32[8,384]{1,0:T(8,128)}, f32[8,384]{1,0:T(8,128)}, f32[8,384]{1,0:T(8,128)}, f32[8,128]{1,0:T(8,128)}) custom-call(bf16[64,512]{1,0:T(8,128)(2,1)} %copy-done.5, bf16[64,512]{1,0:T(8,128)(2,1)} %copy-done.23, bf16[64,512]{1,0:T(8,128)(2,1)} %copy-done.24, bf16[64,512]{1,0:T(8,128)(2,1)} %copy-done.25, ...), custom_call_target="tpu_custom_call" | custom-call | flops 40000000000 | bytes 64000000 | tf_op jit(solution)/shard_map/adjoint/pallas_call | solution.py:609
  98.6 4.4 %collective-permute-start.25 = (f32[8,384]{1,0:T(8,128)}, f32[8,384]{1,0:T(8,128)S(1)}, u32[]{:S(2)}, u32[]{:S(2)}) collective-permute-start(f32[8,384]{1,0:T(8,128)} %get-tuple-element.105), channel_id=1, source_target_pairs={{0,8},{8,16},{16,24},{1,9},{9,17},{17,25},{2,10},{10,18},{18,26},{... | collective-permute-start | bytes 36872 | tf_op jit(solution)/shard_map/ppermute | solution.py:919
  103.0 1.9 %collective-permute-start.26 = (f32[8,384]{1,0:T(8,128)}, f32[8,384]{1,0:T(8,128)S(1)}, u32[]{:S(2)}, u32[]{:S(2)}) collective-permute-start(f32[8,384]{1,0:T(8,128)} %get-tuple-element.106), channel_id=1, source_target_pairs={{8,0},{16,8},{24,16},{9,1},{17,9},{25,17},{10,2},{18,10},{26,18},{... | collective-permute-start | bytes 36872 | tf_op jit(solution)/shard_map/ppermute | solution.py:918
  105.0 4.7 %collective-permute-done.26.from_below.refs_16_ = f32[8,384]{1,0:T(8,128)S(1)} collective-permute-done((f32[8,384]{1,0:T(8,128)}, f32[8,384]{1,0:T(8,128)S(1)}, u32[]{:S(2)}, u32[]{:S(2)}) %collective-permute-start.26) | collective-permute-done | bytes 12320 | tf_op jit(solution)/shard_map/ppermute | solution.py:918
  111.8 1.9 %collective-permute-start.28 = (f32[8,384]{1,0:T(8,128)}, f32[8,384]{1,0:T(8,128)S(1)}, u32[]{:S(2)}, u32[]{:S(2)}) collective-permute-start(f32[8,384]{1,0:T(8,128)} %get-tuple-element.108), channel_id=1, source_target_pairs={{0,1},{1,2},{2,3},{3,4},{4,5},{5,6},{6,7},{8,9},{9,10},{10,11},{11... | collective-permute-start | bytes 36872 | tf_op jit(solution)/shard_map/ppermute | solution.py:932
  113.7 1.9 %collective-permute-done.30.refs_18_ = f32[8,128]{1,0:T(8,128)S(1)} collective-permute-done((f32[8,128]{1,0:T(8,128)}, f32[8,128]{1,0:T(8,128)S(1)}, u32[]{:S(2)}, u32[]{:S(2)}) %collective-permute-start.30) | collective-permute-done | bytes 4128 | tf_op jit(solution)/shard_map/ppermute | solution.py:916
  115.6 1.9 %collective-permute-start.29 = (f32[8,384]{1,0:T(8,128)}, f32[8,384]{1,0:T(8,128)S(1)}, u32[]{:S(2)}, u32[]{:S(2)}) collective-permute-start(f32[8,384]{1,0:T(8,128)} %get-tuple-element.109), channel_id=1, source_target_pairs={{1,0},{2,1},{3,2},{4,3},{5,4},{6,5},{7,6},{9,8},{10,9},{11,10},{12... | collective-permute-start | bytes 36872 | tf_op jit(solution)/shard_map/ppermute | solution.py:933
  117.5 5.9 %collective-permute-done.28.refs_13_ = f32[8,384]{1,0:T(8,128)S(1)} collective-permute-done((f32[8,384]{1,0:T(8,128)}, f32[8,384]{1,0:T(8,128)S(1)}, u32[]{:S(2)}, u32[]{:S(2)}) %collective-permute-start.28) | collective-permute-done | bytes 12320 | tf_op jit(solution)/shard_map/ppermute | solution.py:932
  125.1 9.9 %collective-permute-done.20.refs_2_ = bf16[512,512]{1,0:T(8,128)(2,1)S(1)} collective-permute-done((bf16[512,512]{1,0:T(8,128)(2,1)S(1)}, bf16[512,512]{1,0:T(8,128)(2,1)S(1)}, u32[]{:S(2)}, u32[]{:S(2)}) %collective-permute-start.20) | collective-permute-done | bytes 524320 | tf_op jit(solution)/shard_map/ppermute | solution.py:815
  135.0 1.9 %collective-permute-done.21.refs_3_ = bf16[512,512]{1,0:T(8,128)(2,1)S(1)} collective-permute-done((bf16[512,512]{1,0:T(8,128)(2,1)S(1)}, bf16[512,512]{1,0:T(8,128)(2,1)S(1)}, u32[]{:S(2)}, u32[]{:S(2)}) %collective-permute-start.21) | collective-permute-done | bytes 524320 | tf_op jit(solution)/shard_map/ppermute | solution.py:815
  137.7 7.2 %adjoint.3 = (f32[512,512]{1,0:T(8,128)}, f32[256,256]{1,0:T(8,128)}, f32[128,128]{1,0:T(8,128)}, f32[1,1]{1,0:T(1,128)}) custom-call(bf16[512,512]{1,0:T(8,128)(2,1)} %copy-done.2, bf16[512,512]{1,0:T(8,128)(2,1)} %copy-done.7, bf16[512,512]{1,0:T(8,128)(2,1)} %copy-done.8, bf16[512,512]{1,0:T(8,128)(2,1)} %copy-done.9, bf16[4,9,256,256]{3,2,1,0:T(8,128)(2,1)} %refs_4_.5, ...), custom_call_target="tpu_custom_call" | custom-call | tf_op jit(solution)/shard_map/adjoint/pallas_call | solution.py:609
  (127 shorter events, 23.4 us)
Async XLA Ops:
  4.1 12.0 %collective-permute-start = (f32[22,128]{1,0:T(8,128)S(1)}, f32[22,128]{1,0:T(8,128)S(1)}, u32[]{:S(2)}, u32[]{:S(2)}) collective-permute-start(f32[22,128]{1,0:T(8,128)S(1)} %pad_maximum_fusion.1.refs_6_), channel_id=1, source_target_pairs={{0,1},{1,2},{2,3},{3,4},{4,5},{5,6},{6,7},{8,9},{9,10},{10,11},{11... | collective-permute-start | bytes 33800 | tf_op jit(solution)/shard_map/ppermute | solution.py:847
  6.4 9.7 %collective-permute-start.1 = (f32[22,128]{1,0:T(8,128)S(1)}, f32[22,128]{1,0:T(8,128)S(1)}, u32[]{:S(2)}, u32[]{:S(2)}) collective-permute-start(f32[22,128]{1,0:T(8,128)S(1)} %pad_maximum_fusion.2.refs_5_), channel_id=1, source_target_pairs={{1,0},{2,1},{3,2},{4,3},{5,4},{6,5},{7,6},{9,8},{10,9},{11,10},{12... | collective-permute-start | bytes 33800 | tf_op jit(solution)/shard_map/ppermute | solution.py:848
  16.1 33.4 %collective-permute-start.8 = (bf16[512,512]{1,0:T(8,128)(2,1)}, bf16[512,512]{1,0:T(8,128)(2,1)S(1)}, u32[]{:S(2)}, u32[]{:S(2)}) collective-permute-start(bf16[512,512]{1,0:T(8,128)(2,1)} %sky.2), channel_id=1, source_target_pairs={{0,4},{1,5},{2,6},{3,7},{4,0},{5,1},{6,2},{7,3},{8,12},{9,13},{10,... | collective-permute-start | bytes 1572872 | tf_op jit(solution)/shard_map/ppermute | solution.py:819
  18.8 30.8 %collective-permute-start.7 = (bf16[512,512]{1,0:T(8,128)(2,1)}, bf16[512,512]{1,0:T(8,128)(2,1)S(1)}, u32[]{:S(2)}, u32[]{:S(2)}) collective-permute-start(bf16[512,512]{1,0:T(8,128)(2,1)} %sky.2), channel_id=1, source_target_pairs={{0,2},{1,3},{2,0},{3,1},{4,6},{5,7},{6,4},{7,5},{8,10},{9,11},{10,... | collective-permute-start | bytes 1572872 | tf_op jit(solution)/shard_map/ppermute | solution.py:819
  24.1 6.1 %collective-permute-start.2 = (f32[22,132]{1,0:T(8,128)}, f32[22,132]{1,0:T(8,128)S(1)}, u32[]{:S(2)}, u32[]{:S(2)}) collective-permute-start(f32[22,132]{1,0:T(8,128)} %get-tuple-element.68), channel_id=1, source_target_pairs={{0,8},{8,16},{16,24},{1,9},{9,17},{17,25},{2,10},{10,18},{18,26},{... | collective-permute-start | bytes 34856 | tf_op jit(solution)/shard_map/ppermute | solution.py:334
  27.5 6.8 %collective-permute-start.3 = (f32[22,132]{1,0:T(8,128)}, f32[22,132]{1,0:T(8,128)S(1)}, u32[]{:S(2)}, u32[]{:S(2)}) collective-permute-start(f32[22,132]{1,0:T(8,128)} %get-tuple-element.69), channel_id=1, source_target_pairs={{8,0},{16,8},{24,16},{9,1},{17,9},{25,17},{10,2},{18,10},{26,18},{... | collective-permute-start | bytes 34856 | tf_op jit(solution)/shard_map/ppermute | solution.py:334
  30.1 15.3 %collective-permute-start.9 = (f32[2,8]{0,1:T(8,128)S(1)}, f32[2,8]{0,1:T(8,128)S(1)}, u32[]{:S(2)}, u32[]{:S(2)}) collective-permute-start(f32[2,8]{0,1:T(8,128)S(1)} %copy.32), channel_id=1, source_target_pairs={{0,1},{1,0},{2,3},{3,2},{4,5},{5,4},{6,7},{7,6},{8,9},{9,8},{10,11... | collective-permute-start | bytes 200 | tf_op jit(solution)/shard_map/ppermute | solution.py:827
  34.9 29.5 %copy-start = (bf16[1,2,1024,512]{3,2,1,0:T(8,128)(2,1)S(1)}, bf16[1,2,1024,512]{3,2,1,0:T(8,128)(2,1)}, u32[]{:S(2)}) copy-start(bf16[1,2,1024,512]{3,2,1,0:T(8,128)(2,1)} %refs_12_.2) | copy-start | bytes 6291460
  41.4 4.6 %collective-permute-start.6 = (bf16[32,512]{1,0:T(8,128)(2,1)}, bf16[32,512]{1,0:T(8,128)(2,1)S(1)}, u32[]{:S(2)}, u32[]{:S(2)}) collective-permute-start(bf16[32,512]{1,0:T(8,128)(2,1)} %get-tuple-element.71), channel_id=1, source_target_pairs={{0,6},{1,7},{2,4},{3,5},{4,2},{5,3},{6,0},{7,1},{8,14},{9,15},{10,... | collective-permute-start | bytes 98312 | tf_op jit(solution)/shard_map/ppermute | solution.py:819
  41.9 5.9 %collective-permute-start.5 = (bf16[32,512]{1,0:T(8,128)(2,1)}, bf16[32,512]{1,0:T(8,128)(2,1)S(1)}, u32[]{:S(2)}, u32[]{:S(2)}) collective-permute-start(bf16[32,512]{1,0:T(8,128)(2,1)} %get-tuple-element.71), channel_id=1, source_target_pairs={{0,4},{1,5},{2,6},{3,7},{4,0},{5,1},{6,2},{7,3},{8,12},{9,13},{10,... | collective-permute-start | bytes 98312 | tf_op jit(solution)/shard_map/ppermute | solution.py:819
  45.4 4.1 %collective-permute-start.4 = (bf16[32,512]{1,0:T(8,128)(2,1)}, bf16[32,512]{1,0:T(8,128)(2,1)S(1)}, u32[]{:S(2)}, u32[]{:S(2)}) collective-permute-start(bf16[32,512]{1,0:T(8,128)(2,1)} %get-tuple-element.71), channel_id=1, source_target_pairs={{0,2},{1,3},{2,0},{3,1},{4,6},{5,7},{6,4},{7,5},{8,10},{9,11},{10,... | collective-permute-start | bytes 98312 | tf_op jit(solution)/shard_map/ppermute | solution.py:819
  49.6 12.0 %collective-permute-start.10 = (bf16[512,512]{1,0:T(8,128)(2,1)}, bf16[512,512]{1,0:T(8,128)(2,1)}, u32[]{:S(2)}, u32[]{:S(2)}) collective-permute-start(bf16[512,512]{1,0:T(8,128)(2,1)} %get-tuple-element.78.refs_0_), channel_id=1, source_target_pairs={{2,4},{3,5},{4,2},{5,3},{10,12},{11,13},{12,10},{13,11},{18,20},{1... | collective-permute-start | bytes 1572872 | tf_op jit(solution)/shard_map/ppermute | solution.py:819
  51.5 10.1 %collective-permute-start.11 = (bf16[512,512]{1,0:T(8,128)(2,1)S(1)}, bf16[512,512]{1,0:T(8,128)(2,1)}, u32[]{:S(2)}, u32[]{:S(2)}) collective-permute-start(bf16[512,512]{1,0:T(8,128)(2,1)S(1)} %collective-permute-done.8.refs_2_), channel_id=1, source_target_pairs={{4,6},{5,7},{2,0},{3,1},{12,14},{13,15},{10,8},{11,9},{20,22},{21,... | collective-permute-start | bytes 1572872 | tf_op jit(solution)/shard_map/ppermute | solution.py:819
  53.8 1.3 collective-permute-start.17
  53.9 8.3 %collective-permute-start.12 = (bf16[512,512]{1,0:T(8,128)(2,1)}, bf16[512,512]{1,0:T(8,128)(2,1)S(1)}, u32[]{:S(2)}, u32[]{:S(2)}) collective-permute-start(bf16[512,512]{1,0:T(8,128)(2,1)} %get-tuple-element.78.refs_0_), channel_id=1, source_target_pairs={{0,1},{1,0},{2,3},{3,2},{4,5},{5,4},{6,7},{7,6},{8,9},{9,8},{10,11... | collective-permute-start | bytes 1572872 | tf_op jit(solution)/shard_map/ppermute | solution.py:827
  54.4 7.8 %collective-permute-start.14 = (bf16[512,512]{1,0:T(8,128)(2,1)S(1)}, bf16[512,512]{1,0:T(8,128)(2,1)S(1)}, u32[]{:S(2)}, u32[]{:S(2)}) collective-permute-start(bf16[512,512]{1,0:T(8,128)(2,1)S(1)} %collective-permute-done.8.refs_2_), channel_id=1, source_target_pairs={{0,1},{1,0},{2,3},{3,2},{4,5},{5,4},{6,7},{7,6},{8,9},{9,8},{10,11... | collective-permute-start | bytes 1572872 | tf_op jit(solution)/shard_map/ppermute | solution.py:827
  55.1 7.1 %collective-permute-start.13 = (bf16[512,512]{1,0:T(8,128)(2,1)S(1)}, bf16[512,512]{1,0:T(8,128)(2,1)S(1)}, u32[]{:S(2)}, u32[]{:S(2)}) collective-permute-start(bf16[512,512]{1,0:T(8,128)(2,1)S(1)} %collective-permute-done.7.refs_1_), channel_id=1, source_target_pairs={{0,1},{1,0},{2,3},{3,2},{4,5},{5,4},{6,7},{7,6},{8,9},{9,8},{10,11... | collective-permute-start | bytes 1572872 | tf_op jit(solution)/shard_map/ppermute | solution.py:827
  61.6 2.1 %collective-permute-start.15 = (bf16[512,512]{1,0:T(8,128)(2,1)}, bf16[512,512]{1,0:T(8,128)(2,1)S(1)}, u32[]{:S(2)}, u32[]{:S(2)}) collective-permute-start(bf16[512,512]{1,0:T(8,128)(2,1)} %collective-permute-done.10.refs_3_), channel_id=1, source_target_pairs={{0,1},{1,0},{2,3},{3,2},{4,5},{5,4},{6,7},{7,6},{8,9},{9,8},{10,11... | collective-permute-start | bytes 1572872 | tf_op jit(solution)/shard_map/ppermute | solution.py:827
  61.6 2.9 %collective-permute-start.16 = (bf16[512,512]{1,0:T(8,128)(2,1)}, bf16[512,512]{1,0:T(8,128)(2,1)S(1)}, u32[]{:S(2)}, u32[]{:S(2)}) collective-permute-start(bf16[512,512]{1,0:T(8,128)(2,1)} %collective-permute-done.11.refs_4_), channel_id=1, source_target_pairs={{0,1},{1,0},{2,3},{3,2},{4,5},{5,4},{6,7},{7,6},{8,9},{9,8},{10,11... | collective-permute-start | bytes 1572872 | tf_op jit(solution)/shard_map/ppermute | solution.py:827
  77.7 2.8 %collective-permute-start.18 = (bf16[1056,512]{1,0:T(8,128)(2,1)S(1)}, bf16[1056,512]{1,0:T(8,128)(2,1)S(1)}, u32[]{:S(2)}, u32[]{:S(2)}) collective-permute-start(bf16[1056,512]{1,0:T(8,128)(2,1)S(1)} %facets.1.mine), channel_id=1, source_target_pairs={{0,1},{1,0},{2,3},{3,2},{4,5},{5,4},{6,7},{7,6},{8,9},{9,8},{10,11... | collective-permute-start | bytes 3244040 | tf_op jit(solution)/shard_map/ppermute | solution.py:827
  82.3 9.9 %collective-permute-start.22 = (bf16[64,512]{1,0:T(8,128)(2,1)S(1)}, bf16[64,512]{1,0:T(8,128)(2,1)S(1)}, u32[]{:S(2)}, u32[]{:S(2)}) collective-permute-start(bf16[64,512]{1,0:T(8,128)(2,1)S(1)} %get-tuple-element.94), channel_id=1, source_target_pairs={{0,2},{1,3},{2,4},{3,5},{4,6},{5,7},{6,0},{7,1},{8,10},{9,11},{10,... | collective-permute-start | bytes 196616 | tf_op jit(solution)/shard_map/ppermute | solution.py:815
  82.6 9.7 %collective-permute-start.23 = (bf16[64,512]{1,0:T(8,128)(2,1)S(1)}, bf16[64,512]{1,0:T(8,128)(2,1)S(1)}, u32[]{:S(2)}, u32[]{:S(2)}) collective-permute-start(bf16[64,512]{1,0:T(8,128)(2,1)S(1)} %get-tuple-element.95), channel_id=1, source_target_pairs={{0,4},{1,5},{2,6},{3,7},{4,0},{5,1},{6,2},{7,3},{8,12},{9,13},{10,... | collective-permute-start | bytes 196616 | tf_op jit(solution)/shard_map/ppermute | solution.py:815
  85.3 7.0 %collective-permute-start.24 = (bf16[64,512]{1,0:T(8,128)(2,1)S(1)}, bf16[64,512]{1,0:T(8,128)(2,1)S(1)}, u32[]{:S(2)}, u32[]{:S(2)}) collective-permute-start(bf16[64,512]{1,0:T(8,128)(2,1)S(1)} %get-tuple-element.96), channel_id=1, source_target_pairs={{0,6},{1,7},{2,0},{3,1},{4,2},{5,3},{6,4},{7,5},{8,14},{9,15},{10,... | collective-permute-start | bytes 196616 | tf_op jit(solution)/shard_map/ppermute | solution.py:815
  88.2 36.9 %collective-permute-start.19 = (bf16[512,512]{1,0:T(8,128)(2,1)S(1)}, bf16[512,512]{1,0:T(8,128)(2,1)S(1)}, u32[]{:S(2)}, u32[]{:S(2)}) collective-permute-start(bf16[512,512]{1,0:T(8,128)(2,1)S(1)} %get-tuple-element.90), channel_id=1, source_target_pairs={{0,2},{1,3},{2,4},{3,5},{4,6},{5,7},{6,0},{7,1},{8,10},{9,11},{10,... | collective-permute-start | bytes 1572872 | tf_op jit(solution)/shard_map/ppermute | solution.py:815
  90.2 44.7 %collective-permute-start.20 = (bf16[512,512]{1,0:T(8,128)(2,1)S(1)}, bf16[512,512]{1,0:T(8,128)(2,1)S(1)}, u32[]{:S(2)}, u32[]{:S(2)}) collective-permute-start(bf16[512,512]{1,0:T(8,128)(2,1)S(1)} %get-tuple-element.91), channel_id=1, source_target_pairs={{0,4},{1,5},{2,6},{3,7},{4,0},{5,1},{6,2},{7,3},{8,12},{9,13},{10,... | collective-permute-start | bytes 1572872 | tf_op jit(solution)/shard_map/ppermute | solution.py:815
  92.2 44.6 %collective-permute-start.21 = (bf16[512,512]{1,0:T(8,128)(2,1)S(1)}, bf16[512,512]{1,0:T(8,128)(2,1)S(1)}, u32[]{:S(2)}, u32[]{:S(2)}) collective-permute-start(bf16[512,512]{1,0:T(8,128)(2,1)S(1)} %get-tuple-element.92), channel_id=1, source_target_pairs={{0,6},{1,7},{2,0},{3,1},{4,2},{5,3},{6,4},{7,5},{8,14},{9,15},{10,... | collective-permute-start | bytes 1572872 | tf_op jit(solution)/shard_map/ppermute | solution.py:815
  98.5 4.5 %collective-permute-start.27 = (f32[8,128]{1,0:T(8,128)}, f32[8,128]{1,0:T(8,128)S(1)}, u32[]{:S(2)}, u32[]{:S(2)}) collective-permute-start(f32[8,128]{1,0:T(8,128)} %get-tuple-element.107.total), channel_id=1, source_target_pairs={{0,8},{8,0},{16,24},{24,16},{1,9},{9,1},{17,25},{25,17},{2,10},{10... | collective-permute-start | bytes 12296 | tf_op jit(solution)/shard_map/ppermute | solution.py:916
  98.6 6.4 %collective-permute-start.25 = (f32[8,384]{1,0:T(8,128)}, f32[8,384]{1,0:T(8,128)S(1)}, u32[]{:S(2)}, u32[]{:S(2)}) collective-permute-start(f32[8,384]{1,0:T(8,128)} %get-tuple-element.105), channel_id=1, source_target_pairs={{0,8},{8,16},{16,24},{1,9},{9,17},{17,25},{2,10},{10,18},{18,26},{... | collective-permute-start | bytes 36872 | tf_op jit(solution)/shard_map/ppermute | solution.py:919
  103.0 6.7 %collective-permute-start.26 = (f32[8,384]{1,0:T(8,128)}, f32[8,384]{1,0:T(8,128)S(1)}, u32[]{:S(2)}, u32[]{:S(2)}) collective-permute-start(f32[8,384]{1,0:T(8,128)} %get-tuple-element.106), channel_id=1, source_target_pairs={{8,0},{16,8},{24,16},{9,1},{17,9},{25,17},{10,2},{18,10},{26,18},{... | collective-permute-start | bytes 36872 | tf_op jit(solution)/shard_map/ppermute | solution.py:918
  111.8 3.8 %collective-permute-start.30 = (f32[8,128]{1,0:T(8,128)}, f32[8,128]{1,0:T(8,128)S(1)}, u32[]{:S(2)}, u32[]{:S(2)}) collective-permute-start(f32[8,128]{1,0:T(8,128)} %get-tuple-element.110.refs_17_), channel_id=1, source_target_pairs={{0,16},{8,24},{16,0},{24,8},{1,17},{9,25},{17,1},{25,9},{2,18},{10... | collective-permute-start | bytes 12296 | tf_op jit(solution)/shard_map/ppermute | solution.py:916
  111.8 11.7 %collective-permute-start.28 = (f32[8,384]{1,0:T(8,128)}, f32[8,384]{1,0:T(8,128)S(1)}, u32[]{:S(2)}, u32[]{:S(2)}) collective-permute-start(f32[8,384]{1,0:T(8,128)} %get-tuple-element.108), channel_id=1, source_target_pairs={{0,1},{1,2},{2,3},{3,4},{4,5},{5,6},{6,7},{8,9},{9,10},{10,11},{11... | collective-permute-start | bytes 36872 | tf_op jit(solution)/shard_map/ppermute | solution.py:932
  115.6 7.9 %collective-permute-start.29 = (f32[8,384]{1,0:T(8,128)}, f32[8,384]{1,0:T(8,128)S(1)}, u32[]{:S(2)}, u32[]{:S(2)}) collective-permute-start(f32[8,384]{1,0:T(8,128)} %get-tuple-element.109), channel_id=1, source_target_pairs={{1,0},{2,1},{3,2},{4,3},{5,4},{6,5},{7,6},{9,8},{10,9},{11,10},{12... | collective-permute-start | bytes 36872 | tf_op jit(solution)/shard_map/ppermute | solution.py:933
  (26 other events, 160.7 us)

commit v9 on v8

--- a/solution.py
+++ b/solution.py
@@ -864,7 +864,9 @@
     mixing = jnp.sum(
         weights[:, :, None] * (lists[:, :, None] == ids[None, None, :]).astype(f32), axis=1
     )
-    order = 2 * ((me // 2 + jnp.arange(chips, dtype=jnp.int32)) % chips) + me % 2
+    steps = jnp.arange(chips, dtype=jnp.int32)
+    order = (me // 2) ^ steps if chips == 4 else (me // 2 + steps) % chips
+    order = 2 * order + me % 2
     scale = jnp.concatenate([mixing, swapped(mixing)])[:, order].T
     hops = range(1, chips)
     chip, other_core = me // 2, jnp.where(lists % 2 == me % 2, 0, 1)
@@ -903,12 +905,24 @@
     theirs = swapped(dsums)
     strips = mixed(dsums, theirs, scale, True)
     strips, dsums, theirs = lax.optimization_barrier((strips, dsums, theirs))
-    edges = [strips[0]] + [chip_shift(strips[hop], hop) for hop in hops]
+    send = paired if chips == 4 else chip_shift
+    edges = [strips[0]] + [send(strips[hop], hop) for hop in hops]
     parts = mixed(dsums, theirs, scale, False)
     edges, _ = lax.optimization_barrier((edges, parts))
-    parts = [parts[0]] + [chip_shift(parts[hop], hop) for hop in hops]
     around = (above, below, lefts, rights)
-    to_left, to_right, upper, lower, total = adjoint(True, edges, around, fields)
+    if chips == 4:
+        middle = by_chips(parts[3], ((1, 2), (2, 1)))
+        onward = by_chips(parts[3], ((0, 1), (3, 2)))
+    outgoing = adjoint(True, edges, around, fields)
+    if chips == 4:
+        onward, middle, parts, outgoing = lax.optimization_barrier(
+            (onward, middle, parts, outgoing)
+        )
+        both = (parts[2].astype(f32) + onward.astype(f32)).astype(bf16)
+        parts = [parts[0], paired(parts[1], 1), paired(both, 2), middle]
+    else:
+        parts = [parts[0]] + [chip_shift(parts[hop], hop) for hop in hops]
+    to_left, to_right, upper, lower, total = outgoing
     size = lax.axis_size("gx")
     steps = [1 << i for i in range(size.bit_length()) if 1 << i < size]
 

time: 148 us -> 141 us (0.953)
  waiting for transfers between devices: 45.5 us -> 33.7 us
  starting transfers between devices: 41.3 us -> 49.8 us
  Pallas kernels: 43.1 us -> 39.4 us
    ppermute x6 -> x0, waiting for transfers between devices: 13.4 us -> none  [chip_shift(): lax.ppermute(x, 'gy', [(i, (i + 2 * hop) % size) for i in range(size)])]
    ppermute x7 -> x14, starting transfers between devices: 11.3 us -> 22.6 us  [by_chips(): lax.ppermute(x, 'gy', [(2 * a + c, 2 * b + c) for a, b in pairs for c in...]
    ppermute x7 -> x14, waiting for transfers between devices: 9.77 us -> 17.5 us  [by_chips(): lax.ppermute(x, 'gy', [(2 * a + c, 2 * b + c) for a, b in pairs for c in...]
    ppermute x6 -> x0, starting transfers between devices: 7 us -> none  [chip_shift(): lax.ppermute(x, 'gy', [(i, (i + 2 * hop) % size) for i in range(size)])]
    ppermute x1, waiting for transfers between devices: 5.95 us -> 0.01 us  [body(): from_left = lax.ppermute(to_right, 'gy', right)]
    ppermute x2, waiting for transfers between devices: 1.9 us -> 6.25 us  [across(): return lax.ppermute(x, 'gx', [(i, i ^ hop) for i in range(size)])]
    ppermute x1, waiting for transfers between devices: 4.75 us -> 0.54 us  [body(): from_below = lax.ppermute(upper, 'gx', up)]
    pallas_call x1, Pallas kernels: 11.5 us -> 7.85 us  [facets(): pl.pallas_call(functools.partial(facets_kernel, 512, len(tiles)), in_spec...]
  transfers between devices with their start and end apart: 31 -> 32, of which waited for: 14 -> 14; matrix products, arithmetic and copies ran while one was open for 3% -> 3% of each run, Pallas kernels for 16% -> 17%
where the time goes in v9:
time: 141 us; the launch traced here: 139 us
  starting transfers between devices  49.8 us (35%)
  Pallas kernels  39.4 us (28%)
  waiting for transfers between devices  33.7 us (24%)
  local copies, waits for them, and re-layouts  11 us (8%)
  other arithmetic  3.78 us (3%)
    ppermute x14, starting transfers between devices, by_chips(): lax.ppermute(x, 'gy', [(2 * a + c, 2 * b + c) for a, b in pairs for c in...  22.6 us
    ppermute x14, waiting for transfers between devices, by_chips(): lax.ppermute(x, 'gy', [(2 * a + c, 2 * b + c) for a, b in pairs for c in...  17.5 us
    pallas_call x2, Pallas kernels, adjoint(): pl.pallas_call(functools.partial(adjoint_kernel, edge, len(parts), cells)...  12.8 us
    pallas_call x2, Pallas kernels, sky_of(): pl.pallas_call(functools.partial(sky_kernel, alone), in_specs=[anywhere]...  12.5 us
    pallas_call x1, Pallas kernels, facets(): pl.pallas_call(functools.partial(facets_kernel, 512, len(tiles)), in_spec...  7.85 us
    unnamed x62, local copies, waits for them, and re-layouts  6.73 us
    ppermute x2, waiting for transfers between devices, across(): return lax.ppermute(x, 'gx', [(i, i ^ hop) for i in range(size)])  6.25 us
    ppermute x8, waiting for transfers between devices, swapped(): lax.ppermute(x, 'gy', [(i, i ^ 1) for i in range(lax.axis_size('gy'))])  5.21 us
  transfers between devices with their start and end apart: 32, of which 14 were waited for; matrix products, arithmetic and copies ran while one was open for 3% of the time, Pallas kernels for 17%

profile of v9, /device:TPU:10, one launch (start us, length us, event | category | flops | bytes accessed | tf_op | source)
XLA Modules:
  0.0 139.2 jit_solution(2922912842695208547)
XLA Ops:
  1.8 1.8 %convert_reduce_fusion = (f32[2,9,128]{2,1,0:T(8,128)S(1)}, f32[2,9,128]{2,1,0:T(8,128)S(1)}) fusion(bf16[4,9,128,128]{3,2,1,0:T(8,128)(2,1)} %refs_5_.3), kind=kLoop, calls=%fused_computation.1 | loop fusion | flops 4608 | bytes 27648 | tf_op jit(solution)/shard_map/convert_element_type | solution.py:304
  4.1 1.9 %collective-permute-start = (f32[22,128]{1,0:T(8,128)S(1)}, f32[22,128]{1,0:T(8,128)S(1)}, u32[]{:S(2)}, u32[]{:S(2)}) collective-permute-start(f32[22,128]{1,0:T(8,128)S(1)} %pad_maximum_fusion.1.refs_6_), channel_id=1, source_target_pairs={{0,1},{1,2},{2,3},{3,4},{4,5},{5,6},{6,7},{8,9},{9,10},{10,11},{11... | collective-permute-start | bytes 33800 | tf_op jit(solution)/shard_map/ppermute | solution.py:847
  6.4 3.6 %collective-permute-start.1 = (f32[22,128]{1,0:T(8,128)S(1)}, f32[22,128]{1,0:T(8,128)S(1)}, u32[]{:S(2)}, u32[]{:S(2)}) collective-permute-start(f32[22,128]{1,0:T(8,128)S(1)} %pad_maximum_fusion.2.refs_5_), channel_id=1, source_target_pairs={{1,0},{2,1},{3,2},{4,3},{5,4},{6,5},{7,6},{9,8},{10,9},{11,10},{12... | collective-permute-start | bytes 33800 | tf_op jit(solution)/shard_map/ppermute | solution.py:848
  10.1 6.0 %sky.2 = bf16[512,512]{1,0:T(8,128)(2,1)} custom-call(f32[128,128]{1,0:T(8,128)} %refs_12_.3, bf16[4,9,128,128]{3,2,1,0:T(8,128)(2,1)} %refs_5_.3, f32[256,256]{1,0:T(8,128)} %refs_11_.1, bf16[4,9,256,256]{3,2,1,0:T(8,128)(2,1)} %refs_4_.5, f32[512,512]{1,0:T(8,128)} %refs_10_.3), custom_call_target="tpu_custom_call" | custom-call | tf_op jit(solution)/shard_map/sky/pallas_call | solution.py:348
  16.1 2.7 %collective-permute-start.8 = (bf16[512,512]{1,0:T(8,128)(2,1)}, bf16[512,512]{1,0:T(8,128)(2,1)S(1)}, u32[]{:S(2)}, u32[]{:S(2)}) collective-permute-start(bf16[512,512]{1,0:T(8,128)(2,1)} %sky.2), channel_id=1, source_target_pairs={{0,4},{1,5},{2,6},{3,7},{4,0},{5,1},{6,2},{7,3},{8,12},{9,13},{10,... | collective-permute-start | bytes 1572872 | tf_op jit(solution)/shard_map/ppermute | solution.py:819
  24.1 3.4 %collective-permute-start.2 = (f32[22,132]{1,0:T(8,128)}, f32[22,132]{1,0:T(8,128)S(1)}, u32[]{:S(2)}, u32[]{:S(2)}) collective-permute-start(f32[22,132]{1,0:T(8,128)} %get-tuple-element.78), channel_id=1, source_target_pairs={{0,8},{8,16},{16,24},{1,9},{9,17},{17,25},{2,10},{10,18},{18,26},{... | collective-permute-start | bytes 34856 | tf_op jit(solution)/shard_map/ppermute | solution.py:334
  27.5 2.4 %collective-permute-start.3 = (f32[22,132]{1,0:T(8,128)}, f32[22,132]{1,0:T(8,128)S(1)}, u32[]{:S(2)}, u32[]{:S(2)}) collective-permute-start(f32[22,132]{1,0:T(8,128)} %get-tuple-element.79), channel_id=1, source_target_pairs={{8,0},{16,8},{24,16},{9,1},{17,9},{25,17},{10,2},{18,10},{26,18},{... | collective-permute-start | bytes 34856 | tf_op jit(solution)/shard_map/ppermute | solution.py:334
  30.2 4.2 %collective-permute-done.3.refs_2_.refs_7_ = f32[22,132]{1,0:T(8,128)S(1)} collective-permute-done((f32[22,132]{1,0:T(8,128)}, f32[22,132]{1,0:T(8,128)S(1)}, u32[]{:S(2)}, u32[]{:S(2)}) %collective-permute-start.3) | collective-permute-done | bytes 11648 | tf_op jit(solution)/shard_map/ppermute | solution.py:334
  34.9 6.5 %sky.3 = (bf16[512,512]{1,0:T(8,128)(2,1)}, bf16[32,512]{1,0:T(8,128)(2,1)}, f32[8,128]{1,0:T(8,128)}, f32[22,132]{1,0:T(8,128)}, f32[22,132]{1,0:T(8,128)}) custom-call(f32[128,128]{1,0:T(8,128)} %refs_12_.3, f32[22,132]{1,0:T(8,128)} %copy-done.10, f32[22,132]{1,0:T(8,128)} %copy-done.11, f32[22,128]{1,0:T(8,128)} %copy-done.16, f32[22,128]{1,0:T(8,128)} %copy-done.17, ...), custom_call_target="tpu_custom_call" | custom-call | tf_op jit(solution)/shard_map/sky/pallas_call | solution.py:348
  41.9 3.5 %collective-permute-start.5 = (bf16[32,512]{1,0:T(8,128)(2,1)}, bf16[32,512]{1,0:T(8,128)(2,1)S(1)}, u32[]{:S(2)}, u32[]{:S(2)}) collective-permute-start(bf16[32,512]{1,0:T(8,128)(2,1)} %get-tuple-element.81), channel_id=1, source_target_pairs={{0,4},{1,5},{2,6},{3,7},{4,0},{5,1},{6,2},{7,3},{8,12},{9,13},{10,... | collective-permute-start | bytes 98312 | tf_op jit(solution)/shard_map/ppermute | solution.py:819
  46.1 1.8 %collective-permute-done.5 = bf16[32,512]{1,0:T(8,128)(2,1)S(1)} collective-permute-done((bf16[32,512]{1,0:T(8,128)(2,1)}, bf16[32,512]{1,0:T(8,128)(2,1)S(1)}, u32[]{:S(2)}, u32[]{:S(2)}) %collective-permute-start.5) | collective-permute-done | bytes 32800 | tf_op jit(solution)/shard_map/ppermute | solution.py:819
  47.9 1.7 %collective-permute-done.4 = bf16[32,512]{1,0:T(8,128)(2,1)S(1)} collective-permute-done((bf16[32,512]{1,0:T(8,128)(2,1)}, bf16[32,512]{1,0:T(8,128)(2,1)S(1)}, u32[]{:S(2)}, u32[]{:S(2)}) %collective-permute-start.4) | collective-permute-done | bytes 32800 | tf_op jit(solution)/shard_map/ppermute | solution.py:819
  49.6 1.9 %collective-permute-start.10 = (bf16[512,512]{1,0:T(8,128)(2,1)}, bf16[512,512]{1,0:T(8,128)(2,1)}, u32[]{:S(2)}, u32[]{:S(2)}) collective-permute-start(bf16[512,512]{1,0:T(8,128)(2,1)} %get-tuple-element.88.refs_0_), channel_id=1, source_target_pairs={{2,4},{3,5},{4,2},{5,3},{10,12},{11,13},{12,10},{13,11},{18,20},{1... | collective-permute-start | bytes 1572872 | tf_op jit(solution)/shard_map/ppermute | solution.py:819
  51.5 2.3 %collective-permute-start.11 = (bf16[512,512]{1,0:T(8,128)(2,1)S(1)}, bf16[512,512]{1,0:T(8,128)(2,1)}, u32[]{:S(2)}, u32[]{:S(2)}) collective-permute-start(bf16[512,512]{1,0:T(8,128)(2,1)S(1)} %collective-permute-done.8.refs_2_), channel_id=1, source_target_pairs={{4,6},{5,7},{2,0},{3,1},{12,14},{13,15},{10,8},{11,9},{20,22},{21,... | collective-permute-start | bytes 1572872 | tf_op jit(solution)/shard_map/ppermute | solution.py:819
  55.3 6.3 %collective-permute-done.10.refs_3_ = bf16[512,512]{1,0:T(8,128)(2,1)} collective-permute-done((bf16[512,512]{1,0:T(8,128)(2,1)}, bf16[512,512]{1,0:T(8,128)(2,1)}, u32[]{:S(2)}, u32[]{:S(2)}) %collective-permute-start.10) | collective-permute-done | bytes 524320 | tf_op jit(solution)/shard_map/ppermute | solution.py:819
  66.2 7.8 %facets.1.mine = bf16[1056,512]{1,0:T(8,128)(2,1)S(1)} custom-call(s32[2,5]{1,0:T(2,128)S(1)} %pad_add_fusion.ints, f32[2,2]{1,0:T(2,128)S(1)} %bitcast.14, bf16[512,512]{1,0:T(8,128)(2,1)S(1)} %copy-done.1, bf16[512,512]{1,0:T(8,128)(2,1)S(1)} %collective-permute-done.7.refs_1_, bf16[512,512]{1,0:T(8,128)(2,1)S(1)} %collective-permute-done.8.refs_2_, ...), custom_call_target="tpu_custom_call" | custom-call | tf_op jit(solution)/shard_map/facets/pallas_call | solution.py:745
  74.0 1.9 %collective-permute-start.18 = (bf16[1056,512]{1,0:T(8,128)(2,1)S(1)}, bf16[1056,512]{1,0:T(8,128)(2,1)S(1)}, u32[]{:S(2)}, u32[]{:S(2)}) collective-permute-start(bf16[1056,512]{1,0:T(8,128)(2,1)S(1)} %facets.1.mine), channel_id=1, source_target_pairs={{0,1},{1,0},{2,3},{3,2},{4,5},{5,4},{6,7},{7,6},{8,9},{9,8},{10,11... | collective-permute-start | bytes 3244040 | tf_op jit(solution)/shard_map/ppermute | solution.py:827
  75.9 2.3 %collective-permute-done.18.theirs = bf16[1056,512]{1,0:T(8,128)(2,1)S(1)} collective-permute-done((bf16[1056,512]{1,0:T(8,128)(2,1)S(1)}, bf16[1056,512]{1,0:T(8,128)(2,1)S(1)}, u32[]{:S(2)}, u32[]{:S(2)}) %collective-permute-start.18) | collective-permute-done | bytes 1081376 | tf_op jit(solution)/shard_map/ppermute | solution.py:827
  80.1 2.8 %collective-permute-start.21 = (bf16[64,512]{1,0:T(8,128)(2,1)S(1)}, bf16[64,512]{1,0:T(8,128)(2,1)S(1)}, u32[]{:S(2)}, u32[]{:S(2)}) collective-permute-start(bf16[64,512]{1,0:T(8,128)(2,1)S(1)} %get-tuple-element.104), channel_id=1, source_target_pairs={{0,2},{1,3},{2,0},{3,1},{4,6},{5,7},{6,4},{7,5},{8,10},{9,11},{10,... | collective-permute-start | bytes 196616 | tf_op jit(solution)/shard_map/ppermute | solution.py:819
  84.7 2.1 %mixed.3 = (bf16[512,512]{1,0:T(8,128)(2,1)S(1)}, bf16[512,512]{1,0:T(8,128)(2,1)S(1)}, bf16[512,512]{1,0:T(8,128)(2,1)S(1)}, bf16[512,512]{1,0:T(8,128)(2,1)S(1)}) custom-call(f32[4,4]{1,0:T(4,128)S(1)} %gather_fusion, bf16[1056,512]{1,0:T(8,128)(2,1)S(1)} %facets.1.mine, bf16[1056,512]{1,0:T(8,128)(2,1)S(1)} %collective-permute-done.18.theirs), custom_call_target="tpu_custom_call" | custom-call | tf_op jit(solution)/shard_map/mixed/pallas_call | solution.py:802
  87.6 3.4 %collective-permute-start.20 = (bf16[512,512]{1,0:T(8,128)(2,1)S(1)}, bf16[512,512]{1,0:T(8,128)(2,1)S(1)}, u32[]{:S(2)}, u32[]{:S(2)}) collective-permute-start(bf16[512,512]{1,0:T(8,128)(2,1)S(1)} %get-tuple-element.99), channel_id=1, source_target_pairs={{2,4},{3,5},{4,2},{5,3},{10,12},{11,13},{12,10},{13,11},{18,20},{1... | collective-permute-start | bytes 1572872 | tf_op jit(solution)/shard_map/ppermute | solution.py:819
  93.0 5.6 %adjoint.2 = (f32[8,384]{1,0:T(8,128)}, f32[8,384]{1,0:T(8,128)}, f32[8,384]{1,0:T(8,128)}, f32[8,384]{1,0:T(8,128)}, f32[8,128]{1,0:T(8,128)}) custom-call(bf16[64,512]{1,0:T(8,128)(2,1)} %copy-done.5, bf16[64,512]{1,0:T(8,128)(2,1)} %copy-done.24, bf16[64,512]{1,0:T(8,128)(2,1)} %copy-done.25, bf16[64,512]{1,0:T(8,128)(2,1)} %copy-done.26, ...), custom_call_target="tpu_custom_call" | custom-call | flops 40000000000 | bytes 64000000 | tf_op jit(solution)/shard_map/adjoint/pallas_call | solution.py:609
  98.6 4.5 %collective-permute-done.20.refs_3_ = bf16[512,512]{1,0:T(8,128)(2,1)S(1)} collective-permute-done((bf16[512,512]{1,0:T(8,128)(2,1)S(1)}, bf16[512,512]{1,0:T(8,128)(2,1)S(1)}, u32[]{:S(2)}, u32[]{:S(2)}) %collective-permute-start.20) | collective-permute-done | bytes 524320 | tf_op jit(solution)/shard_map/ppermute | solution.py:819
  103.2 3.1 %collective-permute-done.19 = bf16[512,512]{1,0:T(8,128)(2,1)S(1)} collective-permute-done((bf16[512,512]{1,0:T(8,128)(2,1)S(1)}, bf16[512,512]{1,0:T(8,128)(2,1)S(1)}, u32[]{:S(2)}, u32[]{:S(2)}) %collective-permute-start.19) | collective-permute-done | bytes 524320 | tf_op jit(solution)/shard_map/ppermute | solution.py:819
  106.5 2.0 %collective-permute-start.24 = (bf16[512,512]{1,0:T(8,128)(2,1)S(1)}, bf16[512,512]{1,0:T(8,128)(2,1)S(1)}, u32[]{:S(2)}, u32[]{:S(2)}) collective-permute-start(bf16[512,512]{1,0:T(8,128)(2,1)S(1)} %get-tuple-element.119), channel_id=1, source_target_pairs={{0,2},{1,3},{2,0},{3,1},{4,6},{5,7},{6,4},{7,5},{8,10},{9,11},{10,... | collective-permute-start | bytes 1572872 | tf_op jit(solution)/shard_map/ppermute | solution.py:819
  108.5 3.6 %collective-permute-start.26 = (f32[8,384]{1,0:T(8,128)S(1)}, f32[8,384]{1,0:T(8,128)S(1)}, u32[]{:S(2)}, u32[]{:S(2)}) collective-permute-start(f32[8,384]{1,0:T(8,128)S(1)} %copy-done.28), channel_id=1, source_target_pairs={{0,8},{8,16},{16,24},{1,9},{9,17},{17,25},{2,10},{10,18},{18,26},{... | collective-permute-start | bytes 36872 | tf_op jit(solution)/shard_map/ppermute | solution.py:933
  112.1 2.2 %collective-permute-start.27 = (f32[8,384]{1,0:T(8,128)S(1)}, f32[8,384]{1,0:T(8,128)S(1)}, u32[]{:S(2)}, u32[]{:S(2)}) collective-permute-start(f32[8,384]{1,0:T(8,128)S(1)} %copy-done.27), channel_id=1, source_target_pairs={{8,0},{16,8},{24,16},{9,1},{17,9},{25,17},{10,2},{18,10},{26,18},{... | collective-permute-start | bytes 36872 | tf_op jit(solution)/shard_map/ppermute | solution.py:932
  114.4 3.6 %collective-permute-done.28.other = f32[8,128]{1,0:T(8,128)S(1)} collective-permute-done((f32[8,128]{1,0:T(8,128)S(1)}, f32[8,128]{1,0:T(8,128)S(1)}, u32[]{:S(2)}, u32[]{:S(2)}) %collective-permute-start.28) | collective-permute-done | bytes 4128 | tf_op jit(solution)/shard_map/ppermute | solution.py:930
  120.7 1.9 %collective-permute-start.29 = (f32[8,384]{1,0:T(8,128)}, f32[8,384]{1,0:T(8,128)S(1)}, u32[]{:S(2)}, u32[]{:S(2)}) collective-permute-start(f32[8,384]{1,0:T(8,128)} %get-tuple-element.128), channel_id=1, source_target_pairs={{0,1},{1,2},{2,3},{3,4},{4,5},{5,6},{6,7},{8,9},{9,10},{10,11},{11... | collective-permute-start | bytes 36872 | tf_op jit(solution)/shard_map/ppermute | solution.py:946
  122.6 3.6 %collective-permute-start.30 = (f32[8,384]{1,0:T(8,128)}, f32[8,384]{1,0:T(8,128)S(1)}, u32[]{:S(2)}, u32[]{:S(2)}) collective-permute-start(f32[8,384]{1,0:T(8,128)} %get-tuple-element.129), channel_id=1, source_target_pairs={{1,0},{2,1},{3,2},{4,3},{5,4},{6,5},{7,6},{9,8},{10,9},{11,10},{12... | collective-permute-start | bytes 36872 | tf_op jit(solution)/shard_map/ppermute | solution.py:947
  127.5 2.7 %collective-permute-done.31.refs_18_ = f32[8,128]{1,0:T(8,128)S(1)} collective-permute-done((f32[8,128]{1,0:T(8,128)}, f32[8,128]{1,0:T(8,128)S(1)}, u32[]{:S(2)}, u32[]{:S(2)}) %collective-permute-start.31) | collective-permute-done | bytes 4128 | tf_op jit(solution)/shard_map/ppermute | solution.py:930
  131.8 7.2 %adjoint.3 = (f32[512,512]{1,0:T(8,128)}, f32[256,256]{1,0:T(8,128)}, f32[128,128]{1,0:T(8,128)}, f32[1,1]{1,0:T(1,128)}) custom-call(bf16[512,512]{1,0:T(8,128)(2,1)} %copy-done.2, bf16[512,512]{1,0:T(8,128)(2,1)} %copy-done.9, bf16[512,512]{1,0:T(8,128)(2,1)} %copy-done.8, bf16[512,512]{1,0:T(8,128)(2,1)} %copy-done.7, bf16[4,9,256,256]{3,2,1,0:T(8,128)(2,1)} %refs_4_.5, ...), custom_call_target="tpu_custom_call" | custom-call | tf_op jit(solution)/shard_map/adjoint/pallas_call | solution.py:609
  (136 shorter events, 27.4 us)
Async XLA Ops:
  4.1 12.0 %collective-permute-start = (f32[22,128]{1,0:T(8,128)S(1)}, f32[22,128]{1,0:T(8,128)S(1)}, u32[]{:S(2)}, u32[]{:S(2)}) collective-permute-start(f32[22,128]{1,0:T(8,128)S(1)} %pad_maximum_fusion.1.refs_6_), channel_id=1, source_target_pairs={{0,1},{1,2},{2,3},{3,4},{4,5},{5,6},{6,7},{8,9},{9,10},{10,11},{11... | collective-permute-start | bytes 33800 | tf_op jit(solution)/shard_map/ppermute | solution.py:847
  6.4 9.7 %collective-permute-start.1 = (f32[22,128]{1,0:T(8,128)S(1)}, f32[22,128]{1,0:T(8,128)S(1)}, u32[]{:S(2)}, u32[]{:S(2)}) collective-permute-start(f32[22,128]{1,0:T(8,128)S(1)} %pad_maximum_fusion.2.refs_5_), channel_id=1, source_target_pairs={{1,0},{2,1},{3,2},{4,3},{5,4},{6,5},{7,6},{9,8},{10,9},{11,10},{12... | collective-permute-start | bytes 33800 | tf_op jit(solution)/shard_map/ppermute | solution.py:848
  16.1 33.4 %collective-permute-start.8 = (bf16[512,512]{1,0:T(8,128)(2,1)}, bf16[512,512]{1,0:T(8,128)(2,1)S(1)}, u32[]{:S(2)}, u32[]{:S(2)}) collective-permute-start(bf16[512,512]{1,0:T(8,128)(2,1)} %sky.2), channel_id=1, source_target_pairs={{0,4},{1,5},{2,6},{3,7},{4,0},{5,1},{6,2},{7,3},{8,12},{9,13},{10,... | collective-permute-start | bytes 1572872 | tf_op jit(solution)/shard_map/ppermute | solution.py:819
  18.8 30.8 %collective-permute-start.7 = (bf16[512,512]{1,0:T(8,128)(2,1)}, bf16[512,512]{1,0:T(8,128)(2,1)S(1)}, u32[]{:S(2)}, u32[]{:S(2)}) collective-permute-start(bf16[512,512]{1,0:T(8,128)(2,1)} %sky.2), channel_id=1, source_target_pairs={{0,2},{1,3},{2,0},{3,1},{4,6},{5,7},{6,4},{7,5},{8,10},{9,11},{10,... | collective-permute-start | bytes 1572872 | tf_op jit(solution)/shard_map/ppermute | solution.py:819
  24.1 6.1 %collective-permute-start.2 = (f32[22,132]{1,0:T(8,128)}, f32[22,132]{1,0:T(8,128)S(1)}, u32[]{:S(2)}, u32[]{:S(2)}) collective-permute-start(f32[22,132]{1,0:T(8,128)} %get-tuple-element.78), channel_id=1, source_target_pairs={{0,8},{8,16},{16,24},{1,9},{9,17},{17,25},{2,10},{10,18},{18,26},{... | collective-permute-start | bytes 34856 | tf_op jit(solution)/shard_map/ppermute | solution.py:334
  27.5 6.8 %collective-permute-start.3 = (f32[22,132]{1,0:T(8,128)}, f32[22,132]{1,0:T(8,128)S(1)}, u32[]{:S(2)}, u32[]{:S(2)}) collective-permute-start(f32[22,132]{1,0:T(8,128)} %get-tuple-element.79), channel_id=1, source_target_pairs={{8,0},{16,8},{24,16},{9,1},{17,9},{25,17},{10,2},{18,10},{26,18},{... | collective-permute-start | bytes 34856 | tf_op jit(solution)/shard_map/ppermute | solution.py:334
  30.1 15.3 %collective-permute-start.9 = (f32[2,8]{0,1:T(8,128)S(1)}, f32[2,8]{0,1:T(8,128)S(1)}, u32[]{:S(2)}, u32[]{:S(2)}) collective-permute-start(f32[2,8]{0,1:T(8,128)S(1)} %copy.32), channel_id=1, source_target_pairs={{0,1},{1,0},{2,3},{3,2},{4,5},{5,4},{6,7},{7,6},{8,9},{9,8},{10,11... | collective-permute-start | bytes 200 | tf_op jit(solution)/shard_map/ppermute | solution.py:827
  41.4 4.6 %collective-permute-start.6 = (bf16[32,512]{1,0:T(8,128)(2,1)}, bf16[32,512]{1,0:T(8,128)(2,1)S(1)}, u32[]{:S(2)}, u32[]{:S(2)}) collective-permute-start(bf16[32,512]{1,0:T(8,128)(2,1)} %get-tuple-element.81), channel_id=1, source_target_pairs={{0,6},{1,7},{2,4},{3,5},{4,2},{5,3},{6,0},{7,1},{8,14},{9,15},{10,... | collective-permute-start | bytes 98312 | tf_op jit(solution)/shard_map/ppermute | solution.py:819
  41.9 5.9 %collective-permute-start.5 = (bf16[32,512]{1,0:T(8,128)(2,1)}, bf16[32,512]{1,0:T(8,128)(2,1)S(1)}, u32[]{:S(2)}, u32[]{:S(2)}) collective-permute-start(bf16[32,512]{1,0:T(8,128)(2,1)} %get-tuple-element.81), channel_id=1, source_target_pairs={{0,4},{1,5},{2,6},{3,7},{4,0},{5,1},{6,2},{7,3},{8,12},{9,13},{10,... | collective-permute-start | bytes 98312 | tf_op jit(solution)/shard_map/ppermute | solution.py:819
  45.4 4.1 %collective-permute-start.4 = (bf16[32,512]{1,0:T(8,128)(2,1)}, bf16[32,512]{1,0:T(8,128)(2,1)S(1)}, u32[]{:S(2)}, u32[]{:S(2)}) collective-permute-start(bf16[32,512]{1,0:T(8,128)(2,1)} %get-tuple-element.81), channel_id=1, source_target_pairs={{0,2},{1,3},{2,0},{3,1},{4,6},{5,7},{6,4},{7,5},{8,10},{9,11},{10,... | collective-permute-start | bytes 98312 | tf_op jit(solution)/shard_map/ppermute | solution.py:819
  49.6 12.0 %collective-permute-start.10 = (bf16[512,512]{1,0:T(8,128)(2,1)}, bf16[512,512]{1,0:T(8,128)(2,1)}, u32[]{:S(2)}, u32[]{:S(2)}) collective-permute-start(bf16[512,512]{1,0:T(8,128)(2,1)} %get-tuple-element.88.refs_0_), channel_id=1, source_target_pairs={{2,4},{3,5},{4,2},{5,3},{10,12},{11,13},{12,10},{13,11},{18,20},{1... | collective-permute-start | bytes 1572872 | tf_op jit(solution)/shard_map/ppermute | solution.py:819
  51.5 10.1 %collective-permute-start.11 = (bf16[512,512]{1,0:T(8,128)(2,1)S(1)}, bf16[512,512]{1,0:T(8,128)(2,1)}, u32[]{:S(2)}, u32[]{:S(2)}) collective-permute-start(bf16[512,512]{1,0:T(8,128)(2,1)S(1)} %collective-permute-done.8.refs_2_), channel_id=1, source_target_pairs={{4,6},{5,7},{2,0},{3,1},{12,14},{13,15},{10,8},{11,9},{20,22},{21,... | collective-permute-start | bytes 1572872 | tf_op jit(solution)/shard_map/ppermute | solution.py:819
  53.8 1.3 collective-permute-start.17
  53.9 8.3 %collective-permute-start.12 = (bf16[512,512]{1,0:T(8,128)(2,1)}, bf16[512,512]{1,0:T(8,128)(2,1)S(1)}, u32[]{:S(2)}, u32[]{:S(2)}) collective-permute-start(bf16[512,512]{1,0:T(8,128)(2,1)} %get-tuple-element.88.refs_0_), channel_id=1, source_target_pairs={{0,1},{1,0},{2,3},{3,2},{4,5},{5,4},{6,7},{7,6},{8,9},{9,8},{10,11... | collective-permute-start | bytes 1572872 | tf_op jit(solution)/shard_map/ppermute | solution.py:827
  54.4 7.8 %collective-permute-start.14 = (bf16[512,512]{1,0:T(8,128)(2,1)S(1)}, bf16[512,512]{1,0:T(8,128)(2,1)S(1)}, u32[]{:S(2)}, u32[]{:S(2)}) collective-permute-start(bf16[512,512]{1,0:T(8,128)(2,1)S(1)} %collective-permute-done.8.refs_2_), channel_id=1, source_target_pairs={{0,1},{1,0},{2,3},{3,2},{4,5},{5,4},{6,7},{7,6},{8,9},{9,8},{10,11... | collective-permute-start | bytes 1572872 | tf_op jit(solution)/shard_map/ppermute | solution.py:827
  55.1 7.1 %collective-permute-start.13 = (bf16[512,512]{1,0:T(8,128)(2,1)S(1)}, bf16[512,512]{1,0:T(8,128)(2,1)S(1)}, u32[]{:S(2)}, u32[]{:S(2)}) collective-permute-start(bf16[512,512]{1,0:T(8,128)(2,1)S(1)} %collective-permute-done.7.refs_1_), channel_id=1, source_target_pairs={{0,1},{1,0},{2,3},{3,2},{4,5},{5,4},{6,7},{7,6},{8,9},{9,8},{10,11... | collective-permute-start | bytes 1572872 | tf_op jit(solution)/shard_map/ppermute | solution.py:827
  61.6 2.1 %collective-permute-start.15 = (bf16[512,512]{1,0:T(8,128)(2,1)}, bf16[512,512]{1,0:T(8,128)(2,1)S(1)}, u32[]{:S(2)}, u32[]{:S(2)}) collective-permute-start(bf16[512,512]{1,0:T(8,128)(2,1)} %collective-permute-done.10.refs_3_), channel_id=1, source_target_pairs={{0,1},{1,0},{2,3},{3,2},{4,5},{5,4},{6,7},{7,6},{8,9},{9,8},{10,11... | collective-permute-start | bytes 1572872 | tf_op jit(solution)/shard_map/ppermute | solution.py:827
  61.6 2.9 %collective-permute-start.16 = (bf16[512,512]{1,0:T(8,128)(2,1)}, bf16[512,512]{1,0:T(8,128)(2,1)S(1)}, u32[]{:S(2)}, u32[]{:S(2)}) collective-permute-start(bf16[512,512]{1,0:T(8,128)(2,1)} %collective-permute-done.11.refs_4_), channel_id=1, source_target_pairs={{0,1},{1,0},{2,3},{3,2},{4,5},{5,4},{6,7},{7,6},{8,9},{9,8},{10,11... | collective-permute-start | bytes 1572872 | tf_op jit(solution)/shard_map/ppermute | solution.py:827
  74.0 4.2 %collective-permute-start.18 = (bf16[1056,512]{1,0:T(8,128)(2,1)S(1)}, bf16[1056,512]{1,0:T(8,128)(2,1)S(1)}, u32[]{:S(2)}, u32[]{:S(2)}) collective-permute-start(bf16[1056,512]{1,0:T(8,128)(2,1)S(1)} %facets.1.mine), channel_id=1, source_target_pairs={{0,1},{1,0},{2,3},{3,2},{4,5},{5,4},{6,7},{7,6},{8,9},{9,8},{10,11... | collective-permute-start | bytes 3244040 | tf_op jit(solution)/shard_map/ppermute | solution.py:827
  80.1 12.2 %collective-permute-start.21 = (bf16[64,512]{1,0:T(8,128)(2,1)S(1)}, bf16[64,512]{1,0:T(8,128)(2,1)S(1)}, u32[]{:S(2)}, u32[]{:S(2)}) collective-permute-start(bf16[64,512]{1,0:T(8,128)(2,1)S(1)} %get-tuple-element.104), channel_id=1, source_target_pairs={{0,2},{1,3},{2,0},{3,1},{4,6},{5,7},{6,4},{7,5},{8,10},{9,11},{10,... | collective-permute-start | bytes 196616 | tf_op jit(solution)/shard_map/ppermute | solution.py:819
  82.9 9.4 %collective-permute-start.22 = (bf16[64,512]{1,0:T(8,128)(2,1)S(1)}, bf16[64,512]{1,0:T(8,128)(2,1)S(1)}, u32[]{:S(2)}, u32[]{:S(2)}) collective-permute-start(bf16[64,512]{1,0:T(8,128)(2,1)S(1)} %get-tuple-element.105), channel_id=1, source_target_pairs={{0,4},{1,5},{2,6},{3,7},{4,0},{5,1},{6,2},{7,3},{8,12},{9,13},{10,... | collective-permute-start | bytes 196616 | tf_op jit(solution)/shard_map/ppermute | solution.py:819
  84.1 8.2 %collective-permute-start.23 = (bf16[64,512]{1,0:T(8,128)(2,1)S(1)}, bf16[64,512]{1,0:T(8,128)(2,1)S(1)}, u32[]{:S(2)}, u32[]{:S(2)}) collective-permute-start(bf16[64,512]{1,0:T(8,128)(2,1)S(1)} %get-tuple-element.106), channel_id=1, source_target_pairs={{0,6},{1,7},{2,4},{3,5},{4,2},{5,3},{6,0},{7,1},{8,14},{9,15},{10,... | collective-permute-start | bytes 196616 | tf_op jit(solution)/shard_map/ppermute | solution.py:819
  87.6 15.5 %collective-permute-start.20 = (bf16[512,512]{1,0:T(8,128)(2,1)S(1)}, bf16[512,512]{1,0:T(8,128)(2,1)S(1)}, u32[]{:S(2)}, u32[]{:S(2)}) collective-permute-start(bf16[512,512]{1,0:T(8,128)(2,1)S(1)} %get-tuple-element.99), channel_id=1, source_target_pairs={{2,4},{3,5},{4,2},{5,3},{10,12},{11,13},{12,10},{13,11},{18,20},{1... | collective-permute-start | bytes 1572872 | tf_op jit(solution)/shard_map/ppermute | solution.py:819
  91.0 15.2 %collective-permute-start.19 = (bf16[512,512]{1,0:T(8,128)(2,1)S(1)}, bf16[512,512]{1,0:T(8,128)(2,1)S(1)}, u32[]{:S(2)}, u32[]{:S(2)}) collective-permute-start(bf16[512,512]{1,0:T(8,128)(2,1)S(1)} %get-tuple-element.99), channel_id=1, source_target_pairs={{0,2},{1,3},{6,4},{7,5},{8,10},{9,11},{14,12},{15,13},{16,18},{17,... | collective-permute-start | bytes 1572872 | tf_op jit(solution)/shard_map/ppermute | solution.py:819
  106.4 23.8 %collective-permute-start.25 = (bf16[512,512]{1,0:T(8,128)(2,1)S(1)}, bf16[512,512]{1,0:T(8,128)(2,1)S(1)}, u32[]{:S(2)}, u32[]{:S(2)}) collective-permute-start(bf16[512,512]{1,0:T(8,128)(2,1)S(1)} %add_convert_fusion), channel_id=1, source_target_pairs={{0,4},{1,5},{2,6},{3,7},{4,0},{5,1},{6,2},{7,3},{8,12},{9,13},{10,... | collective-permute-start | bytes 1572872 | tf_op jit(solution)/shard_map/ppermute | solution.py:819
  106.5 23.8 %collective-permute-start.24 = (bf16[512,512]{1,0:T(8,128)(2,1)S(1)}, bf16[512,512]{1,0:T(8,128)(2,1)S(1)}, u32[]{:S(2)}, u32[]{:S(2)}) collective-permute-start(bf16[512,512]{1,0:T(8,128)(2,1)S(1)} %get-tuple-element.119), channel_id=1, source_target_pairs={{0,2},{1,3},{2,0},{3,1},{4,6},{5,7},{6,4},{7,5},{8,10},{9,11},{10,... | collective-permute-start | bytes 1572872 | tf_op jit(solution)/shard_map/ppermute | solution.py:819
  108.5 9.5 %collective-permute-start.26 = (f32[8,384]{1,0:T(8,128)S(1)}, f32[8,384]{1,0:T(8,128)S(1)}, u32[]{:S(2)}, u32[]{:S(2)}) collective-permute-start(f32[8,384]{1,0:T(8,128)S(1)} %copy-done.28), channel_id=1, source_target_pairs={{0,8},{8,16},{16,24},{1,9},{9,17},{17,25},{2,10},{10,18},{18,26},{... | collective-permute-start | bytes 36872 | tf_op jit(solution)/shard_map/ppermute | solution.py:933
  112.1 6.5 %collective-permute-start.27 = (f32[8,384]{1,0:T(8,128)S(1)}, f32[8,384]{1,0:T(8,128)S(1)}, u32[]{:S(2)}, u32[]{:S(2)}) collective-permute-start(f32[8,384]{1,0:T(8,128)S(1)} %copy-done.27), channel_id=1, source_target_pairs={{8,0},{16,8},{24,16},{9,1},{17,9},{25,17},{10,2},{18,10},{26,18},{... | collective-permute-start | bytes 36872 | tf_op jit(solution)/shard_map/ppermute | solution.py:932
  114.3 3.7 %collective-permute-start.28 = (f32[8,128]{1,0:T(8,128)S(1)}, f32[8,128]{1,0:T(8,128)S(1)}, u32[]{:S(2)}, u32[]{:S(2)}) collective-permute-start(f32[8,128]{1,0:T(8,128)S(1)} %copy-done.21), channel_id=1, source_target_pairs={{0,8},{8,0},{16,24},{24,16},{1,9},{9,1},{17,25},{25,17},{2,10},{10... | collective-permute-start | bytes 12296 | tf_op jit(solution)/shard_map/ppermute | solution.py:930
  120.7 9.5 %collective-permute-start.29 = (f32[8,384]{1,0:T(8,128)}, f32[8,384]{1,0:T(8,128)S(1)}, u32[]{:S(2)}, u32[]{:S(2)}) collective-permute-start(f32[8,384]{1,0:T(8,128)} %get-tuple-element.128), channel_id=1, source_target_pairs={{0,1},{1,2},{2,3},{3,4},{4,5},{5,6},{6,7},{8,9},{9,10},{10,11},{11... | collective-permute-start | bytes 36872 | tf_op jit(solution)/shard_map/ppermute | solution.py:946
  122.6 7.5 %collective-permute-start.30 = (f32[8,384]{1,0:T(8,128)}, f32[8,384]{1,0:T(8,128)S(1)}, u32[]{:S(2)}, u32[]{:S(2)}) collective-permute-start(f32[8,384]{1,0:T(8,128)} %get-tuple-element.129), channel_id=1, source_target_pairs={{1,0},{2,1},{3,2},{4,3},{5,4},{6,5},{7,6},{9,8},{10,9},{11,10},{12... | collective-permute-start | bytes 36872 | tf_op jit(solution)/shard_map/ppermute | solution.py:947
  126.2 3.9 %collective-permute-start.31 = (f32[8,128]{1,0:T(8,128)}, f32[8,128]{1,0:T(8,128)S(1)}, u32[]{:S(2)}, u32[]{:S(2)}) collective-permute-start(f32[8,128]{1,0:T(8,128)} %get-tuple-element.130.refs_17_), channel_id=1, source_target_pairs={{0,16},{8,24},{16,0},{24,8},{1,17},{9,25},{17,1},{25,9},{2,18},{10... | collective-permute-start | bytes 12296 | tf_op jit(solution)/shard_map/ppermute | solution.py:930
  (30 other events, 187.0 us)

commit v10 on v9

--- a/solution.py
+++ b/solution.py
@@ -374,7 +374,7 @@
             pltpu.SemaphoreType.DMA((11,)),
             pltpu.SemaphoreType.DMA((4,)),
         ],
-        compiler_params=pltpu.CompilerParams(vmem_limit_bytes=60 * 1024 * 1024),
+        compiler_params=pltpu.CompilerParams(vmem_limit_bytes=48 * 1024 * 1024),
         name="sky",
     )(*operands)
 
@@ -760,7 +760,7 @@
             pltpu.SemaphoreType.DMA((number, slots)),
             pltpu.SemaphoreType.DMA((number, slots)),
         ],
-        compiler_params=pltpu.CompilerParams(vmem_limit_bytes=44 * 1024 * 1024),
+        compiler_params=pltpu.CompilerParams(vmem_limit_bytes=47 * 1024 * 1024),
         name="facets",
     )(ints, weights, *tiles, *strips, ku, kv, data, squares)
 

time: 141 us -> 138 us (0.979)
  starting transfers between devices: 49.8 us -> 45.7 us
  local copies, waits for them, and re-layouts: 11 us -> 12.5 us
    pallas_call x1, Pallas kernels: 7.85 us -> 11.7 us  [facets(): pl.pallas_call(functools.partial(facets_kernel, 512, len(tiles)), in_spec...]
    pallas_call x2, Pallas kernels: 12.5 us -> 9.47 us  [sky_of(): pl.pallas_call(functools.partial(sky_kernel, alone), in_specs=[anywhere]...]
    unnamed x62 -> x72, local copies, waits for them, and re-layouts: 6.73 us -> 9.5 us
    ppermute x14, starting transfers between devices: 22.6 us -> 20.3 us  [by_chips(): lax.ppermute(x, 'gy', [(2 * a + c, 2 * b + c) for a, b in pairs for c in...]
    ppermute x8, starting transfers between devices: 3.12 us -> 1.35 us  [swapped(): lax.ppermute(x, 'gy', [(i, i ^ 1) for i in range(lax.axis_size('gy'))])]
  transfers between devices with their start and end apart: 32 -> 32, of which waited for: 14 -> 13; matrix products, arithmetic and copies ran while one was open for 3% -> 2% of each run, Pallas kernels for 17% -> 15%
where the time goes in v10:
time: 138 us; the launch traced here: 137 us
  starting transfers between devices  45.7 us (33%)
  Pallas kernels  40.3 us (29%)
  waiting for transfers between devices  33.8 us (24%)
  local copies, waits for them, and re-layouts  12.5 us (9%)
  other arithmetic  3 us (2%)
  between operations  1.49 us (1%)
    ppermute x14, starting transfers between devices, by_chips(): lax.ppermute(x, 'gy', [(2 * a + c, 2 * b + c) for a, b in pairs for c in...  20.3 us
    ppermute x14, waiting for transfers between devices, by_chips(): lax.ppermute(x, 'gy', [(2 * a + c, 2 * b + c) for a, b in pairs for c in...  17.8 us
    pallas_call x2, Pallas kernels, adjoint(): pl.pallas_call(functools.partial(adjoint_kernel, edge, len(parts), cells)...  12.8 us
    pallas_call x1, Pallas kernels, facets(): pl.pallas_call(functools.partial(facets_kernel, 512, len(tiles)), in_spec...  11.7 us
    unnamed x72, local copies, waits for them, and re-layouts  9.5 us
    pallas_call x2, Pallas kernels, sky_of(): pl.pallas_call(functools.partial(sky_kernel, alone), in_specs=[anywhere]...  9.47 us
    ppermute x2, waiting for transfers between devices, across(): return lax.ppermute(x, 'gx', [(i, i ^ hop) for i in range(size)])  6.23 us
    ppermute x8, waiting for transfers between devices, swapped(): lax.ppermute(x, 'gy', [(i, i ^ 1) for i in range(lax.axis_size('gy'))])  5.36 us
  transfers between devices with their start and end apart: 32, of which 13 were waited for; matrix products, arithmetic and copies ran while one was open for 2% of the time, Pallas kernels for 15%

profile of v10, /device:TPU:10, one launch (start us, length us, event | category | flops | bytes accessed | tf_op | source)
XLA Modules:
  0.0 136.8 jit_solution(3945504728596449049)
XLA Ops:
  2.0 1.8 %convert_reduce_fusion = (f32[2,9,128]{2,1,0:T(8,128)S(1)}, f32[2,9,128]{2,1,0:T(8,128)S(1)}) fusion(bf16[4,9,128,128]{3,2,1,0:T(8,128)(2,1)} %refs_5_.3), kind=kLoop, calls=%fused_computation.1 | loop fusion | flops 4608 | bytes 27648 | tf_op jit(solution)/shard_map/convert_element_type | solution.py:304
  4.2 1.9 %collective-permute-start = (f32[22,128]{1,0:T(8,128)S(1)}, f32[22,128]{1,0:T(8,128)S(1)}, u32[]{:S(2)}, u32[]{:S(2)}) collective-permute-start(f32[22,128]{1,0:T(8,128)S(1)} %pad_maximum_fusion.1.refs_6_), channel_id=1, source_target_pairs={{0,1},{1,2},{2,3},{3,4},{4,5},{5,6},{6,7},{8,9},{9,10},{10,11},{11... | collective-permute-start | bytes 33800 | tf_op jit(solution)/shard_map/ppermute | solution.py:847
  6.5 3.6 %collective-permute-start.1 = (f32[22,128]{1,0:T(8,128)S(1)}, f32[22,128]{1,0:T(8,128)S(1)}, u32[]{:S(2)}, u32[]{:S(2)}) collective-permute-start(f32[22,128]{1,0:T(8,128)S(1)} %pad_maximum_fusion.2.refs_5_), channel_id=1, source_target_pairs={{1,0},{2,1},{3,2},{4,3},{5,4},{6,5},{7,6},{9,8},{10,9},{11,10},{12... | collective-permute-start | bytes 33800 | tf_op jit(solution)/shard_map/ppermute | solution.py:848
  11.2 4.8 %sky.2 = bf16[512,512]{1,0:T(8,128)(2,1)} custom-call(f32[128,128]{1,0:T(8,128)S(1)} %copy-done.4, bf16[4,9,128,128]{3,2,1,0:T(8,128)(2,1)S(1)} %copy-done, f32[256,256]{1,0:T(8,128)S(1)} %copy-done.2, bf16[4,9,256,256]{3,2,1,0:T(8,128)(2,1)} %refs_4_.5, f32[512,512]{1,0:T(8,128)S(1)} %copy-done.1), custom_call_target="tpu_custom_call" | custom-call | tf_op jit(solution)/shard_map/sky/pallas_call | solution.py:348
  16.0 2.7 %collective-permute-start.8 = (bf16[512,512]{1,0:T(8,128)(2,1)}, bf16[512,512]{1,0:T(8,128)(2,1)S(1)}, u32[]{:S(2)}, u32[]{:S(2)}) collective-permute-start(bf16[512,512]{1,0:T(8,128)(2,1)} %sky.2), channel_id=1, source_target_pairs={{0,4},{1,5},{2,6},{3,7},{4,0},{5,1},{6,2},{7,3},{8,12},{9,13},{10,... | collective-permute-start | bytes 1572872 | tf_op jit(solution)/shard_map/ppermute | solution.py:819
  20.3 1.5 %sides.1 = (f32[22,132]{1,0:T(8,128)}, f32[22,132]{1,0:T(8,128)}) custom-call(f32[22,128]{1,0:T(8,128)} %copy-done.12, f32[22,128]{1,0:T(8,128)} %copy-done.14, f32[22,128]{1,0:T(8,128)} %get-tuple-element.157.first_side, f32[22,128]{1,0:T(8,128)} %get-tuple-element.158.last_side), custom_call_target="tpu_custom_call" | custom-call | flops 40000000000 | bytes 64000000 | tf_op jit(solution)/shard_map/sides/pallas_call | solution.py:325
  21.9 3.4 %collective-permute-start.2 = (f32[22,132]{1,0:T(8,128)}, f32[22,132]{1,0:T(8,128)S(1)}, u32[]{:S(2)}, u32[]{:S(2)}) collective-permute-start(f32[22,132]{1,0:T(8,128)} %get-tuple-element.78), channel_id=1, source_target_pairs={{0,8},{8,16},{16,24},{1,9},{9,17},{17,25},{2,10},{10,18},{18,26},{... | collective-permute-start | bytes 34856 | tf_op jit(solution)/shard_map/ppermute | solution.py:334
  25.3 2.4 %collective-permute-start.3 = (f32[22,132]{1,0:T(8,128)}, f32[22,132]{1,0:T(8,128)S(1)}, u32[]{:S(2)}, u32[]{:S(2)}) collective-permute-start(f32[22,132]{1,0:T(8,128)} %get-tuple-element.79), channel_id=1, source_target_pairs={{8,0},{16,8},{24,16},{9,1},{17,9},{25,17},{10,2},{18,10},{26,18},{... | collective-permute-start | bytes 34856 | tf_op jit(solution)/shard_map/ppermute | solution.py:334
  27.9 4.2 %collective-permute-done.3.refs_2_.refs_7_ = f32[22,132]{1,0:T(8,128)S(1)} collective-permute-done((f32[22,132]{1,0:T(8,128)}, f32[22,132]{1,0:T(8,128)S(1)}, u32[]{:S(2)}, u32[]{:S(2)}) %collective-permute-start.3) | collective-permute-done | bytes 11648 | tf_op jit(solution)/shard_map/ppermute | solution.py:334
  33.5 4.6 %sky.3 = (bf16[512,512]{1,0:T(8,128)(2,1)S(1)}, bf16[32,512]{1,0:T(8,128)(2,1)S(1)}, f32[8,128]{1,0:T(8,128)S(1)}, f32[22,132]{1,0:T(8,128)S(1)}, f32[22,132]{1,0:T(8,128)S(1)}) custom-call(f32[128,128]{1,0:T(8,128)S(1)} %copy-done.4, f32[22,132]{1,0:T(8,128)S(1)} %collective-permute-done.2.refs_1_.refs_6_, ...), custom_call_target="tpu_custom_call" | custom-call | tf_op jit(solution)/shard_map/sky/pallas_call | solution.py:348
  40.6 3.5 %collective-permute-start.5 = (bf16[32,512]{1,0:T(8,128)(2,1)S(1)}, bf16[32,512]{1,0:T(8,128)(2,1)S(1)}, u32[]{:S(2)}, u32[]{:S(2)}) collective-permute-start(bf16[32,512]{1,0:T(8,128)(2,1)S(1)} %get-tuple-element.81), channel_id=1, source_target_pairs={{0,4},{1,5},{2,6},{3,7},{4,0},{5,1},{6,2},{7,3},{8,12},{9,13},{10,... | collective-permute-start | bytes 98312 | tf_op jit(solution)/shard_map/ppermute | solution.py:819
  44.7 1.6 %collective-permute-done.5 = bf16[32,512]{1,0:T(8,128)(2,1)S(1)} collective-permute-done((bf16[32,512]{1,0:T(8,128)(2,1)S(1)}, bf16[32,512]{1,0:T(8,128)(2,1)S(1)}, u32[]{:S(2)}, u32[]{:S(2)}) %collective-permute-start.5) | collective-permute-done | bytes 32800 | tf_op jit(solution)/shard_map/ppermute | solution.py:819
  46.3 1.7 %collective-permute-done.4 = bf16[32,512]{1,0:T(8,128)(2,1)S(1)} collective-permute-done((bf16[32,512]{1,0:T(8,128)(2,1)S(1)}, bf16[32,512]{1,0:T(8,128)(2,1)S(1)}, u32[]{:S(2)}, u32[]{:S(2)}) %collective-permute-start.4) | collective-permute-done | bytes 32800 | tf_op jit(solution)/shard_map/ppermute | solution.py:819
  48.0 1.9 %collective-permute-start.10 = (bf16[512,512]{1,0:T(8,128)(2,1)}, bf16[512,512]{1,0:T(8,128)(2,1)S(1)}, u32[]{:S(2)}, u32[]{:S(2)}) collective-permute-start(bf16[512,512]{1,0:T(8,128)(2,1)} %copy-done.5), channel_id=1, source_target_pairs={{2,4},{3,5},{4,2},{5,3},{10,12},{11,13},{12,10},{13,11},{18,20},{1... | collective-permute-start | bytes 1572872 | tf_op jit(solution)/shard_map/ppermute | solution.py:819
  52.8 7.1 %collective-permute-done.10.refs_3_ = bf16[512,512]{1,0:T(8,128)(2,1)S(1)} collective-permute-done((bf16[512,512]{1,0:T(8,128)(2,1)}, bf16[512,512]{1,0:T(8,128)(2,1)S(1)}, u32[]{:S(2)}, u32[]{:S(2)}) %collective-permute-start.10) | collective-permute-done | bytes 524320 | tf_op jit(solution)/shard_map/ppermute | solution.py:819
  63.6 11.7 %facets.1.mine = bf16[1056,512]{1,0:T(8,128)(2,1)S(1)} custom-call(s32[2,5]{1,0:T(2,128)S(1)} %pad_add_fusion.ints, f32[2,2]{1,0:T(2,128)S(1)} %bitcast.14, bf16[512,512]{1,0:T(8,128)(2,1)S(1)} %copy-done.6, bf16[512,512]{1,0:T(8,128)(2,1)} %collective-permute-done.7.refs_1_, bf16[512,512]{1,0:T(8,128)(2,1)S(1)} %collective-permute-done.8.refs_2_, ...), custom_call_target="tpu_custom_call" | custom-call | tf_op jit(solution)/shard_map/facets/pallas_call | solution.py:745
  75.4 2.7 %collective-permute-done.18.theirs = bf16[1056,512]{1,0:T(8,128)(2,1)S(1)} collective-permute-done((bf16[1056,512]{1,0:T(8,128)(2,1)S(1)}, bf16[1056,512]{1,0:T(8,128)(2,1)S(1)}, u32[]{:S(2)}, u32[]{:S(2)}) %collective-permute-start.18) | collective-permute-done | bytes 1081376 | tf_op jit(solution)/shard_map/ppermute | solution.py:827
  81.6 1.4 collective-permute-start.23
  82.9 2.1 %mixed.3 = (bf16[512,512]{1,0:T(8,128)(2,1)S(1)}, bf16[512,512]{1,0:T(8,128)(2,1)S(1)}, bf16[512,512]{1,0:T(8,128)(2,1)S(1)}, bf16[512,512]{1,0:T(8,128)(2,1)S(1)}) custom-call(f32[4,4]{1,0:T(4,128)S(1)} %gather_fusion, bf16[1056,512]{1,0:T(8,128)(2,1)S(1)} %facets.1.mine, bf16[1056,512]{1,0:T(8,128)(2,1)S(1)} %collective-permute-done.18.theirs), custom_call_target="tpu_custom_call" | custom-call | tf_op jit(solution)/shard_map/mixed/pallas_call | solution.py:802
  85.8 2.6 %collective-permute-start.20 = (bf16[512,512]{1,0:T(8,128)(2,1)S(1)}, bf16[512,512]{1,0:T(8,128)(2,1)S(1)}, u32[]{:S(2)}, u32[]{:S(2)}) collective-permute-start(bf16[512,512]{1,0:T(8,128)(2,1)S(1)} %get-tuple-element.99), channel_id=1, source_target_pairs={{2,4},{3,5},{4,2},{5,3},{10,12},{11,13},{12,10},{13,11},{18,20},{1... | collective-permute-start | bytes 1572872 | tf_op jit(solution)/shard_map/ppermute | solution.py:819
  90.4 5.6 %adjoint.2 = (f32[8,384]{1,0:T(8,128)}, f32[8,384]{1,0:T(8,128)}, f32[8,384]{1,0:T(8,128)}, f32[8,384]{1,0:T(8,128)}, f32[8,128]{1,0:T(8,128)}) custom-call(bf16[64,512]{1,0:T(8,128)(2,1)} %copy-done.17, bf16[64,512]{1,0:T(8,128)(2,1)} %copy-done.29, bf16[64,512]{1,0:T(8,128)(2,1)} %copy-done.30, bf16[64,512]{1,0:T(8,128)(2,1)} %copy-done.31, ...), custom_call_target="tpu_custom_call" | custom-call | flops 40000000000 | bytes 64000000 | tf_op jit(solution)/shard_map/adjoint/pallas_call | solution.py:609
  96.0 4.8 %collective-permute-done.20.refs_3_ = bf16[512,512]{1,0:T(8,128)(2,1)S(1)} collective-permute-done((bf16[512,512]{1,0:T(8,128)(2,1)S(1)}, bf16[512,512]{1,0:T(8,128)(2,1)S(1)}, u32[]{:S(2)}, u32[]{:S(2)}) %collective-permute-start.20) | collective-permute-done | bytes 524320 | tf_op jit(solution)/shard_map/ppermute | solution.py:819
  100.9 2.6 %collective-permute-done.19 = bf16[512,512]{1,0:T(8,128)(2,1)S(1)} collective-permute-done((bf16[512,512]{1,0:T(8,128)(2,1)S(1)}, bf16[512,512]{1,0:T(8,128)(2,1)S(1)}, u32[]{:S(2)}, u32[]{:S(2)}) %collective-permute-start.19) | collective-permute-done | bytes 524320 | tf_op jit(solution)/shard_map/ppermute | solution.py:819
  103.7 2.5 %collective-permute-start.24 = (bf16[512,512]{1,0:T(8,128)(2,1)S(1)}, bf16[512,512]{1,0:T(8,128)(2,1)S(1)}, u32[]{:S(2)}, u32[]{:S(2)}) collective-permute-start(bf16[512,512]{1,0:T(8,128)(2,1)S(1)} %get-tuple-element.119), channel_id=1, source_target_pairs={{0,2},{1,3},{2,0},{3,1},{4,6},{5,7},{6,4},{7,5},{8,10},{9,11},{10,... | collective-permute-start | bytes 1572872 | tf_op jit(solution)/shard_map/ppermute | solution.py:819
  106.2 3.3 %collective-permute-start.26 = (f32[8,384]{1,0:T(8,128)S(1)}, f32[8,384]{1,0:T(8,128)S(1)}, u32[]{:S(2)}, u32[]{:S(2)}) collective-permute-start(f32[8,384]{1,0:T(8,128)S(1)} %copy-done.33), channel_id=1, source_target_pairs={{0,8},{8,16},{16,24},{1,9},{9,17},{17,25},{2,10},{10,18},{18,26},{... | collective-permute-start | bytes 36872 | tf_op jit(solution)/shard_map/ppermute | solution.py:933
  109.5 2.5 %collective-permute-start.27 = (f32[8,384]{1,0:T(8,128)S(1)}, f32[8,384]{1,0:T(8,128)S(1)}, u32[]{:S(2)}, u32[]{:S(2)}) collective-permute-start(f32[8,384]{1,0:T(8,128)S(1)} %copy-done.32), channel_id=1, source_target_pairs={{8,0},{16,8},{24,16},{9,1},{17,9},{25,17},{10,2},{18,10},{26,18},{... | collective-permute-start | bytes 36872 | tf_op jit(solution)/shard_map/ppermute | solution.py:932
  112.1 3.6 %collective-permute-done.28.other = f32[8,128]{1,0:T(8,128)S(1)} collective-permute-done((f32[8,128]{1,0:T(8,128)S(1)}, f32[8,128]{1,0:T(8,128)S(1)}, u32[]{:S(2)}, u32[]{:S(2)}) %collective-permute-start.28) | collective-permute-done | bytes 4128 | tf_op jit(solution)/shard_map/ppermute | solution.py:930
  116.9 1.5 %corners.1 = (f32[8,384]{1,0:T(8,128)}, f32[8,384]{1,0:T(8,128)}, f32[8,128]{1,0:T(8,128)}) custom-call(f32[8,384]{1,0:T(8,128)} %get-tuple-element.123.left, f32[8,384]{1,0:T(8,128)} %get-tuple-element.124.right, f32[8,384]{1,0:T(8,128)} %copy-done.21, f32[8,384]{1,0:T(8,128)} %copy-done.22, f32[8,128]{1,0:T(8,128)} %get-tuple-element.127.total, ...), custom_call_target="tpu_custom_call" | custom-call | tf_op jit(solution)/shard_map/corners/pallas_call | solution.py:936
  118.4 1.9 %collective-permute-start.29 = (f32[8,384]{1,0:T(8,128)}, f32[8,384]{1,0:T(8,128)S(1)}, u32[]{:S(2)}, u32[]{:S(2)}) collective-permute-start(f32[8,384]{1,0:T(8,128)} %get-tuple-element.128), channel_id=1, source_target_pairs={{0,1},{1,2},{2,3},{3,4},{4,5},{5,6},{6,7},{8,9},{9,10},{10,11},{11... | collective-permute-start | bytes 36872 | tf_op jit(solution)/shard_map/ppermute | solution.py:946
  120.3 3.6 %collective-permute-start.30 = (f32[8,384]{1,0:T(8,128)}, f32[8,384]{1,0:T(8,128)S(1)}, u32[]{:S(2)}, u32[]{:S(2)}) collective-permute-start(f32[8,384]{1,0:T(8,128)} %get-tuple-element.129), channel_id=1, source_target_pairs={{1,0},{2,1},{3,2},{4,3},{5,4},{6,5},{7,6},{9,8},{10,9},{11,10},{12... | collective-permute-start | bytes 36872 | tf_op jit(solution)/shard_map/ppermute | solution.py:947
  125.2 2.6 %collective-permute-done.31.refs_18_ = f32[8,128]{1,0:T(8,128)S(1)} collective-permute-done((f32[8,128]{1,0:T(8,128)}, f32[8,128]{1,0:T(8,128)S(1)}, u32[]{:S(2)}, u32[]{:S(2)}) %collective-permute-start.31) | collective-permute-done | bytes 4128 | tf_op jit(solution)/shard_map/ppermute | solution.py:930
  129.4 7.2 %adjoint.3 = (f32[512,512]{1,0:T(8,128)}, f32[256,256]{1,0:T(8,128)}, f32[128,128]{1,0:T(8,128)}, f32[1,1]{1,0:T(1,128)}) custom-call(bf16[512,512]{1,0:T(8,128)(2,1)} %copy-done.7, bf16[512,512]{1,0:T(8,128)(2,1)} %copy-done.20, bf16[512,512]{1,0:T(8,128)(2,1)} %copy-done.19, bf16[512,512]{1,0:T(8,128)(2,1)} %copy-done.18, ...), custom_call_target="tpu_custom_call" | custom-call | tf_op jit(solution)/shard_map/adjoint/pallas_call | solution.py:609
  (146 shorter events, 26.3 us)
Async XLA Ops:
  4.2 11.8 %collective-permute-start = (f32[22,128]{1,0:T(8,128)S(1)}, f32[22,128]{1,0:T(8,128)S(1)}, u32[]{:S(2)}, u32[]{:S(2)}) collective-permute-start(f32[22,128]{1,0:T(8,128)S(1)} %pad_maximum_fusion.1.refs_6_), channel_id=1, source_target_pairs={{0,1},{1,2},{2,3},{3,4},{4,5},{5,6},{6,7},{8,9},{9,10},{10,11},{11... | collective-permute-start | bytes 33800 | tf_op jit(solution)/shard_map/ppermute | solution.py:847
  6.5 9.5 %collective-permute-start.1 = (f32[22,128]{1,0:T(8,128)S(1)}, f32[22,128]{1,0:T(8,128)S(1)}, u32[]{:S(2)}, u32[]{:S(2)}) collective-permute-start(f32[22,128]{1,0:T(8,128)S(1)} %pad_maximum_fusion.2.refs_5_), channel_id=1, source_target_pairs={{1,0},{2,1},{3,2},{4,3},{5,4},{6,5},{7,6},{9,8},{10,9},{11,10},{12... | collective-permute-start | bytes 33800 | tf_op jit(solution)/shard_map/ppermute | solution.py:848
  16.0 32.0 %collective-permute-start.8 = (bf16[512,512]{1,0:T(8,128)(2,1)}, bf16[512,512]{1,0:T(8,128)(2,1)S(1)}, u32[]{:S(2)}, u32[]{:S(2)}) collective-permute-start(bf16[512,512]{1,0:T(8,128)(2,1)} %sky.2), channel_id=1, source_target_pairs={{0,4},{1,5},{2,6},{3,7},{4,0},{5,1},{6,2},{7,3},{8,12},{9,13},{10,... | collective-permute-start | bytes 1572872 | tf_op jit(solution)/shard_map/ppermute | solution.py:819
  18.7 29.3 %collective-permute-start.7 = (bf16[512,512]{1,0:T(8,128)(2,1)}, bf16[512,512]{1,0:T(8,128)(2,1)}, u32[]{:S(2)}, u32[]{:S(2)}) collective-permute-start(bf16[512,512]{1,0:T(8,128)(2,1)} %sky.2), channel_id=1, source_target_pairs={{0,2},{1,3},{2,0},{3,1},{4,6},{5,7},{6,4},{7,5},{8,10},{9,11},{10,... | collective-permute-start | bytes 1572872 | tf_op jit(solution)/shard_map/ppermute | solution.py:819
  21.9 6.1 %collective-permute-start.2 = (f32[22,132]{1,0:T(8,128)}, f32[22,132]{1,0:T(8,128)S(1)}, u32[]{:S(2)}, u32[]{:S(2)}) collective-permute-start(f32[22,132]{1,0:T(8,128)} %get-tuple-element.78), channel_id=1, source_target_pairs={{0,8},{8,16},{16,24},{1,9},{9,17},{17,25},{2,10},{10,18},{18,26},{... | collective-permute-start | bytes 34856 | tf_op jit(solution)/shard_map/ppermute | solution.py:334
  25.3 6.8 %collective-permute-start.3 = (f32[22,132]{1,0:T(8,128)}, f32[22,132]{1,0:T(8,128)S(1)}, u32[]{:S(2)}, u32[]{:S(2)}) collective-permute-start(f32[22,132]{1,0:T(8,128)} %get-tuple-element.79), channel_id=1, source_target_pairs={{8,0},{16,8},{24,16},{9,1},{17,9},{25,17},{10,2},{18,10},{26,18},{... | collective-permute-start | bytes 34856 | tf_op jit(solution)/shard_map/ppermute | solution.py:334
  27.9 16.2 %collective-permute-start.9 = (f32[2,8]{0,1:T(8,128)S(1)}, f32[2,8]{0,1:T(8,128)S(1)}, u32[]{:S(2)}, u32[]{:S(2)}) collective-permute-start(f32[2,8]{0,1:T(8,128)S(1)} %copy.32), channel_id=1, source_target_pairs={{0,1},{1,0},{2,3},{3,2},{4,5},{5,4},{6,7},{7,6},{8,9},{9,8},{10,11... | collective-permute-start | bytes 200 | tf_op jit(solution)/shard_map/ppermute | solution.py:827
  40.2 4.6 %collective-permute-start.6 = (bf16[32,512]{1,0:T(8,128)(2,1)S(1)}, bf16[32,512]{1,0:T(8,128)(2,1)S(1)}, u32[]{:S(2)}, u32[]{:S(2)}) collective-permute-start(bf16[32,512]{1,0:T(8,128)(2,1)S(1)} %get-tuple-element.81), channel_id=1, source_target_pairs={{0,6},{1,7},{2,4},{3,5},{4,2},{5,3},{6,0},{7,1},{8,14},{9,15},{10,... | collective-permute-start | bytes 98312 | tf_op jit(solution)/shard_map/ppermute | solution.py:819
  40.6 5.7 %collective-permute-start.5 = (bf16[32,512]{1,0:T(8,128)(2,1)S(1)}, bf16[32,512]{1,0:T(8,128)(2,1)S(1)}, u32[]{:S(2)}, u32[]{:S(2)}) collective-permute-start(bf16[32,512]{1,0:T(8,128)(2,1)S(1)} %get-tuple-element.81), channel_id=1, source_target_pairs={{0,4},{1,5},{2,6},{3,7},{4,0},{5,1},{6,2},{7,3},{8,12},{9,13},{10,... | collective-permute-start | bytes 98312 | tf_op jit(solution)/shard_map/ppermute | solution.py:819
  44.1 3.9 %collective-permute-start.4 = (bf16[32,512]{1,0:T(8,128)(2,1)S(1)}, bf16[32,512]{1,0:T(8,128)(2,1)S(1)}, u32[]{:S(2)}, u32[]{:S(2)}) collective-permute-start(bf16[32,512]{1,0:T(8,128)(2,1)S(1)} %get-tuple-element.81), channel_id=1, source_target_pairs={{0,2},{1,3},{2,0},{3,1},{4,6},{5,7},{6,4},{7,5},{8,10},{9,11},{10,... | collective-permute-start | bytes 98312 | tf_op jit(solution)/shard_map/ppermute | solution.py:819
  48.0 11.9 %collective-permute-start.10 = (bf16[512,512]{1,0:T(8,128)(2,1)}, bf16[512,512]{1,0:T(8,128)(2,1)S(1)}, u32[]{:S(2)}, u32[]{:S(2)}) collective-permute-start(bf16[512,512]{1,0:T(8,128)(2,1)} %copy-done.5), channel_id=1, source_target_pairs={{2,4},{3,5},{4,2},{5,3},{10,12},{11,13},{12,10},{13,11},{18,20},{1... | collective-permute-start | bytes 1572872 | tf_op jit(solution)/shard_map/ppermute | solution.py:819
  50.0 9.9 %collective-permute-start.11 = (bf16[512,512]{1,0:T(8,128)(2,1)S(1)}, bf16[512,512]{1,0:T(8,128)(2,1)S(1)}, u32[]{:S(2)}, u32[]{:S(2)}) collective-permute-start(bf16[512,512]{1,0:T(8,128)(2,1)S(1)} %collective-permute-done.8.refs_2_), channel_id=1, source_target_pairs={{4,6},{5,7},{2,0},{3,1},{12,14},{13,15},{10,8},{11,9},{20,22},{21,... | collective-permute-start | bytes 1572872 | tf_op jit(solution)/shard_map/ppermute | solution.py:819
  51.3 1.4 collective-permute-start.17
  51.5 9.0 %collective-permute-start.12 = (bf16[512,512]{1,0:T(8,128)(2,1)}, bf16[512,512]{1,0:T(8,128)(2,1)S(1)}, u32[]{:S(2)}, u32[]{:S(2)}) collective-permute-start(bf16[512,512]{1,0:T(8,128)(2,1)} %copy-done.5), channel_id=1, source_target_pairs={{0,1},{1,0},{2,3},{3,2},{4,5},{5,4},{6,7},{7,6},{8,9},{9,8},{10,11... | collective-permute-start | bytes 1572872 | tf_op jit(solution)/shard_map/ppermute | solution.py:827
  52.0 8.6 %collective-permute-start.14 = (bf16[512,512]{1,0:T(8,128)(2,1)S(1)}, bf16[512,512]{1,0:T(8,128)(2,1)S(1)}, u32[]{:S(2)}, u32[]{:S(2)}) collective-permute-start(bf16[512,512]{1,0:T(8,128)(2,1)S(1)} %collective-permute-done.8.refs_2_), channel_id=1, source_target_pairs={{0,1},{1,0},{2,3},{3,2},{4,5},{5,4},{6,7},{7,6},{8,9},{9,8},{10,11... | collective-permute-start | bytes 1572872 | tf_op jit(solution)/shard_map/ppermute | solution.py:827
  52.7 7.9 %collective-permute-start.13 = (bf16[512,512]{1,0:T(8,128)(2,1)}, bf16[512,512]{1,0:T(8,128)(2,1)S(1)}, u32[]{:S(2)}, u32[]{:S(2)}) collective-permute-start(bf16[512,512]{1,0:T(8,128)(2,1)} %collective-permute-done.7.refs_1_), channel_id=1, source_target_pairs={{0,1},{1,0},{2,3},{3,2},{4,5},{5,4},{6,7},{7,6},{8,9},{9,8},{10,11... | collective-permute-start | bytes 1572872 | tf_op jit(solution)/shard_map/ppermute | solution.py:827
  59.9 1.9 %collective-permute-start.15 = (bf16[512,512]{1,0:T(8,128)(2,1)S(1)}, bf16[512,512]{1,0:T(8,128)(2,1)S(1)}, u32[]{:S(2)}, u32[]{:S(2)}) collective-permute-start(bf16[512,512]{1,0:T(8,128)(2,1)S(1)} %collective-permute-done.10.refs_3_), channel_id=1, source_target_pairs={{0,1},{1,0},{2,3},{3,2},{4,5},{5,4},{6,7},{7,6},{8,9},{9,8},{10,11... | collective-permute-start | bytes 1572872 | tf_op jit(solution)/shard_map/ppermute | solution.py:827
  59.9 2.7 %collective-permute-start.16 = (bf16[512,512]{1,0:T(8,128)(2,1)S(1)}, bf16[512,512]{1,0:T(8,128)(2,1)S(1)}, u32[]{:S(2)}, u32[]{:S(2)}) collective-permute-start(bf16[512,512]{1,0:T(8,128)(2,1)S(1)} %collective-permute-done.11.refs_4_), channel_id=1, source_target_pairs={{0,1},{1,0},{2,3},{3,2},{4,5},{5,4},{6,7},{7,6},{8,9},{9,8},{10,11... | collective-permute-start | bytes 1572872 | tf_op jit(solution)/shard_map/ppermute | solution.py:827
  75.3 2.8 %collective-permute-start.18 = (bf16[1056,512]{1,0:T(8,128)(2,1)S(1)}, bf16[1056,512]{1,0:T(8,128)(2,1)S(1)}, u32[]{:S(2)}, u32[]{:S(2)}) collective-permute-start(bf16[1056,512]{1,0:T(8,128)(2,1)S(1)} %facets.1.mine), channel_id=1, source_target_pairs={{0,1},{1,0},{2,3},{3,2},{4,5},{5,4},{6,7},{7,6},{8,9},{9,8},{10,11... | collective-permute-start | bytes 3244040 | tf_op jit(solution)/shard_map/ppermute | solution.py:827
  79.4 10.4 %collective-permute-start.21 = (bf16[64,512]{1,0:T(8,128)(2,1)S(1)}, bf16[64,512]{1,0:T(8,128)(2,1)S(1)}, u32[]{:S(2)}, u32[]{:S(2)}) collective-permute-start(bf16[64,512]{1,0:T(8,128)(2,1)S(1)} %get-tuple-element.104), channel_id=1, source_target_pairs={{0,2},{1,3},{2,0},{3,1},{4,6},{5,7},{6,4},{7,5},{8,10},{9,11},{10,... | collective-permute-start | bytes 196616 | tf_op jit(solution)/shard_map/ppermute | solution.py:819
  80.3 9.4 %collective-permute-start.22 = (bf16[64,512]{1,0:T(8,128)(2,1)S(1)}, bf16[64,512]{1,0:T(8,128)(2,1)S(1)}, u32[]{:S(2)}, u32[]{:S(2)}) collective-permute-start(bf16[64,512]{1,0:T(8,128)(2,1)S(1)} %get-tuple-element.105), channel_id=1, source_target_pairs={{0,4},{1,5},{2,6},{3,7},{4,0},{5,1},{6,2},{7,3},{8,12},{9,13},{10,... | collective-permute-start | bytes 196616 | tf_op jit(solution)/shard_map/ppermute | solution.py:819
  81.6 8.2 %collective-permute-start.23 = (bf16[64,512]{1,0:T(8,128)(2,1)S(1)}, bf16[64,512]{1,0:T(8,128)(2,1)S(1)}, u32[]{:S(2)}, u32[]{:S(2)}) collective-permute-start(bf16[64,512]{1,0:T(8,128)(2,1)S(1)} %get-tuple-element.106), channel_id=1, source_target_pairs={{0,6},{1,7},{2,4},{3,5},{4,2},{5,3},{6,0},{7,1},{8,14},{9,15},{10,... | collective-permute-start | bytes 196616 | tf_op jit(solution)/shard_map/ppermute | solution.py:819
  85.8 15.0 %collective-permute-start.20 = (bf16[512,512]{1,0:T(8,128)(2,1)S(1)}, bf16[512,512]{1,0:T(8,128)(2,1)S(1)}, u32[]{:S(2)}, u32[]{:S(2)}) collective-permute-start(bf16[512,512]{1,0:T(8,128)(2,1)S(1)} %get-tuple-element.99), channel_id=1, source_target_pairs={{2,4},{3,5},{4,2},{5,3},{10,12},{11,13},{12,10},{13,11},{18,20},{1... | collective-permute-start | bytes 1572872 | tf_op jit(solution)/shard_map/ppermute | solution.py:819
  88.4 15.0 %collective-permute-start.19 = (bf16[512,512]{1,0:T(8,128)(2,1)S(1)}, bf16[512,512]{1,0:T(8,128)(2,1)S(1)}, u32[]{:S(2)}, u32[]{:S(2)}) collective-permute-start(bf16[512,512]{1,0:T(8,128)(2,1)S(1)} %get-tuple-element.99), channel_id=1, source_target_pairs={{0,2},{1,3},{6,4},{7,5},{8,10},{9,11},{14,12},{15,13},{16,18},{17,... | collective-permute-start | bytes 1572872 | tf_op jit(solution)/shard_map/ppermute | solution.py:819
  103.6 24.3 %collective-permute-start.25 = (bf16[512,512]{1,0:T(8,128)(2,1)S(1)}, bf16[512,512]{1,0:T(8,128)(2,1)S(1)}, u32[]{:S(2)}, u32[]{:S(2)}) collective-permute-start(bf16[512,512]{1,0:T(8,128)(2,1)S(1)} %add_convert_fusion), channel_id=1, source_target_pairs={{0,4},{1,5},{2,6},{3,7},{4,0},{5,1},{6,2},{7,3},{8,12},{9,13},{10,... | collective-permute-start | bytes 1572872 | tf_op jit(solution)/shard_map/ppermute | solution.py:819
  103.7 24.2 %collective-permute-start.24 = (bf16[512,512]{1,0:T(8,128)(2,1)S(1)}, bf16[512,512]{1,0:T(8,128)(2,1)S(1)}, u32[]{:S(2)}, u32[]{:S(2)}) collective-permute-start(bf16[512,512]{1,0:T(8,128)(2,1)S(1)} %get-tuple-element.119), channel_id=1, source_target_pairs={{0,2},{1,3},{2,0},{3,1},{4,6},{5,7},{6,4},{7,5},{8,10},{9,11},{10,... | collective-permute-start | bytes 1572872 | tf_op jit(solution)/shard_map/ppermute | solution.py:819
  106.2 9.5 %collective-permute-start.26 = (f32[8,384]{1,0:T(8,128)S(1)}, f32[8,384]{1,0:T(8,128)S(1)}, u32[]{:S(2)}, u32[]{:S(2)}) collective-permute-start(f32[8,384]{1,0:T(8,128)S(1)} %copy-done.33), channel_id=1, source_target_pairs={{0,8},{8,16},{16,24},{1,9},{9,17},{17,25},{2,10},{10,18},{18,26},{... | collective-permute-start | bytes 36872 | tf_op jit(solution)/shard_map/ppermute | solution.py:933
  109.5 6.5 %collective-permute-start.27 = (f32[8,384]{1,0:T(8,128)S(1)}, f32[8,384]{1,0:T(8,128)S(1)}, u32[]{:S(2)}, u32[]{:S(2)}) collective-permute-start(f32[8,384]{1,0:T(8,128)S(1)} %copy-done.32), channel_id=1, source_target_pairs={{8,0},{16,8},{24,16},{9,1},{17,9},{25,17},{10,2},{18,10},{26,18},{... | collective-permute-start | bytes 36872 | tf_op jit(solution)/shard_map/ppermute | solution.py:932
  112.0 3.7 %collective-permute-start.28 = (f32[8,128]{1,0:T(8,128)S(1)}, f32[8,128]{1,0:T(8,128)S(1)}, u32[]{:S(2)}, u32[]{:S(2)}) collective-permute-start(f32[8,128]{1,0:T(8,128)S(1)} %copy-done.26), channel_id=1, source_target_pairs={{0,8},{8,0},{16,24},{24,16},{1,9},{9,1},{17,25},{25,17},{2,10},{10... | collective-permute-start | bytes 12296 | tf_op jit(solution)/shard_map/ppermute | solution.py:930
  118.4 9.5 %collective-permute-start.29 = (f32[8,384]{1,0:T(8,128)}, f32[8,384]{1,0:T(8,128)S(1)}, u32[]{:S(2)}, u32[]{:S(2)}) collective-permute-start(f32[8,384]{1,0:T(8,128)} %get-tuple-element.128), channel_id=1, source_target_pairs={{0,1},{1,2},{2,3},{3,4},{4,5},{5,6},{6,7},{8,9},{9,10},{10,11},{11... | collective-permute-start | bytes 36872 | tf_op jit(solution)/shard_map/ppermute | solution.py:946
  120.3 7.5 %collective-permute-start.30 = (f32[8,384]{1,0:T(8,128)}, f32[8,384]{1,0:T(8,128)S(1)}, u32[]{:S(2)}, u32[]{:S(2)}) collective-permute-start(f32[8,384]{1,0:T(8,128)} %get-tuple-element.129), channel_id=1, source_target_pairs={{1,0},{2,1},{3,2},{4,3},{5,4},{6,5},{7,6},{9,8},{10,9},{11,10},{12... | collective-permute-start | bytes 36872 | tf_op jit(solution)/shard_map/ppermute | solution.py:947
  123.9 3.9 %collective-permute-start.31 = (f32[8,128]{1,0:T(8,128)}, f32[8,128]{1,0:T(8,128)S(1)}, u32[]{:S(2)}, u32[]{:S(2)}) collective-permute-start(f32[8,128]{1,0:T(8,128)} %get-tuple-element.130.refs_17_), channel_id=1, source_target_pairs={{0,16},{8,24},{16,0},{24,8},{1,17},{9,25},{17,1},{25,9},{2,18},{10... | collective-permute-start | bytes 12296 | tf_op jit(solution)/shard_map/ppermute | solution.py:930
  (35 other events, 186.4 us)

commit v11 on v10

--- a/solution.py
+++ b/solution.py
@@ -252,7 +252,7 @@
     shifted[1] = jnp.zeros(shifted.shape[1:], f32)
     for tile in range(2 * cols // 128):
         lanes = slice(tile * 128, (tile + 1) * 128)
-        shifted[1, 8:last, lanes] = mix[tile] + xi[:, lanes]
+        shifted[1, 8:last, lanes] = mix[tile, : 2 * rows] + xi[:, lanes]
     shifted[1, 7:8, :] = lines[0:1]
     shifted[1, last : last + 1, :] = lines[1:2]
     pad = jnp.zeros((1, 7), f32)
@@ -271,7 +271,7 @@
     copies[-1].wait()
     for tile in range(4 * cols // 128):
         lanes = slice(tile * 128, (tile + 1) * 128)
-        sky_ref[:, lanes] = (fine_mix[tile] + xi_fine[:, lanes]).astype(bf16)
+        sky_ref[:, lanes] = (fine_mix[tile, : 4 * rows] + xi_fine[:, lanes]).astype(bf16)
     if alone:
         return
     strips_ref, sq_ref, lefts_ref, rights_ref = outs[1:]
@@ -363,13 +363,13 @@
             pltpu.VMEM((9, rows, cols), f32),
             pltpu.VMEM((2 * cols, 2 * cols), bf16),
             pltpu.VMEM((4 * rows, 2 * cols), bf16),
-            pltpu.VMEM((2 * cols // 128, 2 * rows, 128), f32),
+            pltpu.VMEM((2 * cols // 128, 2 * rows + 8, 128), f32),
             pltpu.VMEM((3, rows + 16, cols), f32),
             pltpu.VMEM((3, 2 * rows + 16, 2 * cols), f32),
             pltpu.VMEM((9, 2 * rows, 2 * cols), f32),
             pltpu.VMEM((4 * cols, 4 * cols), bf16),
             pltpu.VMEM((8 * rows, 4 * cols), bf16),
-            pltpu.VMEM((4 * cols // 128, 4 * rows, 128), f32),
+            pltpu.VMEM((4 * cols // 128, 4 * rows + 8, 128), f32),
             *[pltpu.VMEM((22, rows + 4), f32) for _ in range(4)],
             pltpu.SemaphoreType.DMA((11,)),
             pltpu.SemaphoreType.DMA((4,)),
@@ -471,7 +471,7 @@
         leaving.start()
     split = moved(g, fine_perm[...])
     for tile in range(4 * cols // 128):
-        fine_mix[tile] = split[:, tile * 128 : (tile + 1) * 128]
+        fine_mix[tile, : 4 * rows] = split[:, tile * 128 : (tile + 1) * 128]
     spread(fine_mix, coef_fine, fine_terms, 2 * rows, 2 * cols, chunks)
     row_sums(fine_terms, fine_rowed)
     main, left, right = joined(fine_rowed, 2 * cols)
@@ -491,7 +491,7 @@
         middle_ref[2 * rows - 1 :] += from_below[2:3, 1 : 2 * cols + 1]
     split = moved(inner, perm[...])
     for tile in range(2 * cols // 128):
-        mix[tile] = split[:, tile * 128 : (tile + 1) * 128]
+        mix[tile, : 2 * rows] = split[:, tile * 128 : (tile + 1) * 128]
     spread(mix, coef_middle, terms, rows, cols)
     ring_above, ring_below = main[7:8], main[last : last + 1]
     lines = [ring_above, ring_below, left[:, 8:last], right[:, 8:last]]
@@ -614,11 +614,11 @@
         scratch_shapes=[pltpu.VMEM(x.shape, x.dtype) for x in (*parts, *operands)]
         + [
             pltpu.VMEM((4 * cols, 4 * cols), bf16),
-            pltpu.VMEM((4 * cols // 128, 4 * rows, 128), f32),
+            pltpu.VMEM((4 * cols // 128, 4 * rows + 8, 128), f32),
             pltpu.VMEM((9, 2 * rows + 32, 2 * cols), f32),
             pltpu.VMEM((3, 2 * rows + 128, 2 * cols), f32),
             pltpu.VMEM((2 * cols, 2 * cols), bf16),
-            pltpu.VMEM((2 * cols // 128, 2 * rows, 128), f32),
+            pltpu.VMEM((2 * cols // 128, 2 * rows + 8, 128), f32),
             pltpu.VMEM((9, rows + 32, cols), f32),
             pltpu.VMEM((3, rows + 128, cols), f32),
             pltpu.VMEM((4 * rows, 4 * cols), f32),

time: 138 us -> 138 us (level)
  starting transfers between devices: 45.7 us -> 48 us
  Pallas kernels: 40.3 us -> 38.6 us
    ppermute x8, starting transfers between devices: 1.35 us -> 3.39 us  [swapped(): lax.ppermute(x, 'gy', [(i, i ^ 1) for i in range(lax.axis_size('gy'))])]
    pallas_call x1, Pallas kernels: 11.7 us -> 10 us  [facets(): pl.pallas_call(functools.partial(facets_kernel, 512, len(tiles)), in_spec...]
  transfers between devices with their start and end apart: 32 -> 32, of which waited for: 13 -> 12; matrix products, arithmetic and copies ran while one was open for 2% -> 2% of each run, Pallas kernels for 15% -> 15%
where the time goes in v11:
time: 138 us; the launch traced here: 137 us
  starting transfers between devices  48 us (35%)
  Pallas kernels  38.6 us (28%)
  waiting for transfers between devices  33.2 us (24%)
  local copies, waits for them, and re-layouts  12.7 us (9%)
  other arithmetic  3 us (2%)
  between operations  1.48 us (1%)
    ppermute x14, starting transfers between devices, by_chips(): lax.ppermute(x, 'gy', [(2 * a + c, 2 * b + c) for a, b in pairs for c in...  20.5 us
    ppermute x14, waiting for transfers between devices, by_chips(): lax.ppermute(x, 'gy', [(2 * a + c, 2 * b + c) for a, b in pairs for c in...  17.8 us
    pallas_call x2, Pallas kernels, adjoint(): pl.pallas_call(functools.partial(adjoint_kernel, edge, len(parts), cells)...  12.8 us
    pallas_call x1, Pallas kernels, facets(): pl.pallas_call(functools.partial(facets_kernel, 512, len(tiles)), in_spec...  10 us
    unnamed x72, local copies, waits for them, and re-layouts  9.76 us
    pallas_call x2, Pallas kernels, sky_of(): pl.pallas_call(functools.partial(sky_kernel, alone), in_specs=[anywhere]...  9.44 us
    ppermute x2, waiting for transfers between devices, across(): return lax.ppermute(x, 'gx', [(i, i ^ hop) for i in range(size)])  6.26 us
    ppermute x8, waiting for transfers between devices, swapped(): lax.ppermute(x, 'gy', [(i, i ^ 1) for i in range(lax.axis_size('gy'))])  5 us
  transfers between devices with their start and end apart: 32, of which 12 were waited for; matrix products, arithmetic and copies ran while one was open for 2% of the time, Pallas kernels for 15%

profile of v11, /device:TPU:10, one launch (start us, length us, event | category | flops | bytes accessed | tf_op | source)
XLA Modules:
  0.0 137.1 jit_solution(10340313674758151201)
XLA Ops:
  2.0 1.8 %convert_reduce_fusion = (f32[2,9,128]{2,1,0:T(8,128)S(1)}, f32[2,9,128]{2,1,0:T(8,128)S(1)}) fusion(bf16[4,9,128,128]{3,2,1,0:T(8,128)(2,1)} %refs_5_.3), kind=kLoop, calls=%fused_computation.1 | loop fusion | flops 4608 | bytes 27648 | tf_op jit(solution)/shard_map/convert_element_type | solution.py:304
  4.2 1.9 %collective-permute-start = (f32[22,128]{1,0:T(8,128)S(1)}, f32[22,128]{1,0:T(8,128)S(1)}, u32[]{:S(2)}, u32[]{:S(2)}) collective-permute-start(f32[22,128]{1,0:T(8,128)S(1)} %pad_maximum_fusion.1.refs_6_), channel_id=1, source_target_pairs={{0,1},{1,2},{2,3},{3,4},{4,5},{5,6},{6,7},{8,9},{9,10},{10,11},{11... | collective-permute-start | bytes 33800 | tf_op jit(solution)/shard_map/ppermute | solution.py:847
  6.5 3.6 %collective-permute-start.1 = (f32[22,128]{1,0:T(8,128)S(1)}, f32[22,128]{1,0:T(8,128)S(1)}, u32[]{:S(2)}, u32[]{:S(2)}) collective-permute-start(f32[22,128]{1,0:T(8,128)S(1)} %pad_maximum_fusion.2.refs_5_), channel_id=1, source_target_pairs={{1,0},{2,1},{3,2},{4,3},{5,4},{6,5},{7,6},{9,8},{10,9},{11,10},{12... | collective-permute-start | bytes 33800 | tf_op jit(solution)/shard_map/ppermute | solution.py:848
  11.2 4.8 %sky.2 = bf16[512,512]{1,0:T(8,128)(2,1)} custom-call(f32[128,128]{1,0:T(8,128)S(1)} %copy-done.4, bf16[4,9,128,128]{3,2,1,0:T(8,128)(2,1)S(1)} %copy-done, f32[256,256]{1,0:T(8,128)S(1)} %copy-done.2, bf16[4,9,256,256]{3,2,1,0:T(8,128)(2,1)} %refs_4_.5, f32[512,512]{1,0:T(8,128)S(1)} %copy-done.1), custom_call_target="tpu_custom_call" | custom-call | tf_op jit(solution)/shard_map/sky/pallas_call | solution.py:348
  16.0 2.6 %collective-permute-start.8 = (bf16[512,512]{1,0:T(8,128)(2,1)}, bf16[512,512]{1,0:T(8,128)(2,1)S(1)}, u32[]{:S(2)}, u32[]{:S(2)}) collective-permute-start(bf16[512,512]{1,0:T(8,128)(2,1)} %sky.2), channel_id=1, source_target_pairs={{0,4},{1,5},{2,6},{3,7},{4,0},{5,1},{6,2},{7,3},{8,12},{9,13},{10,... | collective-permute-start | bytes 1572872 | tf_op jit(solution)/shard_map/ppermute | solution.py:819
  20.3 1.5 %sides.1 = (f32[22,132]{1,0:T(8,128)}, f32[22,132]{1,0:T(8,128)}) custom-call(f32[22,128]{1,0:T(8,128)} %copy-done.12, f32[22,128]{1,0:T(8,128)} %copy-done.14, f32[22,128]{1,0:T(8,128)} %get-tuple-element.157.first_side, f32[22,128]{1,0:T(8,128)} %get-tuple-element.158.last_side), custom_call_target="tpu_custom_call" | custom-call | flops 40000000000 | bytes 64000000 | tf_op jit(solution)/shard_map/sides/pallas_call | solution.py:325
  21.9 3.4 %collective-permute-start.2 = (f32[22,132]{1,0:T(8,128)}, f32[22,132]{1,0:T(8,128)S(1)}, u32[]{:S(2)}, u32[]{:S(2)}) collective-permute-start(f32[22,132]{1,0:T(8,128)} %get-tuple-element.78), channel_id=1, source_target_pairs={{0,8},{8,16},{16,24},{1,9},{9,17},{17,25},{2,10},{10,18},{18,26},{... | collective-permute-start | bytes 34856 | tf_op jit(solution)/shard_map/ppermute | solution.py:334
  25.2 2.4 %collective-permute-start.3 = (f32[22,132]{1,0:T(8,128)}, f32[22,132]{1,0:T(8,128)S(1)}, u32[]{:S(2)}, u32[]{:S(2)}) collective-permute-start(f32[22,132]{1,0:T(8,128)} %get-tuple-element.79), channel_id=1, source_target_pairs={{8,0},{16,8},{24,16},{9,1},{17,9},{25,17},{10,2},{18,10},{26,18},{... | collective-permute-start | bytes 34856 | tf_op jit(solution)/shard_map/ppermute | solution.py:334
  27.9 4.1 %collective-permute-done.3.refs_2_.refs_7_ = f32[22,132]{1,0:T(8,128)S(1)} collective-permute-done((f32[22,132]{1,0:T(8,128)}, f32[22,132]{1,0:T(8,128)S(1)}, u32[]{:S(2)}, u32[]{:S(2)}) %collective-permute-start.3) | collective-permute-done | bytes 11648 | tf_op jit(solution)/shard_map/ppermute | solution.py:334
  33.5 4.6 %sky.3 = (bf16[512,512]{1,0:T(8,128)(2,1)S(1)}, bf16[32,512]{1,0:T(8,128)(2,1)S(1)}, f32[8,128]{1,0:T(8,128)S(1)}, f32[22,132]{1,0:T(8,128)S(1)}, f32[22,132]{1,0:T(8,128)S(1)}) custom-call(f32[128,128]{1,0:T(8,128)S(1)} %copy-done.4, f32[22,132]{1,0:T(8,128)S(1)} %collective-permute-done.2.refs_1_.refs_6_, ...), custom_call_target="tpu_custom_call" | custom-call | tf_op jit(solution)/shard_map/sky/pallas_call | solution.py:348
  40.6 3.5 %collective-permute-start.5 = (bf16[32,512]{1,0:T(8,128)(2,1)S(1)}, bf16[32,512]{1,0:T(8,128)(2,1)S(1)}, u32[]{:S(2)}, u32[]{:S(2)}) collective-permute-start(bf16[32,512]{1,0:T(8,128)(2,1)S(1)} %get-tuple-element.81), channel_id=1, source_target_pairs={{0,4},{1,5},{2,6},{3,7},{4,0},{5,1},{6,2},{7,3},{8,12},{9,13},{10,... | collective-permute-start | bytes 98312 | tf_op jit(solution)/shard_map/ppermute | solution.py:819
  44.7 1.6 %collective-permute-done.5 = bf16[32,512]{1,0:T(8,128)(2,1)S(1)} collective-permute-done((bf16[32,512]{1,0:T(8,128)(2,1)S(1)}, bf16[32,512]{1,0:T(8,128)(2,1)S(1)}, u32[]{:S(2)}, u32[]{:S(2)}) %collective-permute-start.5) | collective-permute-done | bytes 32800 | tf_op jit(solution)/shard_map/ppermute | solution.py:819
  46.3 1.7 %collective-permute-done.4 = bf16[32,512]{1,0:T(8,128)(2,1)S(1)} collective-permute-done((bf16[32,512]{1,0:T(8,128)(2,1)S(1)}, bf16[32,512]{1,0:T(8,128)(2,1)S(1)}, u32[]{:S(2)}, u32[]{:S(2)}) %collective-permute-start.4) | collective-permute-done | bytes 32800 | tf_op jit(solution)/shard_map/ppermute | solution.py:819
  48.0 1.9 %collective-permute-start.10 = (bf16[512,512]{1,0:T(8,128)(2,1)}, bf16[512,512]{1,0:T(8,128)(2,1)S(1)}, u32[]{:S(2)}, u32[]{:S(2)}) collective-permute-start(bf16[512,512]{1,0:T(8,128)(2,1)} %copy-done.5), channel_id=1, source_target_pairs={{2,4},{3,5},{4,2},{5,3},{10,12},{11,13},{12,10},{13,11},{18,20},{1... | collective-permute-start | bytes 1572872 | tf_op jit(solution)/shard_map/ppermute | solution.py:819
  52.8 7.1 %collective-permute-done.10.refs_3_ = bf16[512,512]{1,0:T(8,128)(2,1)S(1)} collective-permute-done((bf16[512,512]{1,0:T(8,128)(2,1)}, bf16[512,512]{1,0:T(8,128)(2,1)S(1)}, u32[]{:S(2)}, u32[]{:S(2)}) %collective-permute-start.10) | collective-permute-done | bytes 524320 | tf_op jit(solution)/shard_map/ppermute | solution.py:819
  63.6 10.0 %facets.1.mine = bf16[1056,512]{1,0:T(8,128)(2,1)S(1)} custom-call(s32[2,5]{1,0:T(2,128)S(1)} %pad_add_fusion.ints, f32[2,2]{1,0:T(2,128)S(1)} %bitcast.14, bf16[512,512]{1,0:T(8,128)(2,1)S(1)} %copy-done.6, bf16[512,512]{1,0:T(8,128)(2,1)} %collective-permute-done.7.refs_1_, bf16[512,512]{1,0:T(8,128)(2,1)S(1)} %collective-permute-done.8.refs_2_, ...), custom_call_target="tpu_custom_call" | custom-call | tf_op jit(solution)/shard_map/facets/pallas_call | solution.py:745
  73.7 2.1 %collective-permute-start.18 = (bf16[1056,512]{1,0:T(8,128)(2,1)S(1)}, bf16[1056,512]{1,0:T(8,128)(2,1)S(1)}, u32[]{:S(2)}, u32[]{:S(2)}) collective-permute-start(bf16[1056,512]{1,0:T(8,128)(2,1)S(1)} %facets.1.mine), channel_id=1, source_target_pairs={{0,1},{1,0},{2,3},{3,2},{4,5},{5,4},{6,7},{7,6},{8,9},{9,8},{10,11... | collective-permute-start | bytes 3244040 | tf_op jit(solution)/shard_map/ppermute | solution.py:827
  75.8 2.3 %collective-permute-done.18.theirs = bf16[1056,512]{1,0:T(8,128)(2,1)S(1)} collective-permute-done((bf16[1056,512]{1,0:T(8,128)(2,1)S(1)}, bf16[1056,512]{1,0:T(8,128)(2,1)S(1)}, u32[]{:S(2)}, u32[]{:S(2)}) %collective-permute-start.18) | collective-permute-done | bytes 1081376 | tf_op jit(solution)/shard_map/ppermute | solution.py:827
  82.9 2.1 %mixed.3 = (bf16[512,512]{1,0:T(8,128)(2,1)S(1)}, bf16[512,512]{1,0:T(8,128)(2,1)S(1)}, bf16[512,512]{1,0:T(8,128)(2,1)S(1)}, bf16[512,512]{1,0:T(8,128)(2,1)S(1)}) custom-call(f32[4,4]{1,0:T(4,128)S(1)} %gather_fusion, bf16[1056,512]{1,0:T(8,128)(2,1)S(1)} %facets.1.mine, bf16[1056,512]{1,0:T(8,128)(2,1)S(1)} %collective-permute-done.18.theirs), custom_call_target="tpu_custom_call" | custom-call | tf_op jit(solution)/shard_map/mixed/pallas_call | solution.py:802
  85.9 2.5 %collective-permute-start.20 = (bf16[512,512]{1,0:T(8,128)(2,1)S(1)}, bf16[512,512]{1,0:T(8,128)(2,1)S(1)}, u32[]{:S(2)}, u32[]{:S(2)}) collective-permute-start(bf16[512,512]{1,0:T(8,128)(2,1)S(1)} %get-tuple-element.99), channel_id=1, source_target_pairs={{2,4},{3,5},{4,2},{5,3},{10,12},{11,13},{12,10},{13,11},{18,20},{1... | collective-permute-start | bytes 1572872 | tf_op jit(solution)/shard_map/ppermute | solution.py:819
  90.4 5.6 %adjoint.2 = (f32[8,384]{1,0:T(8,128)}, f32[8,384]{1,0:T(8,128)}, f32[8,384]{1,0:T(8,128)}, f32[8,384]{1,0:T(8,128)}, f32[8,128]{1,0:T(8,128)}) custom-call(bf16[64,512]{1,0:T(8,128)(2,1)} %copy-done.17, bf16[64,512]{1,0:T(8,128)(2,1)} %copy-done.29, bf16[64,512]{1,0:T(8,128)(2,1)} %copy-done.30, bf16[64,512]{1,0:T(8,128)(2,1)} %copy-done.31, ...), custom_call_target="tpu_custom_call" | custom-call | flops 40000000000 | bytes 64000000 | tf_op jit(solution)/shard_map/adjoint/pallas_call | solution.py:609
  96.0 5.1 %collective-permute-done.20.refs_3_ = bf16[512,512]{1,0:T(8,128)(2,1)S(1)} collective-permute-done((bf16[512,512]{1,0:T(8,128)(2,1)S(1)}, bf16[512,512]{1,0:T(8,128)(2,1)S(1)}, u32[]{:S(2)}, u32[]{:S(2)}) %collective-permute-start.20) | collective-permute-done | bytes 524320 | tf_op jit(solution)/shard_map/ppermute | solution.py:819
  101.1 2.3 %collective-permute-done.19 = bf16[512,512]{1,0:T(8,128)(2,1)S(1)} collective-permute-done((bf16[512,512]{1,0:T(8,128)(2,1)S(1)}, bf16[512,512]{1,0:T(8,128)(2,1)S(1)}, u32[]{:S(2)}, u32[]{:S(2)}) %collective-permute-start.19) | collective-permute-done | bytes 524320 | tf_op jit(solution)/shard_map/ppermute | solution.py:819
  103.9 2.5 %collective-permute-start.24 = (bf16[512,512]{1,0:T(8,128)(2,1)S(1)}, bf16[512,512]{1,0:T(8,128)(2,1)S(1)}, u32[]{:S(2)}, u32[]{:S(2)}) collective-permute-start(bf16[512,512]{1,0:T(8,128)(2,1)S(1)} %get-tuple-element.119), channel_id=1, source_target_pairs={{0,2},{1,3},{2,0},{3,1},{4,6},{5,7},{6,4},{7,5},{8,10},{9,11},{10,... | collective-permute-start | bytes 1572872 | tf_op jit(solution)/shard_map/ppermute | solution.py:819
  106.4 2.0 %collective-permute-start.26 = (f32[8,384]{1,0:T(8,128)S(1)}, f32[8,384]{1,0:T(8,128)S(1)}, u32[]{:S(2)}, u32[]{:S(2)}) collective-permute-start(f32[8,384]{1,0:T(8,128)S(1)} %copy-done.33), channel_id=1, source_target_pairs={{0,8},{8,16},{16,24},{1,9},{9,17},{17,25},{2,10},{10,18},{18,26},{... | collective-permute-start | bytes 36872 | tf_op jit(solution)/shard_map/ppermute | solution.py:933
  108.5 3.8 %collective-permute-start.27 = (f32[8,384]{1,0:T(8,128)S(1)}, f32[8,384]{1,0:T(8,128)S(1)}, u32[]{:S(2)}, u32[]{:S(2)}) collective-permute-start(f32[8,384]{1,0:T(8,128)S(1)} %copy-done.32), channel_id=1, source_target_pairs={{8,0},{16,8},{24,16},{9,1},{17,9},{25,17},{10,2},{18,10},{26,18},{... | collective-permute-start | bytes 36872 | tf_op jit(solution)/shard_map/ppermute | solution.py:932
  112.4 3.6 %collective-permute-done.28.other = f32[8,128]{1,0:T(8,128)S(1)} collective-permute-done((f32[8,128]{1,0:T(8,128)S(1)}, f32[8,128]{1,0:T(8,128)S(1)}, u32[]{:S(2)}, u32[]{:S(2)}) %collective-permute-start.28) | collective-permute-done | bytes 4128 | tf_op jit(solution)/shard_map/ppermute | solution.py:930
  117.1 1.5 %corners.1 = (f32[8,384]{1,0:T(8,128)}, f32[8,384]{1,0:T(8,128)}, f32[8,128]{1,0:T(8,128)}) custom-call(f32[8,384]{1,0:T(8,128)} %get-tuple-element.123.left, f32[8,384]{1,0:T(8,128)} %get-tuple-element.124.right, f32[8,384]{1,0:T(8,128)} %copy-done.21, f32[8,384]{1,0:T(8,128)} %copy-done.22, f32[8,128]{1,0:T(8,128)} %get-tuple-element.127.total, ...), custom_call_target="tpu_custom_call" | custom-call | tf_op jit(solution)/shard_map/corners/pallas_call | solution.py:936
  118.6 1.9 %collective-permute-start.29 = (f32[8,384]{1,0:T(8,128)}, f32[8,384]{1,0:T(8,128)S(1)}, u32[]{:S(2)}, u32[]{:S(2)}) collective-permute-start(f32[8,384]{1,0:T(8,128)} %get-tuple-element.128), channel_id=1, source_target_pairs={{0,1},{1,2},{2,3},{3,4},{4,5},{5,6},{6,7},{8,9},{9,10},{10,11},{11... | collective-permute-start | bytes 36872 | tf_op jit(solution)/shard_map/ppermute | solution.py:946
  120.5 3.6 %collective-permute-start.30 = (f32[8,384]{1,0:T(8,128)}, f32[8,384]{1,0:T(8,128)S(1)}, u32[]{:S(2)}, u32[]{:S(2)}) collective-permute-start(f32[8,384]{1,0:T(8,128)} %get-tuple-element.129), channel_id=1, source_target_pairs={{1,0},{2,1},{3,2},{4,3},{5,4},{6,5},{7,6},{9,8},{10,9},{11,10},{12... | collective-permute-start | bytes 36872 | tf_op jit(solution)/shard_map/ppermute | solution.py:947
  125.4 2.7 %collective-permute-done.31.refs_18_ = f32[8,128]{1,0:T(8,128)S(1)} collective-permute-done((f32[8,128]{1,0:T(8,128)}, f32[8,128]{1,0:T(8,128)S(1)}, u32[]{:S(2)}, u32[]{:S(2)}) %collective-permute-start.31) | collective-permute-done | bytes 4128 | tf_op jit(solution)/shard_map/ppermute | solution.py:930
  129.7 7.2 %adjoint.3 = (f32[512,512]{1,0:T(8,128)}, f32[256,256]{1,0:T(8,128)}, f32[128,128]{1,0:T(8,128)}, f32[1,1]{1,0:T(1,128)}) custom-call(bf16[512,512]{1,0:T(8,128)(2,1)} %copy-done.7, bf16[512,512]{1,0:T(8,128)(2,1)} %copy-done.20, bf16[512,512]{1,0:T(8,128)(2,1)} %copy-done.19, bf16[512,512]{1,0:T(8,128)(2,1)} %copy-done.18, ...), custom_call_target="tpu_custom_call" | custom-call | tf_op jit(solution)/shard_map/adjoint/pallas_call | solution.py:609
  (146 shorter events, 27.9 us)
Async XLA Ops:
  4.2 11.8 %collective-permute-start = (f32[22,128]{1,0:T(8,128)S(1)}, f32[22,128]{1,0:T(8,128)S(1)}, u32[]{:S(2)}, u32[]{:S(2)}) collective-permute-start(f32[22,128]{1,0:T(8,128)S(1)} %pad_maximum_fusion.1.refs_6_), channel_id=1, source_target_pairs={{0,1},{1,2},{2,3},{3,4},{4,5},{5,6},{6,7},{8,9},{9,10},{10,11},{11... | collective-permute-start | bytes 33800 | tf_op jit(solution)/shard_map/ppermute | solution.py:847
  6.5 9.5 %collective-permute-start.1 = (f32[22,128]{1,0:T(8,128)S(1)}, f32[22,128]{1,0:T(8,128)S(1)}, u32[]{:S(2)}, u32[]{:S(2)}) collective-permute-start(f32[22,128]{1,0:T(8,128)S(1)} %pad_maximum_fusion.2.refs_5_), channel_id=1, source_target_pairs={{1,0},{2,1},{3,2},{4,3},{5,4},{6,5},{7,6},{9,8},{10,9},{11,10},{12... | collective-permute-start | bytes 33800 | tf_op jit(solution)/shard_map/ppermute | solution.py:848
  16.0 32.0 %collective-permute-start.8 = (bf16[512,512]{1,0:T(8,128)(2,1)}, bf16[512,512]{1,0:T(8,128)(2,1)S(1)}, u32[]{:S(2)}, u32[]{:S(2)}) collective-permute-start(bf16[512,512]{1,0:T(8,128)(2,1)} %sky.2), channel_id=1, source_target_pairs={{0,4},{1,5},{2,6},{3,7},{4,0},{5,1},{6,2},{7,3},{8,12},{9,13},{10,... | collective-permute-start | bytes 1572872 | tf_op jit(solution)/shard_map/ppermute | solution.py:819
  18.7 29.3 %collective-permute-start.7 = (bf16[512,512]{1,0:T(8,128)(2,1)}, bf16[512,512]{1,0:T(8,128)(2,1)}, u32[]{:S(2)}, u32[]{:S(2)}) collective-permute-start(bf16[512,512]{1,0:T(8,128)(2,1)} %sky.2), channel_id=1, source_target_pairs={{0,2},{1,3},{2,0},{3,1},{4,6},{5,7},{6,4},{7,5},{8,10},{9,11},{10,... | collective-permute-start | bytes 1572872 | tf_op jit(solution)/shard_map/ppermute | solution.py:819
  21.9 6.1 %collective-permute-start.2 = (f32[22,132]{1,0:T(8,128)}, f32[22,132]{1,0:T(8,128)S(1)}, u32[]{:S(2)}, u32[]{:S(2)}) collective-permute-start(f32[22,132]{1,0:T(8,128)} %get-tuple-element.78), channel_id=1, source_target_pairs={{0,8},{8,16},{16,24},{1,9},{9,17},{17,25},{2,10},{10,18},{18,26},{... | collective-permute-start | bytes 34856 | tf_op jit(solution)/shard_map/ppermute | solution.py:334
  25.2 6.8 %collective-permute-start.3 = (f32[22,132]{1,0:T(8,128)}, f32[22,132]{1,0:T(8,128)S(1)}, u32[]{:S(2)}, u32[]{:S(2)}) collective-permute-start(f32[22,132]{1,0:T(8,128)} %get-tuple-element.79), channel_id=1, source_target_pairs={{8,0},{16,8},{24,16},{9,1},{17,9},{25,17},{10,2},{18,10},{26,18},{... | collective-permute-start | bytes 34856 | tf_op jit(solution)/shard_map/ppermute | solution.py:334
  27.9 16.2 %collective-permute-start.9 = (f32[2,8]{0,1:T(8,128)S(1)}, f32[2,8]{0,1:T(8,128)S(1)}, u32[]{:S(2)}, u32[]{:S(2)}) collective-permute-start(f32[2,8]{0,1:T(8,128)S(1)} %copy.32), channel_id=1, source_target_pairs={{0,1},{1,0},{2,3},{3,2},{4,5},{5,4},{6,7},{7,6},{8,9},{9,8},{10,11... | collective-permute-start | bytes 200 | tf_op jit(solution)/shard_map/ppermute | solution.py:827
  40.1 4.6 %collective-permute-start.6 = (bf16[32,512]{1,0:T(8,128)(2,1)S(1)}, bf16[32,512]{1,0:T(8,128)(2,1)S(1)}, u32[]{:S(2)}, u32[]{:S(2)}) collective-permute-start(bf16[32,512]{1,0:T(8,128)(2,1)S(1)} %get-tuple-element.81), channel_id=1, source_target_pairs={{0,6},{1,7},{2,4},{3,5},{4,2},{5,3},{6,0},{7,1},{8,14},{9,15},{10,... | collective-permute-start | bytes 98312 | tf_op jit(solution)/shard_map/ppermute | solution.py:819
  40.6 5.7 %collective-permute-start.5 = (bf16[32,512]{1,0:T(8,128)(2,1)S(1)}, bf16[32,512]{1,0:T(8,128)(2,1)S(1)}, u32[]{:S(2)}, u32[]{:S(2)}) collective-permute-start(bf16[32,512]{1,0:T(8,128)(2,1)S(1)} %get-tuple-element.81), channel_id=1, source_target_pairs={{0,4},{1,5},{2,6},{3,7},{4,0},{5,1},{6,2},{7,3},{8,12},{9,13},{10,... | collective-permute-start | bytes 98312 | tf_op jit(solution)/shard_map/ppermute | solution.py:819
  44.1 3.9 %collective-permute-start.4 = (bf16[32,512]{1,0:T(8,128)(2,1)S(1)}, bf16[32,512]{1,0:T(8,128)(2,1)S(1)}, u32[]{:S(2)}, u32[]{:S(2)}) collective-permute-start(bf16[32,512]{1,0:T(8,128)(2,1)S(1)} %get-tuple-element.81), channel_id=1, source_target_pairs={{0,2},{1,3},{2,0},{3,1},{4,6},{5,7},{6,4},{7,5},{8,10},{9,11},{10,... | collective-permute-start | bytes 98312 | tf_op jit(solution)/shard_map/ppermute | solution.py:819
  48.0 11.9 %collective-permute-start.10 = (bf16[512,512]{1,0:T(8,128)(2,1)}, bf16[512,512]{1,0:T(8,128)(2,1)S(1)}, u32[]{:S(2)}, u32[]{:S(2)}) collective-permute-start(bf16[512,512]{1,0:T(8,128)(2,1)} %copy-done.5), channel_id=1, source_target_pairs={{2,4},{3,5},{4,2},{5,3},{10,12},{11,13},{12,10},{13,11},{18,20},{1... | collective-permute-start | bytes 1572872 | tf_op jit(solution)/shard_map/ppermute | solution.py:819
  49.9 10.0 %collective-permute-start.11 = (bf16[512,512]{1,0:T(8,128)(2,1)S(1)}, bf16[512,512]{1,0:T(8,128)(2,1)S(1)}, u32[]{:S(2)}, u32[]{:S(2)}) collective-permute-start(bf16[512,512]{1,0:T(8,128)(2,1)S(1)} %collective-permute-done.8.refs_2_), channel_id=1, source_target_pairs={{4,6},{5,7},{2,0},{3,1},{12,14},{13,15},{10,8},{11,9},{20,22},{21,... | collective-permute-start | bytes 1572872 | tf_op jit(solution)/shard_map/ppermute | solution.py:819
  51.3 1.4 collective-permute-start.17
  51.5 9.1 %collective-permute-start.12 = (bf16[512,512]{1,0:T(8,128)(2,1)}, bf16[512,512]{1,0:T(8,128)(2,1)S(1)}, u32[]{:S(2)}, u32[]{:S(2)}) collective-permute-start(bf16[512,512]{1,0:T(8,128)(2,1)} %copy-done.5), channel_id=1, source_target_pairs={{0,1},{1,0},{2,3},{3,2},{4,5},{5,4},{6,7},{7,6},{8,9},{9,8},{10,11... | collective-permute-start | bytes 1572872 | tf_op jit(solution)/shard_map/ppermute | solution.py:827
  52.0 8.6 %collective-permute-start.14 = (bf16[512,512]{1,0:T(8,128)(2,1)S(1)}, bf16[512,512]{1,0:T(8,128)(2,1)S(1)}, u32[]{:S(2)}, u32[]{:S(2)}) collective-permute-start(bf16[512,512]{1,0:T(8,128)(2,1)S(1)} %collective-permute-done.8.refs_2_), channel_id=1, source_target_pairs={{0,1},{1,0},{2,3},{3,2},{4,5},{5,4},{6,7},{7,6},{8,9},{9,8},{10,11... | collective-permute-start | bytes 1572872 | tf_op jit(solution)/shard_map/ppermute | solution.py:827
  52.6 7.9 %collective-permute-start.13 = (bf16[512,512]{1,0:T(8,128)(2,1)}, bf16[512,512]{1,0:T(8,128)(2,1)S(1)}, u32[]{:S(2)}, u32[]{:S(2)}) collective-permute-start(bf16[512,512]{1,0:T(8,128)(2,1)} %collective-permute-done.7.refs_1_), channel_id=1, source_target_pairs={{0,1},{1,0},{2,3},{3,2},{4,5},{5,4},{6,7},{7,6},{8,9},{9,8},{10,11... | collective-permute-start | bytes 1572872 | tf_op jit(solution)/shard_map/ppermute | solution.py:827
  59.9 1.9 %collective-permute-start.15 = (bf16[512,512]{1,0:T(8,128)(2,1)S(1)}, bf16[512,512]{1,0:T(8,128)(2,1)S(1)}, u32[]{:S(2)}, u32[]{:S(2)}) collective-permute-start(bf16[512,512]{1,0:T(8,128)(2,1)S(1)} %collective-permute-done.10.refs_3_), channel_id=1, source_target_pairs={{0,1},{1,0},{2,3},{3,2},{4,5},{5,4},{6,7},{7,6},{8,9},{9,8},{10,11... | collective-permute-start | bytes 1572872 | tf_op jit(solution)/shard_map/ppermute | solution.py:827
  59.9 2.7 %collective-permute-start.16 = (bf16[512,512]{1,0:T(8,128)(2,1)S(1)}, bf16[512,512]{1,0:T(8,128)(2,1)S(1)}, u32[]{:S(2)}, u32[]{:S(2)}) collective-permute-start(bf16[512,512]{1,0:T(8,128)(2,1)S(1)} %collective-permute-done.11.refs_4_), channel_id=1, source_target_pairs={{0,1},{1,0},{2,3},{3,2},{4,5},{5,4},{6,7},{7,6},{8,9},{9,8},{10,11... | collective-permute-start | bytes 1572872 | tf_op jit(solution)/shard_map/ppermute | solution.py:827
  73.7 4.5 %collective-permute-start.18 = (bf16[1056,512]{1,0:T(8,128)(2,1)S(1)}, bf16[1056,512]{1,0:T(8,128)(2,1)S(1)}, u32[]{:S(2)}, u32[]{:S(2)}) collective-permute-start(bf16[1056,512]{1,0:T(8,128)(2,1)S(1)} %facets.1.mine), channel_id=1, source_target_pairs={{0,1},{1,0},{2,3},{3,2},{4,5},{5,4},{6,7},{7,6},{8,9},{9,8},{10,11... | collective-permute-start | bytes 3244040 | tf_op jit(solution)/shard_map/ppermute | solution.py:827
  79.4 10.4 %collective-permute-start.21 = (bf16[64,512]{1,0:T(8,128)(2,1)S(1)}, bf16[64,512]{1,0:T(8,128)(2,1)S(1)}, u32[]{:S(2)}, u32[]{:S(2)}) collective-permute-start(bf16[64,512]{1,0:T(8,128)(2,1)S(1)} %get-tuple-element.104), channel_id=1, source_target_pairs={{0,2},{1,3},{2,0},{3,1},{4,6},{5,7},{6,4},{7,5},{8,10},{9,11},{10,... | collective-permute-start | bytes 196616 | tf_op jit(solution)/shard_map/ppermute | solution.py:819
  80.3 9.4 %collective-permute-start.22 = (bf16[64,512]{1,0:T(8,128)(2,1)S(1)}, bf16[64,512]{1,0:T(8,128)(2,1)S(1)}, u32[]{:S(2)}, u32[]{:S(2)}) collective-permute-start(bf16[64,512]{1,0:T(8,128)(2,1)S(1)} %get-tuple-element.105), channel_id=1, source_target_pairs={{0,4},{1,5},{2,6},{3,7},{4,0},{5,1},{6,2},{7,3},{8,12},{9,13},{10,... | collective-permute-start | bytes 196616 | tf_op jit(solution)/shard_map/ppermute | solution.py:819
  81.5 8.2 %collective-permute-start.23 = (bf16[64,512]{1,0:T(8,128)(2,1)S(1)}, bf16[64,512]{1,0:T(8,128)(2,1)S(1)}, u32[]{:S(2)}, u32[]{:S(2)}) collective-permute-start(bf16[64,512]{1,0:T(8,128)(2,1)S(1)} %get-tuple-element.106), channel_id=1, source_target_pairs={{0,6},{1,7},{2,4},{3,5},{4,2},{5,3},{6,0},{7,1},{8,14},{9,15},{10,... | collective-permute-start | bytes 196616 | tf_op jit(solution)/shard_map/ppermute | solution.py:819
  85.9 15.2 %collective-permute-start.20 = (bf16[512,512]{1,0:T(8,128)(2,1)S(1)}, bf16[512,512]{1,0:T(8,128)(2,1)S(1)}, u32[]{:S(2)}, u32[]{:S(2)}) collective-permute-start(bf16[512,512]{1,0:T(8,128)(2,1)S(1)} %get-tuple-element.99), channel_id=1, source_target_pairs={{2,4},{3,5},{4,2},{5,3},{10,12},{11,13},{12,10},{13,11},{18,20},{1... | collective-permute-start | bytes 1572872 | tf_op jit(solution)/shard_map/ppermute | solution.py:819
  88.4 15.0 %collective-permute-start.19 = (bf16[512,512]{1,0:T(8,128)(2,1)S(1)}, bf16[512,512]{1,0:T(8,128)(2,1)S(1)}, u32[]{:S(2)}, u32[]{:S(2)}) collective-permute-start(bf16[512,512]{1,0:T(8,128)(2,1)S(1)} %get-tuple-element.99), channel_id=1, source_target_pairs={{0,2},{1,3},{6,4},{7,5},{8,10},{9,11},{14,12},{15,13},{16,18},{17,... | collective-permute-start | bytes 1572872 | tf_op jit(solution)/shard_map/ppermute | solution.py:819
  103.6 24.5 %collective-permute-start.25 = (bf16[512,512]{1,0:T(8,128)(2,1)S(1)}, bf16[512,512]{1,0:T(8,128)(2,1)S(1)}, u32[]{:S(2)}, u32[]{:S(2)}) collective-permute-start(bf16[512,512]{1,0:T(8,128)(2,1)S(1)} %add_convert_fusion), channel_id=1, source_target_pairs={{0,4},{1,5},{2,6},{3,7},{4,0},{5,1},{6,2},{7,3},{8,12},{9,13},{10,... | collective-permute-start | bytes 1572872 | tf_op jit(solution)/shard_map/ppermute | solution.py:819
  103.9 24.2 %collective-permute-start.24 = (bf16[512,512]{1,0:T(8,128)(2,1)S(1)}, bf16[512,512]{1,0:T(8,128)(2,1)S(1)}, u32[]{:S(2)}, u32[]{:S(2)}) collective-permute-start(bf16[512,512]{1,0:T(8,128)(2,1)S(1)} %get-tuple-element.119), channel_id=1, source_target_pairs={{0,2},{1,3},{2,0},{3,1},{4,6},{5,7},{6,4},{7,5},{8,10},{9,11},{10,... | collective-permute-start | bytes 1572872 | tf_op jit(solution)/shard_map/ppermute | solution.py:819
  106.4 9.5 %collective-permute-start.26 = (f32[8,384]{1,0:T(8,128)S(1)}, f32[8,384]{1,0:T(8,128)S(1)}, u32[]{:S(2)}, u32[]{:S(2)}) collective-permute-start(f32[8,384]{1,0:T(8,128)S(1)} %copy-done.33), channel_id=1, source_target_pairs={{0,8},{8,16},{16,24},{1,9},{9,17},{17,25},{2,10},{10,18},{18,26},{... | collective-permute-start | bytes 36872 | tf_op jit(solution)/shard_map/ppermute | solution.py:933
  108.5 7.5 %collective-permute-start.27 = (f32[8,384]{1,0:T(8,128)S(1)}, f32[8,384]{1,0:T(8,128)S(1)}, u32[]{:S(2)}, u32[]{:S(2)}) collective-permute-start(f32[8,384]{1,0:T(8,128)S(1)} %copy-done.32), channel_id=1, source_target_pairs={{8,0},{16,8},{24,16},{9,1},{17,9},{25,17},{10,2},{18,10},{26,18},{... | collective-permute-start | bytes 36872 | tf_op jit(solution)/shard_map/ppermute | solution.py:932
  112.3 3.7 %collective-permute-start.28 = (f32[8,128]{1,0:T(8,128)S(1)}, f32[8,128]{1,0:T(8,128)S(1)}, u32[]{:S(2)}, u32[]{:S(2)}) collective-permute-start(f32[8,128]{1,0:T(8,128)S(1)} %copy-done.26), channel_id=1, source_target_pairs={{0,8},{8,0},{16,24},{24,16},{1,9},{9,1},{17,25},{25,17},{2,10},{10... | collective-permute-start | bytes 12296 | tf_op jit(solution)/shard_map/ppermute | solution.py:930
  118.6 9.5 %collective-permute-start.29 = (f32[8,384]{1,0:T(8,128)}, f32[8,384]{1,0:T(8,128)S(1)}, u32[]{:S(2)}, u32[]{:S(2)}) collective-permute-start(f32[8,384]{1,0:T(8,128)} %get-tuple-element.128), channel_id=1, source_target_pairs={{0,1},{1,2},{2,3},{3,4},{4,5},{5,6},{6,7},{8,9},{9,10},{10,11},{11... | collective-permute-start | bytes 36872 | tf_op jit(solution)/shard_map/ppermute | solution.py:946
  120.5 7.5 %collective-permute-start.30 = (f32[8,384]{1,0:T(8,128)}, f32[8,384]{1,0:T(8,128)S(1)}, u32[]{:S(2)}, u32[]{:S(2)}) collective-permute-start(f32[8,384]{1,0:T(8,128)} %get-tuple-element.129), channel_id=1, source_target_pairs={{1,0},{2,1},{3,2},{4,3},{5,4},{6,5},{7,6},{9,8},{10,9},{11,10},{12... | collective-permute-start | bytes 36872 | tf_op jit(solution)/shard_map/ppermute | solution.py:947
  124.2 3.9 %collective-permute-start.31 = (f32[8,128]{1,0:T(8,128)}, f32[8,128]{1,0:T(8,128)S(1)}, u32[]{:S(2)}, u32[]{:S(2)}) collective-permute-start(f32[8,128]{1,0:T(8,128)} %get-tuple-element.130.refs_17_), channel_id=1, source_target_pairs={{0,16},{8,24},{16,0},{24,8},{1,17},{9,25},{17,1},{25,9},{2,18},{10... | collective-permute-start | bytes 12296 | tf_op jit(solution)/shard_map/ppermute | solution.py:930
  (35 other events, 185.8 us)
